TPU v7x, 32 devices: a whole 2x2x4 slice. The times are simulated.
32 devices in a mesh: stem: 4 (over y, x), tm: 8 (over z, core).
Axes of the slice: x: 2, y: 2, z: 4, core: 2. Of those that a mesh axis runs over, the one named last changes fastest.
Arguments:
- mixture: bfloat16 [2, 1024, 1024], P(None, 'tm'), may hold values from 0 to 13
- seg_lengths: int32 [4], replicated, may hold values from 1 to 128, 256 in all
- frame_mask: int32 [1024], P('tm'), may hold values 0 or 1
- conv_first: bfloat16 [4, 16, 2, 5, 5], P('stem'), may hold values from -0.875 to 0.875
- encoder_gain_vector: float32 [4, 16], P('stem'), may hold values from 0.1 to 1.9
- shift_first: float32 [4, 16], P('stem'), may hold values from -1.75 to 1.75
- conv_second: bfloat16 [4, 32, 16, 5, 5], P('stem'), may hold values from -0.3125 to 0.3125
- gain_second: float32 [4, 32], P('stem'), may hold values from 0.1 to 1.9
- shift_second: float32 [4, 32], P('stem'), may hold values from -1.75 to 1.75
- deconv_second: bfloat16 [4, 16, 32, 5, 5], P('stem'), may hold values from -0.4375 to 0.4375
- bias_second: float32 [4, 16], P('stem'), may hold values from -1.75 to 1.75
- decoder_gain_vector: float32 [4, 16], P('stem'), may hold values from 0.1 to 1.9
- shift_third: float32 [4, 16], P('stem'), may hold values from -1.75 to 1.75
- deconv_first: bfloat16 [4, 2, 32, 5, 5], P('stem'), may hold values from -0.4375 to 0.4375
- bias_first: float32 [4, 2], P('stem'), may hold values from -3 to 3
- cotangent: bfloat16 [4, 2, 1024, 1024], P(None, None, 'tm', 'stem'), may hold values from -6 to 6
Outputs:
- estimates: bfloat16 [4, 2, 1024, 1024], P(None, None, 'tm', 'stem')
- mixture_grad: float32 [2, 1024, 1024], P(None, 'tm', 'stem')
- conv_first_grad: float32 [4, 16, 2, 5, 5], P('stem')
- gain_first_grad: float32 [4, 16], P('stem')
- shift_first_grad: float32 [4, 16], P('stem')
- conv_second_grad: float32 [4, 32, 16, 5, 5], P('stem')
- gain_second_grad: float32 [4, 32], P('stem')
- shift_second_grad: float32 [4, 32], P('stem')
- deconv_second_grad: float32 [4, 16, 32, 5, 5], P('stem')
- bias_second_grad: float32 [4, 16], P('stem')
- gain_third_grad: float32 [4, 16], P('stem')
- shift_third_grad: float32 [4, 16], P('stem')
- deconv_first_grad: float32 [4, 2, 32, 5, 5], P('stem')
- bias_first_grad: float32 [4, 2], P('stem')
Inputs may be any that keep to these rules, and one draw needn't show every extreme that they name: `seg_lengths`: they sum to 256 and the longest is 128.
All inputs are finite; a program needn't handle non-finite values. No bound on the sum of `frame_mask` on one device may be relied on, other than what follows from the above.
Results may differ from a plain program's by a relative error of at most 0.02.
Values may be sent and summed in bfloat16 or wider, within the bound.
No kernel may reach another device: no remote copies, remote signals or barrier semaphores. Data moves between devices by JAX's collectives and lax.ppermute only.
A program may use at most 448 MiB of HBM per device.

v0:
```python
import jax
import jax.numpy as jnp
from jax import lax
from jax.sharding import PartitionSpec as P

NORM_EPS = 0.001
RATIO_EPS = 1e-10
CONV_LAYOUT = ("NCHW", "OIHW", "NCHW")


def padded_2(cells, sides, width):
    for axis, dim in sides:
        count = lax.axis_size(axis)
        ends = count - 1
        head = lax.slice_in_dim(cells, 0, width, axis=dim)
        tail = lax.slice_in_dim(cells, cells.shape[dim] - width, cells.shape[dim], axis=dim)
        cells = jnp.concatenate(
            [
                lax.ppermute(tail, axis, [(i, (i + 1) % count) for i in range(ends)]),
                cells,
                lax.ppermute(head, axis, [((i + 1) % count, i) for i in range(ends)]),
            ],
            axis=dim,
        )
    return cells


def edge_flags(seg_lengths, device_index, coarse, frame_step):
    starts = 4 * (jnp.cumsum(seg_lengths, dtype=jnp.int32) - seg_lengths)
    frames = (device_index * coarse + jnp.arange(-1, coarse + 1, dtype=jnp.int32)) * (
        2 * frame_step
    )
    left_ok = 1.0 - jnp.any(frames[:, None] == starts[None, :], axis=1).astype(jnp.float32)
    right_ok = 1.0 - jnp.any((frames + 2 * frame_step)[:, None] == starts[None, :], axis=1).astype(
        jnp.float32
    )
    return (left_ok, right_ok)


def bins_down(input_values, kernel):
    return lax.conv_general_dilated(
        input_values[None],
        kernel[:, :, None, :],
        (1, 2),
        ((0, 0), (1, 2)),
        dimension_numbers=CONV_LAYOUT,
        preferred_element_type=jnp.float32,
    )[0]


def bins_up(input_values, kernel):
    return lax.conv_general_dilated(
        input_values[None],
        jnp.flip(kernel, 2)[:, :, None, :],
        (1, 1),
        ((0, 0), (3, 2)),
        lhs_dilation=(1, 2),
        dimension_numbers=CONV_LAYOUT,
        preferred_element_type=jnp.float32,
    )[0]


def bins_weight(big, small):
    coarse_bins = small.shape[2]
    padded = jnp.pad(big, ((0, 0), (0, 0), (1, 2)))
    return jnp.stack(
        [
            jnp.einsum(
                "arp,brp->ab",
                small,
                padded[:, :, offset : offset + 2 * coarse_bins : 2],
                preferred_element_type=jnp.float32,
            )
            for offset in range(5)
        ],
        2,
    )


def down_apply(padded, kernel, left_ok, right_ok, rim_width):
    row_count = padded.shape[1] - 2 * rim_width
    coarse = row_count // 2
    inner_left = left_ok[1 : coarse + 1][None, :, None]
    inner_right = right_ok[1 : coarse + 1][None, :, None]

    def frame_tap(offset):
        return padded[:, offset - 1 + rim_width : offset - 1 + rim_width + row_count : 2]

    middle = bins_down(frame_tap(1), kernel[:, :, 1]) + bins_down(frame_tap(2), kernel[:, :, 2])
    outer_left = inner_left * bins_down(frame_tap(0), kernel[:, :, 0])
    outer_right = inner_right * (
        bins_down(frame_tap(3), kernel[:, :, 3]) + bins_down(frame_tap(4), kernel[:, :, 4])
    )
    return middle + outer_left + outer_right


def up_apply(padded, kernel, left_ok, right_ok, rim_width):
    coarse = padded.shape[1] - 2 * rim_width
    inner_left = left_ok[1 : coarse + 1][None, :, None]
    inner_right = right_ok[1 : coarse + 1][None, :, None]
    current = padded[:, rim_width : rim_width + coarse]
    previous = padded[:, rim_width - 1 : rim_width - 1 + coarse]
    following = padded[:, rim_width + 1 : rim_width + 1 + coarse]
    even_rows = bins_up(current, kernel[:, :, 1]) + inner_left * bins_up(previous, kernel[:, :, 3])
    odd_rows = (
        inner_right * bins_up(following, kernel[:, :, 0])
        + bins_up(current, kernel[:, :, 2])
        + inner_left * bins_up(previous, kernel[:, :, 4])
    )
    return jnp.stack([even_rows, odd_rows], 2).reshape(
        even_rows.shape[0], 2 * coarse, even_rows.shape[2]
    )


def down_back(grad_padded, kernel, inputs, left_ok, right_ok):
    coarse = grad_padded.shape[1] - 2
    here_rows = grad_padded[:, 1 : 1 + coarse]
    before = grad_padded[:, 0:coarse] * right_ok[0:coarse].astype(jnp.bfloat16)[None, :, None]
    after_rows = (
        grad_padded[:, 2 : 2 + coarse] * left_ok[2 : coarse + 2].astype(jnp.bfloat16)[None, :, None]
    )
    flipped = jnp.swapaxes(kernel, 0, 1)
    even_rows = bins_up(here_rows, flipped[:, :, 1]) + bins_up(before, flipped[:, :, 3])
    odd_rows = (
        bins_up(after_rows, flipped[:, :, 0])
        + bins_up(here_rows, flipped[:, :, 2])
        + bins_up(before, flipped[:, :, 4])
    )
    input_grad = jnp.stack([even_rows, odd_rows], 2).reshape(
        even_rows.shape[0], 2 * coarse, even_rows.shape[2]
    )
    even_in = inputs[:, 0::2]
    odd_in = inputs[:, 1::2]
    kernel_grad = jnp.stack(
        [
            bins_weight(odd_in, after_rows),
            bins_weight(even_in, here_rows),
            bins_weight(odd_in, here_rows),
            bins_weight(even_in, before),
            bins_weight(odd_in, before),
        ],
        2,
    )
    return (input_grad, kernel_grad)


def up_back(grad_padded, kernel, inputs, left_ok, right_ok):
    coarse = inputs.shape[1]
    row_count = 2 * coarse

    def grad_row(offset):
        return grad_padded[:, offset : offset + row_count : 2]

    back_right = right_ok[0:coarse].astype(jnp.bfloat16)[None, :, None]
    ahead_left = left_ok[2 : coarse + 2].astype(jnp.bfloat16)[None, :, None]
    here_even = grad_row(2)
    here_odd = grad_row(3)
    before_odd = grad_row(1) * back_right
    after_even = grad_row(4) * ahead_left
    after_odd = grad_row(5) * ahead_left
    flipped = jnp.swapaxes(kernel, 0, 1)
    input_grad = (
        bins_down(here_even, flipped[:, :, 1])
        + bins_down(here_odd, flipped[:, :, 2])
        + bins_down(before_odd, flipped[:, :, 0])
        + bins_down(after_even, flipped[:, :, 3])
        + bins_down(after_odd, flipped[:, :, 4])
    )

    def weight_part(grad_rows):
        return jnp.swapaxes(bins_weight(grad_rows, inputs), 0, 1)

    kernel_grad = jnp.stack(
        [
            weight_part(before_odd),
            weight_part(here_even),
            weight_part(here_odd),
            weight_part(after_even),
            weight_part(after_odd),
        ],
        2,
    )
    return (input_grad, kernel_grad)


def frame_rims(input_values, rim_width):
    return padded_2(input_values, (("tm", 1),), rim_width)


def grad_rims(input_values, rim_width):
    return padded_2(input_values, (("tm", 1),), rim_width)


def moments(input_values):
    return lax.psum(input_values, "tm")


def moment_grads(input_values):
    return lax.psum(input_values, "tm")


def layer_sum(input_values):
    return lax.psum(input_values, "tm")


def local_moments(input_values, kept_row_mask):
    weighted = input_values * kept_row_mask[None, :, None]
    return (jnp.sum(weighted, axis=(1, 2)), jnp.sum(weighted * input_values, axis=(1, 2)))


def norm_forward_pass(
    input_values, first_sum, second_sum, overall_count, gain_vector, shift_vector
):
    norm_average = first_sum / overall_count
    norm_inverse_scale = lax.rsqrt(
        second_sum / overall_count - norm_average * norm_average + NORM_EPS
    )
    centered_scaled = (input_values - norm_average[:, None, None]) * norm_inverse_scale[
        :, None, None
    ]
    return (
        centered_scaled * gain_vector[:, None, None] + shift_vector[:, None, None],
        centered_scaled,
        norm_inverse_scale,
    )


def norm_backward_pass(
    output_gradient, centered_scaled, gain_vector, norm_inverse_scale, kept_row_mask, overall_count
):
    shift_part = jnp.sum(output_gradient, axis=(1, 2))
    gain_portion = jnp.sum(output_gradient * centered_scaled, axis=(1, 2))
    shift_combined, gain_combined = moment_grads((shift_part, gain_portion))
    inner_part = output_gradient - kept_row_mask[None, :, None] / overall_count * (
        shift_combined[:, None, None] + centered_scaled * gain_combined[:, None, None]
    )
    return (
        (norm_inverse_scale * gain_vector)[:, None, None] * inner_part,
        gain_combined,
        shift_combined,
    )


def silu_slope(input_values):
    logistic = jax.nn.sigmoid(input_values)
    return logistic * (1.0 + input_values * (1.0 - logistic))


def per_device(
    mixture,
    seg_lengths,
    frame_mask,
    conv_first,
    encoder_gain_vector,
    shift_first,
    conv_second,
    gain_second,
    shift_second,
    deconv_second,
    bias_second,
    decoder_gain_vector,
    shift_third,
    deconv_first,
    bias_first,
    cotangent,
):
    position = lax.axis_index("tm")
    stem_index = lax.axis_index("stem")
    frames_dev = mixture.shape[1]
    bins_all = mixture.shape[2]
    quarter = bins_all // lax.axis_size("stem")
    single_channels = conv_first.shape[1]
    left_one, right_one = edge_flags(seg_lengths, position, frames_dev // 2, 1)
    left_two, right_two = edge_flags(seg_lengths, position, frames_dev // 4, 2)
    single_keep_mask = jnp.min(frame_mask.reshape(-1, 2), axis=1).astype(jnp.float32)
    keep_two = jnp.min(frame_mask.reshape(-1, 4), axis=1).astype(jnp.float32)
    kernel_one = conv_first[0]
    kernel_two = conv_second[0]
    deconv_two = deconv_second[0]
    deconv_one = deconv_first[0]
    mix_rims = frame_rims(mixture, 2)
    pre_one = down_apply(mix_rims, kernel_one, left_one, right_one, 2)
    first_sum, second_sum = local_moments(pre_one, single_keep_mask)
    kept_counts = jnp.stack([jnp.sum(single_keep_mask), jnp.sum(keep_two)])
    first_sum, second_sum, kept_counts = moments((first_sum, second_sum, kept_counts))
    single_count = kept_counts[0] * (bins_all // 2)
    count_two = kept_counts[1] * (bins_all // 4)
    first_normalized, first_centered_scaled, first_scale_factor = norm_forward_pass(
        pre_one, first_sum, second_sum, single_count, encoder_gain_vector[0], shift_first[0]
    )
    act_one = jax.nn.silu(first_normalized).astype(jnp.bfloat16)
    act_rims = frame_rims(act_one, 2)
    pre_two = down_apply(act_rims, kernel_two, left_two, right_two, 2)
    first_sum, second_sum = moments(local_moments(pre_two, keep_two))
    second_normalized, second_centered_scaled, second_scale_factor = norm_forward_pass(
        pre_two, first_sum, second_sum, count_two, gain_second[0], shift_second[0]
    )
    act_two = jax.nn.silu(second_normalized).astype(jnp.bfloat16)
    deep_rims = frame_rims(act_two, 1)
    up_pre = up_apply(deep_rims, deconv_two, left_two, right_two, 1) + bias_second[0][:, None, None]
    rectified = jax.nn.softplus(up_pre)
    first_sum, second_sum = moments(local_moments(rectified, single_keep_mask))
    third_normalized, third_centered_scaled, third_scale_factor = norm_forward_pass(
        rectified, first_sum, second_sum, single_count, decoder_gain_vector[0], shift_third[0]
    )
    norm_low = third_normalized.astype(jnp.bfloat16)
    norm_rims = frame_rims(norm_low, 1)
    joined = jnp.concatenate([norm_low, act_one], 0)
    joined_rims = jnp.concatenate([norm_rims, act_rims[:, 1:-1]], 0)
    logits = (
        up_apply(joined_rims, deconv_one, left_one, right_one, 1) + bias_first[0][:, None, None]
    )
    sigmoids = jax.nn.sigmoid(logits)
    mask_low = sigmoids.astype(jnp.bfloat16)
    every_mask = lax.all_gather(mask_low[None], "stem", axis=0, tiled=True).astype(jnp.float32)
    every_grad = lax.all_gather(cotangent, "stem", axis=3, tiled=True).astype(jnp.float32)
    mixture_full = mixture.astype(jnp.float32)
    squares = every_mask * every_mask
    power_total = jnp.sum(squares, axis=0) + RATIO_EPS
    ratios = squares / power_total[None]
    weighted = jnp.sum(every_grad * ratios, axis=0)
    own_grad = lax.dynamic_index_in_dim(every_grad, stem_index, 0, keepdims=False)
    own_mask = mask_low.astype(jnp.float32)
    mask_grad = (
        (2.0 * own_mask * mixture_full * (own_grad - weighted) / power_total)
        .astype(jnp.bfloat16)
        .astype(jnp.float32)
    )
    ratio_part = lax.dynamic_slice_in_dim(ratios, stem_index * quarter, quarter, 3)
    mixture_part = lax.dynamic_slice_in_dim(mixture_full, stem_index * quarter, quarter, 2)
    estimates = (mixture_part[None] * ratio_part).astype(jnp.bfloat16)
    direct = lax.dynamic_slice_in_dim(weighted, stem_index * quarter, quarter, 2)
    logit_grad = mask_grad * sigmoids * (1.0 - sigmoids)
    bias_one_grad = jnp.sum(logit_grad, axis=(1, 2))
    logit_rims = grad_rims(logit_grad.astype(jnp.bfloat16), 2)
    combined_gradient, deconv_one_grad = up_back(
        logit_rims, deconv_one, joined, left_one, right_one
    )
    deconv_one_grad, bias_one_grad = layer_sum((deconv_one_grad, bias_one_grad))
    rect_grad, gain_three_grad, shift_three_grad = norm_backward_pass(
        combined_gradient[:single_channels],
        third_centered_scaled,
        decoder_gain_vector[0],
        third_scale_factor,
        single_keep_mask,
        single_count,
    )
    up_grad = rect_grad * jax.nn.sigmoid(up_pre)
    bias_two_grad = jnp.sum(up_grad, axis=(1, 2))
    up_rims = grad_rims(up_grad.astype(jnp.bfloat16), 2)
    deep_grad, deconv_two_grad = up_back(up_rims, deconv_two, act_two, left_two, right_two)
    deconv_two_grad, bias_two_grad = layer_sum((deconv_two_grad, bias_two_grad))
    pre_two_grad, gain_two_grad, shift_two_grad = norm_backward_pass(
        deep_grad * silu_slope(second_normalized),
        second_centered_scaled,
        gain_second[0],
        second_scale_factor,
        keep_two,
        count_two,
    )
    pre_two_rims = grad_rims(pre_two_grad.astype(jnp.bfloat16), 1)
    act_one_grad, conv_two_grad = down_back(pre_two_rims, kernel_two, act_one, left_two, right_two)
    conv_two_grad = layer_sum((conv_two_grad,))[0]
    activation_combined = act_one_grad + combined_gradient[single_channels:]
    pre_one_grad, gain_one_grad, shift_one_grad = norm_backward_pass(
        activation_combined * silu_slope(first_normalized),
        first_centered_scaled,
        encoder_gain_vector[0],
        first_scale_factor,
        single_keep_mask,
        single_count,
    )
    pre_one_rims = grad_rims(pre_one_grad.astype(jnp.bfloat16), 1)
    mixture_net, conv_one_grad = down_back(pre_one_rims, kernel_one, mixture, left_one, right_one)
    conv_one_grad = layer_sum((conv_one_grad,))[0]
    mixture_grad = (
        lax.psum_scatter(
            mixture_net.astype(jnp.bfloat16), "stem", scatter_dimension=2, tiled=True
        ).astype(jnp.float32)
        + direct
    )
    return (
        estimates,
        mixture_grad,
        conv_one_grad[None],
        gain_one_grad[None],
        shift_one_grad[None],
        conv_two_grad[None],
        gain_two_grad[None],
        shift_two_grad[None],
        deconv_two_grad[None],
        bias_two_grad[None],
        gain_three_grad[None],
        shift_three_grad[None],
        deconv_one_grad[None],
        bias_one_grad[None],
    )


def solution(mesh):
    in_specs = (
        P(None, "tm", None),
        P(),
        P("tm"),
        P("stem", None, None, None, None),
        P("stem", None),
        P("stem", None),
        P("stem", None, None, None, None),
        P("stem", None),
        P("stem", None),
        P("stem", None, None, None, None),
        P("stem", None),
        P("stem", None),
        P("stem", None),
        P("stem", None, None, None, None),
        P("stem", None),
        P(None, None, "tm", "stem"),
    )
    out_specs = (
        P(None, None, "tm", "stem"),
        P(None, "tm", "stem"),
        P("stem", None, None, None, None),
        P("stem", None),
        P("stem", None),
        P("stem", None, None, None, None),
        P("stem", None),
        P("stem", None),
        P("stem", None, None, None, None),
        P("stem", None),
        P("stem", None),
        P("stem", None),
        P("stem", None, None, None, None),
        P("stem", None),
    )
    return jax.shard_map(
        per_device, mesh=mesh, in_specs=in_specs, out_specs=out_specs, check_vma=False
    )
```

profile of v0, /device:TPU:0, one launch (start us, length us, event | category | flops | bytes accessed | tf_op | source)
XLA Modules:
  0.0 3839.5 jit_solution(6255756051014950849)
XLA Ops:
  393.2 32.5 fusion.144
  524.6 32.2 fusion.338
  575.2 32.0 fusion.339
  689.4 121.2 %fusion.342 = f32[1,2,64,1024]{1,0,3,2:T(1,128)} fusion(bf16[1,32,64,512]{1,0,3,2:T(2,128)(2,1)} %copy.1329, bf16[2,32,1,5]{1,0,3,2:T(2,128)(2,1)S(1)} %copy-done.199), kind=kOutput, calls=%fused_computation.597 | convolution fusion | flops 20946944 | bytes 2622080 | tf_op jit(solution)/shard_map/conv_general_dilated | solution.py:52
  810.6 121.4 %fusion.345 = f32[1,2,64,1024]{1,0,3,2:T(1,128)} fusion(bf16[1,32,64,512]{1,0,3,2:T(2,128)(2,1)} %copy.1329, bf16[2,32,1,5]{1,0,3,2:T(2,128)(2,1)S(1)} %copy-done.201), kind=kOutput, calls=%fused_computation.600 | convolution fusion | flops 20946944 | bytes 2622080 | tf_op jit(solution)/shard_map/conv_general_dilated | solution.py:52
  932.0 120.2 %fusion.344 = f32[1,2,64,1024]{1,0,3,2:T(1,128)} fusion(bf16[1,32,64,512]{1,0,3,2:T(2,128)(2,1)S(1)} %copy-done.6, bf16[2,32,1,5]{1,0,3,2:T(2,128)(2,1)S(1)} %copy-done.200), kind=kOutput, calls=%fused_computation.599 | convolution fusion | flops 20946944 | bytes 2622080 | tf_op jit(solution)/shard_map/conv_general_dilated | solution.py:52
  1052.2 120.1 %fusion.341 = f32[1,2,64,1024]{1,0,3,2:T(1,128)} fusion(bf16[1,32,64,512]{1,0,3,2:T(2,128)(2,1)S(1)} %copy-done.6, bf16[2,32,1,5]{1,0,3,2:T(2,128)(2,1)S(1)} %copy-done.204), kind=kOutput, calls=%fused_computation.596 | convolution fusion | flops 20946944 | bytes 2622080 | tf_op jit(solution)/shard_map/conv_general_dilated | solution.py:52
  1197.9 121.2 %fusion.343 = f32[1,2,64,1024]{1,0,3,2:T(1,128)} fusion(bf16[1,32,64,512]{1,0,3,2:T(2,128)(2,1)} %copy.1331, bf16[2,32,1,5]{1,0,3,2:T(2,128)(2,1)S(1)} %copy-done.198), kind=kOutput, calls=%fused_computation.598 | convolution fusion | flops 20946944 | bytes 2622080 | tf_op jit(solution)/shard_map/conv_general_dilated | solution.py:52
  1319.1 74.3 %multiply_add_fusion.1 = (f32[2,64,1,1024]{0,3,1,2:T(8,128)}, f32[2,64,1,1024]{0,3,1,2:T(8,128)}) fusion(f32[2,64,1,1024]{0,3,1,2:T(8,128)} %bitcast.854, f32[2,64,1,1024]{0,3,1,2:T(8,128)} %bitcast.851, f32[64]{0:T(128)S(1)} %copy-done.222, f32[2,64,1,1024]{0,3,1,2:T(8,128)} %bitcast.852, f32[2,64,1,1024]{0,3,1,2:T(8,128)} %bitcast.853, ...), kind=kLoop, calls=%fused_computation.4 | loop fusion | flops 786432 | bytes 3670528 | tf_op jit(solution)/shard_map/add | solution.py:104
  1393.4 44.2 %pad_maximum_fusion = f32[2,64,2,1024]{0,3,1,2:T(8,128)} fusion(f32[2,64,1,1024]{0,3,1,2:T(8,128)} %get-tuple-element.230, f32[2,64,1,1024]{0,3,1,2:T(8,128)} %get-tuple-element.229), kind=kLoop, calls=%fused_computation | loop fusion | flops 262144 | bytes 2097152 | tf_op jit(solution)/shard_map/stack | solution.py:110
  1437.6 34.3 copy.1334
  1963.1 45.4 %select_add_fusion = f32[64,8,65,32]{3,1,2,0:T(8,128)} fusion(f32[64,8,65,32]{3,1,2,0:T(8,128)} %fusion.122, f32[64,8,65,32]{3,1,2,0:T(8,128)} %fusion.119, f32[64,8,65,32]{3,1,2,0:T(8,128)} %fusion.116, f32[64,8,65,32]{3,1,2,0:T(8,128)} %fusion.113, pred[8,65]{0,1:T(8,128)(4,1)S(1)} %copy-done.160, bf16[2,64,1,7,4]{3,0,4,1,2:T(2,128)(2,1)S(1)} %slice.828, ...), kind=kOutput, calls=%fused_computation.6 | convolution fusion | flops 31707136 | bytes 21573768 | tf_op jit(solution)/shard_map/conv_general_dilated | solution.py:41
  2526.1 32.2 fusion.138
  2685.9 32.0 fusion.347
  2729.3 32.4 fusion.348
  2829.7 121.4 %fusion.349 = f32[1,2,64,1024]{1,0,3,2:T(1,128)} fusion(bf16[1,16,64,512]{1,0,3,2:T(2,128)(2,1)} %copy.1377, bf16[2,16,1,5]{1,0,3,2:T(2,128)(2,1)S(1)} %copy-done.202), kind=kOutput, calls=%fused_computation.604 | convolution fusion | flops 10473472 | bytes 1573184 | tf_op jit(solution)/shard_map/conv_general_dilated | solution.py:52
  2951.2 120.2 %fusion.351 = f32[1,2,64,1024]{1,0,3,2:T(1,128)} fusion(bf16[1,16,64,512]{1,0,3,2:T(2,128)(2,1)S(1)} %copy-done.8, bf16[2,16,1,5]{1,0,3,2:T(2,128)(2,1)S(1)} %copy-done.197), kind=kOutput, calls=%fused_computation.606 | convolution fusion | flops 10473472 | bytes 1573184 | tf_op jit(solution)/shard_map/conv_general_dilated | solution.py:52
  3110.9 134.4 %add_convert_fusion.1 = bf16[1,2,64,1024]{1,0,3,2:T(2,128)(2,1)} fusion(f32[1,2,64,1024]{1,0,3,2:T(1,128)} %fusion.349, bf16[1,16,64,512]{1,0,3,2:T(2,128)(2,1)} %copy.1378, bf16[2,16,1,5]{1,0,3,2:T(2,128)(2,1)S(1)} %copy-done.196), kind=kOutput, calls=%fused_computation.2 | convolution fusion | flops 10735616 | bytes 1835328 | tf_op jit(solution)/shard_map/conv_general_dilated | solution.py:52
  3245.3 42.8 %copy.1379 = bf16[1,2,64,1024]{3,2,1,0:T(8,128)(2,1)} copy(bf16[1,2,64,1024]{1,0,3,2:T(2,128)(2,1)} %add_convert_fusion.1) | data formatting | bytes 524288 | tf_op jit(solution)/shard_map/convert.3
  3313.5 121.7 %fusion.350 = f32[1,2,64,1024]{1,0,3,2:T(1,128)} fusion(bf16[1,16,64,512]{1,0,3,2:T(2,128)(2,1)} %copy.1380, bf16[2,16,1,5]{1,0,3,2:T(2,128)(2,1)S(1)} %copy-done.194), kind=kOutput, calls=%fused_computation.605 | convolution fusion | flops 10473472 | bytes 1573184 | tf_op jit(solution)/shard_map/conv_general_dilated | solution.py:52
  3435.1 162.8 %add_convert_fusion = bf16[1,2,64,1024]{1,0,3,2:T(2,128)(2,1)} fusion(f32[1,2,64,1024]{1,0,3,2:T(1,128)} %fusion.350, f32[1,2,64,1024]{1,0,3,2:T(1,128)} %fusion.351, bf16[1,16,64,512]{1,0,3,2:T(2,128)(2,1)S(1)} %copy-done.7, bf16[2,16,1,5]{1,0,3,2:T(2,128)(2,1)S(1)} %copy-done.195), kind=kOutput, calls=%fused_computation.1 | convolution fusion | flops 10866688 | bytes 2359616 | tf_op jit(solution)/shard_map/conv_general_dilated | solution.py:52
  3597.9 41.8 %copy.1383 = bf16[1,2,64,1024]{3,2,1,0:T(8,128)(2,1)S(1)} copy(bf16[1,2,64,1024]{1,0,3,2:T(2,128)(2,1)} %add_convert_fusion) | data formatting | bytes 524288 | tf_op jit(solution)/shard_map/convert.2
  3640.3 51.8 %copy.1418 = bf16[2,128,1024]{0,1,2:T(8,128)(2,1)} copy(bf16[2,128,1024]{2,0,1:T(2,128)(2,1)S(1)} %bitcast.877) | data formatting | bytes 1048576
  3692.2 49.6 %reshape.716 = bf16[1024,256]{1,0:T(8,128)(2,1)} reshape(bf16[1024,128,2]{2,1,0:T(8,128)(2,1)} %bitcast.849) | data formatting | bytes 1048576
  (1025 shorter events, 1978.8 us)
Async XLA Ops:
  7.2 1698.2 %all-gather.5.cloned.1.call-start = ((), (), s32[]{:S(2)}) async-start(), calls=%async_computation.2 | async-start | bytes 2621440 | tf_op jit(solution)/shard_map/all_gather | solution.py:316
  8.0 44.6 %collective-permute-start = (bf16[2,2,1024]{2,1,0:T(2,128)(2,1)S(1)}, bf16[2,2,1024]{2,1,0:T(2,128)(2,1)S(1)}, u32[]{:S(2)}, u32[]{:S(2)}) collective-permute-start(bf16[2,2,1024]{2,1,0:T(2,128)(2,1)S(1)} %get-tuple-element.195), channel_id=1, source_target_pairs={{0,1},{1,2},{2,3},{3,4},{4,5},{5,6},{6,7},{8,9},{9,10},{10,11},{11... | collective-permute-start | bytes 24584 | tf_op jit(solution)/shard_map/ppermute | solution.py:19
  10.4 42.2 %collective-permute-start.1 = (bf16[2,2,1024]{2,1,0:T(2,128)(2,1)S(1)}, bf16[2,2,1024]{2,1,0:T(2,128)(2,1)S(1)}, u32[]{:S(2)}, u32[]{:S(2)}) collective-permute-start(bf16[2,2,1024]{2,1,0:T(2,128)(2,1)S(1)} %get-tuple-element.196), channel_id=1, source_target_pairs={{1,0},{2,1},{3,2},{4,3},{5,4},{6,5},{7,6},{9,8},{10,9},{11,10},{12... | collective-permute-start | bytes 24584 | tf_op jit(solution)/shard_map/ppermute | solution.py:21
  11.7 1697.6 %all-gather.3.cloned.1.call-start = ((), (), s32[]{:S(2)}) async-start(), calls=%async_computation.1 | async-start | bytes 2621440 | tf_op jit(solution)/shard_map/all_gather | solution.py:315
  50.5 156.4 %copy-start.221 = (f32[64]{0:T(128)}, f32[64]{0:T(128)S(1)}, u32[]{:S(2)}) copy-start(f32[64]{0:T(128)S(1)} %slice.572) | copy-start | bytes 772
  50.6 156.3 %copy-start.223 = (f32[64]{0:T(128)}, f32[64]{0:T(128)S(1)}, u32[]{:S(2)}) copy-start(f32[64]{0:T(128)S(1)} %slice.575) | copy-start | bytes 772
  244.5 9.8 collective-permute-start.2
  245.8 8.5 collective-permute-start.3
  390.3 85.6 %collective-permute-start.4 = (bf16[32,1,256]{2,0,1:T(8,128)(2,1)S(1)}, bf16[32,1,256]{2,0,1:T(8,128)(2,1)S(1)}, u32[]{:S(2)}, u32[]{:S(2)}) collective-permute-start(bf16[32,1,256]{2,0,1:T(8,128)(2,1)S(1)} %get-tuple-element.194), channel_id=1, source_target_pairs={{0,1},{1,2},{2,3},{3,4},{4,5},{5,6},{6,7},{8,9},{9,10},{10,11},{11... | collective-permute-start | bytes 49160 | tf_op jit(solution)/shard_map/ppermute | solution.py:19
  391.8 84.1 %collective-permute-start.5 = (bf16[32,1,256]{2,0,1:T(8,128)(2,1)S(1)}, bf16[32,1,256]{2,0,1:T(8,128)(2,1)S(1)}, u32[]{:S(2)}, u32[]{:S(2)}) collective-permute-start(bf16[32,1,256]{2,0,1:T(8,128)(2,1)S(1)} %get-tuple-element.193), channel_id=1, source_target_pairs={{1,0},{2,1},{3,2},{4,3},{5,4},{6,5},{7,6},{9,8},{10,9},{11,10},{12... | collective-permute-start | bytes 49160 | tf_op jit(solution)/shard_map/ppermute | solution.py:21
  641.4 3.2 collective-permute-start.6
  642.7 3.1 collective-permute-start.7
  1473.2 2292.5 %reduce-scatter.4.cloned.1.call-start = ((), (), s32[]{:S(2)}) async-start(), calls=%async_computation.3 | async-start | bytes 655360
  1520.0 130.3 %copy-start.55 = (bf16[16,32,512]{2,0,1:T(8,128)(2,1)S(1)}, bf16[16,32,512]{2,0,1:T(8,128)(2,1)}, u32[]{:S(2)}) copy-start(bf16[16,32,512]{2,0,1:T(8,128)(2,1)} %get-tuple-element.172) | copy-start | bytes 1572868
  1590.4 190.4 %copy-start.207 = (bf16[64]{0:T(256)(128)(2,1)}, bf16[64]{0:T(256)(128)(2,1)S(1)}, u32[]{:S(2)}) copy-start(bf16[64]{0:T(256)(128)(2,1)S(1)} %slice.626) | copy-start | bytes 388
  1746.9 32.8 collective-permute-start.8
  1750.1 29.6 collective-permute-start.9
  2135.1 48.3 %collective-permute-start.10 = (bf16[16,2,512]{2,0,1:T(8,128)(2,1)}, bf16[16,2,512]{2,0,1:T(8,128)(2,1)}, u32[]{:S(2)}, u32[]{:S(2)}) collective-permute-start(bf16[16,2,512]{2,0,1:T(8,128)(2,1)} %get-tuple-element.179), channel_id=1, source_target_pairs={{0,1},{1,2},{2,3},{3,4},{4,5},{5,6},{6,7},{8,9},{9,10},{10,11},{11... | collective-permute-start | bytes 98312 | tf_op jit(solution)/shard_map/ppermute | solution.py:19
  2137.0 46.4 %collective-permute-start.11 = (bf16[16,2,512]{2,0,1:T(8,128)(2,1)}, bf16[16,2,512]{2,0,1:T(8,128)(2,1)}, u32[]{:S(2)}, u32[]{:S(2)}) collective-permute-start(bf16[16,2,512]{2,0,1:T(8,128)(2,1)} %get-tuple-element.180), channel_id=1, source_target_pairs={{1,0},{2,1},{3,2},{4,3},{5,4},{6,5},{7,6},{9,8},{10,9},{11,10},{12... | collective-permute-start | bytes 98312 | tf_op jit(solution)/shard_map/ppermute | solution.py:21
  2500.7 116.0 %collective-permute-start.12 = (bf16[32,1,256]{2,0,1:T(8,128)(2,1)}, bf16[32,1,256]{2,0,1:T(8,128)(2,1)}, u32[]{:S(2)}, u32[]{:S(2)}) collective-permute-start(bf16[32,1,256]{2,0,1:T(8,128)(2,1)} %get-tuple-element.188), channel_id=1, source_target_pairs={{0,1},{1,2},{2,3},{3,4},{4,5},{5,6},{6,7},{8,9},{9,10},{10,11},{11... | collective-permute-start | bytes 49160 | tf_op jit(solution)/shard_map/ppermute | solution.py:19
  2502.6 114.1 %collective-permute-start.13 = (bf16[32,1,256]{2,0,1:T(8,128)(2,1)}, bf16[32,1,256]{2,0,1:T(8,128)(2,1)S(1)}, u32[]{:S(2)}, u32[]{:S(2)}) collective-permute-start(bf16[32,1,256]{2,0,1:T(8,128)(2,1)} %get-tuple-element.187), channel_id=1, source_target_pairs={{1,0},{2,1},{3,2},{4,3},{5,4},{6,5},{7,6},{9,8},{10,9},{11,10},{12... | collective-permute-start | bytes 49160 | tf_op jit(solution)/shard_map/ppermute | solution.py:21
  2798.9 278.7 %collective-permute-start.14 = (bf16[16,1,512]{2,0,1:T(8,128)(2,1)}, bf16[16,1,512]{2,0,1:T(8,128)(2,1)}, u32[]{:S(2)}, u32[]{:S(2)}) collective-permute-start(bf16[16,1,512]{2,0,1:T(8,128)(2,1)} %get-tuple-element.177), channel_id=1, source_target_pairs={{0,1},{1,2},{2,3},{3,4},{4,5},{5,6},{6,7},{8,9},{9,10},{10,11},{11... | collective-permute-start | bytes 49160 | tf_op jit(solution)/shard_map/ppermute | solution.py:19
  2800.8 277.5 %collective-permute-start.15 = (bf16[16,1,512]{2,0,1:T(8,128)(2,1)}, bf16[16,1,512]{2,0,1:T(8,128)(2,1)}, u32[]{:S(2)}, u32[]{:S(2)}) collective-permute-start(bf16[16,1,512]{2,0,1:T(8,128)(2,1)} %get-tuple-element.178), channel_id=1, source_target_pairs={{1,0},{2,1},{3,2},{4,3},{5,4},{6,5},{7,6},{9,8},{10,9},{11,10},{12... | collective-permute-start | bytes 49160 | tf_op jit(solution)/shard_map/ppermute | solution.py:21
  3741.8 82.4 %all-reduce.23.cloned.1.call-start = ((), (), s32[]{:S(2)}) async-start(), calls=%async_computation.4 | async-start | bytes 923648 | tf_op jit(solution)/shard_map/psum | solution.py:203
  (241 other events, 6196.0 us)
Sparse Core Ops, SparseCore 0:
  11.8 39.7 all-gather.4
  1473.4 34.4 all-gather.2
  3741.9 23.7 reduce-scatter.3
  3769.8 54.4 all-reduce.22
where the time goes:
time: 3860 us; the launch traced here: 3840 us
  matrix products  1890 us (49%)
  local copies, waits for them, and re-layouts  1540 us (40%)
  other arithmetic  220 us (6%)
  blocking collectives  92.9 us (2%)
  waiting for transfers between devices  48.8 us (1%)
    conv_general_dilated x20, matrix products, bins_up(): lax.conv_general_dilated(input_values[None], jnp.flip(kernel, 2)[:, :, No...  1580 us
    slice x70, local copies, waits for them, and re-layouts, bins_weight(): padded[:, :, offset:offset + 2 * coarse_bins:2]  616 us
    conv_general_dilated x20, matrix products, bins_down(): lax.conv_general_dilated(input_values[None], kernel[:, :, None, :], (1, 2...  251 us
    conv_general_dilated x67, local copies, waits for them, and re-layouts, bins_down(): lax.conv_general_dilated(input_values[None], kernel[:, :, None, :], (1, 2...  196 us
    broadcast_in_dim x11, local copies, waits for them, and re-layouts, bins_up(): input_values[None]  169 us
    unnamed x515, local copies, waits for them, and re-layouts  142 us
    conv_general_dilated x10, local copies, waits for them, and re-layouts, bins_up(): lax.conv_general_dilated(input_values[None], jnp.flip(kernel, 2)[:, :, No...  108 us
    another operation x2, local copies, waits for them, and re-layouts  84.5 us
  transfers between devices with their start and end apart: 20, of which 3 were waited for; matrix products, arithmetic and copies ran while one was open for 55% of the time, Pallas kernels for 0%

commit v1 on v0

v1 whole, which is shorter than its diff:
```python
import jax
import jax.numpy as jnp
from jax import lax
from jax.experimental import pallas as pl
from jax.experimental.pallas import tpu as pltpu
from jax.sharding import PartitionSpec as P

NORM_EPS = 0.001
RATIO_EPS = 1e-10
BF = jnp.bfloat16
F32 = jnp.float32
TAPS = 5
L = 128
M = 32
NJ = 32
R = M * NJ
CHUNK = 256
COLS0 = 1024
COLS1 = 1920
COLS1B = 1536
COLS2 = 1152
GROUPS1 = ((0, 1), (256, 2), (512, 0), (768, 3), (1024, 4))
FULL = pl.BlockSpec(memory_space=pltpu.VMEM)
SCALAR = pl.BlockSpec(memory_space=pltpu.SMEM)


def lane(shape):
    return lax.broadcasted_iota(jnp.int32, shape, 1)


def sub(shape):
    return lax.broadcasted_iota(jnp.int32, shape, 0)


def rows(j, count=M):
    return pl.ds(pl.multiple_of(j * count, count), count)


def run(kernel, name, outs, args, scratch=(), scalars=0, flops=0):
    bytes_all = sum(a.size * a.dtype.itemsize for a in args)
    shapes = [jax.ShapeDtypeStruct(s, d) for s, d in outs]
    bytes_all += sum(s.size * s.dtype.itemsize for s in shapes)
    return pl.pallas_call(
        kernel,
        out_shape=shapes,
        in_specs=[SCALAR] * scalars + [FULL] * (len(args) - scalars),
        out_specs=[FULL] * len(outs),
        scratch_shapes=[pltpu.VMEM(s, d) for s, d in scratch],
        compiler_params=pltpu.CompilerParams(vmem_limit_bytes=48 << 20),
        cost_estimate=pl.CostEstimate(flops=flops, bytes_accessed=bytes_all, transcendentals=0),
        name=name,
    )(*args)


def for_blocks(fn, count=NJ):
    def body(j, carry):
        fn(j)
        return carry

    lax.fori_loop(0, count, body, 0)


def for_blocks_rims(fn):
    def body(j, carry):
        fn(j, True, True)
        return carry

    fn(0, False, True)
    lax.fori_loop(1, NJ - 1, body, 0)
    fn(NJ - 1, True, False)


def from_prev(value, rim, flag):
    rim = jnp.concatenate([rim] * (M // 8), axis=0)
    return jnp.where(sub(value.shape) == 0, rim, pltpu.roll(value, 1, 0)) * flag


def from_next(value, rim, flag):
    rim = jnp.concatenate([rim] * (M // 8), axis=0)
    return jnp.where(sub(value.shape) == M - 1, rim, pltpu.roll(value, M - 1, 0)) * flag


def widen(source, out):
    def group(g):
        for k in range(source.shape[1] // L):
            at = slice(L * k, L * k + L)
            tile = source[rows(g, 8), at]
            for i in range(8):
                out[rows(8 * g + i, 8), at] = jnp.broadcast_to(tile[i : i + 1], (8, L))

    for_blocks(group, NJ // 8)


def mask_bf(cond):
    return jnp.where(cond, 1.0, 0.0).astype(BF)


def fill_rims(cat, parts, low, high):
    def one(j, has_prev, has_next):
        for target, after, before in parts:
            value = None
            if has_next:
                value = cat[rows(j + 1), after : after + L] * low
            if has_prev:
                other = cat[rows(j - 1), before : before + L] * high
                value = other if value is None else value + other
            cat[rows(j), target : target + L] = value

    for_blocks_rims(one)


def rims_1(cat, groups, base):
    at = lane((M, L))
    fill_rims(
        cat,
        [(base + L * k, g, g + L) for k, g in enumerate(groups)],
        mask_bf(at < 32),
        mask_bf(at >= 112),
    )


def rims_2(cat):
    at = lane((M, L))
    fill_rims(
        cat,
        [(768 + L * k, 256 * k, 256 * k + L) for k in range(3)],
        mask_bf(at < 32),
        mask_bf(at >= 96),
    )


def rims_0(cat):
    at = lane((M, L)) % 32
    fill_rims(cat, [(512 + L * k, L * k, L * k) for k in range(4)], mask_bf(at < 2), mask_bf(at == 31))


def matmul(left, right, transposed=False):
    return lax.dot_general(
        left, right, (((1,), (1 if transposed else 0,)), ((), ())), preferred_element_type=F32
    )


def for_chunks(fn, size=CHUNK):
    def body(r, carry):
        fn(pl.ds(pl.multiple_of(r * size, size), size))
        return carry

    lax.fori_loop(0, R // size, body, 0)


def sum8(value):
    total = value[0:8]
    for k in range(1, value.shape[0] // 8):
        total = total + value[8 * k : 8 * k + 8]
    return total


def fold(stats, period):
    step = L // 2
    while step >= period:
        stats = stats + pltpu.roll(stats, step, 1)
        step //= 2
    return stats


def stack_rows(values):
    at = sub((8, L))
    tile = jnp.zeros((8, L), F32)
    for k, value in enumerate(values):
        tile = jnp.where(at == k, value, tile)
    return tile


def total_rows(value):
    return jnp.sum(value, axis=0, keepdims=True)


def norm_terms(moments, count):
    mean = moments[0:1] / count
    return mean, lax.rsqrt(moments[1:2] / count - mean * mean + NORM_EPS)


def silu(v):
    return v / (1.0 + jnp.exp(-v))


def silu_slope(v):
    s = 1.0 / (1.0 + jnp.exp(-v))
    return s * (1.0 + v * (1.0 - s))


def softplus(v):
    return jnp.maximum(v, 0.0) + jnp.log1p(jnp.exp(-jnp.abs(v)))


def softplus_slope(r):
    return jnp.where(r < 0.05, r * (1.0 - r * (0.5 - r * (1.0 / 6.0))), 1.0 - jnp.exp(-r))


def tile_2(w, tap, q, half):
    at = lane((16, L)) // 32
    tile = jnp.zeros((16, L), F32)
    for k in range(4):
        b = q - 2 * (4 * half + k) + 1
        if 0 <= b < TAPS:
            start = (tap * TAPS + b) * 16
            tile = jnp.where(at == k, w[start : start + 16, :], tile)
    return tile.astype(BF)


def matrix_2_down(w, t):
    zero = jnp.zeros((16, L), BF)
    for k, (base, tap) in enumerate(GROUPS1):
        for half in range(2):
            at = slice(L * half, L * half + L)
            for q in range(16):
                t[base + 16 * q : base + 16 * q + 16, at] = tile_2(w, tap, q, half)
            for part in range(8):
                q = {0: 16, 1: 17, 7: -1}.get(part)
                start = 1280 + L * k + 16 * part
                t[start : start + 16, at] = zero if q is None else tile_2(w, tap, q, half)


def matrix_2_up(w, t):
    zero = jnp.zeros((16, L), BF)
    at = lane((16, L))
    for row in range(2):
        for k, tap in enumerate((row + 1, row + 3, row - 1)):
            for q in range(16):
                span = slice(row * 256 + q * 16, row * 256 + q * 16 + 16)
                for half in range(2):
                    cols = slice(256 * k + L * half, 256 * k + L * half + L)
                    t[span, cols] = tile_2(w, tap, q, half) if 0 <= tap < TAPS else zero
                rim = zero
                if 0 <= tap < TAPS and q in (0, 1, 15):
                    b = {0: 3, 1: 4, 15: 0}[q]
                    start = (tap * TAPS + b) * 16
                    cond = at < 32 if q == 15 else at >= 96
                    rim = jnp.where(cond, w[start : start + 16, :], 0.0).astype(BF)
                t[span, 768 + L * k : 768 + L * k + L] = rim


def band(w, tap, channel, offset):
    tile = jnp.zeros((32, L), F32)
    for b in range(TAPS):
        start = (tap * 2 + channel) * TAPS + b
        tile = jnp.where(offset == b, w[start : start + 1, :], tile)
    return tile.astype(BF)


def matrix_1_down(w, t, col):
    q, zero = sub((32, L)), jnp.zeros((32, L), BF)
    for half in range(2):
        p = 8 * half + lane((32, L)) // 16
        inner = q - 2 * p + 1
        rim = jnp.where(q == 31, -2 * p, jnp.where(q == 0, 33 - 2 * p, jnp.where(q == 1, 34 - 2 * p, -9)))
        for row in range(2):
            cols = slice(col + row * 256 + half * L, col + row * 256 + half * L + L)
            for part, frame in enumerate((0, 1, 2, 3, None, -1, 4, 5)):
                tap = -1 if frame is None else frame - 2 * row + 1
                for c in range(2):
                    start = part * 64 + c * 32
                    ok = 0 <= tap < TAPS
                    t[start : start + 32, cols] = band(w, tap, c, inner) if ok else zero
                    t[512 + start : 544 + start, cols] = band(w, tap, c, rim) if ok else zero


def matrix_1_up(w, t, col):
    q, zero = sub((32, L)), jnp.zeros((32, L), BF)
    at = lane((32, L))
    rim = jnp.where(at < 16, q - 31, jnp.where(at >= 112, q + 3, -9))
    for frame in range(4):
        taps = (frame + 1, frame - 1, frame + 3, frame - 3)
        for c in range(2):
            span = slice(frame * 64 + c * 32, frame * 64 + c * 32 + 32)
            for k, tap in enumerate(taps):
                ok = 0 <= tap < TAPS
                for half in range(2):
                    p = 8 * half + at // 16
                    start = col + 256 * k + L * half
                    t[span, start : start + L] = band(w, tap, c, q - 2 * p + 1) if ok else zero
                start = col + 1024 + L * k
                t[span, start : start + L] = band(w, tap, c, rim) if ok else zero


def matrices_first(w1c, t1a):
    matrix_1_down(w1c, t1a, 0)


def matrices_forward(w2c, w2d, w1d, t2a_c, t2b_d, t1b_d):
    matrix_2_down(w2c, t2a_c)
    matrix_2_up(w2d, t2b_d)
    matrix_1_up(w1d.at[0], t1b_d, 0)
    matrix_1_up(w1d.at[1], t1b_d, COLS1B)


def matrices_back(w1c, w2c, w2d, w1d, t1a_d, t2a_d, t2b_c, t1b_c):
    matrix_1_down(w1d.at[0], t1a_d, 0)
    matrix_1_down(w1d.at[1], t1a_d, 512)
    matrix_2_down(w2d, t2a_d)
    matrix_2_up(w2c, t2b_c)
    matrix_1_up(w1c, t1b_c, 0)


def correlate(coarse, fine, d):
    def part(rs, first):
        value = lax.dot_general(
            coarse(rs), fine[rs, :], (((0,), (0,)), ((), ())), preferred_element_type=F32
        )
        d[...] = value if first else d[...] + value

    part(pl.ds(0, CHUNK), True)

    def body(r, carry):
        part(pl.ds(pl.multiple_of(r * CHUNK, CHUNK), CHUNK), False)
        return carry

    lax.fori_loop(1, R // CHUNK, body, 0)


def weight_2(d, out):
    at = lane((32, L))
    for k, (base, tap) in enumerate(GROUPS1):
        total = jnp.zeros((32, L), F32)
        for p in range(8):
            span = slice(32 * p, 32 * p + 32)
            tiles = [d[span, base : base + L], d[span, base + L : base + 256]]
            tiles.append(d[span, 1280 + L * k : 1280 + L * k + L])
            if p == 0:
                value = jnp.where(at < 16, pltpu.roll(tiles[2], 16, 1), pltpu.roll(tiles[0], 16, 1))
            else:
                which, off = divmod(32 * p - 16, L)
                value = pltpu.roll(tiles[which], L - off, 1)
                if off + 80 > L:
                    value = jnp.where(at < L - off, value, pltpu.roll(tiles[which + 1], L - off, 1))
            total = total + value
        out[tap * 32 : tap * 32 + 32, :] = total


def weight_1(d, out, start):
    at = lane((16, L)) % 32
    sums = [jnp.zeros((16, L), F32) for _ in range(3)]
    for row in range(2):
        for k, tile in enumerate((2, 0, 1) if row == 0 else (0, 1, 3)):
            for p in range(16):
                first = row * 256 + p * 16
                span = slice(first, first + 16)
                value = pltpu.roll(d[span, L * tile : L * tile + L], (1 - 2 * p) % L, 1)
                if p in (0, 15):
                    rim = d[span, 512 + L * tile : 512 + L * tile + L]
                    rim = pltpu.roll(rim, L - 31 if p == 0 else 3, 1)
                    value = jnp.where(at == 0 if p == 0 else at >= 3, rim, value)
                sums[k] = sums[k] + value
    for k in range(3):
        out[start + 16 * k : start + 16 * k + 16, :] = sums[k]


def weight_2_kernel(coarse, fine, out, d):
    correlate(lambda rs: coarse[rs, :], fine, d)
    weight_2(d, out)


def weight_1_first(coarse, fine, out, d):
    correlate(lambda rs: coarse[rs, :], fine, d)
    weight_1(d, out, 0)


def weight_1_joined(low, cat1, fine, out, d):
    correlate(lambda rs: low[rs, :], fine, d)
    weight_1(d, out, 0)
    correlate(lambda rs: cat1[rs, 0:512], fine, d)
    weight_1(d, out, 48)


def spread(scr, store):
    at = lane((M, L)) // 32
    for half in range(2):
        parts = [scr[k % 2, pl.ds(2 * half + k // 2, M, stride=4), :] for k in range(4)]
        for block in range(4):
            value = parts[block]
            for k in range(4):
                if k != block:
                    value = jnp.where(at == k, pltpu.roll(parts[k], (32 * (k - block)) % L, 1), value)
            store(block, half, value)


def gather(blocks, scr):
    at = lane((M, L)) // 32
    for half in range(2):
        parts = [blocks(block, half) for block in range(4)]
        for k in range(4):
            value = parts[k]
            for block in range(4):
                if block != k:
                    value = jnp.where(
                        at == block, pltpu.roll(parts[block], (32 * (block - k)) % L, 1), value
                    )
            scr[k % 2, pl.ds(2 * half + k // 2, M, stride=4), :] = value


def layout_kernel(mix, cot, aux, x0, c0, first, last, scr, wide, ends):
    def place(out, block, row):
        def store(k, half, value):
            at = slice(L * half, L * half + L)
            out[rows(block + k), at] = value.astype(BF)
            wide[rows(row + k), at] = value

        return store

    def mix_tile(t):
        for c in range(2):
            scr[c] = mix[c, :, pl.ds(pl.multiple_of(t * L, L), L)].astype(F32)
        spread(scr, place(x0, 4 * t, 4 * t))

    for_blocks(mix_tile, NJ // 4)
    tiles = cot.shape[3] // L

    def cot_tile(t):
        for c in range(2):
            scr[c] = cot[t // tiles, c, :, pl.ds(pl.multiple_of((t % tiles) * L, L), L)].astype(F32)
        spread(scr, place(c0, 4 * t, NJ + 4 * t))

    for_blocks(cot_tile, NJ // 4)
    ends[...] = jnp.zeros(ends.shape, F32)
    end_rows(wide, ends.at[0], ends.at[1], blocks=2 * NJ)
    for k, m in enumerate((0, M - 1)):
        for i in range(3):
            ends[k, 2 * NJ + i : 2 * NJ + i + 1, 0:L] = aux[2 + i, m : m + 1, :]
    first[...] = ends[0].astype(BF)
    last[...] = ends[1].astype(BF)


def columns_0(cat, read, left, right, aux):
    a, a_next = aux[0], aux[1]

    def one(j):
        for half in range(2):
            value = read(j, half)
            cat[rows(j), L * half : L * half + L] = value.astype(BF)
            if half == 1:
                moved = from_prev(value, left[rows(j, 8), L : 2 * L], a)
                cat[rows(j), 256:384] = moved.astype(BF)
            else:
                moved = from_next(value, right[rows(j, 8), 0:L], a_next)
                cat[rows(j), 384:512] = moved.astype(BF)

    for_blocks(one)
    rims_0(cat)


def block_sums(j, z, aux, sums):
    s1, s2 = sums
    for k in range(4):
        value = z[rows(j), L * k : L * k + L]
        kept = value * aux[2 + k // 2]
        s1 = s1 + sum8(kept)
        s2 = s2 + sum8(kept * value)
    return s1, s2


def end_rows(z, first, last, apply=lambda v: v, blocks=NJ):
    def group(g):
        for k in range(z.shape[1] // L):
            at = slice(L * k, L * k + L)
            place = sub((8, L))
            top = low = jnp.zeros((8, L), F32)
            for i in range(8):
                start = pl.multiple_of((8 * g + i) * M, M)
                top = jnp.where(place == i, z[pl.ds(start, 8), at][0:1], top)
                low = jnp.where(place == i, z[pl.ds(start + M - 8, 8), at][7:8], low)
            first[rows(g, 8), at] = apply(top)
            last[rows(g, 8), at] = apply(low)

    for_blocks(group, blocks // 8)


def conv_one_kernel(x0, left, right, aux, t, cat, z, mom, first, last, hx, kept, lf, rf, lw, rw):
    lf[...] = left[...].astype(F32)
    rf[...] = right[...].astype(F32)
    hx[:, 0:L] = rf[0 : 2 * NJ, 0:L]
    hx[:, L : 2 * L] = lf[0 : 2 * NJ, L : 2 * L]
    kept[...] = jnp.zeros(kept.shape, F32)
    kept[0:3, :] = lf[2 * NJ : 2 * NJ + 3, 0:L]
    kept[3:6, :] = rf[2 * NJ : 2 * NJ + 3, 0:L]
    widen(lf.at[0:NJ], lw)
    widen(rf.at[0:NJ], rw)
    columns_0(cat, lambda j, h: x0[rows(j), L * h : L * h + L].astype(F32), lw, rw, aux)

    def chunk(rs):
        z[rs, :] = matmul(cat[rs, :], t[...])

    for_chunks(chunk)

    end_rows(z, first, last)

    def sums(j, carry):
        return block_sums(j, z, aux, carry)

    zero = jnp.zeros((8, L), F32)
    s1, s2 = lax.fori_loop(0, NJ, sums, (zero, zero))
    stats = fold(stack_rows([total_rows(s1), total_rows(s2)]), 16)
    count_one = total_rows(aux[2] + aux[3])
    count_two = total_rows(aux[4])
    at = sub((8, L))
    stats = jnp.where(at == 2, count_one * (NJ * 16.0), stats)
    mom[...] = jnp.where(at == 3, count_two * (NJ * 8.0), stats)


def conv_two_kernel(z1, left, right, mom1, prm, aux, t, cat, ends, z2, mom, first, last, ef, lw, rw):
    mean, scale = norm_terms(mom1, mom1[2:3])
    gain, shift = prm[0:1], prm[1:2]

    def act(value):
        return silu((value - mean) * scale * gain + shift)

    a, a_next = aux[0], aux[1]
    for k in range(4):
        ef[0, :, L * k : L * k + L] = act(left[:, L * k : L * k + L])
        ef[1, :, L * k : L * k + L] = act(right[:, L * k : L * k + L])
    widen(ef.at[0], lw)
    widen(ef.at[1], rw)

    def one(j):
        for k in range(4):
            at = slice(L * k, L * k + L)
            value = act(z1[rows(j), at])
            cat[rows(j), at] = value.astype(BF)
            if k >= 2:
                moved = from_prev(value, lw[rows(j, 8), at], a)
                cat[rows(j), 256 + L * k : 384 + L * k] = moved.astype(BF)
            moved = from_next(value, rw[rows(j, 8), at], a_next)
            cat[rows(j), 768 + L * k : 896 + L * k] = moved.astype(BF)

    for_blocks(one)
    end_rows(z1, ef.at[2], ef.at[3], act)
    ends[...] = ef[...].astype(BF)
    rims_1(cat, [g for g, _ in GROUPS1], 1280)

    def chunk(rs):
        z2[rs, :] = matmul(cat[rs, :], t[...])

    for_chunks(chunk)

    end_rows(z2, first, last)

    def sums(j, carry):
        s1, s2 = carry
        for k in range(2):
            value = z2[rows(j), L * k : L * k + L]
            kept = value * aux[4]
            s1 = s1 + sum8(kept)
            s2 = s2 + sum8(kept * value)
        return s1, s2

    zero = jnp.zeros((8, L), F32)
    s1, s2 = lax.fori_loop(0, NJ, sums, (zero, zero))
    mom[...] = fold(stack_rows([total_rows(s1), total_rows(s2)]), 32)


def columns_2(cat, read, left, right, aux, own=None):
    a, a_next = aux[0], aux[1]

    def one(j):
        for k in range(2):
            at = slice(L * k, L * k + L)
            value = read(j, k)
            low = value.astype(BF)
            cat[rows(j), at] = low
            if own is not None:
                own[rows(j), at] = low
            moved = from_prev(value, left[rows(j, 8), at], a)
            cat[rows(j), 256 + L * k : 384 + L * k] = moved.astype(BF)
            moved = from_next(value, right[rows(j, 8), at], a_next)
            cat[rows(j), 512 + L * k : 640 + L * k] = moved.astype(BF)

    for_blocks(one)
    rims_2(cat)


def up_two_kernel(z2, left, right, mom1, mom2, prm, aux, t, act2, rect, mom, first, last, cat, lf, rf, lw, rw):
    mean, scale = norm_terms(mom2, mom1[3:4])
    gain, shift, bias = prm[2:3], prm[3:4], prm[6:7]

    def act(value):
        return silu((value - mean) * scale * gain + shift)

    for k in range(2):
        at = slice(L * k, L * k + L)
        lf[:, at] = act(left[:, at])
        rf[:, at] = act(right[:, at])
    widen(lf, lw)
    widen(rf, rw)
    columns_2(cat, lambda j, k: act(z2[rows(j), L * k : L * k + L]), lw, rw, aux, act2)

    def chunk(rs):
        rect[rs, :] = matmul(cat[rs, :], t[...], True)

    for_chunks(chunk)

    def sums(j, carry):
        s1, s2 = carry
        for k in range(4):
            at = slice(L * k, L * k + L)
            value = softplus(rect[rows(j), at] + bias)
            rect[rows(j), at] = value
            kept = value * aux[2 + k // 2]
            s1 = s1 + sum8(kept)
            s2 = s2 + sum8(kept * value)
        return s1, s2

    zero = jnp.zeros((8, L), F32)
    s1, s2 = lax.fori_loop(0, NJ, sums, (zero, zero))
    end_rows(rect, first, last)
    mom[...] = fold(stack_rows([total_rows(s1), total_rows(s2)]), 16)


def columns_1b(cat, read, left, right, aux, own=None):
    a, a_next = aux[0], aux[1]

    def one(j):
        for k in range(4):
            at = slice(L * k, L * k + L)
            value = read(j, k)
            low = value.astype(BF)
            cat[rows(j), at] = low
            if own is not None:
                own[rows(j), at] = low
            if k >= 2:
                moved = from_prev(value, left[rows(j, 8), at], a)
                cat[rows(j), 256 + L * k : 384 + L * k] = moved.astype(BF)
            else:
                moved = from_next(value, right[rows(j, 8), at], a_next)
                cat[rows(j), 768 + L * k : 896 + L * k] = moved.astype(BF)

    for_blocks(one)
    rims_1(cat, (0, 256, 512, 768), 1024)


def edge_columns(own, prev, after):
    at = lane((NJ, L))
    place = sub((NJ, L))
    parts = [own, prev, after]
    groups = [own[:, 0:256], own[:, 256:512], prev, after]
    for g in groups:
        low = jnp.where((place == NJ - 1) | (at >= 32), 0.0, pltpu.roll(g[:, 0:L], NJ - 1, 0))
        high = jnp.where((place == 0) | (at < 112), 0.0, pltpu.roll(g[:, L : 2 * L], 1, 0))
        parts.append(low + high)
    return jnp.concatenate(parts, axis=1).astype(BF)


def sigmoid(v):
    return 1.0 / (1.0 + jnp.exp(-v))


def up_one_kernel(
    rect, left, right, mom1, mom3, prm, aux, cat1, ends1, t, own, sig, sigh, mask, cat, lf, rf, ef, hf,
    lw, rw,
):
    mean, scale = norm_terms(mom3, mom1[2:3])
    gain, shift, bias = prm[4:5], prm[5:6], prm[7:8]

    def norm(value):
        return (value - mean) * scale * gain + shift

    for k in range(4):
        at = slice(L * k, L * k + L)
        lf[:, at] = norm(left[:, at])
        rf[:, at] = norm(right[:, at])
    widen(lf, lw)
    widen(rf, rw)
    columns_1b(cat, lambda j, k: norm(rect[rows(j), L * k : L * k + L]), lw, rw, aux, own)
    end_rows(rect, ef.at[0], ef.at[1], norm)
    wide = jnp.concatenate([bias, bias], axis=1)
    zero = jnp.zeros((NJ, 256), F32)
    a, a_end = aux[0, 0:1, 0:1], aux[1, M - 1 : M, 0:1]
    e1 = [ends1[k].astype(F32) for k in range(4)]
    edges = [
        (
            edge_columns(lf[...], zero, ef[0, :, 0:256] * a),
            edge_columns(e1[0], zero, e1[2][:, 0:256] * a),
        ),
        (
            edge_columns(rf[...], ef[1, :, 256:512] * a_end, zero),
            edge_columns(e1[1], e1[3][:, 256:512] * a_end, zero),
        ),
    ]
    for k, half in ((0, 1), (1, 0)):
        value = matmul(edges[k][0], t[:, 0:COLS1B], True)
        value = value + matmul(edges[k][1], t[:, COLS1B : 2 * COLS1B], True)
        sigh[:, L * half : L * half + L] = sigmoid(value[:, L * half : L * half + L] + bias)

    def chunk(rs):
        value = matmul(cat[rs, :], t[:, 0:COLS1B], True)
        value = value + matmul(cat1[rs, 0:1024], t[:, COLS1B : COLS1B + 1024], True)
        value = value + matmul(cat1[rs, 1280:1792], t[:, COLS1B + 1024 : 2 * COLS1B], True)
        sig[rs, :] = sigmoid(value + wide)

    for_chunks(chunk)
    per = R // mask.shape[0]
    blocks = NJ // mask.shape[0]
    for s in range(mask.shape[0]):
        mask[s, 0:per, :] = sig[s * per : (s + 1) * per, :].astype(BF)
        hf[...] = jnp.zeros(hf.shape, F32)
        hf[0:blocks, :] = sigh[s * blocks : (s + 1) * blocks, :]
        mask[s, per : per + 16, :] = hf[...].astype(BF)


def ratio_terms(masks):
    squares = [m * m for m in masks]
    power = squares[0]
    for s in squares[1:]:
        power = power + s
    inverse = 1.0 / (power + RATIO_EPS)
    return [s * inverse for s in squares], inverse


def mask_back(masks, cots, mix):
    ratios, inverse = ratio_terms(masks)
    direct = cots[0] * ratios[0]
    for c, r in zip(cots[1:], ratios[1:]):
        direct = direct + c * r
    common = 2.0 * mix * inverse
    return [m * common * (c - direct) for m, c in zip(masks, cots)], direct


def mask_kernel(index, masks, c0, x0, hx, grad, direct, hf):
    stems = masks.shape[0]
    per, blocks = R // stems, NJ // stems
    mine = index[0]

    def one(j):
        for half in range(2):
            at = slice(L * half, L * half + L)
            m = [masks[s, rows(j), at].astype(F32) for s in range(stems)]
            c = [c0[rows(s * blocks + j), at].astype(F32) for s in range(stems)]
            x = x0[rows(mine * blocks + j), at].astype(F32)
            grads, own = mask_back(m, c, x)
            direct[rows(j), at] = own
            for s in range(stems):
                grad[s, rows(j), at] = grads[s].astype(BF)

    for_blocks(one, blocks)
    m = [masks[s, per : per + 16, :].astype(F32)[0:blocks] for s in range(stems)]
    c = [hx[NJ + s * blocks : NJ + (s + 1) * blocks, :] for s in range(stems)]
    grads, _ = mask_back(m, c, hx[rows(mine, blocks), :])
    for s in range(stems):
        hf[...] = jnp.zeros(hf.shape, F32)
        hf[0:blocks, :] = grads[s]
        grad[s, per : per + 16, :] = hf[...].astype(BF)


def estimate_kernel(index, masks, x0, out, scr, est):
    stems = masks.shape[0]
    blocks = NJ // stems
    mine = index[0]

    def one(j):
        for half in range(2):
            at = slice(L * half, L * half + L)
            m = [masks[s, rows(j), at].astype(F32) for s in range(stems)]
            x = x0[rows(mine * blocks + j), at].astype(F32)
            ratios, _ = ratio_terms(m)
            for s in range(stems):
                est[s, rows(j), at] = x * ratios[s]

    for_blocks(one, blocks)
    for s in range(stems):
        for t in range(blocks // 4):
            gather(
                lambda block, half, s=s, t=t: est[s, rows(4 * t + block), L * half : L * half + L], scr
            )
            for c in range(2):
                out[s, c, :, L * t : L * t + L] = scr[c].astype(BF)


def down_one_back_kernel(
    grad, sig, sigh, aux, t, rect, mom1, mom3, cat, g3, gact, mom, bias, first, last, hf, zf, hw
):
    stems = grad.shape[0]
    per, blocks = R // stems, NJ // stems
    for s in range(stems):
        span = slice(s * blocks, (s + 1) * blocks)
        value = grad[s, per : per + 16, :].astype(F32)[0:blocks]
        own = sigh[span, :]
        hf[span, :] = value * own * (1.0 - own)
    zf[...] = jnp.zeros(zf.shape, F32)

    def read(j, half):
        at = slice(L * half, L * half + L)
        own = sig[rows(j), at]
        value = grad[j // blocks, rows(j % blocks), at].astype(F32) * own * (1.0 - own)
        zf[...] = zf[...] + sum8(value)
        return value

    widen(hf, hw)
    columns_0(cat, read, hw, hw, aux)
    bias[...] = zf[...]

    def chunk(rs):
        value = matmul(cat[rs, :], t[...])
        g3[rs, :] = value[:, 0:512]
        gact[rs, :] = value[:, 512:1024]

    for_chunks(chunk)
    mean, scale = norm_terms(mom3, mom1[2:3])

    end_rows(g3, first, last)

    def sums(j, carry):
        s1, s2 = carry
        for k in range(4):
            at = slice(L * k, L * k + L)
            value = g3[rows(j), at]
            s1 = s1 + sum8(value)
            s2 = s2 + sum8(value * (rect[rows(j), at] - mean))
        return s1, s2

    zero = jnp.zeros((8, L), F32)
    s1, s2 = lax.fori_loop(0, NJ, sums, (zero, zero))
    mom[...] = fold(stack_rows([total_rows(s1), total_rows(s2) * scale]), 16)


def norm_back(g, xhat, kept, moments, count, factor):
    return factor * (g - kept * ((moments[0:1] + xhat * moments[1:2]) / count))


def up_two_back_kernel(
    g3, left, right, mom4, mom1, mom3, mom2, prm, aux, kept, rect, rleft, rright, t, z2,
    cat, g2, mom, first, last, lf, rf, lw, rw,
):
    count = mom1[2:3]
    mean, scale = norm_terms(mom3, count)
    factor = scale * prm[4:5]

    def back(g, r, keep):
        xhat = (r - mean) * scale
        return norm_back(g, xhat, keep, mom4, count, factor) * softplus_slope(r)

    for k in range(4):
        at = slice(L * k, L * k + L)
        row = k // 2
        lf[:, at] = back(left[:, at], rleft[:, at], kept[row : row + 1, :])
        rf[:, at] = back(right[:, at], rright[:, at], kept[3 + row : 4 + row, :])
    widen(lf, lw)
    widen(rf, rw)
    a, a_next = aux[0], aux[1]

    def one(j, total):
        for k in range(4):
            at = slice(L * k, L * k + L)
            value = back(g3[rows(j), at], rect[rows(j), at], aux[2 + k // 2])
            total = total + sum8(value)
            cat[rows(j), at] = value.astype(BF)
            if k >= 2:
                moved = from_prev(value, lw[rows(j, 8), at], a)
                cat[rows(j), 256 + L * k : 384 + L * k] = moved.astype(BF)
            moved = from_next(value, rw[rows(j, 8), at], a_next)
            cat[rows(j), 768 + L * k : 896 + L * k] = moved.astype(BF)
        return total

    zero = jnp.zeros((8, L), F32)
    bias = lax.fori_loop(0, NJ, one, zero)
    rims_1(cat, [g for g, _ in GROUPS1], 1280)

    def chunk(rs):
        g2[rs, :] = matmul(cat[rs, :], t[...])

    for_chunks(chunk)
    mean2, scale2 = norm_terms(mom2, mom1[3:4])
    gain, shift = prm[2:3], prm[3:4]

    def sums(j, carry):
        s1, s2 = carry
        for k in range(2):
            at = slice(L * k, L * k + L)
            xhat = (z2[rows(j), at] - mean2) * scale2
            value = g2[rows(j), at] * silu_slope(xhat * gain + shift)
            g2[rows(j), at] = value
            s1 = s1 + sum8(value)
            s2 = s2 + sum8(value * xhat)
        return s1, s2

    s1, s2 = lax.fori_loop(0, NJ, sums, (zero, zero))
    stats = fold(stack_rows([total_rows(s1), total_rows(s2)]), 32)
    bias = fold(stack_rows([total_rows(bias)] * 3), 16)
    end_rows(g2, first, last)
    mom[...] = jnp.where(sub((8, L)) == 2, bias, stats)


def down_two_back_kernel(
    g2, left, right, mom5, mom1, mom2, prm, aux, kept, z2, zleft, zright, t, gact, z1,
    own, g1, mom, first, last, cat, lf, rf, lw, rw,
):
    count = mom1[3:4]
    mean, scale = norm_terms(mom2, count)
    factor = scale * prm[2:3]

    def back(g, z, keep):
        return norm_back(g, (z - mean) * scale, keep, mom5, count, factor)

    for k in range(2):
        at = slice(L * k, L * k + L)
        lf[:, at] = back(left[:, at], zleft[:, at], kept[2:3, :])
        rf[:, at] = back(right[:, at], zright[:, at], kept[5:6, :])

    def read(j, k):
        at = slice(L * k, L * k + L)
        return back(g2[rows(j), at], z2[rows(j), at], aux[4])

    widen(lf, lw)
    widen(rf, rw)
    columns_2(cat, read, lw, rw, aux, own)

    def chunk(rs):
        g1[rs, :] = matmul(cat[rs, :], t[...], True) + gact[rs, :]

    for_chunks(chunk)
    mean1, scale1 = norm_terms(mom1, mom1[2:3])
    gain, shift = prm[0:1], prm[1:2]

    def sums(j, carry):
        s1, s2 = carry
        for k in range(4):
            at = slice(L * k, L * k + L)
            xhat = (z1[rows(j), at] - mean1) * scale1
            value = g1[rows(j), at] * silu_slope(xhat * gain + shift)
            g1[rows(j), at] = value
            s1 = s1 + sum8(value)
            s2 = s2 + sum8(value * xhat)
        return s1, s2

    zero = jnp.zeros((8, L), F32)
    s1, s2 = lax.fori_loop(0, NJ, sums, (zero, zero))
    end_rows(g1, first, last)
    mom[...] = fold(stack_rows([total_rows(s1), total_rows(s2)]), 16)


def up_one_back_kernel(
    g1, left, right, mom6, mom1, prm, aux, kept, z1, zleft, zright, t, own, net, cat, lf, rf,
    lw, rw,
):
    count = mom1[2:3]
    mean, scale = norm_terms(mom1, count)
    factor = scale * prm[0:1]

    def back(g, z, keep):
        return norm_back(g, (z - mean) * scale, keep, mom6, count, factor)

    for k in range(4):
        at = slice(L * k, L * k + L)
        row = k // 2
        lf[:, at] = back(left[:, at], zleft[:, at], kept[row : row + 1, :])
        rf[:, at] = back(right[:, at], zright[:, at], kept[3 + row : 4 + row, :])

    def read(j, k):
        at = slice(L * k, L * k + L)
        return back(g1[rows(j), at], z1[rows(j), at], aux[2 + k // 2])

    widen(lf, lw)
    widen(rf, rw)
    columns_1b(cat, read, lw, rw, aux, own)

    def chunk(rs):
        net[rs, :] = matmul(cat[rs, :], t[...], True).astype(BF)

    for_chunks(chunk)


def mixture_kernel(parts, direct, out, scr):
    stems = parts.shape[0]

    def tile(t):
        def block(k, half):
            at = slice(L * half, L * half + L)
            value = parts[0, rows(4 * t + k), at].astype(F32)
            for s in range(1, stems):
                value = value + parts[s, rows(4 * t + k), at].astype(F32)
            return value + direct[rows(4 * t + k), at]

        gather(block, scr)
        for c in range(2):
            out[c, :, pl.ds(pl.multiple_of(t * L, L), L)] = scr[c]

    for_blocks(tile, NJ // stems // 4)


def sum_over(values, axis):
    count = lax.axis_size(axis)
    if count & (count - 1):
        return lax.psum(values, axis)
    step = 1
    while step < count:
        radix = 2 if step == 1 or count // step == 2 else 4
        moved = [
            lax.ppermute(values, axis, [(i, i ^ (step * k)) for i in range(count)])
            for k in range(1, radix)
        ]
        for m in moved:
            values = values + m
        step *= radix
    return values


def from_left(values, axis):
    count = lax.axis_size(axis)
    return lax.ppermute(values, axis, [(i, i + 1) for i in range(count - 1)])


def from_right(values, axis):
    count = lax.axis_size(axis)
    return lax.ppermute(values, axis, [(i + 1, i) for i in range(count - 1)])


def swap(values, axis):
    return lax.all_to_all(values, axis, 0, 0, tiled=True)


def flags(seg_lengths, frame_mask, position, total):
    order = jnp.arange(seg_lengths.shape[0])
    earlier = order[None, :] < order[:, None]
    starts = 4 * jnp.sum(jnp.where(earlier, seg_lengths[None, :], 0), axis=1)
    frames = (position * M + jnp.arange(M + 1, dtype=jnp.int32)) * 4
    shut = jnp.any(frames[:, None] == starts[None, :], axis=1) | (frames == total)
    a = 1.0 - shut.astype(F32)
    keep_one = jnp.min(frame_mask.reshape(M, 2, 2), axis=2).astype(F32)
    keep_two = jnp.min(frame_mask.reshape(M, 4), axis=1).astype(F32)
    columns = jnp.stack([a[:M], a[1:], keep_one[:, 0], keep_one[:, 1], keep_two])
    return jnp.broadcast_to(columns[:, :, None], (5, M, L))


def per_device(
    mixture,
    seg_lengths,
    frame_mask,
    conv_first,
    encoder_gain_vector,
    shift_first,
    conv_second,
    gain_second,
    shift_second,
    deconv_second,
    bias_second,
    decoder_gain_vector,
    shift_third,
    deconv_first,
    bias_first,
    cotangent,
):
    position = lax.axis_index("tm")
    stems = lax.axis_size("stem")
    index = lax.axis_index("stem").astype(jnp.int32).reshape(1)
    frames = mixture.shape[1]
    per, blocks = R // stems, NJ // stems
    aux = flags(seg_lengths, frame_mask, position, frames * lax.axis_size("tm"))
    prm = jnp.stack(
        [
            jnp.tile(encoder_gain_vector[0], 8),
            jnp.tile(shift_first[0], 8),
            jnp.tile(gain_second[0], 4),
            jnp.tile(shift_second[0], 4),
            jnp.tile(decoder_gain_vector[0], 8),
            jnp.tile(shift_third[0], 8),
            jnp.tile(bias_second[0], 8),
            jnp.tile(jnp.repeat(bias_first[0], 32), 2),
        ]
    )
    w1c = jnp.tile(conv_first[0].transpose(2, 1, 3, 0).reshape(50, 16).astype(F32), (1, 8))
    w1d = deconv_first[0].transpose(2, 0, 3, 1).reshape(50, 2, 16).astype(F32)
    w1d = jnp.tile(w1d.transpose(1, 0, 2), (1, 1, 8))
    w2c = jnp.tile(conv_second[0].transpose(2, 3, 1, 0).reshape(400, 32).astype(F32), (1, 4))
    w2d = jnp.tile(deconv_second[0].transpose(2, 3, 0, 1).reshape(400, 32).astype(F32), (1, 4))

    x0, c0, first, last = run(
        layout_kernel,
        "layout",
        [((R, 256), BF), ((R, 256), BF), ((2 * NJ + 16, 256), BF), ((2 * NJ + 16, 256), BF)],
        [mixture, cotangent, aux],
        [((2, frames, L), F32), ((2 * R, 256), F32), ((2, 2 * NJ + 16, 256), F32)],
    )
    left0, right0 = from_left(last, "tm"), from_right(first, "tm")
    (t1a_c,) = run(matrices_first, "matrices_first", [((COLS0, 512), BF)], [w1c])
    t2a_c, t2b_d, t1b_d = run(
        matrices_forward,
        "matrices_forward",
        [((COLS1, 256), BF), ((512, COLS2), BF), ((256, 2 * COLS1B), BF)],
        [w2c, w2d, w1d],
    )
    t1a_d, t2a_d, t2b_c, t1b_c = run(
        matrices_back,
        "matrices_back",
        [((COLS0, 1024), BF), ((COLS1, 256), BF), ((512, COLS2), BF), ((256, COLS1B), BF)],
        [w1c, w2c, w2d, w1d],
    )
    wide = lambda lanes: [((8 * NJ, lanes), F32)] * 2
    halo = lambda lanes: [((NJ, lanes), F32), ((NJ, lanes), F32)]
    mom_out = [((8, L), F32)]
    cat0, z1, mom1, first, last, hx, kept = run(
        conv_one_kernel,
        "conv_one",
        [((R, COLS0), BF), ((R, 512), F32)] + mom_out + halo(512) + [((2 * NJ, 256), F32)] + mom_out,
        [x0, left0, right0, aux, t1a_c],
        [((2 * NJ + 16, 256), F32)] * 2 + wide(256),
        flops=2 * R * COLS0 * 512,
    )
    h1l, h1r = from_left(last, "tm"), from_right(first, "tm")
    mom1 = sum_over(mom1, "tm")
    cat1, ends1, z2, mom2, first, last = run(
        conv_two_kernel,
        "conv_two",
        [((R, COLS1), BF), ((4, NJ, 512), BF), ((R, 256), F32)] + mom_out + halo(256),
        [z1, h1l, h1r, mom1, prm, aux, t2a_c],
        [((4, NJ, 512), F32)] + wide(512),
        flops=2 * R * COLS1 * 256,
    )
    h2l, h2r = from_left(last, "tm"), from_right(first, "tm")
    mom2 = sum_over(mom2, "tm")
    act2, rect, mom3, first, last = run(
        up_two_kernel,
        "up_two",
        [((R, 256), BF), ((R, 512), F32)] + mom_out + halo(512),
        [z2, h2l, h2r, mom1, mom2, prm, aux, t2b_d],
        [((R, COLS2), BF)] + halo(256) + wide(256),
        flops=2 * R * COLS2 * 512,
    )
    h3l, h3r = from_left(last, "tm"), from_right(first, "tm")
    mom3 = sum_over(mom3, "tm")
    low3, sig, sigh, mask = run(
        up_one_kernel,
        "up_one",
        [((R, 512), BF), ((R, 256), F32), ((NJ, 256), F32), ((stems, per + 16, 256), BF)],
        [rect, h3l, h3r, mom1, mom3, prm, aux, cat1, ends1, t1b_d],
        [((R, COLS1B), BF)] + halo(512) + [((2, NJ, 512), F32), ((16, 256), F32)] + wide(512),
        flops=2 * R * 2 * COLS1B * 256,
    )
    masks = swap(mask, "stem")
    grad, direct = run(
        mask_kernel,
        "mask",
        [((stems, per + 16, 256), BF), ((per, 256), F32)],
        [index, masks, c0, x0, hx],
        [((16, 256), F32)],
        scalars=1,
    )
    grad = swap(grad, "stem")
    (estimates,) = run(
        estimate_kernel,
        "estimate",
        [((stems, 2, frames, blocks * 32), BF)],
        [index, masks, x0],
        [((2, frames, L), F32), ((stems, per, 256), F32)],
        scalars=1,
    )
    cat0g, g3, gact, mom4, bias_one, first, last = run(
        down_one_back_kernel,
        "down_one_back",
        [((R, COLS0), BF), ((R, 512), F32), ((R, 512), F32)] + mom_out + mom_out + halo(512),
        [grad, sig, sigh, aux, t1a_d, rect, mom1, mom3],
        [((NJ, 256), F32), ((8, L), F32), ((8 * NJ, 256), F32)],
        flops=2 * R * COLS0 * 1024,
    )
    h4l, h4r = from_left(last, "tm"), from_right(first, "tm")
    mom4 = sum_over(mom4, "tm")
    (w1d_grad,) = run(
        weight_1_joined,
        "weight_up_one",
        [((96, L), F32)],
        [low3, cat1, cat0g],
        [((512, COLS0), F32)],
        flops=2 * R * COLS0 * 1024,
    )
    cat1g, g2, mom5, first, last = run(
        up_two_back_kernel,
        "up_two_back",
        [((R, COLS1), BF), ((R, 256), F32)] + mom_out + halo(256),
        [g3, h4l, h4r, mom4, mom1, mom3, mom2, prm, aux, kept, rect, h3l, h3r, t2a_d, z2],
        halo(512) + wide(512),
        flops=2 * R * COLS1 * 256,
    )
    h5l, h5r = from_left(last, "tm"), from_right(first, "tm")
    mom5 = sum_over(mom5, "tm")
    (w2d_grad,) = run(
        weight_2_kernel,
        "weight_up_two",
        [((160, L), F32)],
        [act2, cat1g],
        [((256, COLS1), F32)],
        flops=2 * R * COLS1 * 256,
    )
    low2, g1, mom6, first, last = run(
        down_two_back_kernel,
        "down_two_back",
        [((R, 256), BF), ((R, 512), F32)] + mom_out + halo(512),
        [g2, h5l, h5r, mom5, mom1, mom2, prm, aux, kept, z2, h2l, h2r, t2b_c, gact, z1],
        [((R, COLS2), BF)] + halo(256) + wide(256),
        flops=2 * R * COLS2 * 512,
    )
    h6l, h6r = from_left(last, "tm"), from_right(first, "tm")
    mom6 = sum_over(mom6, "tm")
    (w2c_grad,) = run(
        weight_2_kernel,
        "weight_down_two",
        [((160, L), F32)],
        [low2, cat1],
        [((256, COLS1), F32)],
        flops=2 * R * COLS1 * 256,
    )
    low1, net = run(
        up_one_back_kernel,
        "up_one_back",
        [((R, 512), BF), ((R, 256), BF)],
        [g1, h6l, h6r, mom6, mom1, prm, aux, kept, z1, h1l, h1r, t1b_c],
        [((R, COLS1B), BF)] + halo(512) + wide(512),
        flops=2 * R * COLS1B * 256,
    )
    parts = swap(net.reshape(stems, per, 256), "stem")
    (w1c_grad,) = run(
        weight_1_first,
        "weight_down_one",
        [((48, L), F32)],
        [low1, cat0],
        [((512, COLS0), F32)],
        flops=2 * R * COLS0 * 512,
    )
    (mixture_grad,) = run(
        mixture_kernel,
        "mixture",
        [((2, frames, blocks * 32), F32)],
        [parts, direct],
        [((2, frames, L), F32)],
    )
    early = sum_over(jnp.concatenate([w1d_grad, w2d_grad, w2c_grad, bias_one]), "tm")
    w1c_grad = sum_over(w1c_grad, "tm")

    def outer(tiles):
        taps = tiles.reshape(3, 16, 2, 2, 32)[..., :TAPS].transpose(1, 3, 0, 2, 4)
        return taps.reshape(16, 2, 6, TAPS)[:, :, 1:]

    def inner(tiles):
        return tiles[:, :80].reshape(TAPS, 32, TAPS, 16).transpose(1, 3, 0, 2)

    w1d_grad = jnp.concatenate([outer(early[0:48]), outer(early[48:96])]).transpose(1, 0, 2, 3)
    return (
        estimates,
        mixture_grad,
        outer(w1c_grad)[None],
        mom6[1, :16][None],
        mom6[0, :16][None],
        inner(early[256:416])[None],
        mom5[1, :32][None],
        mom5[0, :32][None],
        inner(early[96:256]).transpose(1, 0, 2, 3)[None],
        mom5[2, :16][None],
        mom4[1, :16][None],
        mom4[0, :16][None],
        w1d_grad[None],
        early[416:424].reshape(8, 2, 2, 32).sum((0, 1, 3))[None],
    )


def solution(mesh):
    in_specs = (
        P(None, "tm", None),
        P(),
        P("tm"),
        P("stem", None, None, None, None),
        P("stem", None),
        P("stem", None),
        P("stem", None, None, None, None),
        P("stem", None),
        P("stem", None),
        P("stem", None, None, None, None),
        P("stem", None),
        P("stem", None),
        P("stem", None),
        P("stem", None, None, None, None),
        P("stem", None),
        P(None, None, "tm", "stem"),
    )
    out_specs = (
        P(None, None, "tm", "stem"),
        P(None, "tm", "stem"),
        P("stem", None, None, None, None),
        P("stem", None),
        P("stem", None),
        P("stem", None, None, None, None),
        P("stem", None),
        P("stem", None),
        P("stem", None, None, None, None),
        P("stem", None),
        P("stem", None),
        P("stem", None),
        P("stem", None, None, None, None),
        P("stem", None),
    )
    return jax.shard_map(
        per_device, mesh=mesh, in_specs=in_specs, out_specs=out_specs, check_vma=False
    )
```

time: 3860 us -> 254 us (0.07)
  matrix products: 1890 us -> 0 us
  local copies, waits for them, and re-layouts: 1540 us -> 34.5 us
  other arithmetic: 220 us -> 4.83 us
  blocking collectives: 92.9 us -> 0 us
  Pallas kernels: 0 us -> 82.6 us
  starting transfers between devices: 25.8 us -> 85.1 us
    conv_general_dilated x40 -> x0, matrix products: 1830 us -> none  [the longest x20 1580 us: bins_up(): lax.conv_general_dilated(input_values[None], jnp.flip(kernel, 2)[:, :, No...]
    slice x103 -> x11, local copies, waits for them, and re-layouts: 636 us -> 2.45 us  [the longest x1 0.52 us: per_device(): mom4[0, :16][None]]
    conv_general_dilated x77 -> x0, local copies, waits for them, and re-layouts: 305 us -> none  [the longest x67 196 us: bins_down(): lax.conv_general_dilated(input_values[None], kernel[:, :, None, :], (1, 2...]
    broadcast_in_dim x44 -> x3, local copies, waits for them, and re-layouts: 188 us -> 0.77 us  [the longest x1 0.61 us: per_device(): outer(w1c_grad)[None]]
    another operation x10 -> x28, local copies, waits for them, and re-layouts: 122 us -> 1.36 us  [the longest x9 0.68 us: per_device(): jnp.stack([jnp.tile(encoder_gain_vector[0], 8), jnp.tile(shift_first[0],...]
    unnamed x515 -> x136, local copies, waits for them, and re-layouts: 142 us -> 26.7 us
    add x14 -> x0, local copies, waits for them, and re-layouts: 99.9 us -> none  [the longest x6 45.2 us: up_back(): bins_down(here_even, flipped[:, :, 1])]
    psum x6 -> x0, blocking collectives: 92.9 us -> none  [the longest x3 48.5 us: moments(): return lax.psum(input_values, 'tm')]
  transfers between devices with their start and end apart: 20 -> 49, of which waited for: 3 -> 14; matrix products, arithmetic and copies ran while one was open for 55% -> 4% of each run, Pallas kernels for 0% -> 6%
where the time goes in v1:
time: 254 us; the launch traced here: 253 us
  starting transfers between devices  85.1 us (34%)
  Pallas kernels  82.6 us (33%)
  waiting for transfers between devices  43.8 us (17%)
  local copies, waits for them, and re-layouts  34.5 us (14%)
  other arithmetic  4.83 us (2%)
    pallas_call x19, Pallas kernels, run(): pl.pallas_call(kernel, out_shape=shapes, in_specs=[SCALAR] * scalars + [F...  82.6 us
    ppermute x32, starting transfers between devices, sum_over(): lax.ppermute(values, axis, [(i, i ^ step * k) for i in range(count)])  52.1 us
    unnamed x136, local copies, waits for them, and re-layouts  26.7 us
    ppermute x32, waiting for transfers between devices, sum_over(): lax.ppermute(values, axis, [(i, i ^ step * k) for i in range(count)])  19.4 us
    ppermute x7, waiting for transfers between devices, from_right(): return lax.ppermute(values, axis, [(i + 1, i) for i in range(count - 1)])  12.6 us
    ppermute x7, starting transfers between devices, from_left(): return lax.ppermute(values, axis, [(i, i + 1) for i in range(count - 1)])  12.4 us
    all_to_all x3, waiting for transfers between devices, swap(): return lax.all_to_all(values, axis, 0, 0, tiled=True)  11.8 us
    all_to_all x3, starting transfers between devices, swap(): return lax.all_to_all(values, axis, 0, 0, tiled=True)  11.4 us
  transfers between devices with their start and end apart: 49, of which 14 were waited for; matrix products, arithmetic and copies ran while one was open for 4% of the time, Pallas kernels for 6%

profile of v1, /device:TPU:0, one launch (start us, length us, event | category | flops | bytes accessed | tf_op | source)
XLA Modules:
  0.0 252.7 jit_solution(5627314985731117948)
XLA Ops:
  17.3 4.0 %conv_one.1 = (bf16[1024,1024]{1,0:T(8,128)(2,1)S(1)}, f32[1024,512]{1,0:T(8,128)S(1)}, f32[8,128]{1,0:T(8,128)S(1)}, f32[32,512]{1,0:T(8,128)S(1)}, f32[32,512]...) custom-call(bf16[1024,256]{1,0:T(8,128)(2,1)S(1)} %get-tuple-element.68.x0, ...), custom_call_target="tpu_custom_call" | custom-call | flops 1073741824 | bytes 6135808 | tf_op jit(solution)/shard_map/conv_one/pallas_call | solution.py:43
  27.5 2.8 %collective-permute-start.7 = (f32[8,128]{1,0:T(8,128)S(1)}, f32[8,128]{1,0:T(8,128)S(1)}, u32[]{:S(2)}, u32[]{:S(2)}) collective-permute-start(f32[8,128]{1,0:T(8,128)S(1)} %add.108), channel_id=1, source_target_pairs={{0,6},{1,7},{2,4},{3,5},{4,2},{5,3},{6,0},{7,1},{8,14},{9,15},{10,... | collective-permute-start | bytes 12296 | tf_op jit(solution)/shard_map/ppermute | solution.py:995
  44.6 6.9 %conv_two.1 = (bf16[1024,1920]{1,0:T(8,128)(2,1)}, bf16[4,32,512]{2,1,0:T(8,128)(2,1)S(1)}, f32[1024,256]{1,0:T(8,128)S(1)}, f32[8,128]{1,0:T(8,128)S(1)}, f32[32,256]{1,0:T(8,128)S(1)}, /*index=5*/f32[32,256]{1,0:T(8,128)S(1)}) custom-call(f32[1024,512]{1,0:T(8,128)S(1)} %get-tuple-element.71.z1, f32[32,512]{1,0:T(8,128)S(1)} %collective-permute-done.2.left.zleft, ...), custom_call_target="tpu_custom_call" | custom-call | flops 1006632960 | bytes 8482816 | tf_op jit(solution)/shard_map/conv_two/pallas_call | solution.py:43
  51.6 2.9 %collective-permute-start.10 = (f32[8,128]{1,0:T(8,128)S(1)}, f32[8,128]{1,0:T(8,128)S(1)}, u32[]{:S(2)}, u32[]{:S(2)}) collective-permute-start(f32[8,128]{1,0:T(8,128)S(1)} %get-tuple-element.79), channel_id=1, source_target_pairs={{0,1},{1,0},{2,3},{3,2},{4,5},{5,4},{6,7},{7,6},{8,9},{9,8},{10,11... | collective-permute-start | bytes 12296 | tf_op jit(solution)/shard_map/ppermute | solution.py:995
  65.0 6.0 %up_two.1 = (bf16[1024,256]{1,0:T(8,128)(2,1)S(1)}, f32[1024,512]{1,0:T(8,128)S(1)}, f32[8,128]{1,0:T(8,128)S(1)}, f32[32,512]{1,0:T(8,128)S(1)}, f32[32,512]{1,0:T(8,128)S(1)}) custom-call(f32[1024,256]{1,0:T(8,128)S(1)} %get-tuple-element.76.z2, f32[32,256]{1,0:T(8,128)S(1)} %collective-permute-done.8.left.zleft, ...), custom_call_target="tpu_custom_call" | custom-call | flops 1207959552 | bytes 5144576 | tf_op jit(solution)/shard_map/up_two/pallas_call | solution.py:43
  83.7 2.7 %collective-permute-done.15.right.rright = f32[32,512]{1,0:T(8,128)S(1)} collective-permute-done((f32[32,512]{1,0:T(8,128)S(1)}, f32[32,512]{1,0:T(8,128)S(1)}, u32[]{:S(2)}, u32[]{:S(2)}) %collective-permute-start.15) | collective-permute-done | bytes 65568 | tf_op jit(solution)/shard_map/ppermute | solution.py:1011
  87.2 9.1 %up_one.1 = (bf16[1024,512]{1,0:T(8,128)(2,1)S(1)}, f32[1024,256]{1,0:T(8,128)S(1)}, f32[32,256]{1,0:T(8,128)S(1)}, bf16[4,272,256]{2,1,0:T(8,128)(2,1)}) custom-call(f32[1024,512]{1,0:T(8,128)} %copy-done.2, f32[32,512]{1,0:T(8,128)S(1)} %collective-permute-done.14.left.rleft, f32[32,512]{1,0:T(8,128)S(1)} %collective-permute-done.15.right.rright, ...), custom_call_target="tpu_custom_call" | custom-call | flops 1610612736 | bytes 10645504 | tf_op jit(solution)/shard_map/up_one/pallas_call | solution.py:43
  99.0 3.8 %all-to-all-start = ((bf16[4,272,256]{2,1,0:T(8,128)(2,1)}), bf16[4,272,256]{2,1,0:T(8,128)(2,1)S(1)}, u32[]{:S(2)}, u32[]{:S(2)}) async-start(bf16[4,272,256]{2,1,0:T(8,128)(2,1)} %get-tuple-element.88), calls=%async_computation | async-start | bytes 1114112 | tf_op jit(solution)/shard_map/all_to_all | solution.py:1015
  102.9 8.0 %all-to-all-done.masks = bf16[4,272,256]{2,1,0:T(8,128)(2,1)S(1)} async-done(((bf16[4,272,256]{2,1,0:T(8,128)(2,1)}), bf16[4,272,256]{2,1,0:T(8,128)(2,1)S(1)}, u32[]{:S(2)}, u32[]{:S(2)}) %all-to-all-start) | async-done | bytes 557088 | tf_op jit(solution)/shard_map/all_to_all | solution.py:1015
  113.7 4.1 %all-to-all-start.1 = ((bf16[4,272,256]{2,1,0:T(8,128)(2,1)}), bf16[4,272,256]{2,1,0:T(8,128)(2,1)}, u32[]{:S(2)}, u32[]{:S(2)}) async-start(bf16[4,272,256]{2,1,0:T(8,128)(2,1)} %get-tuple-element.91), calls=%async_computation.1 | async-start | bytes 1114112 | tf_op jit(solution)/shard_map/all_to_all | solution.py:1015
  123.4 3.8 %all-to-all-done.1.grad = bf16[4,272,256]{2,1,0:T(8,128)(2,1)} async-done(((bf16[4,272,256]{2,1,0:T(8,128)(2,1)}), bf16[4,272,256]{2,1,0:T(8,128)(2,1)}, u32[]{:S(2)}, u32[]{:S(2)}) %all-to-all-start.1) | async-done | bytes 557088 | tf_op jit(solution)/shard_map/all_to_all | solution.py:1015
  129.1 9.0 %down_one_back.1 = (bf16[1024,1024]{1,0:T(8,128)(2,1)S(1)}, f32[1024,512]{1,0:T(8,128)S(1)}, f32[1024,512]{1,0:T(8,128)}, f32[8,128]{1,0:T(8,128)S(1)}, f32[8,12...) custom-call(bf16[4,272,256]{2,1,0:T(8,128)(2,1)} %all-to-all-done.1.grad, f32[1024,256]{1,0:T(8,128)S(1)} %copy-done.50, ...), custom_call_target="tpu_custom_call" | custom-call | flops 2147483648 | bytes 12353536 | tf_op jit(solution)/shard_map/down_one_back/pallas_call | solution.py:43
  144.1 6.5 %collective-permute-start.25 = (f32[8,128]{1,0:T(8,128)S(1)}, f32[8,128]{1,0:T(8,128)S(1)}, u32[]{:S(2)}, u32[]{:S(2)}) collective-permute-start(f32[8,128]{1,0:T(8,128)S(1)} %add.120), channel_id=1, source_target_pairs={{0,6},{1,7},{2,4},{3,5},{4,2},{5,3},{6,0},{7,1},{8,14},{9,15},{10,... | collective-permute-start | bytes 12296 | tf_op jit(solution)/shard_map/ppermute | solution.py:995
  151.7 6.2 %weight_up_one.1 = f32[96,128]{1,0:T(8,128)S(1)} custom-call(bf16[1024,512]{1,0:T(8,128)(2,1)S(1)} %copy-done.48, bf16[1024,1920]{1,0:T(8,128)(2,1)} %get-tuple-element.85.cat1.fine, bf16[1024,1024]{1,0:T(8,128)(2,1)S(1)} %get-tuple-element.117.fine), custom_call_target="tpu_custom_call" | custom-call | flops 2147483648 | bytes 7127040 | tf_op jit(solution)/shard_map/weight_up_one/pallas_call | solution.py:43
  158.1 10.1 %up_two_back.1 = (bf16[1024,1920]{1,0:T(8,128)(2,1)}, f32[1024,256]{1,0:T(8,128)S(1)}, f32[8,128]{1,0:T(8,128)S(1)}, f32[32,256]{1,0:T(8,128)S(1)}, f32[32,256]{1,0:T(8,128)S(1)}) custom-call(f32[1024,512]{1,0:T(8,128)S(1)} %get-tuple-element.95.g3, f32[32,512]{1,0:T(8,128)S(1)} %collective-permute-done.20.left, ...), custom_call_target="tpu_custom_call" | custom-call | flops 1006632960 | bytes 11644928 | tf_op jit(solution)/shard_map/up_two_back/pallas_call | solution.py:43
  172.4 5.1 %collective-permute-start.31 = (f32[8,128]{1,0:T(8,128)S(1)}, f32[8,128]{1,0:T(8,128)S(1)}, u32[]{:S(2)}, u32[]{:S(2)}) collective-permute-start(f32[8,128]{1,0:T(8,128)S(1)} %add.124), channel_id=1, source_target_pairs={{0,6},{1,7},{2,4},{3,5},{4,2},{5,3},{6,0},{7,1},{8,14},{9,15},{10,... | collective-permute-start | bytes 12296 | tf_op jit(solution)/shard_map/ppermute | solution.py:995
  182.6 9.1 %down_two_back.1 = (bf16[1024,256]{1,0:T(8,128)(2,1)S(1)}, f32[1024,512]{1,0:T(8,128)}, f32[8,128]{1,0:T(8,128)S(1)}, f32[32,512]{1,0:T(8,128)S(1)}, f32[32,512]{1,0:T(8,128)S(1)}) custom-call(f32[1024,256]{1,0:T(8,128)S(1)} %get-tuple-element.101.g2, f32[32,256]{1,0:T(8,128)S(1)} %collective-permute-done.26.left, ...), custom_call_target="tpu_custom_call" | custom-call | flops 1207959552 | bytes 10461184 | tf_op jit(solution)/shard_map/down_two_back/pallas_call | solution.py:43
  192.8 3.8 %collective-permute-start.37 = (f32[8,128]{1,0:T(8,128)S(1)}, f32[8,128]{1,0:T(8,128)S(1)}, u32[]{:S(2)}, u32[]{:S(2)}) collective-permute-start(f32[8,128]{1,0:T(8,128)S(1)} %add.128), channel_id=1, source_target_pairs={{0,6},{1,7},{2,4},{3,5},{4,2},{5,3},{6,0},{7,1},{8,14},{9,15},{10,... | collective-permute-start | bytes 12296 | tf_op jit(solution)/shard_map/ppermute | solution.py:995
  202.4 3.0 %collective-permute-done.33.right = f32[32,512]{1,0:T(8,128)S(1)} collective-permute-done((f32[32,512]{1,0:T(8,128)S(1)}, f32[32,512]{1,0:T(8,128)S(1)}, u32[]{:S(2)}, u32[]{:S(2)}) %collective-permute-start.33) | collective-permute-done | bytes 65568 | tf_op jit(solution)/shard_map/ppermute | solution.py:1011
  205.5 6.2 %up_one_back.1 = (bf16[1024,512]{1,0:T(8,128)(2,1)S(1)}, bf16[1024,256]{1,0:T(8,128)(2,1)}) custom-call(f32[1024,512]{1,0:T(8,128)S(1)} %copy-done.6, f32[32,512]{1,0:T(8,128)S(1)} %collective-permute-done.32.left, f32[32,512]{1,0:T(8,128)S(1)} %collective-permute-done.33.right, f32[8,128]{1,0:T(8,128)S(1)} %add_add_fusion.2.mom6, f32[8,128]{1,0:T(8,128)S(1)} %copy-done.31, ...), custom_call_target="tpu_custom_call" | custom-call | flops 805306368 | bytes 6914048 | tf_op jit(solution)/shard_map/up_one_back/pallas_call | solution.py:43
  213.8 3.0 %collective-permute-start.38 = (f32[48,128]{1,0:T(8,128)S(1)}, f32[48,128]{1,0:T(8,128)S(1)}, u32[]{:S(2)}, u32[]{:S(2)}) collective-permute-start(f32[48,128]{1,0:T(8,128)S(1)} %weight_down_one.1), channel_id=1, source_target_pairs={{0,1},{1,0},{2,3},{3,2},{4,5},{5,4},{6,7},{7,6},{8,9},{9,8},{10,11... | collective-permute-start | bytes 73736 | tf_op jit(solution)/shard_map/ppermute | solution.py:995
  222.6 3.5 %all-to-all-start.2 = ((bf16[4,256,256]{2,1,0:T(8,128)(2,1)}), bf16[4,256,256]{2,1,0:T(8,128)(2,1)S(1)}, u32[]{:S(2)}, u32[]{:S(2)}) async-start(bf16[4,256,256]{2,1,0:T(8,128)(2,1)} %bitcast.27), calls=%async_computation.2 | async-start | bytes 1048576 | tf_op jit(solution)/shard_map/all_to_all | solution.py:1015
  231.5 5.2 %collective-permute-done.45 = f32[424,128]{1,0:T(8,128)S(1)} collective-permute-done((f32[424,128]{1,0:T(8,128)S(1)}, f32[424,128]{1,0:T(8,128)S(1)}, u32[]{:S(2)}, u32[]{:S(2)}) %collective-permute-start.45) | collective-permute-done | bytes 217120 | tf_op jit(solution)/shard_map/ppermute | solution.py:995
  236.7 10.9 %collective-permute-done.44 = f32[424,128]{1,0:T(8,128)S(1)} collective-permute-done((f32[424,128]{1,0:T(8,128)S(1)}, f32[424,128]{1,0:T(8,128)S(1)}, u32[]{:S(2)}, u32[]{:S(2)}) %collective-permute-start.44) | collective-permute-done | bytes 217120 | tf_op jit(solution)/shard_map/ppermute | solution.py:995
  (326 shorter events, 115.0 us)
Async XLA Ops:
  9.6 5.9 %collective-permute-start = (bf16[80,256]{1,0:T(8,128)(2,1)S(1)}, bf16[80,256]{1,0:T(8,128)(2,1)S(1)}, u32[]{:S(2)}, u32[]{:S(2)}) collective-permute-start(bf16[80,256]{1,0:T(8,128)(2,1)S(1)} %get-tuple-element.69), channel_id=1, source_target_pairs={{0,1},{1,2},{2,3},{3,4},{4,5},{5,6},{6,7},{8,9},{9,10},{10,11},{11... | collective-permute-start | bytes 122888 | tf_op jit(solution)/shard_map/ppermute | solution.py:1006
  27.5 13.3 %collective-permute-start.7 = (f32[8,128]{1,0:T(8,128)S(1)}, f32[8,128]{1,0:T(8,128)S(1)}, u32[]{:S(2)}, u32[]{:S(2)}) collective-permute-start(f32[8,128]{1,0:T(8,128)S(1)} %add.108), channel_id=1, source_target_pairs={{0,6},{1,7},{2,4},{3,5},{4,2},{5,3},{6,0},{7,1},{8,14},{9,15},{10,... | collective-permute-start | bytes 12296 | tf_op jit(solution)/shard_map/ppermute | solution.py:995
  30.3 10.5 %collective-permute-start.6 = (f32[8,128]{1,0:T(8,128)S(1)}, f32[8,128]{1,0:T(8,128)S(1)}, u32[]{:S(2)}, u32[]{:S(2)}) collective-permute-start(f32[8,128]{1,0:T(8,128)S(1)} %add.108), channel_id=1, source_target_pairs={{0,4},{1,5},{2,6},{3,7},{4,0},{5,1},{6,2},{7,3},{8,12},{9,13},{10,... | collective-permute-start | bytes 12296 | tf_op jit(solution)/shard_map/ppermute | solution.py:995
  30.5 10.3 %collective-permute-start.5 = (f32[8,128]{1,0:T(8,128)S(1)}, f32[8,128]{1,0:T(8,128)S(1)}, u32[]{:S(2)}, u32[]{:S(2)}) collective-permute-start(f32[8,128]{1,0:T(8,128)S(1)} %add.108), channel_id=1, source_target_pairs={{0,2},{1,3},{2,0},{3,1},{4,6},{5,7},{6,4},{7,5},{8,10},{9,11},{10,... | collective-permute-start | bytes 12296 | tf_op jit(solution)/shard_map/ppermute | solution.py:995
  55.3 7.1 %collective-permute-start.13 = (f32[8,128]{1,0:T(8,128)S(1)}, f32[8,128]{1,0:T(8,128)S(1)}, u32[]{:S(2)}, u32[]{:S(2)}) collective-permute-start(f32[8,128]{1,0:T(8,128)S(1)} %add.112), channel_id=1, source_target_pairs={{0,6},{1,7},{2,4},{3,5},{4,2},{5,3},{6,0},{7,1},{8,14},{9,15},{10,... | collective-permute-start | bytes 12296 | tf_op jit(solution)/shard_map/ppermute | solution.py:995
  76.6 7.1 %collective-permute-start.19 = (f32[8,128]{1,0:T(8,128)S(1)}, f32[8,128]{1,0:T(8,128)S(1)}, u32[]{:S(2)}, u32[]{:S(2)}) collective-permute-start(f32[8,128]{1,0:T(8,128)S(1)} %add.116), channel_id=1, source_target_pairs={{0,6},{1,7},{2,4},{3,5},{4,2},{5,3},{6,0},{7,1},{8,14},{9,15},{10,... | collective-permute-start | bytes 12296 | tf_op jit(solution)/shard_map/ppermute | solution.py:995
  99.0 11.8 %all-to-all-start = ((bf16[4,272,256]{2,1,0:T(8,128)(2,1)}), bf16[4,272,256]{2,1,0:T(8,128)(2,1)S(1)}, u32[]{:S(2)}, u32[]{:S(2)}) async-start(bf16[4,272,256]{2,1,0:T(8,128)(2,1)} %get-tuple-element.88), calls=%async_computation | async-start | bytes 1114112 | tf_op jit(solution)/shard_map/all_to_all | solution.py:1015
  113.7 13.4 %all-to-all-start.1 = ((bf16[4,272,256]{2,1,0:T(8,128)(2,1)}), bf16[4,272,256]{2,1,0:T(8,128)(2,1)}, u32[]{:S(2)}, u32[]{:S(2)}) async-start(bf16[4,272,256]{2,1,0:T(8,128)(2,1)} %get-tuple-element.91), calls=%async_computation.1 | async-start | bytes 1114112 | tf_op jit(solution)/shard_map/all_to_all | solution.py:1015
  138.2 5.9 %collective-permute-start.22 = (f32[8,128]{1,0:T(8,128)S(1)}, f32[8,128]{1,0:T(8,128)S(1)}, u32[]{:S(2)}, u32[]{:S(2)}) collective-permute-start(f32[8,128]{1,0:T(8,128)S(1)} %get-tuple-element.98), channel_id=1, source_target_pairs={{0,1},{1,0},{2,3},{3,2},{4,5},{5,4},{6,7},{7,6},{8,9},{9,8},{10,11... | collective-permute-start | bytes 12296 | tf_op jit(solution)/shard_map/ppermute | solution.py:995
  140.5 17.5 %collective-permute-start.20 = (f32[32,512]{1,0:T(8,128)S(1)}, f32[32,512]{1,0:T(8,128)S(1)}, u32[]{:S(2)}, u32[]{:S(2)}) collective-permute-start(f32[32,512]{1,0:T(8,128)S(1)} %get-tuple-element.96), channel_id=1, source_target_pairs={{0,1},{1,2},{2,3},{3,4},{4,5},{5,6},{6,7},{8,9},{9,10},{10,11},{11... | collective-permute-start | bytes 196616 | tf_op jit(solution)/shard_map/ppermute | solution.py:1006
  142.6 15.4 %collective-permute-start.21 = (f32[32,512]{1,0:T(8,128)S(1)}, f32[32,512]{1,0:T(8,128)S(1)}, u32[]{:S(2)}, u32[]{:S(2)}) collective-permute-start(f32[32,512]{1,0:T(8,128)S(1)} %get-tuple-element.97), channel_id=1, source_target_pairs={{1,0},{2,1},{3,2},{4,3},{5,4},{6,5},{7,6},{9,8},{10,9},{11,10},{12... | collective-permute-start | bytes 196616 | tf_op jit(solution)/shard_map/ppermute | solution.py:1011
  144.1 13.9 %collective-permute-start.25 = (f32[8,128]{1,0:T(8,128)S(1)}, f32[8,128]{1,0:T(8,128)S(1)}, u32[]{:S(2)}, u32[]{:S(2)}) collective-permute-start(f32[8,128]{1,0:T(8,128)S(1)} %add.120), channel_id=1, source_target_pairs={{0,6},{1,7},{2,4},{3,5},{4,2},{5,3},{6,0},{7,1},{8,14},{9,15},{10,... | collective-permute-start | bytes 12296 | tf_op jit(solution)/shard_map/ppermute | solution.py:995
  150.6 7.4 %collective-permute-start.24 = (f32[8,128]{1,0:T(8,128)S(1)}, f32[8,128]{1,0:T(8,128)S(1)}, u32[]{:S(2)}, u32[]{:S(2)}) collective-permute-start(f32[8,128]{1,0:T(8,128)S(1)} %add.120), channel_id=1, source_target_pairs={{0,4},{1,5},{2,6},{3,7},{4,0},{5,1},{6,2},{7,3},{8,12},{9,13},{10,... | collective-permute-start | bytes 12296 | tf_op jit(solution)/shard_map/ppermute | solution.py:995
  151.7 6.3 %collective-permute-start.23 = (f32[8,128]{1,0:T(8,128)S(1)}, f32[8,128]{1,0:T(8,128)S(1)}, u32[]{:S(2)}, u32[]{:S(2)}) collective-permute-start(f32[8,128]{1,0:T(8,128)S(1)} %add.120), channel_id=1, source_target_pairs={{0,2},{1,3},{2,0},{3,1},{4,6},{5,7},{6,4},{7,5},{8,10},{9,11},{10,... | collective-permute-start | bytes 12296 | tf_op jit(solution)/shard_map/ppermute | solution.py:995
  169.1 13.4 %collective-permute-start.26 = (f32[32,256]{1,0:T(8,128)S(1)}, f32[32,256]{1,0:T(8,128)S(1)}, u32[]{:S(2)}, u32[]{:S(2)}) collective-permute-start(f32[32,256]{1,0:T(8,128)S(1)} %get-tuple-element.102), channel_id=1, source_target_pairs={{0,1},{1,2},{2,3},{3,4},{4,5},{5,6},{6,7},{8,9},{9,10},{10,11},{11... | collective-permute-start | bytes 98312 | tf_op jit(solution)/shard_map/ppermute | solution.py:1006
  171.1 11.5 %collective-permute-start.27 = (f32[32,256]{1,0:T(8,128)S(1)}, f32[32,256]{1,0:T(8,128)S(1)}, u32[]{:S(2)}, u32[]{:S(2)}) collective-permute-start(f32[32,256]{1,0:T(8,128)S(1)} %get-tuple-element.103), channel_id=1, source_target_pairs={{1,0},{2,1},{3,2},{4,3},{5,4},{6,5},{7,6},{9,8},{10,9},{11,10},{12... | collective-permute-start | bytes 98312 | tf_op jit(solution)/shard_map/ppermute | solution.py:1011
  172.4 10.1 %collective-permute-start.31 = (f32[8,128]{1,0:T(8,128)S(1)}, f32[8,128]{1,0:T(8,128)S(1)}, u32[]{:S(2)}, u32[]{:S(2)}) collective-permute-start(f32[8,128]{1,0:T(8,128)S(1)} %add.124), channel_id=1, source_target_pairs={{0,6},{1,7},{2,4},{3,5},{4,2},{5,3},{6,0},{7,1},{8,14},{9,15},{10,... | collective-permute-start | bytes 12296 | tf_op jit(solution)/shard_map/ppermute | solution.py:995
  192.8 9.6 %collective-permute-start.37 = (f32[8,128]{1,0:T(8,128)S(1)}, f32[8,128]{1,0:T(8,128)S(1)}, u32[]{:S(2)}, u32[]{:S(2)}) collective-permute-start(f32[8,128]{1,0:T(8,128)S(1)} %add.128), channel_id=1, source_target_pairs={{0,6},{1,7},{2,4},{3,5},{4,2},{5,3},{6,0},{7,1},{8,14},{9,15},{10,... | collective-permute-start | bytes 12296 | tf_op jit(solution)/shard_map/ppermute | solution.py:995
  216.8 9.6 %collective-permute-start.42 = (f32[424,128]{1,0:T(8,128)S(1)}, f32[424,128]{1,0:T(8,128)S(1)}, u32[]{:S(2)}, u32[]{:S(2)}) collective-permute-start(f32[424,128]{1,0:T(8,128)S(1)} %pad_maximum_fusion), channel_id=1, source_target_pairs={{0,1},{1,0},{2,3},{3,2},{4,5},{5,4},{6,7},{7,6},{8,9},{9,8},{10,11... | collective-permute-start | bytes 651272 | tf_op jit(solution)/shard_map/ppermute | solution.py:995
  217.7 8.4 %collective-permute-start.41 = (f32[48,128]{1,0:T(8,128)S(1)}, f32[48,128]{1,0:T(8,128)S(1)}, u32[]{:S(2)}, u32[]{:S(2)}) collective-permute-start(f32[48,128]{1,0:T(8,128)S(1)} %add.132), channel_id=1, source_target_pairs={{0,6},{1,7},{2,4},{3,5},{4,2},{5,3},{6,0},{7,1},{8,14},{9,15},{10,... | collective-permute-start | bytes 73736 | tf_op jit(solution)/shard_map/ppermute | solution.py:995
  222.6 29.0 %all-to-all-start.2 = ((bf16[4,256,256]{2,1,0:T(8,128)(2,1)}), bf16[4,256,256]{2,1,0:T(8,128)(2,1)S(1)}, u32[]{:S(2)}, u32[]{:S(2)}) async-start(bf16[4,256,256]{2,1,0:T(8,128)(2,1)} %bitcast.27), calls=%async_computation.2 | async-start | bytes 1048576 | tf_op jit(solution)/shard_map/all_to_all | solution.py:1015
  226.4 10.2 %collective-permute-start.45 = (f32[424,128]{1,0:T(8,128)S(1)}, f32[424,128]{1,0:T(8,128)S(1)}, u32[]{:S(2)}, u32[]{:S(2)}) collective-permute-start(f32[424,128]{1,0:T(8,128)S(1)} %fusion.1), channel_id=1, source_target_pairs={{0,6},{1,7},{2,4},{3,5},{4,2},{5,3},{6,0},{7,1},{8,14},{9,15},{10,... | collective-permute-start | bytes 651272 | tf_op jit(solution)/shard_map/ppermute | solution.py:995
  229.1 18.5 %collective-permute-start.44 = (f32[424,128]{1,0:T(8,128)S(1)}, f32[424,128]{1,0:T(8,128)S(1)}, u32[]{:S(2)}, u32[]{:S(2)}) collective-permute-start(f32[424,128]{1,0:T(8,128)S(1)} %fusion.1), channel_id=1, source_target_pairs={{0,4},{1,5},{2,6},{3,7},{4,0},{5,1},{6,2},{7,3},{8,12},{9,13},{10,... | collective-permute-start | bytes 651272 | tf_op jit(solution)/shard_map/ppermute | solution.py:995
  229.1 18.5 %collective-permute-start.43 = (f32[424,128]{1,0:T(8,128)S(1)}, f32[424,128]{1,0:T(8,128)S(1)}, u32[]{:S(2)}, u32[]{:S(2)}) collective-permute-start(f32[424,128]{1,0:T(8,128)S(1)} %fusion.1), channel_id=1, source_target_pairs={{0,2},{1,3},{2,0},{3,1},{4,6},{5,7},{6,4},{7,5},{8,10},{9,11},{10,... | collective-permute-start | bytes 651272 | tf_op jit(solution)/shard_map/ppermute | solution.py:995
  (92 other events, 752.4 us)

commit v2 on v1

v2 whole, which is shorter than its diff:
```python
import jax
import jax.numpy as jnp
from jax import lax
from jax.experimental import pallas as pl
from jax.experimental.pallas import tpu as pltpu
from jax.sharding import PartitionSpec as P

NORM_EPS = 0.001
RATIO_EPS = 1e-10
BF = jnp.bfloat16
F32 = jnp.float32
TAPS = 5
L = 128
M = 32
NJ = 32
R = M * NJ
CHUNK = 256
COLS0 = 1024
COLS1 = 1920
COLS1B = 1536
COLS2 = 1152
GROUPS1 = ((0, 1024, 1), (256, 1152, 2), (512, 1280, 0), (768, 1408, 3), (1536, 1792, 4))
FULL = pl.BlockSpec(memory_space=pltpu.VMEM)
SCALAR = pl.BlockSpec(memory_space=pltpu.SMEM)
FAR = pl.BlockSpec(memory_space=pltpu.HBM)


class Far:
    def __init__(self, array, columns=None):
        self.array, self.columns = array, columns


class Arriving:
    def __init__(self, source, target, sem):
        self.copy, self.target, self.waited = pltpu.make_async_copy(source, target, sem), target, False
        self.copy.start()

    def get(self):
        if not self.waited:
            self.copy.wait()
            self.waited = True
        return self.target


class Leaving:
    def __init__(self, target, sem):
        self.target, self.sem, self.copy = target, sem, None

    def put(self, source):
        self.copy = pltpu.make_async_copy(source, self.target, self.sem)
        self.copy.start()


def run(kernel, name, outs, args, scratch=(), flops=0):
    arrays = [a.array if isinstance(a, Far) else a for a in args]
    far_in = [k for k, a in enumerate(args) if isinstance(a, Far)]
    far_out = [k for k, o in enumerate(outs) if len(o) == 3]
    n_in, n_out, n_own = len(args), len(outs), len(scratch)
    placed = [
        pltpu.with_memory_space_constraint(a.array, pltpu.HBM) if isinstance(a, Far) else a for a in args
    ]
    landing = []
    for k in far_in:
        shape = args[k].array.shape
        if args[k].columns is not None:
            shape = (shape[0], args[k].columns)
        landing.append(pltpu.VMEM(shape, args[k].array.dtype))

    def body(*refs):
        ins, results = list(refs[:n_in]), list(refs[n_in : n_in + n_out])
        own = refs[n_in + n_out : n_in + n_out + n_own]
        targets = refs[n_in + n_out + n_own : n_in + n_out + n_own + len(far_in)]
        sems = refs[-1]
        for i, k in enumerate(far_in):
            source = ins[k] if args[k].columns is None else ins[k].at[:, 0 : args[k].columns]
            ins[k] = Arriving(source, targets[i], sems.at[i])
        for i, k in enumerate(far_out):
            results[k] = Leaving(results[k], sems.at[len(far_in) + i])
        kernel(*ins, *results, *own)
        for k in far_in:
            ins[k].get()
        for k in far_out:
            results[k].copy.wait()

    in_specs = []
    for a in args:
        if isinstance(a, Far):
            in_specs.append(FAR)
        else:
            in_specs.append(SCALAR if a.dtype == jnp.int32 else FULL)
    bytes_all = sum(a.size * a.dtype.itemsize for a in arrays)
    bytes_all += sum(jnp.zeros((), o[1]).dtype.itemsize * o[0][0] * o[0][-1] for o in outs)
    return pl.pallas_call(
        body,
        out_shape=[
            pltpu.HBM(o[0], o[1]) if len(o) == 3 else jax.ShapeDtypeStruct(o[0], o[1]) for o in outs
        ],
        in_specs=in_specs,
        out_specs=[FAR if len(o) == 3 else FULL for o in outs],
        scratch_shapes=[pltpu.VMEM(s, d) for s, d in scratch]
        + landing
        + [pltpu.SemaphoreType.DMA((max(1, len(far_in) + len(far_out)),))],
        compiler_params=pltpu.CompilerParams(vmem_limit_bytes=24 << 20),
        cost_estimate=pl.CostEstimate(flops=flops, bytes_accessed=bytes_all, transcendentals=0),
        name=name,
    )(*placed)


def lane(shape):
    return lax.broadcasted_iota(jnp.int32, shape, 1)


def sub(shape):
    return lax.broadcasted_iota(jnp.int32, shape, 0)


def rows(j, count=M):
    return pl.ds(pl.multiple_of(j * count, count), count)


def tiles(width):
    return [slice(L * k, L * k + L) for k in range(width // L)]


def for_blocks(fn, count=NJ):
    def body(j, carry):
        fn(j)
        return carry

    lax.fori_loop(0, count, body, 0)


def for_blocks_rims(fn):
    def body(j, carry):
        fn(j, True, True)
        return carry

    fn(0, False, True)
    lax.fori_loop(1, NJ - 1, body, 0)
    fn(NJ - 1, True, False)


def from_prev(value, rim, flag):
    rim = jnp.concatenate([rim] * (M // 8), axis=0)
    return jnp.where(sub(value.shape) == 0, rim, pltpu.roll(value, 1, 0)) * flag


def from_next(value, rim, flag):
    rim = jnp.concatenate([rim] * (M // 8), axis=0)
    return jnp.where(sub(value.shape) == M - 1, rim, pltpu.roll(value, M - 1, 0)) * flag


def widen(source, out):
    def group(g):
        for at in tiles(source.shape[1]):
            tile = source[rows(g, 8), at]
            for i in range(8):
                out[rows(8 * g + i, 8), at] = jnp.broadcast_to(tile[i : i + 1], (8, L))

    for_blocks(group, NJ // 8)


def mask_bf(cond):
    return jnp.where(cond, 1.0, 0.0).astype(BF)


def fill_rims(cat, parts, low, high):
    def one(j, has_prev, has_next):
        for target, after, before in parts:
            value = None
            if has_next:
                value = cat[rows(j + 1), after : after + L] * low
            if has_prev:
                other = cat[rows(j - 1), before : before + L] * high
                value = other if value is None else value + other
            cat[rows(j), target : target + L] = value

    for_blocks_rims(one)


def rims_1(cat, groups):
    at = lane((M, L))
    parts = [(rim, base, base + L) for base, rim, _ in groups]
    fill_rims(cat, parts, mask_bf(at < 32), mask_bf(at >= 112))


def rims_2(cat):
    at = lane((M, L))
    parts = [(768 + L * k, 256 * k, 256 * k + L) for k in range(3)]
    fill_rims(cat, parts, mask_bf(at < 32), mask_bf(at >= 96))


def rims_0(cat):
    at = lane((M, L)) % 32
    fill_rims(cat, [(512 + L * k, L * k, L * k) for k in range(4)], mask_bf(at < 2), mask_bf(at == 31))


def matmul(left, right, transposed=False):
    return lax.dot_general(
        left, right, (((1,), (1 if transposed else 0,)), ((), ())), preferred_element_type=F32
    )


def for_chunks(fn, size=CHUNK):
    def body(r, carry):
        fn(pl.ds(pl.multiple_of(r * size, size), size))
        return carry

    lax.fori_loop(0, R // size, body, 0)


def sum8(value):
    total = value[0:8]
    for k in range(1, value.shape[0] // 8):
        total = total + value[8 * k : 8 * k + 8]
    return total


def sum_blocks(fn):
    def body(j, carry):
        return fn(j, *carry)

    zero = jnp.zeros((8, L), F32)
    return [total_rows(s) for s in lax.fori_loop(0, NJ, body, (zero, zero))]


def fold(stats, period):
    step = L // 2
    while step >= period:
        stats = stats + pltpu.roll(stats, step, 1)
        step //= 2
    return stats


def stack_rows(values):
    at = sub((8, L))
    tile = jnp.zeros((8, L), F32)
    for k, value in enumerate(values):
        tile = jnp.where(at == k, value, tile)
    return tile


def total_rows(value):
    return jnp.sum(value, axis=0, keepdims=True)


def norm_terms(moments, count):
    mean = moments[0:1] / count
    return mean, lax.rsqrt(moments[1:2] / count - mean * mean + NORM_EPS)


def silu(v):
    return v / (1.0 + jnp.exp(-v))


def silu_slope(v):
    s = 1.0 / (1.0 + jnp.exp(-v))
    return s * (1.0 + v * (1.0 - s))


def sigmoid(v):
    return 1.0 / (1.0 + jnp.exp(-v))


def softplus(v):
    return jnp.maximum(v, 0.0) + jnp.log1p(jnp.exp(-jnp.abs(v)))


def softplus_slope(r):
    return jnp.where(r < 0.05, r * (1.0 - r * (0.5 - r * (1.0 / 6.0))), 1.0 - jnp.exp(-r))


def end_rows(z, group_out, blocks=NJ):
    def group(g):
        for at in tiles(z.shape[1]):
            place = sub((8, L))
            top = low = jnp.zeros((8, L), F32)
            for i in range(8):
                start = pl.multiple_of((8 * g + i) * M, M)
                top = jnp.where(place == i, z[pl.ds(start, 8), at][0:1], top)
                low = jnp.where(place == i, z[pl.ds(start + M - 8, 8), at][7:8], low)
            group_out(rows(g, 8), at, top, low)

    for_blocks(group, blocks // 8)


def pack_ends(z, index, cross, core, blocks=NJ):
    even = index[1] == 0

    def group_out(rs, at, top, low):
        cross[rs, at] = jnp.where(even, top, low)
        core[rs, at] = jnp.where(even, low, top)

    end_rows(z, group_out, blocks)


def pack_moments(mom, cross, value):
    mom[...] = value
    cross[NJ : NJ + 8, 0:L] = value


def sides(index, cross, core, at):
    even = index[1] == 0
    a, b = cross[0:NJ, at], core[0:NJ, at]
    return jnp.where(even, a, b), jnp.where(even, b, a)


def tile_2(w, tap, q, half):
    at = lane((16, L)) // 32
    tile = jnp.zeros((16, L), F32)
    for k in range(4):
        b = q - 2 * (4 * half + k) + 1
        if 0 <= b < TAPS:
            start = (tap * TAPS + b) * 16
            tile = jnp.where(at == k, w[start : start + 16, :], tile)
    return tile.astype(BF)


def matrix_2_down(w, t):
    zero = jnp.zeros((16, L), BF)
    for base, rim, tap in GROUPS1:
        for half in range(2):
            at = slice(L * half, L * half + L)
            for q in range(16):
                t[base + 16 * q : base + 16 * q + 16, at] = tile_2(w, tap, q, half)
            for part in range(8):
                q = {0: 16, 1: 17, 7: -1}.get(part)
                start = rim + 16 * part
                t[start : start + 16, at] = zero if q is None else tile_2(w, tap, q, half)


def matrix_2_up(w, t):
    zero = jnp.zeros((16, L), BF)
    at = lane((16, L))
    for row in range(2):
        for k, tap in enumerate((row + 1, row + 3, row - 1)):
            for q in range(16):
                span = slice(row * 256 + q * 16, row * 256 + q * 16 + 16)
                for half in range(2):
                    cols = slice(256 * k + L * half, 256 * k + L * half + L)
                    t[span, cols] = tile_2(w, tap, q, half) if 0 <= tap < TAPS else zero
                rim = zero
                if 0 <= tap < TAPS and q in (0, 1, 15):
                    b = {0: 3, 1: 4, 15: 0}[q]
                    start = (tap * TAPS + b) * 16
                    cond = at < 32 if q == 15 else at >= 96
                    rim = jnp.where(cond, w[start : start + 16, :], 0.0).astype(BF)
                t[span, 768 + L * k : 768 + L * k + L] = rim


def band(w, tap, channel, offset):
    tile = jnp.zeros((32, L), F32)
    for b in range(TAPS):
        start = (tap * 2 + channel) * TAPS + b
        tile = jnp.where(offset == b, w[start : start + 1, :], tile)
    return tile.astype(BF)


def matrix_1_down(w, t, col):
    q, zero = sub((32, L)), jnp.zeros((32, L), BF)
    for half in range(2):
        p = 8 * half + lane((32, L)) // 16
        inner = q - 2 * p + 1
        rim = jnp.where(q == 31, -2 * p, jnp.where(q == 0, 33 - 2 * p, jnp.where(q == 1, 34 - 2 * p, -9)))
        for row in range(2):
            cols = slice(col + row * 256 + half * L, col + row * 256 + half * L + L)
            for part, frame in enumerate((0, 1, 2, 3, None, -1, 4, 5)):
                tap = -1 if frame is None else frame - 2 * row + 1
                for c in range(2):
                    start = part * 64 + c * 32
                    ok = 0 <= tap < TAPS
                    t[start : start + 32, cols] = band(w, tap, c, inner) if ok else zero
                    t[512 + start : 544 + start, cols] = band(w, tap, c, rim) if ok else zero


def matrix_1_up(w, t, col):
    q, zero = sub((32, L)), jnp.zeros((32, L), BF)
    at = lane((32, L))
    rim = jnp.where(at < 16, q - 31, jnp.where(at >= 112, q + 3, -9))
    for frame in range(4):
        taps = (frame + 1, frame - 1, frame + 3, frame - 3)
        for c in range(2):
            span = slice(frame * 64 + c * 32, frame * 64 + c * 32 + 32)
            for k, tap in enumerate(taps):
                ok = 0 <= tap < TAPS
                for half in range(2):
                    p = 8 * half + at // 16
                    start = col + 256 * k + L * half
                    t[span, start : start + L] = band(w, tap, c, q - 2 * p + 1) if ok else zero
                start = col + 1024 + L * k
                t[span, start : start + L] = band(w, tap, c, rim) if ok else zero


def matrices_first(w1c, t1a):
    matrix_1_down(w1c, t1a, 0)


def matrices_forward(w2c, w2d, w1d, t2a_c, t2b_d, t1b_d, a, b, c):
    matrix_2_down(w2c, a)
    t2a_c.put(a)
    matrix_2_up(w2d, b)
    t2b_d.put(b)
    matrix_1_up(w1d.at[0], c, 0)
    matrix_1_up(w1d.at[1], c, COLS1B)
    t1b_d.put(c)


def matrices_back(w1c, w2c, w2d, w1d, t1a_d, t2a_d, t2b_c, t1b_c, a, b, c, d):
    w1c, w2c, w2d, w1d = [w.get() for w in (w1c, w2c, w2d, w1d)]
    matrix_1_down(w1d.at[0], a, 0)
    matrix_1_down(w1d.at[1], a, 512)
    t1a_d.put(a)
    matrix_2_down(w2d, b)
    t2a_d.put(b)
    matrix_2_up(w2c, c)
    t2b_c.put(c)
    matrix_1_up(w1c, d, 0)
    t1b_c.put(d)


def correlate(coarse, fine, d):
    def part(rs, first):
        value = lax.dot_general(
            coarse[rs, :], fine[rs, :], (((0,), (0,)), ((), ())), preferred_element_type=F32
        )
        d[...] = value if first else d[...] + value

    part(pl.ds(0, CHUNK), True)

    def body(r, carry):
        part(pl.ds(pl.multiple_of(r * CHUNK, CHUNK), CHUNK), False)
        return carry

    lax.fori_loop(1, R // CHUNK, body, 0)


def weight_2(d, out):
    at = lane((32, L))
    sums = {}
    for base, rim, tap in GROUPS1:
        total = jnp.zeros((32, L), F32)
        for p in range(8):
            span = slice(32 * p, 32 * p + 32)
            parts = [d[span, base : base + L], d[span, base + L : base + 256], d[span, rim : rim + L]]
            if p == 0:
                value = jnp.where(at < 16, pltpu.roll(parts[2], 16, 1), pltpu.roll(parts[0], 16, 1))
            else:
                which, off = divmod(32 * p - 16, L)
                value = pltpu.roll(parts[which], L - off, 1)
                if off + 80 > L:
                    value = jnp.where(at < L - off, value, pltpu.roll(parts[which + 1], L - off, 1))
            total = total + value
        sums[tap] = total
    out[0:32, :] = jnp.where(at < 80, sums[0], pltpu.roll(sums[4], 80, 1))
    out[32:64, :] = jnp.where(at < 80, sums[1], pltpu.roll(sums[4], 32, 1))
    out[64:96, :] = sums[2]
    out[96:128, :] = sums[3]


def weight_1(d, out, start):
    at = lane((16, L)) % 32
    result = jnp.zeros((16, L), F32)
    for k in range(3):
        total = jnp.zeros((16, L), F32)
        for row in range(2):
            tile = (2, 0, 1)[k] if row == 0 else (0, 1, 3)[k]
            for p in range(16):
                first = row * 256 + p * 16
                span = slice(first, first + 16)
                value = pltpu.roll(d[span, L * tile : L * tile + L], (1 - 2 * p) % L, 1)
                if p in (0, 15):
                    rim = d[span, 512 + L * tile : 512 + L * tile + L]
                    rim = pltpu.roll(rim, L - 31 if p == 0 else 3, 1)
                    value = jnp.where(at == 0 if p == 0 else at >= 3, rim, value)
                total = total + value
        if k > 0:
            total = pltpu.roll(total, 8 * k, 1)
        result = jnp.where((at >= 8 * k) & (at < 8 * k + TAPS), total, result)
    out[start : start + 16, :] = result


def weight_2_kernel(coarse, fine, out, d):
    correlate(ready(coarse), ready(fine), d)
    weight_2(d, out)


def weight_1_first(coarse, fine, out, d):
    correlate(ready(coarse), ready(fine), d)
    weight_1(d, out, 0)


def weight_1_joined(low, cat1, fine, out, d):
    correlate(ready(low), ready(fine), d)
    weight_1(d, out, 0)
    correlate(ready(cat1), ready(fine), d)
    weight_1(d, out, 16)


def ready(ref):
    return ref.get() if isinstance(ref, Arriving) else ref


def spread(scr, store):
    at = lane((M, L)) // 32
    for half in range(2):
        parts = [scr[k % 2, pl.ds(2 * half + k // 2, M, stride=4), :] for k in range(4)]
        for block in range(4):
            value = parts[block]
            for k in range(4):
                if k != block:
                    value = jnp.where(at == k, pltpu.roll(parts[k], (32 * (k - block)) % L, 1), value)
            store(block, half, value)


def gather(blocks, scr):
    at = lane((M, L)) // 32
    for half in range(2):
        parts = [blocks(block, half) for block in range(4)]
        for k in range(4):
            value = parts[k]
            for block in range(4):
                if block != k:
                    value = jnp.where(
                        at == block, pltpu.roll(parts[block], (32 * (block - k)) % L, 1), value
                    )
            scr[k % 2, pl.ds(2 * half + k // 2, M, stride=4), :] = value


def layout_kernel(index, frame_mask, mix, cot, cross, core, x0, c0, scr, wide, xf, cf, ends):
    def place(out, block, row):
        def store(k, half, value):
            at = slice(L * half, L * half + L)
            out[rows(block + k), at] = value.astype(BF)
            wide[rows(row + k), at] = value

        return store

    m = mix.get()

    def mix_tile(t):
        for c in range(2):
            scr[c] = m[c, :, pl.ds(pl.multiple_of(t * L, L), L)].astype(F32)
        spread(scr, place(xf, 4 * t, 4 * t))

    for_blocks(mix_tile, NJ // 4)
    x0.put(xf)
    g = cot.get()
    per_stem = g.shape[3] // L

    def cot_tile(t):
        for c in range(2):
            lanes = pl.ds(pl.multiple_of((t % per_stem) * L, L), L)
            scr[c] = g[t // per_stem, c, :, lanes].astype(F32)
        spread(scr, place(cf, 4 * t, NJ + 4 * t))

    for_blocks(cot_tile, NJ // 4)
    c0.put(cf)
    ends[...] = jnp.zeros(ends.shape, F32)
    pack_ends(wide, index, ends.at[0], ends.at[1], 2 * NJ)
    even = index[1] == 0

    def least(first, count):
        value = frame_mask[first]
        for k in range(1, count):
            value = jnp.minimum(value, frame_mask[first + k])
        return value.astype(F32)

    for i, (first, count) in enumerate(((0, 2), (2, 2), (0, 4))):
        top, low = least(first, count), least(4 * M - 4 + first, count)
        row = 2 * NJ + i
        ends[0, row : row + 1, :] = jnp.full((1, 2 * L), jnp.where(even, top, low))
        ends[1, row : row + 1, :] = jnp.full((1, 2 * L), jnp.where(even, low, top))
    cross[...] = ends[0].astype(BF)
    core[...] = ends[1].astype(BF)


def columns_0(cat, blocks, read, left, right, aux):
    a, a_next = aux[0], aux[1]
    for which, (first, count) in enumerate(blocks):

        def one(i, which=which, first=first):
            j = first + i
            for half in range(2):
                value = read(which, j, half)
                cat[rows(j), L * half : L * half + L] = value.astype(BF)
                if half == 1:
                    moved = from_prev(value, left[rows(j, 8), L : 2 * L], a)
                    cat[rows(j), 256:384] = moved.astype(BF)
                else:
                    moved = from_next(value, right[rows(j, 8), 0:L], a_next)
                    cat[rows(j), 384:512] = moved.astype(BF)

        for_blocks(one, count)
    rims_0(cat)


def conv_one_kernel(
    index, x0, cross_in, core_in, aux, t,
    z, cross, core, mom, hx, kept, zfar, catfar, cat, lf, rf, lw, rw,
):
    even = index[1] == 0
    a, b = cross_in[...].astype(F32), core_in[...].astype(F32)
    lf[...] = jnp.where(even, a, b)
    rf[...] = jnp.where(even, b, a)
    hx[:, 0:L] = rf[0 : 2 * NJ, 0:L]
    hx[:, L : 2 * L] = lf[0 : 2 * NJ, L : 2 * L]
    kept[...] = jnp.zeros(kept.shape, F32)
    kept[0:3, :] = lf[2 * NJ : 2 * NJ + 3, 0:L]
    kept[3:6, :] = rf[2 * NJ : 2 * NJ + 3, 0:L]
    widen(lf.at[0:NJ], lw)
    widen(rf.at[0:NJ], rw)
    x = ready(x0)
    read = lambda which, j, h: x[rows(j), L * h : L * h + L].astype(F32)
    columns_0(cat, [(0, NJ)], read, lw, rw, aux)
    catfar.put(cat)
    weights = ready(t)

    def chunk(rs):
        z[rs, :] = matmul(cat[rs, :], weights[...])

    for_chunks(chunk)
    zfar.put(z)
    pack_ends(z, index, cross, core)

    def sums(j, s1, s2):
        for k, at in enumerate(tiles(512)):
            value = z[rows(j), at]
            part = value * aux[2 + k // 2]
            s1 = s1 + sum8(part)
            s2 = s2 + sum8(part * value)
        return s1, s2

    stats = fold(stack_rows(sum_blocks(sums)), 16)
    at = sub((8, L))
    stats = jnp.where(at == 2, total_rows(aux[2] + aux[3]) * (NJ * 16.0), stats)
    stats = jnp.where(at == 3, total_rows(aux[4]) * (NJ * 8.0), stats)
    pack_moments(mom, cross, stats)


def conv_two_kernel(
    index, z1, cross_in, core_in, mom1, prm, aux, t,
    z2, cross, core, mom, ends, h1, zfar, catfar, cat, ef, hf, lw, rw,
):
    mean, scale = norm_terms(mom1, mom1[2:3])
    gain, shift = prm[0:1], prm[1:2]

    def act(value):
        return silu((value - mean) * scale * gain + shift)

    a, a_next = aux[0], aux[1]
    for at in tiles(512):
        left, right = sides(index, cross_in, core_in, at)
        hf[0, :, at] = left
        hf[1, :, at] = right
        ef[0, :, at] = act(left)
        ef[1, :, at] = act(right)
    h1.put(hf)
    widen(ef.at[0], lw)
    widen(ef.at[1], rw)

    def one(j):
        for k, at in enumerate(tiles(512)):
            value = act(z1[rows(j), at])
            cat[rows(j), at] = value.astype(BF)
            if k >= 2:
                moved = from_prev(value, lw[rows(j, 8), at], a)
                cat[rows(j), 256 + L * k : 384 + L * k] = moved.astype(BF)
            start = 768 + L * k if k < 2 else 1280 + L * k
            moved = from_next(value, rw[rows(j, 8), at], a_next)
            cat[rows(j), start : start + L] = moved.astype(BF)

    for_blocks(one)
    rims_1(cat, GROUPS1)
    catfar.put(cat)
    weights = ready(t)

    def chunk(rs):
        z2[rs, :] = matmul(cat[rs, :], weights[...])

    for_chunks(chunk)
    zfar.put(z2)
    pack_ends(z2, index, cross, core)

    def sums(j, s1, s2):
        for at in tiles(256):
            value = z2[rows(j), at]
            part = value * aux[4]
            s1 = s1 + sum8(part)
            s2 = s2 + sum8(part * value)
        return s1, s2

    pack_moments(mom, cross, fold(stack_rows(sum_blocks(sums)), 32))

    def group_out(rs, at, top, low):
        ef[2, rs, at] = act(top)
        ef[3, rs, at] = act(low)

    end_rows(z1, group_out)
    ends[...] = ef[...].astype(BF)


def columns_2(cat, read, left, right, aux):
    a, a_next = aux[0], aux[1]

    def one(j):
        for k, at in enumerate(tiles(256)):
            value = read(j, at)
            cat[rows(j), at] = value.astype(BF)
            moved = from_prev(value, left[rows(j, 8), at], a)
            cat[rows(j), 256 + L * k : 384 + L * k] = moved.astype(BF)
            moved = from_next(value, right[rows(j, 8), at], a_next)
            cat[rows(j), 512 + L * k : 640 + L * k] = moved.astype(BF)

    for_blocks(one)
    rims_2(cat)


def up_two_kernel(
    index, z2, cross_in, core_in, mom1, mom2, prm, aux, t,
    rect, cross, core, mom, h2, act2, rectfar, cat, hf, lf, rf, lw, rw,
):
    mean, scale = norm_terms(mom2, mom1[3:4])
    gain, shift, bias = prm[2:3], prm[3:4], prm[6:7]

    def act(value):
        return silu((value - mean) * scale * gain + shift)

    for at in tiles(256):
        left, right = sides(index, cross_in, core_in, at)
        hf[0, :, at] = left
        hf[1, :, at] = right
        lf[:, at] = act(left)
        rf[:, at] = act(right)
    h2.put(hf)
    widen(lf, lw)
    widen(rf, rw)
    columns_2(cat, lambda j, at: act(z2[rows(j), at]), lw, rw, aux)
    act2.put(cat.at[:, 0:256])
    weights = ready(t)

    def chunk(rs):
        rect[rs, :] = matmul(cat[rs, :], weights[...], True)

    for_chunks(chunk)

    def sums(j, s1, s2):
        for k, at in enumerate(tiles(512)):
            value = softplus(rect[rows(j), at] + bias)
            rect[rows(j), at] = value
            part = value * aux[2 + k // 2]
            s1 = s1 + sum8(part)
            s2 = s2 + sum8(part * value)
        return s1, s2

    stats = sum_blocks(sums)
    rectfar.put(rect)
    pack_moments(mom, cross, fold(stack_rows(stats), 16))
    pack_ends(rect, index, cross, core)


def columns_1b(cat, read, left, right, aux):
    a, a_next = aux[0], aux[1]

    def one(j):
        for k, at in enumerate(tiles(512)):
            value = read(j, k, at)
            cat[rows(j), at] = value.astype(BF)
            if k >= 2:
                moved = from_prev(value, left[rows(j, 8), at], a)
                cat[rows(j), 256 + L * k : 384 + L * k] = moved.astype(BF)
            else:
                moved = from_next(value, right[rows(j, 8), at], a_next)
                cat[rows(j), 768 + L * k : 896 + L * k] = moved.astype(BF)

    for_blocks(one)
    rims_1(cat, GROUPS1[:4])


def edge_columns(own, prev, after):
    at = lane((NJ, L))
    place = sub((NJ, L))
    parts = [own, prev, after]
    groups = [own[:, 0:256], own[:, 256:512], prev, after]
    for g in groups:
        low = jnp.where((place == NJ - 1) | (at >= 32), 0.0, pltpu.roll(g[:, 0:L], NJ - 1, 0))
        high = jnp.where((place == 0) | (at < 112), 0.0, pltpu.roll(g[:, L : 2 * L], 1, 0))
        parts.append(low + high)
    return jnp.concatenate(parts, axis=1).astype(BF)


def quarter_blocks(index, stems):
    count = NJ // stems
    return [((index[0] ^ k) * count, count) for k in range(stems)]


def up_one_kernel(
    index, rect, cross_in, core_in, mom1, mom3, prm, aux, ends1, cat1, t,
    m0, m1, m2, m3, h3, low3, sig, sigh, cat, hf, lf, rf, ef, ff, sf, shf, lw, rw,
):
    mean, scale = norm_terms(mom3, mom1[2:3])
    gain, shift, bias = prm[4:5], prm[5:6], prm[7:8]

    def norm(value):
        return (value - mean) * scale * gain + shift

    for at in tiles(512):
        left, right = sides(index, cross_in, core_in, at)
        hf[0, :, at] = left
        hf[1, :, at] = right
        lf[:, at] = norm(left)
        rf[:, at] = norm(right)
    h3.put(hf)
    widen(lf, lw)
    widen(rf, rw)
    columns_1b(cat, lambda j, k, at: norm(rect[rows(j), at]), lw, rw, aux)
    low3.put(cat.at[:, 0:512])

    def group_out(rs, at, top, low):
        ef[0, rs, at] = norm(top)
        ef[1, rs, at] = norm(low)

    end_rows(rect, group_out)
    wide = jnp.concatenate([bias, bias], axis=1)
    zero = jnp.zeros((NJ, 256), F32)
    a, a_end = aux[0, 0:1, 0:1], aux[1, M - 1 : M, 0:1]
    e1 = [ends1[k].astype(F32) for k in range(4)]
    edges = [
        (
            edge_columns(lf[...], zero, ef[0, :, 0:256] * a),
            edge_columns(e1[0], zero, e1[2][:, 0:256] * a),
        ),
        (
            edge_columns(rf[...], ef[1, :, 256:512] * a_end, zero),
            edge_columns(e1[1], e1[3][:, 256:512] * a_end, zero),
        ),
    ]
    weights, other = ready(t), ready(cat1)
    for k, half in ((0, 1), (1, 0)):
        value = matmul(edges[k][0], weights[:, 0:COLS1B], True)
        value = value + matmul(edges[k][1], weights[:, COLS1B : 2 * COLS1B], True)
        shf[:, L * half : L * half + L] = sigmoid(value[:, L * half : L * half + L] + bias)
    sigh.put(shf)
    masks = (m0, m1, m2, m3)
    per = R // len(masks)
    for mask, (first, count) in zip(masks, quarter_blocks(index, len(masks))):
        rs = rows(lax.div(first, count), per)
        value = matmul(cat[rs, :], weights[:, 0:COLS1B], True)
        value = value + matmul(other[rs, :], weights[:, COLS1B : 2 * COLS1B], True)
        value = sigmoid(value + wide)
        sf[rs, :] = value
        mask[0:per, :] = value.astype(BF)
        ff[...] = jnp.zeros(ff.shape, F32)
        ff[0:count, :] = shf[rows(lax.div(first, count), count), :]
        mask[per : per + 16, :] = ff[...].astype(BF)
    sig.put(sf)


def ratio_terms(masks):
    squares = [m * m for m in masks]
    power = squares[0]
    for s in squares[1:]:
        power = power + s
    inverse = 1.0 / (power + RATIO_EPS)
    return [s * inverse for s in squares], inverse


def mask_back(masks, cots, mix):
    ratios, inverse = ratio_terms(masks)
    direct = cots[0] * ratios[0]
    for c, r in zip(cots[1:], ratios[1:]):
        direct = direct + c * r
    common = 2.0 * mix * inverse
    return [m * common * (c - direct) for m, c in zip(masks, cots)], direct


def mask_kernel(index, m0, m1, m2, m3, c0, x0, hx, g0, g1, g2, g3, direct, df, ff):
    masks, grads = (m0, m1, m2, m3), (g0, g1, g2, g3)
    stems = len(masks)
    per, blocks = R // stems, NJ // stems
    mine = index[0]
    cots, mix, rim = ready(c0), ready(x0), ready(hx)

    def one(j):
        for at in tiles(256):
            m = [masks[s][rows(j), at].astype(F32) for s in range(stems)]
            c = [cots[rows((mine ^ s) * blocks + j), at].astype(F32) for s in range(stems)]
            x = mix[rows(mine * blocks + j), at].astype(F32)
            values, own = mask_back(m, c, x)
            df[rows(j), at] = own
            for s in range(stems):
                grads[s][rows(j), at] = values[s].astype(BF)

    for_blocks(one, blocks)
    direct.put(df)
    m = [masks[s][per : per + 16, :].astype(F32)[0:blocks] for s in range(stems)]
    c = [rim[rows(stems + (mine ^ s), blocks), :] for s in range(stems)]
    values, _ = mask_back(m, c, rim[rows(mine, blocks), :])
    for s in range(stems):
        ff[...] = jnp.zeros(ff.shape, F32)
        ff[0:blocks, :] = values[s]
        grads[s][per : per + 16, :] = ff[...].astype(BF)


def estimate_kernel(index, m0, m1, m2, m3, x0, out, scr, est):
    masks = (m0, m1, m2, m3)
    stems = len(masks)
    blocks = NJ // stems
    mine = index[0]
    mix = ready(x0)

    def one(j):
        for at in tiles(256):
            m = [masks[s][rows(j), at].astype(F32) for s in range(stems)]
            x = mix[rows(mine * blocks + j), at].astype(F32)
            ratios, _ = ratio_terms(m)
            for s in range(stems):
                est[s, rows(j), at] = x * ratios[s]

    for_blocks(one, blocks)
    for s in range(stems):
        for t in range(blocks // 4):
            gather(
                lambda block, half, s=s, t=t: est[s, rows(4 * t + block), L * half : L * half + L], scr
            )
            for c in range(2):
                out[mine ^ s, c, :, L * t : L * t + L] = scr[c].astype(BF)


def down_one_back_kernel(
    index, q0, q1, q2, q3, sigh, sig, aux, mom1, mom3, rect, t,
    g3, cat, cross, core, mom, bias, gact, gf, hf, zf, hw,
):
    grads = (q0, q1, q2, q3)
    blocks = quarter_blocks(index, len(grads))
    per = R // len(grads)
    rim = ready(sigh)
    for grad, (first, count) in zip(grads, blocks):
        span = rows(lax.div(first, count), count)
        value = grad[per : per + 16, :].astype(F32)[0:count]
        own = rim[span, :]
        hf[span, :] = value * own * (1.0 - own)
    zf[...] = jnp.zeros(zf.shape, F32)
    widen(hf, hw)
    sigs = ready(sig)

    def read(which, j, half):
        at = slice(L * half, L * half + L)
        own = sigs[rows(j), at]
        value = grads[which][rows(j - blocks[which][0]), at].astype(F32) * own * (1.0 - own)
        zf[...] = zf[...] + sum8(value)
        return value

    columns_0(cat, blocks, read, hw, hw, aux)
    bias[...] = zf[...]
    weights = ready(t)

    def chunk(rs):
        value = matmul(cat[rs, :], weights[...])
        g3[rs, :] = value[:, 0:512]
        gf[rs, :] = value[:, 512:1024]

    for_chunks(chunk)
    gact.put(gf)
    mean, scale = norm_terms(mom3, mom1[2:3])
    pack_ends(g3, index, cross, core)
    r = ready(rect)

    def sums(j, s1, s2):
        for at in tiles(512):
            value = g3[rows(j), at]
            s1 = s1 + sum8(value)
            s2 = s2 + sum8(value * (r[rows(j), at] - mean))
        return s1, s2

    s1, s2 = sum_blocks(sums)
    pack_moments(mom, cross, fold(stack_rows([s1, s2 * scale]), 16))


def norm_back(g, xhat, kept, moments, count, factor):
    return factor * (g - kept * ((moments[0:1] + xhat * moments[1:2]) / count))


def up_two_back_kernel(
    index, g3, cross_in, core_in, mom4, mom1, mom3, mom2, prm, aux, kept, rect, h3, t, z2,
    g2, cat, cross, core, mom, lf, rf, lw, rw,
):
    count = mom1[2:3]
    mean, scale = norm_terms(mom3, count)
    factor = scale * prm[4:5]
    inverse = 1.0 / count

    def back(g, r, keep):
        xhat = (r - mean) * scale
        value = factor * (g - keep * ((mom4[0:1] + xhat * mom4[1:2]) * inverse))
        return value * softplus_slope(r)

    r, h = ready(rect), ready(h3)
    for k, at in enumerate(tiles(512)):
        left, right = sides(index, cross_in, core_in, at)
        row = k // 2
        lf[:, at] = back(left, h[0, :, at], kept[row : row + 1, :])
        rf[:, at] = back(right, h[1, :, at], kept[3 + row : 4 + row, :])
    widen(lf, lw)
    widen(rf, rw)
    a, a_next = aux[0], aux[1]

    def one(j, total):
        for k, at in enumerate(tiles(512)):
            value = back(g3[rows(j), at], r[rows(j), at], aux[2 + k // 2])
            total = total + sum8(value)
            cat[rows(j), at] = value.astype(BF)
            if k >= 2:
                moved = from_prev(value, lw[rows(j, 8), at], a)
                cat[rows(j), 256 + L * k : 384 + L * k] = moved.astype(BF)
            start = 768 + L * k if k < 2 else 1280 + L * k
            moved = from_next(value, rw[rows(j, 8), at], a_next)
            cat[rows(j), start : start + L] = moved.astype(BF)
        return total

    bias = lax.fori_loop(0, NJ, one, jnp.zeros((8, L), F32))
    rims_1(cat, GROUPS1)
    weights = ready(t)

    def chunk(rs):
        g2[rs, :] = matmul(cat[rs, :], weights[...])

    for_chunks(chunk)
    mean2, scale2 = norm_terms(mom2, mom1[3:4])
    gain, shift = prm[2:3], prm[3:4]
    z = ready(z2)

    def sums(j, s1, s2):
        for at in tiles(256):
            xhat = (z[rows(j), at] - mean2) * scale2
            value = g2[rows(j), at] * silu_slope(xhat * gain + shift)
            g2[rows(j), at] = value
            s1 = s1 + sum8(value)
            s2 = s2 + sum8(value * xhat)
        return s1, s2

    stats = fold(stack_rows(sum_blocks(sums)), 32)
    pack_ends(g2, index, cross, core)
    bias = fold(stack_rows([total_rows(bias)] * 3), 16)
    pack_moments(mom, cross, jnp.where(sub((8, L)) == 2, bias, stats))


def down_two_back_kernel(
    index, g2, cross_in, core_in, mom5, mom1, mom2, prm, aux, kept, z2, h2, t, gact, z1,
    g1, low2, cross, core, mom, cat, lf, rf, lw, rw,
):
    count = mom1[3:4]
    mean, scale = norm_terms(mom2, count)
    factor = scale * prm[2:3]
    inverse = 1.0 / count

    def back(g, z, keep):
        xhat = (z - mean) * scale
        return factor * (g - keep * ((mom5[0:1] + xhat * mom5[1:2]) * inverse))

    z, h = ready(z2), ready(h2)
    for at in tiles(256):
        left, right = sides(index, cross_in, core_in, at)
        lf[:, at] = back(left, h[0, :, at], kept[2:3, :])
        rf[:, at] = back(right, h[1, :, at], kept[5:6, :])
    widen(lf, lw)
    widen(rf, rw)
    columns_2(cat, lambda j, at: back(g2[rows(j), at], z[rows(j), at], aux[4]), lw, rw, aux)
    low2[...] = cat[:, 0:256]
    weights, added = ready(t), ready(gact)

    def chunk(rs):
        g1[rs, :] = matmul(cat[rs, :], weights[...], True) + added[rs, :]

    for_chunks(chunk)
    mean1, scale1 = norm_terms(mom1, mom1[2:3])
    gain, shift = prm[0:1], prm[1:2]
    z = ready(z1)

    def sums(j, s1, s2):
        for at in tiles(512):
            xhat = (z[rows(j), at] - mean1) * scale1
            value = g1[rows(j), at] * silu_slope(xhat * gain + shift)
            g1[rows(j), at] = value
            s1 = s1 + sum8(value)
            s2 = s2 + sum8(value * xhat)
        return s1, s2

    stats = fold(stack_rows(sum_blocks(sums)), 16)
    pack_ends(g1, index, cross, core)
    pack_moments(mom, cross, stats)


def up_one_back_kernel(
    index, g1, cross_in, core_in, mom6, mom1, prm, aux, kept, z1, h1, t,
    n0, n1, n2, n3, low1, cat, lf, rf, lw, rw,
):
    count = mom1[2:3]
    mean, scale = norm_terms(mom1, count)
    factor = scale * prm[0:1]
    inverse = 1.0 / count

    def back(g, z, keep):
        xhat = (z - mean) * scale
        return factor * (g - keep * ((mom6[0:1] + xhat * mom6[1:2]) * inverse))

    z, h = ready(z1), ready(h1)
    for k, at in enumerate(tiles(512)):
        left, right = sides(index, cross_in, core_in, at)
        row = k // 2
        lf[:, at] = back(left, h[0, :, at], kept[row : row + 1, :])
        rf[:, at] = back(right, h[1, :, at], kept[3 + row : 4 + row, :])
    widen(lf, lw)
    widen(rf, rw)
    columns_1b(
        cat, lambda j, k, at: back(g1[rows(j), at], z[rows(j), at], aux[2 + k // 2]), lw, rw, aux
    )
    low1[...] = cat[:, 0:512]
    weights = ready(t)
    nets = (n0, n1, n2, n3)
    per = R // len(nets)
    for net, (first, blocks) in zip(nets, quarter_blocks(index, len(nets))):
        rs = rows(lax.div(first, blocks), per)
        net[...] = matmul(cat[rs, :], weights[...], True).astype(BF)


def mixture_kernel(p0, p1, p2, p3, direct, out, scr):
    parts = (p0, p1, p2, p3)
    own = ready(direct)

    def tile(t):
        def block(k, half):
            at = slice(L * half, L * half + L)
            value = own[rows(4 * t + k), at]
            for part in parts:
                value = value + part[rows(4 * t + k), at].astype(F32)
            return value

        gather(block, scr)
        for c in range(2):
            out[c, :, pl.ds(pl.multiple_of(t * L, L), L)] = scr[c]

    for_blocks(tile, NJ // len(parts) // 4)


def pairs(count, offset):
    there = [(i, (i + offset) % count) for i in range(0, count, 2)]
    return there + [(b, a) for a, b in there]


def flip(values, axis, bit):
    return lax.ppermute(values, axis, [(i, i ^ bit) for i in range(lax.axis_size(axis))])


def sum_over(values, axis):
    count = lax.axis_size(axis)
    if count & (count - 1):
        return lax.psum(values, axis)
    step = 1
    while step < count:
        radix = 2 if step == 1 or count // step == 2 else 4
        moved = [flip(values, axis, step * k) for k in range(1, radix)]
        for m in moved:
            values = values + m
        step *= radix
    return values


def sum_halves(values, axis, odd):
    count = lax.axis_size(axis)
    half = values.shape[0] // 2
    top, low = values[:half], values[half:]
    mine = jnp.where(odd, low, top) + flip(jnp.where(odd, top, low), axis, 1)
    if count == 8:
        moved = [flip(mine, axis, bit) for bit in (2, 4, 6)]
        mine = mine + moved[0] + moved[1] + moved[2]
    else:
        step = 2
        while step < count:
            mine = mine + flip(mine, axis, step)
            step *= 2
    other = flip(mine, axis, 1)
    return jnp.where(odd, jnp.concatenate([other, mine]), jnp.concatenate([mine, other]))


def exchange(cross, core, mom, axis):
    count = lax.axis_size(axis)
    near = lax.ppermute(cross, axis, pairs(count, -1))
    if count == 8:
        far = lax.ppermute(mom, axis, pairs(count, 3))
        across = flip(mom, axis, 4)
        inside = flip(core, axis, 1)
        part = mom + near[NJ:, 0:L] + far + across
        return near, inside, part + flip(part, axis, 1)
    return near, flip(core, axis, 1), sum_over(mom, axis)


def swap(blocks, axis):
    return [blocks[0]] + [flip(blocks[k], axis, k) for k in range(1, len(blocks))]


def flags(seg_lengths, frame_mask, position, total):
    order = jnp.arange(seg_lengths.shape[0])
    earlier = order[None, :] < order[:, None]
    starts = 4 * jnp.sum(jnp.where(earlier, seg_lengths[None, :], 0), axis=1)
    frames = (position * M + jnp.arange(M + 1, dtype=jnp.int32)) * 4
    shut = jnp.any(frames[:, None] == starts[None, :], axis=1) | (frames == total)
    a = 1.0 - shut.astype(F32)
    keep_one = jnp.min(frame_mask.reshape(M, 2, 2), axis=2).astype(F32)
    keep_two = jnp.min(frame_mask.reshape(M, 4), axis=1).astype(F32)
    columns = jnp.stack([a[:M], a[1:], keep_one[:, 0], keep_one[:, 1], keep_two])
    return jnp.broadcast_to(columns[:, :, None], (5, M, L))


def per_device(
    mixture,
    seg_lengths,
    frame_mask,
    conv_first,
    encoder_gain_vector,
    shift_first,
    conv_second,
    gain_second,
    shift_second,
    deconv_second,
    bias_second,
    decoder_gain_vector,
    shift_third,
    deconv_first,
    bias_first,
    cotangent,
):
    position = lax.axis_index("tm")
    stems = lax.axis_size("stem")
    odd = position % 2
    index = jnp.stack([lax.axis_index("stem"), odd]).astype(jnp.int32)
    frames = mixture.shape[1]
    per, blocks = R // stems, NJ // stems
    aux = flags(seg_lengths, frame_mask, position, frames * lax.axis_size("tm"))
    prm = jnp.stack(
        [
            jnp.tile(encoder_gain_vector[0], 8),
            jnp.tile(shift_first[0], 8),
            jnp.tile(gain_second[0], 4),
            jnp.tile(shift_second[0], 4),
            jnp.tile(decoder_gain_vector[0], 8),
            jnp.tile(shift_third[0], 8),
            jnp.tile(bias_second[0], 8),
            jnp.tile(jnp.repeat(bias_first[0], 32), 2),
        ]
    )
    w1c = jnp.tile(conv_first[0].transpose(2, 1, 3, 0).reshape(50, 16).astype(F32), (1, 8))
    w1d = deconv_first[0].transpose(2, 0, 3, 1).reshape(50, 2, 16).astype(F32)
    w1d = jnp.tile(w1d.transpose(1, 0, 2), (1, 1, 8))
    w2c = jnp.tile(conv_second[0].transpose(2, 3, 1, 0).reshape(400, 32).astype(F32), (1, 4))
    w2d = jnp.tile(deconv_second[0].transpose(2, 3, 0, 1).reshape(400, 32).astype(F32), (1, 4))

    edge = 2 * NJ + 16
    cross, core, x0, c0 = run(
        layout_kernel,
        "layout",
        [((edge, 256), BF), ((edge, 256), BF), ((R, 256), BF, True), ((R, 256), BF, True)],
        [index, frame_mask, Far(mixture), Far(cotangent)],
        [((2, frames, L), F32), ((2 * R, 256), F32), ((R, 256), BF), ((R, 256), BF)]
        + [((2, edge, 256), F32)],
    )
    near = lax.ppermute(cross, "tm", pairs(lax.axis_size("tm"), -1))
    inside = flip(core, "tm", 1)
    (t1a_c,) = run(matrices_first, "matrices_first", [((COLS0, 512), BF)], [w1c])
    t2a_c, t2b_d, t1b_d = run(
        matrices_forward,
        "matrices_forward",
        [((COLS1, 256), BF, True), ((512, COLS2), BF, True), ((256, 2 * COLS1B), BF, True)],
        [w2c, w2d, w1d],
        [((COLS1, 256), BF), ((512, COLS2), BF), ((256, 2 * COLS1B), BF)],
    )
    t1a_d, t2a_d, t2b_c, t1b_c = run(
        matrices_back,
        "matrices_back",
        [((COLS0, 1024), BF, True), ((COLS1, 256), BF, True), ((512, COLS2), BF, True)]
        + [((256, COLS1B), BF, True)],
        [Far(w1c), Far(w2c), Far(w2d), Far(w1d)],
        [((COLS0, 1024), BF), ((COLS1, 256), BF), ((512, COLS2), BF), ((256, COLS1B), BF)],
    )

    def packet(lanes):
        return [((NJ + 8, lanes), F32), ((NJ, lanes), F32), ((8, L), F32)]

    def rim(lanes):
        return [((NJ, lanes), F32)] * 2

    def wide(lanes):
        return [((8 * NJ, lanes), F32)] * 2

    z1, cross, core, mom, hx, kept, z1_far, cat0 = run(
        conv_one_kernel,
        "conv_one",
        [((R, 512), F32)] + packet(512)
        + [((2 * NJ, 256), F32), ((8, L), F32), ((R, 512), F32, True), ((R, COLS0), BF, True)],
        [index, Far(x0), near, inside, aux, t1a_c],
        [((R, COLS0), BF), ((edge, 256), F32), ((edge, 256), F32)] + wide(256),
        flops=2 * R * COLS0 * 512,
    )
    near, inside, mom1 = exchange(cross, core, mom, "tm")
    z2, cross, core, mom, ends1, h1, z2_far, cat1 = run(
        conv_two_kernel,
        "conv_two",
        [((R, 256), F32)] + packet(256)
        + [((4, NJ, 512), BF), ((2, NJ, 512), F32, True), ((R, 256), F32, True), ((R, COLS1), BF, True)],
        [index, z1, near, inside, mom1, prm, aux, Far(t2a_c)],
        [((R, COLS1), BF), ((4, NJ, 512), F32), ((2, NJ, 512), F32)] + wide(512),
        flops=2 * R * COLS1 * 256,
    )
    near, inside, mom2 = exchange(cross, core, mom, "tm")
    rect, cross, core, mom, h2, act2, rect_far = run(
        up_two_kernel,
        "up_two",
        [((R, 512), F32)] + packet(512)
        + [((2, NJ, 256), F32, True), ((R, 256), BF, True), ((R, 512), F32, True)],
        [index, z2, near, inside, mom1, mom2, prm, aux, Far(t2b_d)],
        [((R, COLS2), BF), ((2, NJ, 256), F32)] + rim(256) + wide(256),
        flops=2 * R * COLS2 * 512,
    )
    near, inside, mom3 = exchange(cross, core, mom, "tm")
    *masks, h3, low3, sig, sigh = run(
        up_one_kernel,
        "up_one",
        [((per + 16, 256), BF)] * stems
        + [((2, NJ, 512), F32, True), ((R, 512), BF, True), ((R, 256), F32, True), ((NJ, 256), F32, True)],
        [index, rect, near, inside, mom1, mom3, prm, aux, ends1, Far(cat1, COLS1B), Far(t1b_d)],
        [((R, COLS1B), BF), ((2, NJ, 512), F32)] + rim(512)
        + [((2, NJ, 512), F32), ((16, 256), F32), ((R, 256), F32), ((NJ, 256), F32)] + wide(512),
        flops=2 * R * 2 * COLS1B * 256,
    )
    masks = swap(masks, "stem")
    *grads, direct = run(
        mask_kernel,
        "mask",
        [((per + 16, 256), BF)] * stems + [((per, 256), F32, True)],
        [index, *masks, Far(c0), Far(x0), Far(hx)],
        [((per, 256), F32), ((16, 256), F32)],
    )
    grads = swap(grads, "stem")
    (estimates,) = run(
        estimate_kernel,
        "estimate",
        [((stems, 2, frames, blocks * 32), BF)],
        [index, *masks, Far(x0)],
        [((2, frames, L), F32), ((stems, per, 256), F32)],
    )
    g3, cat0g, cross, core, mom, bias_one, gact = run(
        down_one_back_kernel,
        "down_one_back",
        [((R, 512), F32), ((R, COLS0), BF)] + packet(512) + [((8, L), F32), ((R, 512), F32, True)],
        [index, *grads, Far(sigh), Far(sig), aux, mom1, mom3, Far(rect_far), Far(t1a_d)],
        [((R, 512), F32), ((NJ, 256), F32), ((8, L), F32), ((8 * NJ, 256), F32)],
        flops=2 * R * COLS0 * 1024,
    )
    near, inside, mom4 = exchange(cross, core, mom, "tm")
    (w1d_grad,) = run(
        weight_1_joined,
        "weight_up_one",
        [((32, L), F32)],
        [Far(low3), Far(cat1, 512), cat0g],
        [((512, COLS0), F32)],
        flops=2 * R * COLS0 * 1024,
    )
    g2, cat1g, cross, core, mom = run(
        up_two_back_kernel,
        "up_two_back",
        [((R, 256), F32), ((R, COLS1), BF)] + packet(256),
        [index, g3, near, inside, mom4, mom1, mom3, mom2, prm, aux, kept]
        + [Far(rect_far), Far(h3), Far(t2a_d), Far(z2_far)],
        rim(512) + wide(512),
        flops=2 * R * COLS1 * 256,
    )
    near, inside, mom5 = exchange(cross, core, mom, "tm")
    (w2d_grad,) = run(
        weight_2_kernel,
        "weight_up_two",
        [((128, L), F32)],
        [Far(act2), cat1g],
        [((256, COLS1), F32)],
        flops=2 * R * COLS1 * 256,
    )
    g1, low2, cross, core, mom = run(
        down_two_back_kernel,
        "down_two_back",
        [((R, 512), F32), ((R, 256), BF)] + packet(512),
        [index, g2, near, inside, mom5, mom1, mom2, prm, aux, kept]
        + [Far(z2_far), Far(h2), Far(t2b_c), Far(gact), Far(z1_far)],
        [((R, COLS2), BF)] + rim(256) + wide(256),
        flops=2 * R * COLS2 * 512,
    )
    near, inside, mom6 = exchange(cross, core, mom, "tm")
    (w2c_grad,) = run(
        weight_2_kernel,
        "weight_down_two",
        [((128, L), F32)],
        [low2, Far(cat1)],
        [((256, COLS1), F32)],
        flops=2 * R * COLS1 * 256,
    )
    *nets, low1 = run(
        up_one_back_kernel,
        "up_one_back",
        [((per, 256), BF)] * stems + [((R, 512), BF)],
        [index, g1, near, inside, mom6, mom1, prm, aux, kept, Far(z1_far), Far(h1), Far(t1b_c)],
        [((R, COLS1B), BF)] + rim(512) + wide(512),
        flops=2 * R * COLS1B * 256,
    )
    nets = swap(nets, "stem")
    (w1c_grad,) = run(
        weight_1_first,
        "weight_down_one",
        [((16, L), F32)],
        [low1, Far(cat0)],
        [((512, COLS0), F32)],
        flops=2 * R * COLS0 * 512,
    )
    (mixture_grad,) = run(
        mixture_kernel,
        "mixture",
        [((2, frames, blocks * 32), F32)],
        [*nets, Far(direct)],
        [((2, frames, L), F32)],
    )
    spare = jnp.zeros((8, L), F32)
    early = sum_halves(jnp.concatenate([w1d_grad, bias_one, spare, w2d_grad]), "tm", odd)
    w2c_grad = sum_halves(w2c_grad, "tm", odd)
    w1c_grad = sum_over(w1c_grad, "tm")

    def outer(packed):
        taps = packed.reshape(16, 2, 2, 4, 8)[:, :, :, :3, :TAPS].transpose(0, 2, 3, 1, 4)
        return taps.reshape(16, 2, 6, TAPS)[:, :, 1:]

    def inner(packed):
        last = jnp.concatenate([packed[0:32, 80:], packed[32:64, 80:112]], axis=1)
        taps = jnp.concatenate([packed[:, :80].reshape(4, 32, 80), last[None]])
        return taps.reshape(TAPS, 32, TAPS, 16).transpose(1, 3, 0, 2)

    w1d_grad = jnp.concatenate([outer(early[0:16]), outer(early[16:32])]).transpose(1, 0, 2, 3)
    return (
        estimates,
        mixture_grad,
        outer(w1c_grad)[None],
        mom6[1, :16][None],
        mom6[0, :16][None],
        inner(w2c_grad)[None],
        mom5[1, :32][None],
        mom5[0, :32][None],
        inner(early[48:176]).transpose(1, 0, 2, 3)[None],
        mom5[2, :16][None],
        mom4[1, :16][None],
        mom4[0, :16][None],
        w1d_grad[None],
        early[32:40].reshape(8, 2, 2, 32).sum((0, 1, 3))[None],
    )


def solution(mesh):
    in_specs = (
        P(None, "tm", None),
        P(),
        P("tm"),
        P("stem", None, None, None, None),
        P("stem", None),
        P("stem", None),
        P("stem", None, None, None, None),
        P("stem", None),
        P("stem", None),
        P("stem", None, None, None, None),
        P("stem", None),
        P("stem", None),
        P("stem", None),
        P("stem", None, None, None, None),
        P("stem", None),
        P(None, None, "tm", "stem"),
    )
    out_specs = (
        P(None, None, "tm", "stem"),
        P(None, "tm", "stem"),
        P("stem", None, None, None, None),
        P("stem", None),
        P("stem", None),
        P("stem", None, None, None, None),
        P("stem", None),
        P("stem", None),
        P("stem", None, None, None, None),
        P("stem", None),
        P("stem", None),
        P("stem", None),
        P("stem", None, None, None, None),
        P("stem", None),
    )
    return jax.shard_map(
        per_device, mesh=mesh, in_specs=in_specs, out_specs=out_specs, check_vma=False
    )
```

time: 254 us -> 200 us (0.79)
  starting transfers between devices: 85.1 us -> 58 us
  local copies, waits for them, and re-layouts: 34.5 us -> 14.4 us
  waiting for transfers between devices: 43.8 us -> 26.8 us
  Pallas kernels: 82.6 us -> 92.8 us
    unnamed x136 -> x38, local copies, waits for them, and re-layouts: 26.7 us -> 5.67 us
    ppermute x46 -> x55, starting transfers between devices: 73.7 us -> 58 us  [the longest x42 32.9 us: flip(): lax.ppermute(values, axis, [(i, i ^ bit) for i in range(lax.axis_size(axi...]
    all_to_all x3 -> x0, waiting for transfers between devices: 11.8 us -> none  [swap(): return lax.all_to_all(values, axis, 0, 0, tiled=True)]
    all_to_all x3 -> x0, starting transfers between devices: 11.4 us -> none  [swap(): return lax.all_to_all(values, axis, 0, 0, tiled=True)]
    pallas_call x19, Pallas kernels: 82.6 us -> 92.8 us  [run(): pl.pallas_call(body, out_shape=[pltpu.HBM(o[0], o[1]) if len(o) == 3 else...]
    ppermute x46 -> x55, waiting for transfers between devices: 32 us -> 26.8 us  [the longest x42 23.3 us: flip(): lax.ppermute(values, axis, [(i, i ^ bit) for i in range(lax.axis_size(axi...]
  transfers between devices with their start and end apart: 49 -> 55, of which waited for: 14 -> 17; matrix products, arithmetic and copies ran while one was open for 4% -> 8% of each run, Pallas kernels for 6% -> 20%
where the time goes in v2:
time: 200 us
  Pallas kernels  92.8 us (46%)
  starting transfers between devices  58 us (29%)
  waiting for transfers between devices  26.8 us (13%)
  local copies, waits for them, and re-layouts  14.4 us (7%)
  other arithmetic  6 us (3%)
    pallas_call x19, Pallas kernels, run(): pl.pallas_call(body, out_shape=[pltpu.HBM(o[0], o[1]) if len(o) == 3 else...  92.8 us
    ppermute x42, starting transfers between devices, flip(): lax.ppermute(values, axis, [(i, i ^ bit) for i in range(lax.axis_size(axi...  32.9 us
    ppermute x42, waiting for transfers between devices, flip(): lax.ppermute(values, axis, [(i, i ^ bit) for i in range(lax.axis_size(axi...  23.3 us
    ppermute x6, starting transfers between devices, exchange(): near = lax.ppermute(cross, axis, pairs(count, -1))  13.7 us
    ppermute x6, starting transfers between devices, exchange(): far = lax.ppermute(mom, axis, pairs(count, 3))  6.77 us
    unnamed x38, local copies, waits for them, and re-layouts  5.67 us
    ppermute x1, starting transfers between devices, per_device(): near = lax.ppermute(cross, 'tm', pairs(lax.axis_size('tm'), -1))  4.55 us
  transfers between devices with their start and end apart: 55, of which 17 were waited for; matrix products, arithmetic and copies ran while one was open for 8% of the time, Pallas kernels for 20%

profile of v2, /device:TPU:0, one launch (start us, length us, event | category | flops | bytes accessed | tf_op | source)
XLA Modules:
  0.0 199.7 jit_solution(4386912286690597011)
XLA Ops:
  1.4 4.7 %layout.1 = (bf16[80,256]{1,0:T(8,128)(2,1)S(1)}, bf16[80,256]{1,0:T(8,128)(2,1)S(1)}, bf16[1024,256]{1,0:T(8,128)(2,1)}, bf16[1024,256]{1,0:T(8,128)(2,1)}) custom-call(s32[2]{0:T(128)S(1)} %pad_add_fusion.refs_0_, s32[128]{0:T(128)S(1)} %copy-done.5, bf16[2,128,1024]{2,1,0:T(8,128)(2,1)} %refs_2_.1, bf16[4,2,128,256]{3,2,1,0:T(8,128)(2,1)} %refs_3_.1), custom_call_target="tpu_custom_call" | custom-call | bytes 2179592 | tf_op jit(solution)/shard_map/layout/pallas_call | solution.py:93
  6.1 4.6 %collective-permute-start = (bf16[80,256]{1,0:T(8,128)(2,1)S(1)}, bf16[80,256]{1,0:T(8,128)(2,1)S(1)}, u32[]{:S(2)}, u32[]{:S(2)}) collective-permute-start(bf16[80,256]{1,0:T(8,128)(2,1)S(1)} %get-tuple-element.84), channel_id=1, source_target_pairs={{0,7},{2,1},{4,3},{6,5},{7,0},{1,2},{3,4},{5,6},{8,15},{10,9},{12,... | collective-permute-start | bytes 122888 | tf_op jit(solution)/shard_map/ppermute | solution.py:1266
  17.2 6.1 %conv_one.1 = (f32[1024,512]{1,0:T(8,128)S(1)}, f32[40,512]{1,0:T(8,128)S(1)}, f32[32,512]{1,0:T(8,128)S(1)}, f32[8,128]{1,0:T(8,128)S(1)}, f32[64,256]{1,0:T(8,...) custom-call(s32[2]{0:T(128)S(1)} %pad_add_fusion.refs_0_, ...), custom_call_target="tpu_custom_call" | custom-call | flops 1073741824 | bytes 8249352 | tf_op jit(solution)/shard_map/conv_one/pallas_call | solution.py:93
  25.2 2.9 %collective-permute-start.2 = (f32[40,512]{1,0:T(8,128)S(1)}, f32[40,512]{1,0:T(8,128)S(1)}, u32[]{:S(2)}, u32[]{:S(2)}) collective-permute-start(f32[40,512]{1,0:T(8,128)S(1)} %get-tuple-element.87), channel_id=1, source_target_pairs={{0,7},{2,1},{4,3},{6,5},{7,0},{1,2},{3,4},{5,6},{8,15},{10,9},{12,... | collective-permute-start | bytes 245768 | tf_op jit(solution)/shard_map/ppermute | solution.py:1187
  28.5 3.2 %collective-permute-done.2.refs_2_ = f32[40,512]{1,0:T(8,128)S(1)} collective-permute-done((f32[40,512]{1,0:T(8,128)S(1)}, f32[40,512]{1,0:T(8,128)S(1)}, u32[]{:S(2)}, u32[]{:S(2)}) %collective-permute-start.2) | collective-permute-done | bytes 81952 | tf_op jit(solution)/shard_map/ppermute | solution.py:1187
  36.7 5.9 %conv_two.1 = (f32[1024,256]{1,0:T(8,128)S(1)}, f32[40,256]{1,0:T(8,128)S(1)}, f32[32,256]{1,0:T(8,128)S(1)}, f32[8,128]{1,0:T(8,128)S(1)}, bf16[4,32,512]{2,1,0...) custom-call(s32[2]{0:T(128)S(1)} %pad_add_fusion.refs_0_, ...), custom_call_target="tpu_custom_call" | custom-call | flops 1006632960 | bytes 9433096 | tf_op jit(solution)/shard_map/conv_two/pallas_call | solution.py:93
  51.3 7.6 %up_two.1 = (f32[1024,512]{1,0:T(8,128)S(1)}, f32[40,512]{1,0:T(8,128)S(1)}, f32[32,512]{1,0:T(8,128)S(1)}, f32[8,128]{1,0:T(8,128)S(1)}, f32[2,32,256]{2,1,0:T(...) custom-call(s32[2]{0:T(128)S(1)} %pad_add_fusion.refs_0_, f32[1024,256]{1,0:T(8,128)S(1)} %get-tuple-element.91.refs_1_, ...), custom_call_target="tpu_custom_call" | custom-call | flops 1207959552 | bytes 7268360 | tf_op jit(solution)/shard_map/up_two/pallas_call | solution.py:93
  67.0 6.9 %up_one.1 = (bf16[272,256]{1,0:T(8,128)(2,1)S(1)}, bf16[272,256]{1,0:T(8,128)(2,1)S(1)}, bf16[272,256]{1,0:T(8,128)(2,1)S(1)}, bf16[272,256]{1,0:T(8,128)(2,1)S(...) custom-call(s32[2]{0:T(128)S(1)} %pad_add_fusion.refs_0_, ...), custom_call_target="tpu_custom_call" | custom-call | flops 1610612736 | bytes 10665992 | tf_op jit(solution)/shard_map/up_one/pallas_call | solution.py:93
  77.5 3.0 %collective-permute-done.17.refs_2_ = bf16[272,256]{1,0:T(8,128)(2,1)S(1)} collective-permute-done((bf16[272,256]{1,0:T(8,128)(2,1)S(1)}, bf16[272,256]{1,0:T(8,128)(2,1)S(1)}, u32[]{:S(2)}, u32[]{:S(2)}) %collective-permute-start.17) | collective-permute-done | bytes 139296 | tf_op jit(solution)/shard_map/ppermute | solution.py:1151
  80.5 3.6 %collective-permute-done.18.refs_3_ = bf16[272,256]{1,0:T(8,128)(2,1)S(1)} collective-permute-done((bf16[272,256]{1,0:T(8,128)(2,1)S(1)}, bf16[272,256]{1,0:T(8,128)(2,1)S(1)}, u32[]{:S(2)}, u32[]{:S(2)}) %collective-permute-start.18) | collective-permute-done | bytes 139296 | tf_op jit(solution)/shard_map/ppermute | solution.py:1151
  84.1 3.0 %mask.1 = (bf16[272,256]{1,0:T(8,128)(2,1)S(1)}, bf16[272,256]{1,0:T(8,128)(2,1)S(1)}, bf16[272,256]{1,0:T(8,128)(2,1)S(1)}, bf16[272,256]{1,0:T(8,128)(2,1)S(1)}, f32[256,256]{1,0:T(8,128)}) custom-call(s32[2]{0:T(128)S(1)} %pad_add_fusion.refs_0_, bf16[272,256]{1,0:T(8,128)(2,1)S(1)} %get-tuple-element.103.refs_1_, ...), custom_call_target="tpu_custom_call" | custom-call | bytes 2490376 | tf_op jit(solution)/shard_map/mask/pallas_call | solution.py:93
  90.6 4.4 %matrices_back.1 = (bf16[1024,1024]{1,0:T(8,128)(2,1)}, bf16[1920,256]{1,0:T(8,128)(2,1)}, bf16[512,1152]{1,0:T(8,128)(2,1)}, bf16[256,1536]{1,0:T(8,128)(2,1)}) custom-call(f32[50,128]{1,0:T(8,128)} %copy-done.3, f32[400,128]{1,0:T(8,128)} %copy-done, f32[400,128]{1,0:T(8,128)} %copy-done.1, f32[2,50,128]{2,1,0:T(8,128)} %copy-done.2), custom_call_target="tpu_custom_call" | custom-call | bytes 5532672 | tf_op jit(solution)/shard_map/matrices_back/pallas_call | solution.py:93
  96.2 7.6 %down_one_back.1 = (f32[1024,512]{1,0:T(8,128)S(1)}, bf16[1024,1024]{1,0:T(8,128)(2,1)S(1)}, f32[40,512]{1,0:T(8,128)S(1)}, f32[32,512]{1,0:T(8,128)S(1)}, f32[8...) custom-call(s32[2]{0:T(128)S(1)} %pad_add_fusion.refs_0_, ...), custom_call_target="tpu_custom_call" | custom-call | flops 2147483648 | bytes 12369928 | tf_op jit(solution)/shard_map/down_one_back/pallas_call | solution.py:93
  105.5 3.6 %collective-permute-start.23 = (f32[40,512]{1,0:T(8,128)S(1)}, f32[40,512]{1,0:T(8,128)S(1)}, u32[]{:S(2)}, u32[]{:S(2)}) collective-permute-start(f32[40,512]{1,0:T(8,128)S(1)} %get-tuple-element.118), channel_id=1, source_target_pairs={{0,7},{2,1},{4,3},{6,5},{7,0},{1,2},{3,4},{5,6},{8,15},{10,9},{12,... | collective-permute-start | bytes 245768 | tf_op jit(solution)/shard_map/ppermute | solution.py:1187
  109.2 3.7 %estimate.1 = bf16[4,2,128,256]{3,2,1,0:T(8,128)(2,1)} custom-call(s32[2]{0:T(128)S(1)} %pad_add_fusion.refs_0_, bf16[272,256]{1,0:T(8,128)(2,1)S(1)} %get-tuple-element.103.refs_1_, bf16[272,256]{1,0:T(8,128)(2,1)S(1)} %collective-permute-done.17.refs_2_, bf16[272,256]{1,0:T(8,128)(2,1)S(1)} %collective-permute-done.18.refs_3_, ...), custom_call_target="tpu_custom_call" | custom-call | bytes 1083400 | tf_op jit(solution)/shard_map/estimate/pallas_call | solution.py:93
  115.3 5.6 %weight_up_one.1 = f32[32,128]{1,0:T(8,128)S(1)} custom-call(bf16[1024,512]{1,0:T(8,128)(2,1)} %get-tuple-element.149.refs_0_, bf16[1024,1920]{1,0:T(8,128)(2,1)} %get-tuple-element.101.refs_9_.refs_1_, bf16[1024,1024]{1,0:T(8,128)(2,1)S(1)} %copy-done.7), custom_call_target="tpu_custom_call" | custom-call | flops 2147483648 | bytes 7094272 | tf_op jit(solution)/shard_map/weight_up_one/pallas_call | solution.py:93
  121.4 8.8 %up_two_back.1 = (f32[1024,256]{1,0:T(8,128)S(1)}, bf16[1024,1920]{1,0:T(8,128)(2,1)S(1)}, f32[40,256]{1,0:T(8,128)S(1)}, f32[32,256]{1,0:T(8,128)S(1)}, f32[8,128]{1,0:T(8,128)S(1)}) custom-call(s32[2]{0:T(128)S(1)} %pad_add_fusion.refs_0_, f32[1024,512]{1,0:T(8,128)S(1)} %get-tuple-element.117.refs_1_, f32[40,512]{1,0:T(8,128)S(1)} %collective-permute-done.23.refs_2_, ...), custom_call_target="tpu_custom_call" | custom-call | flops 1006632960 | bytes 11669512 | tf_op jit(solution)/shard_map/up_two_back/pallas_call | solution.py:93
  134.4 3.3 %weight_up_two.1 = f32[128,128]{1,0:T(8,128)S(1)} custom-call(bf16[1024,256]{1,0:T(8,128)(2,1)} %get-tuple-element.147.refs_0_, bf16[1024,1920]{1,0:T(8,128)(2,1)S(1)} %get-tuple-element.148.refs_1_), custom_call_target="tpu_custom_call" | custom-call | flops 1006632960 | bytes 4521984 | tf_op jit(solution)/shard_map/weight_up_two/pallas_call | solution.py:93
  140.2 7.4 %down_two_back.1 = (f32[1024,512]{1,0:T(8,128)S(1)}, bf16[1024,256]{1,0:T(8,128)(2,1)S(1)}, f32[40,512]{1,0:T(8,128)S(1)}, f32[32,512]{1,0:T(8,128)S(1)}, f32[8,128]{1,0:T(8,128)S(1)}) custom-call(s32[2]{0:T(128)S(1)} %pad_add_fusion.refs_0_, f32[1024,256]{1,0:T(8,128)S(1)} %get-tuple-element.125.refs_1_, f32[40,256]{1,0:T(8,128)S(1)} %collective-permute-done.28.refs_2_, ...), custom_call_target="tpu_custom_call" | custom-call | flops 1207959552 | bytes 10485768 | tf_op jit(solution)/shard_map/down_two_back/pallas_call | solution.py:93
  149.6 4.3 %weight_down_two.1 = f32[128,128]{1,0:T(8,128)S(1)} custom-call(bf16[1024,256]{1,0:T(8,128)(2,1)S(1)} %get-tuple-element.146.refs_0_, bf16[1024,1920]{1,0:T(8,128)(2,1)} %get-tuple-element.101.refs_9_.refs_1_), custom_call_target="tpu_custom_call" | custom-call | flops 1006632960 | bytes 4521984 | tf_op jit(solution)/shard_map/weight_down_two/pallas_call | solution.py:93
  165.2 3.0 %collective-permute-start.46 = (f32[64,128]{1,0:T(8,128)S(1)}, f32[64,128]{1,0:T(8,128)S(1)}, u32[]{:S(2)}, u32[]{:S(2)}) collective-permute-start(f32[64,128]{1,0:T(8,128)S(1)} %select_add_fusion.1), channel_id=1, source_target_pairs={{0,2},{1,3},{2,0},{3,1},{4,6},{5,7},{6,4},{7,5},{8,10},{9,11},{10,... | collective-permute-start | bytes 98312 | tf_op jit(solution)/shard_map/ppermute | solution.py:1151
  171.1 5.3 %up_one_back.1 = (bf16[256,256]{1,0:T(8,128)(2,1)S(1)}, bf16[256,256]{1,0:T(8,128)(2,1)S(1)}, bf16[256,256]{1,0:T(8,128)(2,1)S(1)}, bf16[256,256]{1,0:T(8,128)(2,1)S(1)}, bf16[1024,512]{1,0:T(8,128)(2,1)S(1)}) custom-call(s32[2]{0:T(128)S(1)} %pad_add_fusion.refs_0_, f32[1024,512]{1,0:T(8,128)S(1)} %get-tuple-element.133.refs_1_, ...), custom_call_target="tpu_custom_call" | custom-call | flops 805306368 | bytes 6930440 | tf_op jit(solution)/shard_map/up_one_back/pallas_call | solution.py:93
  176.4 3.9 %weight_down_one.1 = f32[16,128]{1,0:T(8,128)S(1)} custom-call(bf16[1024,512]{1,0:T(8,128)(2,1)S(1)} %get-tuple-element.144.refs_0_, bf16[1024,1024]{1,0:T(8,128)(2,1)} %get-tuple-element.145.refs_1_), custom_call_target="tpu_custom_call" | custom-call | flops 1073741824 | bytes 3153920 | tf_op jit(solution)/shard_map/weight_down_one/pallas_call | solution.py:93
  193.8 3.8 %collective-permute-done.40.refs_3_ = bf16[256,256]{1,0:T(8,128)(2,1)S(1)} collective-permute-done((bf16[256,256]{1,0:T(8,128)(2,1)S(1)}, bf16[256,256]{1,0:T(8,128)(2,1)S(1)}, u32[]{:S(2)}, u32[]{:S(2)}) %collective-permute-start.40) | collective-permute-done | bytes 131104 | tf_op jit(solution)/shard_map/ppermute | solution.py:1151
  (258 shorter events, 82.2 us)
Async XLA Ops:
  6.1 11.0 %collective-permute-start = (bf16[80,256]{1,0:T(8,128)(2,1)S(1)}, bf16[80,256]{1,0:T(8,128)(2,1)S(1)}, u32[]{:S(2)}, u32[]{:S(2)}) collective-permute-start(bf16[80,256]{1,0:T(8,128)(2,1)S(1)} %get-tuple-element.84), channel_id=1, source_target_pairs={{0,7},{2,1},{4,3},{6,5},{7,0},{1,2},{3,4},{5,6},{8,15},{10,9},{12,... | collective-permute-start | bytes 122888 | tf_op jit(solution)/shard_map/ppermute | solution.py:1266
  28.1 8.6 %collective-permute-start.3 = (f32[32,512]{1,0:T(8,128)S(1)}, f32[32,512]{1,0:T(8,128)S(1)}, u32[]{:S(2)}, u32[]{:S(2)}) collective-permute-start(f32[32,512]{1,0:T(8,128)S(1)} %get-tuple-element.88), channel_id=1, source_target_pairs={{0,1},{1,0},{2,3},{3,2},{4,5},{5,4},{6,7},{7,6},{8,9},{9,8},{10,11... | collective-permute-start | bytes 196616 | tf_op jit(solution)/shard_map/ppermute | solution.py:1151
  75.5 8.6 %collective-permute-start.18 = (bf16[272,256]{1,0:T(8,128)(2,1)S(1)}, bf16[272,256]{1,0:T(8,128)(2,1)S(1)}, u32[]{:S(2)}, u32[]{:S(2)}) collective-permute-start(bf16[272,256]{1,0:T(8,128)(2,1)S(1)} %get-tuple-element.105), channel_id=1, source_target_pairs={{0,16},{8,24},{16,0},{24,8},{1,17},{9,25},{17,1},{25,9},{2,18},{10... | collective-permute-start | bytes 417800 | tf_op jit(solution)/shard_map/ppermute | solution.py:1151
  77.0 7.1 %collective-permute-start.19 = (bf16[272,256]{1,0:T(8,128)(2,1)S(1)}, bf16[272,256]{1,0:T(8,128)(2,1)S(1)}, u32[]{:S(2)}, u32[]{:S(2)}) collective-permute-start(bf16[272,256]{1,0:T(8,128)(2,1)S(1)} %get-tuple-element.106), channel_id=1, source_target_pairs={{0,24},{8,16},{16,8},{24,0},{1,25},{9,17},{17,9},{25,1},{2,26},{10... | collective-permute-start | bytes 417800 | tf_op jit(solution)/shard_map/ppermute | solution.py:1151
  87.1 8.0 %collective-permute-start.20 = (bf16[272,256]{1,0:T(8,128)(2,1)S(1)}, bf16[272,256]{1,0:T(8,128)(2,1)S(1)}, u32[]{:S(2)}, u32[]{:S(2)}) collective-permute-start(bf16[272,256]{1,0:T(8,128)(2,1)S(1)} %get-tuple-element.110), channel_id=1, source_target_pairs={{0,8},{8,0},{16,24},{24,16},{1,9},{9,1},{17,25},{25,17},{2,10},{10... | collective-permute-start | bytes 417800 | tf_op jit(solution)/shard_map/ppermute | solution.py:1151
  88.4 7.8 %collective-permute-start.21 = (bf16[272,256]{1,0:T(8,128)(2,1)S(1)}, bf16[272,256]{1,0:T(8,128)(2,1)S(1)}, u32[]{:S(2)}, u32[]{:S(2)}) collective-permute-start(bf16[272,256]{1,0:T(8,128)(2,1)S(1)} %get-tuple-element.111), channel_id=1, source_target_pairs={{0,16},{8,24},{16,0},{24,8},{1,17},{9,25},{17,1},{25,9},{2,18},{10... | collective-permute-start | bytes 417800 | tf_op jit(solution)/shard_map/ppermute | solution.py:1151
  89.2 7.0 %collective-permute-start.22 = (bf16[272,256]{1,0:T(8,128)(2,1)S(1)}, bf16[272,256]{1,0:T(8,128)(2,1)S(1)}, u32[]{:S(2)}, u32[]{:S(2)}) collective-permute-start(bf16[272,256]{1,0:T(8,128)(2,1)S(1)} %get-tuple-element.112), channel_id=1, source_target_pairs={{0,24},{8,16},{16,8},{24,0},{1,25},{9,17},{17,9},{25,1},{2,26},{10... | collective-permute-start | bytes 417800 | tf_op jit(solution)/shard_map/ppermute | solution.py:1151
  105.1 8.0 %collective-permute-start.26 = (f32[8,128]{1,0:T(8,128)S(1)}, f32[8,128]{1,0:T(8,128)S(1)}, u32[]{:S(2)}, u32[]{:S(2)}) collective-permute-start(f32[8,128]{1,0:T(8,128)S(1)} %get-tuple-element.120), channel_id=1, source_target_pairs={{0,4},{1,5},{2,6},{3,7},{4,0},{5,1},{6,2},{7,3},{8,12},{9,13},{10,... | collective-permute-start | bytes 12296 | tf_op jit(solution)/shard_map/ppermute | solution.py:1151
  105.5 7.5 %collective-permute-start.25 = (f32[8,128]{1,0:T(8,128)S(1)}, f32[8,128]{1,0:T(8,128)S(1)}, u32[]{:S(2)}, u32[]{:S(2)}) collective-permute-start(f32[8,128]{1,0:T(8,128)S(1)} %get-tuple-element.120), channel_id=1, source_target_pairs={{0,3},{2,5},{4,7},{6,1},{3,0},{5,2},{7,4},{1,6},{8,11},{10,13},{12... | collective-permute-start | bytes 12296 | tf_op jit(solution)/shard_map/ppermute | solution.py:1189
  105.5 7.6 %collective-permute-start.23 = (f32[40,512]{1,0:T(8,128)S(1)}, f32[40,512]{1,0:T(8,128)S(1)}, u32[]{:S(2)}, u32[]{:S(2)}) collective-permute-start(f32[40,512]{1,0:T(8,128)S(1)} %get-tuple-element.118), channel_id=1, source_target_pairs={{0,7},{2,1},{4,3},{6,5},{7,0},{1,2},{3,4},{5,6},{8,15},{10,9},{12,... | collective-permute-start | bytes 245768 | tf_op jit(solution)/shard_map/ppermute | solution.py:1187
  113.0 8.4 %collective-permute-start.24 = (f32[32,512]{1,0:T(8,128)S(1)}, f32[32,512]{1,0:T(8,128)S(1)}, u32[]{:S(2)}, u32[]{:S(2)}) collective-permute-start(f32[32,512]{1,0:T(8,128)S(1)} %get-tuple-element.119), channel_id=1, source_target_pairs={{0,1},{1,0},{2,3},{3,2},{4,5},{5,4},{6,7},{7,6},{8,9},{9,8},{10,11... | collective-permute-start | bytes 196616 | tf_op jit(solution)/shard_map/ppermute | solution.py:1151
  113.1 7.8 %collective-permute-start.27 = (f32[8,128]{1,0:T(8,128)S(1)}, f32[8,128]{1,0:T(8,128)S(1)}, u32[]{:S(2)}, u32[]{:S(2)}) collective-permute-start(f32[8,128]{1,0:T(8,128)S(1)} %fusion.6), channel_id=1, source_target_pairs={{0,1},{1,0},{2,3},{3,2},{4,5},{5,4},{6,7},{7,6},{8,9},{9,8},{10,11... | collective-permute-start | bytes 12296 | tf_op jit(solution)/shard_map/ppermute | solution.py:1151
  130.2 7.5 %collective-permute-start.31 = (f32[8,128]{1,0:T(8,128)S(1)}, f32[8,128]{1,0:T(8,128)S(1)}, u32[]{:S(2)}, u32[]{:S(2)}) collective-permute-start(f32[8,128]{1,0:T(8,128)S(1)} %get-tuple-element.128), channel_id=1, source_target_pairs={{0,4},{1,5},{2,6},{3,7},{4,0},{5,1},{6,2},{7,3},{8,12},{9,13},{10,... | collective-permute-start | bytes 12296 | tf_op jit(solution)/shard_map/ppermute | solution.py:1151
  130.3 7.4 %collective-permute-start.30 = (f32[8,128]{1,0:T(8,128)S(1)}, f32[8,128]{1,0:T(8,128)S(1)}, u32[]{:S(2)}, u32[]{:S(2)}) collective-permute-start(f32[8,128]{1,0:T(8,128)S(1)} %get-tuple-element.128), channel_id=1, source_target_pairs={{0,3},{2,5},{4,7},{6,1},{3,0},{5,2},{7,4},{1,6},{8,11},{10,13},{12... | collective-permute-start | bytes 12296 | tf_op jit(solution)/shard_map/ppermute | solution.py:1189
  131.7 8.5 %collective-permute-start.29 = (f32[32,256]{1,0:T(8,128)S(1)}, f32[32,256]{1,0:T(8,128)S(1)}, u32[]{:S(2)}, u32[]{:S(2)}) collective-permute-start(f32[32,256]{1,0:T(8,128)S(1)} %get-tuple-element.127), channel_id=1, source_target_pairs={{0,1},{1,0},{2,3},{3,2},{4,5},{5,4},{6,7},{7,6},{8,9},{9,8},{10,11... | collective-permute-start | bytes 98312 | tf_op jit(solution)/shard_map/ppermute | solution.py:1151
  138.1 16.3 %collective-permute-start.50 = (f32[88,128]{1,0:T(8,128)S(1)}, f32[88,128]{1,0:T(8,128)S(1)}, u32[]{:S(2)}, u32[]{:S(2)}) collective-permute-start(f32[88,128]{1,0:T(8,128)S(1)} %slice_select_fusion), channel_id=1, source_target_pairs={{0,1},{1,0},{2,3},{3,2},{4,5},{5,4},{6,7},{7,6},{8,9},{9,8},{10,11... | collective-permute-start | bytes 135176 | tf_op jit(solution)/shard_map/ppermute | solution.py:1151
  147.6 16.5 %collective-permute-start.36 = (f32[8,128]{1,0:T(8,128)S(1)}, f32[8,128]{1,0:T(8,128)S(1)}, u32[]{:S(2)}, u32[]{:S(2)}) collective-permute-start(f32[8,128]{1,0:T(8,128)S(1)} %get-tuple-element.136), channel_id=1, source_target_pairs={{0,4},{1,5},{2,6},{3,7},{4,0},{5,1},{6,2},{7,3},{8,12},{9,13},{10,... | collective-permute-start | bytes 12296 | tf_op jit(solution)/shard_map/ppermute | solution.py:1151
  148.2 17.0 %collective-permute-start.35 = (f32[8,128]{1,0:T(8,128)S(1)}, f32[8,128]{1,0:T(8,128)S(1)}, u32[]{:S(2)}, u32[]{:S(2)}) collective-permute-start(f32[8,128]{1,0:T(8,128)S(1)} %get-tuple-element.136), channel_id=1, source_target_pairs={{0,3},{2,5},{4,7},{6,1},{3,0},{5,2},{7,4},{1,6},{8,11},{10,13},{12... | collective-permute-start | bytes 12296 | tf_op jit(solution)/shard_map/ppermute | solution.py:1189
  156.7 6.9 %collective-permute-start.51 = (f32[88,128]{1,0:T(8,128)S(1)}, f32[88,128]{1,0:T(8,128)S(1)}, u32[]{:S(2)}, u32[]{:S(2)}) collective-permute-start(f32[88,128]{1,0:T(8,128)S(1)} %select_add_fusion), channel_id=1, source_target_pairs={{0,2},{1,3},{2,0},{3,1},{4,6},{5,7},{6,4},{7,5},{8,10},{9,11},{10,... | collective-permute-start | bytes 135176 | tf_op jit(solution)/shard_map/ppermute | solution.py:1151
  160.6 10.5 %collective-permute-start.34 = (f32[32,512]{1,0:T(8,128)S(1)}, f32[32,512]{1,0:T(8,128)S(1)}, u32[]{:S(2)}, u32[]{:S(2)}) collective-permute-start(f32[32,512]{1,0:T(8,128)S(1)} %get-tuple-element.135), channel_id=1, source_target_pairs={{0,1},{1,0},{2,3},{3,2},{4,5},{5,4},{6,7},{7,6},{8,9},{9,8},{10,11... | collective-permute-start | bytes 196616 | tf_op jit(solution)/shard_map/ppermute | solution.py:1151
  168.1 14.7 %collective-permute-start.54 = (f32[88,128]{1,0:T(8,128)S(1)}, f32[88,128]{1,0:T(8,128)S(1)}, u32[]{:S(2)}, u32[]{:S(2)}) collective-permute-start(f32[88,128]{1,0:T(8,128)S(1)} %add_add_fusion), channel_id=1, source_target_pairs={{0,1},{1,0},{2,3},{3,2},{4,5},{5,4},{6,7},{7,6},{8,9},{9,8},{10,11... | collective-permute-start | bytes 135176 | tf_op jit(solution)/shard_map/ppermute | solution.py:1151
  170.3 18.8 %collective-permute-start.49 = (f32[64,128]{1,0:T(8,128)S(1)}, f32[64,128]{1,0:T(8,128)S(1)}, u32[]{:S(2)}, u32[]{:S(2)}) collective-permute-start(f32[64,128]{1,0:T(8,128)S(1)} %add_add_fusion.1), channel_id=1, source_target_pairs={{0,1},{1,0},{2,3},{3,2},{4,5},{5,4},{6,7},{7,6},{8,9},{9,8},{10,11... | collective-permute-start | bytes 98312 | tf_op jit(solution)/shard_map/ppermute | solution.py:1151
  180.7 13.1 %collective-permute-start.38 = (bf16[256,256]{1,0:T(8,128)(2,1)S(1)}, bf16[256,256]{1,0:T(8,128)(2,1)S(1)}, u32[]{:S(2)}, u32[]{:S(2)}) collective-permute-start(bf16[256,256]{1,0:T(8,128)(2,1)S(1)} %get-tuple-element.140), channel_id=1, source_target_pairs={{0,8},{8,0},{16,24},{24,16},{1,9},{9,1},{17,25},{25,17},{2,10},{10... | collective-permute-start | bytes 393224 | tf_op jit(solution)/shard_map/ppermute | solution.py:1151
  181.7 12.1 %collective-permute-start.39 = (bf16[256,256]{1,0:T(8,128)(2,1)S(1)}, bf16[256,256]{1,0:T(8,128)(2,1)S(1)}, u32[]{:S(2)}, u32[]{:S(2)}) collective-permute-start(bf16[256,256]{1,0:T(8,128)(2,1)S(1)} %get-tuple-element.141), channel_id=1, source_target_pairs={{0,16},{8,24},{16,0},{24,8},{1,17},{9,25},{17,1},{25,9},{2,18},{10... | collective-permute-start | bytes 393224 | tf_op jit(solution)/shard_map/ppermute | solution.py:1151
  (49 other events, 329.8 us)

commit v3 on v2

--- a/solution.py
+++ b/solution.py
@@ -15,6 +15,7 @@
 NJ = 32
 R = M * NJ
 CHUNK = 256
+UNROLL = 4
 COLS0 = 1024
 COLS1 = 1920
 COLS1B = 1536
@@ -43,17 +44,35 @@
 
 
 class Leaving:
-    def __init__(self, target, sem):
-        self.target, self.sem, self.copy = target, sem, None
-
-    def put(self, source):
-        self.copy = pltpu.make_async_copy(source, self.target, self.sem)
-        self.copy.start()
-
-
-def run(kernel, name, outs, args, scratch=(), flops=0):
+    def __init__(self, target, sems):
+        self.target, self.sems, self.copies = target, sems, []
+
+    def put(self, source, part=None):
+        target = self.target if part is None else self.target.at[part]
+        source = source if part is None else source.at[part]
+        copy = pltpu.make_async_copy(source, target, self.sems.at[len(self.copies)])
+        copy.start()
+        self.copies.append(copy)
+
+    def wait(self):
+        for copy in self.copies:
+            copy.wait()
+
+
+PARTS = 6
+
+
+def run(kernel, name, outs, args, scratch=(), flops=0, fetch=(), token=None):
+    n_args = len(args)
+    args = list(args) + list(fetch) + ([] if token is None else [token])
+    n_made = len(outs)
+    outs = list(outs)
+    for f in fetch:
+        outs.append(((f.array.shape[0], f.columns or f.array.shape[1]) + f.array.shape[2:], f.array.dtype))
     arrays = [a.array if isinstance(a, Far) else a for a in args]
-    far_in = [k for k, a in enumerate(args) if isinstance(a, Far)]
+    if token is not None:
+        outs.append((token.shape, token.dtype))
+    far_in = [k for k, a in enumerate(args[:n_args]) if isinstance(a, Far)]
     far_out = [k for k, o in enumerate(outs) if len(o) == 3]
     n_in, n_out, n_own = len(args), len(outs), len(scratch)
     placed = [
@@ -70,17 +89,27 @@
         ins, results = list(refs[:n_in]), list(refs[n_in : n_in + n_out])
         own = refs[n_in + n_out : n_in + n_out + n_own]
         targets = refs[n_in + n_out + n_own : n_in + n_out + n_own + len(far_in)]
-        sems = refs[-1]
+        in_sems, out_sems = refs[-2:]
+
+        def cut(k):
+            return ins[k] if args[k].columns is None else ins[k].at[:, 0 : args[k].columns]
+
         for i, k in enumerate(far_in):
-            source = ins[k] if args[k].columns is None else ins[k].at[:, 0 : args[k].columns]
-            ins[k] = Arriving(source, targets[i], sems.at[i])
+            ins[k] = Arriving(cut(k), targets[i], in_sems.at[i])
+        fetched = [
+            Arriving(cut(n_args + i), results[n_made + i], in_sems.at[len(far_in) + i]) for i in range(len(fetch))
+        ]
         for i, k in enumerate(far_out):
-            results[k] = Leaving(results[k], sems.at[len(far_in) + i])
-        kernel(*ins, *results, *own)
+            results[k] = Leaving(results[k], out_sems.at[i])
+        if token is not None:
+            results[-1][...] = ins[-1][...]
+        kernel(*ins[:n_args], *results[:n_made], *own)
         for k in far_in:
             ins[k].get()
+        for f in fetched:
+            f.get()
         for k in far_out:
-            results[k].copy.wait()
+            results[k].wait()
 
     in_specs = []
     for a in args:
@@ -99,7 +128,10 @@
         out_specs=[FAR if len(o) == 3 else FULL for o in outs],
         scratch_shapes=[pltpu.VMEM(s, d) for s, d in scratch]
         + landing
-        + [pltpu.SemaphoreType.DMA((max(1, len(far_in) + len(far_out)),))],
+        + [
+            pltpu.SemaphoreType.DMA((max(1, len(far_in) + len(fetch)),)),
+            pltpu.SemaphoreType.DMA((max(1, len(far_out)), PARTS)),
+        ],
         compiler_params=pltpu.CompilerParams(vmem_limit_bytes=24 << 20),
         cost_estimate=pl.CostEstimate(flops=flops, bytes_accessed=bytes_all, transcendentals=0),
         name=name,
@@ -123,11 +155,14 @@
 
 
 def for_blocks(fn, count=NJ):
+    step = UNROLL if isinstance(count, int) and count % UNROLL == 0 else 1
+
     def body(j, carry):
-        fn(j)
+        for i in range(step):
+            fn(j * step + i)
         return carry
 
-    lax.fori_loop(0, count, body, 0)
+    lax.fori_loop(0, count // step, body, 0)
 
 
 def for_blocks_rims(fn):
@@ -201,6 +236,11 @@
     )
 
 
+def quarters(fn):
+    for k in range(4):
+        fn(slice(R // 4 * k, R // 4 * (k + 1)))
+
+
 def for_chunks(fn, size=CHUNK):
     def body(r, carry):
         fn(pl.ds(pl.multiple_of(r * size, size), size))
@@ -218,10 +258,12 @@
 
 def sum_blocks(fn):
     def body(j, carry):
-        return fn(j, *carry)
+        for i in range(UNROLL):
+            carry = fn(j * UNROLL + i, *carry)
+        return carry
 
     zero = jnp.zeros((8, L), F32)
-    return [total_rows(s) for s in lax.fori_loop(0, NJ, body, (zero, zero))]
+    return [total_rows(s) for s in lax.fori_loop(0, NJ // UNROLL, body, (zero, zero))]
 
 
 def fold(stats, period):
@@ -316,7 +358,14 @@
     return tile.astype(BF)
 
 
-def matrix_2_down(w, t):
+def repeat_lanes(w, out):
+    for k in range(w.shape[0] // 16):
+        span = slice(16 * k, 16 * k + 16)
+        out[span, :] = jnp.concatenate([w[span, :].astype(F32)] * (L // 32), axis=1)
+
+
+def matrix_2_down(narrow, t, w):
+    repeat_lanes(narrow, w)
     zero = jnp.zeros((16, L), BF)
     for base, rim, tap in GROUPS1:
         for half in range(2):
@@ -329,7 +378,8 @@
                 t[start : start + 16, at] = zero if q is None else tile_2(w, tap, q, half)
 
 
-def matrix_2_up(w, t):
+def matrix_2_up(narrow, t, w):
+    repeat_lanes(narrow, w)
     zero = jnp.zeros((16, L), BF)
     at = lane((16, L))
     for row in range(2):
@@ -351,7 +401,7 @@
 def band(w, tap, channel, offset):
     tile = jnp.zeros((32, L), F32)
     for b in range(TAPS):
-        start = (tap * 2 + channel) * TAPS + b
+        start = (tap * TAPS + b) * 2 + channel
         tile = jnp.where(offset == b, w[start : start + 1, :], tile)
     return tile.astype(BF)
 
@@ -391,31 +441,25 @@
                 t[span, start : start + L] = band(w, tap, c, rim) if ok else zero
 
 
-def matrices_first(w1c, t1a):
-    matrix_1_down(w1c, t1a, 0)
-
-
-def matrices_forward(w2c, w2d, w1d, t2a_c, t2b_d, t1b_d, a, b, c):
-    matrix_2_down(w2c, a)
-    t2a_c.put(a)
-    matrix_2_up(w2d, b)
-    t2b_d.put(b)
-    matrix_1_up(w1d.at[0], c, 0)
-    matrix_1_up(w1d.at[1], c, COLS1B)
-    t1b_d.put(c)
-
-
-def matrices_back(w1c, w2c, w2d, w1d, t1a_d, t2a_d, t2b_c, t1b_c, a, b, c, d):
-    w1c, w2c, w2d, w1d = [w.get() for w in (w1c, w2c, w2d, w1d)]
-    matrix_1_down(w1d.at[0], a, 0)
-    matrix_1_down(w1d.at[1], a, 512)
-    t1a_d.put(a)
-    matrix_2_down(w2d, b)
-    t2a_d.put(b)
-    matrix_2_up(w2c, c)
-    t2b_c.put(c)
-    matrix_1_up(w1c, d, 0)
-    t1b_c.put(d)
+def window_0(w1c, t):
+    matrix_1_down(w1c, t, 0)
+
+
+def window_1(w2c, t, w):
+    matrix_2_down(w2c, t, w)
+
+
+def window_2(w2d, t, w):
+    matrix_2_up(w2d, t, w)
+
+
+def window_3(w1d, t):
+    matrix_1_up(w1d.at[0], t, 0)
+    matrix_1_up(w1d.at[1], t, COLS1B)
+
+
+def window_swap(spare, out):
+    out[...] = spare[...]
 
 
 def correlate(coarse, fine, d):
@@ -479,21 +523,76 @@
     out[start : start + 16, :] = result
 
 
-def weight_2_kernel(coarse, fine, out, d):
+def window_4(low, act, fine, w2d, t, out, d, w, kept):
+    matrix_2_down(w2d, t, w)
+    correlate(ready(low), ready(fine), d)
+    weight_1(d, kept, 0)
+    correlate(ready(act), ready(fine), d)
+    weight_1(d, kept, 16)
+    out.put(kept)
+
+
+def window_5(coarse, fine, w2c, t, out, d, w, kept):
+    matrix_2_up(w2c, t, w)
     correlate(ready(coarse), ready(fine), d)
-    weight_2(d, out)
-
-
-def weight_1_first(coarse, fine, out, d):
+    weight_2(d, kept)
+    out.put(kept)
+
+
+def window_6(coarse, fine, w1c, t, out, d, kept):
+    matrix_1_up(w1c, t, 0)
     correlate(ready(coarse), ready(fine), d)
-    weight_1(d, out, 0)
-
-
-def weight_1_joined(low, cat1, fine, out, d):
-    correlate(ready(low), ready(fine), d)
-    weight_1(d, out, 0)
-    correlate(ready(cat1), ready(fine), d)
-    weight_1(d, out, 16)
+    weight_2(d, kept)
+    out.put(kept)
+
+
+HALF = 160
+
+
+def window_7(index, coarse, fine, bias, w1d, w2d, w2c, keep, give, d, first):
+    correlate(ready(coarse), ready(fine), d)
+    weight_1(d, first, 0)
+    even = index[1] == 0
+    up_two, up_one, down_two = ready(w2d), ready(w1d), ready(w2c)
+    spare = jnp.zeros((8, L), F32)
+
+    def place(span, a, b):
+        keep[span, :] = jnp.where(even, a, b)
+        give[span, :] = jnp.where(even, b, a)
+
+    place(slice(0, 128), up_two[...], down_two[...])
+    place(slice(128, 144), up_one[0:16, :], first[...])
+    place(slice(144, 160), up_one[16:32, :], jnp.concatenate([bias[...], spare]))
+
+
+def unpack_kernel(index, mine, other, w1c, w2c, w2d, w1d, bias):
+    even = index[1] == 0
+    a, b = mine[...], other[...]
+    up, down = jnp.where(even, a, b), jnp.where(even, b, a)
+    for half, out in ((up, w2d), (down, w2c)):
+        turned = half[0:128].T
+        moved = [turned] + [pltpu.roll(turned, L - 32 * tap, 1) for tap in range(1, 4)]
+        for tap in range(TAPS):
+            for b in range(TAPS):
+                if tap < 4:
+                    value = moved[tap][16 * b : 16 * b + 16]
+                else:
+                    value = moved[b // 3][80 + 16 * (b % 3) : 96 + 16 * (b % 3)]
+                out[tap * TAPS + b] = value[:, 0:32]
+    tall = jnp.concatenate([up[128:160], down[128:144], jnp.zeros((80, L), F32)]).T
+    other_tall = pltpu.roll(tall, L - 32, 1)
+    for tap in range(TAPS):
+        for b in range(TAPS):
+            for c in range(2):
+                row = (tap + 1) % 2 * 64 + c * 32 + (tap + 1) // 2 * 8 + b
+                w1d[tap * TAPS + b, c : c + 1, :] = tall[row : row + 1, 0:32]
+                w1c[tap * TAPS + b, c : c + 1, :] = other_tall[row : row + 1, 0:16]
+    total = total_rows(down[144:152])
+    total = jnp.broadcast_to(total, (8, L))
+    total = total + pltpu.roll(total, 64, 1)
+    for step in (16, 8, 4, 2, 1):
+        total = total + pltpu.roll(total, L - step, 1)
+    bias[...] = jnp.where(lane((8, L)) == 0, total, pltpu.roll(total, L - 31, 1))
 
 
 def ready(ref):
@@ -526,7 +625,7 @@
             scr[k % 2, pl.ds(2 * half + k // 2, M, stride=4), :] = value
 
 
-def layout_kernel(index, frame_mask, mix, cot, cross, core, x0, c0, scr, wide, xf, cf, ends):
+def layout_kernel(index, frame_mask, mix, cot, cross, core, xf, x0, c0, scr, wide, cf, ends):
     def place(out, block, row):
         def store(k, half, value):
             at = slice(L * half, L * half + L)
@@ -596,7 +695,7 @@
 
 def conv_one_kernel(
     index, x0, cross_in, core_in, aux, t,
-    z, cross, core, mom, hx, kept, zfar, catfar, cat, lf, rf, lw, rw,
+    cross, core, mom, kept, hxfar, zfar, catfar, z, hx, cat, lf, rf, lw, rw,
 ):
     even = index[1] == 0
     a, b = cross_in[...].astype(F32), core_in[...].astype(F32)
@@ -604,6 +703,7 @@
     rf[...] = jnp.where(even, b, a)
     hx[:, 0:L] = rf[0 : 2 * NJ, 0:L]
     hx[:, L : 2 * L] = lf[0 : 2 * NJ, L : 2 * L]
+    hxfar.put(hx)
     kept[...] = jnp.zeros(kept.shape, F32)
     kept[0:3, :] = lf[2 * NJ : 2 * NJ + 3, 0:L]
     kept[3:6, :] = rf[2 * NJ : 2 * NJ + 3, 0:L]
@@ -617,9 +717,9 @@
 
     def chunk(rs):
         z[rs, :] = matmul(cat[rs, :], weights[...])
-
-    for_chunks(chunk)
-    zfar.put(z)
+        zfar.put(z, (rs, slice(None)))
+
+    quarters(chunk)
     pack_ends(z, index, cross, core)
 
     def sums(j, s1, s2):
@@ -639,7 +739,7 @@
 
 def conv_two_kernel(
     index, z1, cross_in, core_in, mom1, prm, aux, t,
-    z2, cross, core, mom, ends, h1, zfar, catfar, cat, ef, hf, lw, rw,
+    cross, core, mom, ends, h1, zfar, catfar, z2, cat, ef, eb, hf, lw, rw,
 ):
     mean, scale = norm_terms(mom1, mom1[2:3])
     gain, shift = prm[0:1], prm[1:2]
@@ -670,15 +770,25 @@
             cat[rows(j), start : start + L] = moved.astype(BF)
 
     for_blocks(one)
+    catfar.put(cat, (slice(None), slice(0, 1024)))
+    catfar.put(cat, (slice(None), slice(1536, 1792)))
     rims_1(cat, GROUPS1)
-    catfar.put(cat)
+    catfar.put(cat, (slice(None), slice(1024, 1536)))
+    catfar.put(cat, (slice(None), slice(1792, 1920)))
+    def group_out(rs, at, top, low):
+        ef[2, rs, at] = act(top)
+        ef[3, rs, at] = act(low)
+
+    end_rows(z1, group_out)
+    eb[...] = ef[...].astype(BF)
+    ends.put(eb)
     weights = ready(t)
 
     def chunk(rs):
         z2[rs, :] = matmul(cat[rs, :], weights[...])
-
-    for_chunks(chunk)
-    zfar.put(z2)
+        zfar.put(z2, (rs, slice(None)))
+
+    quarters(chunk)
     pack_ends(z2, index, cross, core)
 
     def sums(j, s1, s2):
@@ -690,13 +800,6 @@
         return s1, s2
 
     pack_moments(mom, cross, fold(stack_rows(sum_blocks(sums)), 32))
-
-    def group_out(rs, at, top, low):
-        ef[2, rs, at] = act(top)
-        ef[3, rs, at] = act(low)
-
-    end_rows(z1, group_out)
-    ends[...] = ef[...].astype(BF)
 
 
 def columns_2(cat, read, left, right, aux):
@@ -717,7 +820,7 @@
 
 def up_two_kernel(
     index, z2, cross_in, core_in, mom1, mom2, prm, aux, t,
-    rect, cross, core, mom, h2, act2, rectfar, cat, hf, lf, rf, lw, rw,
+    cross, core, mom, h2, act2, rectfar, rect, cat, hf, lf, rf, lw, rw,
 ):
     mean, scale = norm_terms(mom2, mom1[3:4])
     gain, shift, bias = prm[2:3], prm[3:4], prm[6:7]
@@ -901,11 +1004,13 @@
         grads[s][per : per + 16, :] = ff[...].astype(BF)
 
 
-def estimate_kernel(index, m0, m1, m2, m3, x0, out, scr, est):
+def estimate_kernel(index, m0, m1, m2, m3, x0, w1d, out, t, scr, est):
     masks = (m0, m1, m2, m3)
     stems = len(masks)
     blocks = NJ // stems
     mine = index[0]
+    matrix_1_down(w1d.at[0], t, 0)
+    matrix_1_down(w1d.at[1], t, 512)
     mix = ready(x0)
 
     def one(j):
@@ -958,9 +1063,9 @@
         value = matmul(cat[rs, :], weights[...])
         g3[rs, :] = value[:, 0:512]
         gf[rs, :] = value[:, 512:1024]
-
-    for_chunks(chunk)
-    gact.put(gf)
+        gact.put(gf, (rs, slice(None)))
+
+    quarters(chunk)
     mean, scale = norm_terms(mom3, mom1[2:3])
     pack_ends(g3, index, cross, core)
     r = ready(rect)
@@ -1017,7 +1122,12 @@
             cat[rows(j), start : start + L] = moved.astype(BF)
         return total
 
-    bias = lax.fori_loop(0, NJ, one, jnp.zeros((8, L), F32))
+    def four(j, total):
+        for i in range(UNROLL):
+            total = one(j * UNROLL + i, total)
+        return total
+
+    bias = lax.fori_loop(0, NJ // UNROLL, four, jnp.zeros((8, L), F32))
     rims_1(cat, GROUPS1)
     weights = ready(t)
 
@@ -1165,33 +1275,34 @@
     return values
 
 
-def sum_halves(values, axis, odd):
+def sum_halves(keep, give, axis):
     count = lax.axis_size(axis)
-    half = values.shape[0] // 2
-    top, low = values[:half], values[half:]
-    mine = jnp.where(odd, low, top) + flip(jnp.where(odd, top, low), axis, 1)
+    mine = keep + flip(give, axis, 1)
     if count == 8:
-        moved = [flip(mine, axis, bit) for bit in (2, 4, 6)]
-        mine = mine + moved[0] + moved[1] + moved[2]
+        low = mine.astype(BF)
+        moved = [flip(low, axis, bit) for bit in (2, 4, 6)]
+        mine = low.astype(F32) + moved[0].astype(F32) + moved[1].astype(F32) + moved[2].astype(F32)
     else:
         step = 2
         while step < count:
             mine = mine + flip(mine, axis, step)
             step *= 2
-    other = flip(mine, axis, 1)
-    return jnp.where(odd, jnp.concatenate([other, mine]), jnp.concatenate([mine, other]))
-
-
-def exchange(cross, core, mom, axis):
+    return mine, flip(mine, axis, 1)
+
+
+def exchange(cross, core, mom, axis, beside):
     count = lax.axis_size(axis)
     near = lax.ppermute(cross, axis, pairs(count, -1))
     if count == 8:
         far = lax.ppermute(mom, axis, pairs(count, 3))
         across = flip(mom, axis, 4)
         inside = flip(core, axis, 1)
+        *made, mom = beside(mom)
         part = mom + near[NJ:, 0:L] + far + across
-        return near, inside, part + flip(part, axis, 1)
-    return near, flip(core, axis, 1), sum_over(mom, axis)
+        return near, inside, part + flip(part, axis, 1), made
+    inside = flip(core, axis, 1)
+    *made, mom = beside(mom)
+    return near, inside, sum_over(mom, axis), made
 
 
 def swap(blocks, axis):
@@ -1248,212 +1359,228 @@
             jnp.tile(jnp.repeat(bias_first[0], 32), 2),
         ]
     )
-    w1c = jnp.tile(conv_first[0].transpose(2, 1, 3, 0).reshape(50, 16).astype(F32), (1, 8))
-    w1d = deconv_first[0].transpose(2, 0, 3, 1).reshape(50, 2, 16).astype(F32)
+    w1c = jnp.tile(conv_first[0].transpose(2, 3, 1, 0).reshape(50, 16).astype(F32), (1, 8))
+    w1d = deconv_first[0].transpose(2, 3, 0, 1).reshape(50, 2, 16).astype(F32)
     w1d = jnp.tile(w1d.transpose(1, 0, 2), (1, 1, 8))
-    w2c = jnp.tile(conv_second[0].transpose(2, 3, 1, 0).reshape(400, 32).astype(F32), (1, 4))
-    w2d = jnp.tile(deconv_second[0].transpose(2, 3, 0, 1).reshape(400, 32).astype(F32), (1, 4))
-
+    w2c = conv_second[0].transpose(2, 3, 1, 0).reshape(400, 32)
+    w2d = deconv_second[0].transpose(2, 3, 0, 1).reshape(400, 32)
     edge = 2 * NJ + 16
-    cross, core, x0, c0 = run(
+
+    def packet(lanes):
+        return [((NJ + 8, lanes), F32), ((NJ, lanes), F32), ((8, L), F32)]
+
+    def rim(lanes):
+        return [((NJ, lanes), F32)] * 2
+
+    def wide(lanes):
+        return [((8 * NJ, lanes), F32)] * 2
+
+    def far(*shape, kind=F32):
+        return [(shape, kind, True)]
+
+    cross, core, x0, x0_far, c0 = run(
         layout_kernel,
         "layout",
-        [((edge, 256), BF), ((edge, 256), BF), ((R, 256), BF, True), ((R, 256), BF, True)],
+        [((edge, 256), BF), ((edge, 256), BF), ((R, 256), BF)] + far(R, 256, kind=BF) + far(R, 256, kind=BF),
         [index, frame_mask, Far(mixture), Far(cotangent)],
-        [((2, frames, L), F32), ((2 * R, 256), F32), ((R, 256), BF), ((R, 256), BF)]
-        + [((2, edge, 256), F32)],
+        [((2, frames, L), F32), ((2 * R, 256), F32), ((R, 256), BF), ((2, edge, 256), F32)],
     )
     near = lax.ppermute(cross, "tm", pairs(lax.axis_size("tm"), -1))
     inside = flip(core, "tm", 1)
-    (t1a_c,) = run(matrices_first, "matrices_first", [((COLS0, 512), BF)], [w1c])
-    t2a_c, t2b_d, t1b_d = run(
-        matrices_forward,
-        "matrices_forward",
-        [((COLS1, 256), BF, True), ((512, COLS2), BF, True), ((256, 2 * COLS1B), BF, True)],
-        [w2c, w2d, w1d],
-        [((COLS1, 256), BF), ((512, COLS2), BF), ((256, 2 * COLS1B), BF)],
-    )
-    t1a_d, t2a_d, t2b_c, t1b_c = run(
-        matrices_back,
-        "matrices_back",
-        [((COLS0, 1024), BF, True), ((COLS1, 256), BF, True), ((512, COLS2), BF, True)]
-        + [((256, COLS1B), BF, True)],
-        [Far(w1c), Far(w2c), Far(w2d), Far(w1d)],
-        [((COLS0, 1024), BF), ((COLS1, 256), BF), ((512, COLS2), BF), ((256, COLS1B), BF)],
-    )
-
-    def packet(lanes):
-        return [((NJ + 8, lanes), F32), ((NJ, lanes), F32), ((8, L), F32)]
-
-    def rim(lanes):
-        return [((NJ, lanes), F32)] * 2
-
-    def wide(lanes):
-        return [((8 * NJ, lanes), F32)] * 2
-
-    z1, cross, core, mom, hx, kept, z1_far, cat0 = run(
+    (t,) = run(window_0, "window_0", [((COLS0, 512), BF)], [w1c])
+    cross, core, mom, kept, hx, z1, cat0 = run(
         conv_one_kernel,
         "conv_one",
-        [((R, 512), F32)] + packet(512)
-        + [((2 * NJ, 256), F32), ((8, L), F32), ((R, 512), F32, True), ((R, COLS0), BF, True)],
-        [index, Far(x0), near, inside, aux, t1a_c],
-        [((R, COLS0), BF), ((edge, 256), F32), ((edge, 256), F32)] + wide(256),
+        packet(512) + [((8, L), F32)] + far(2 * NJ, 256) + far(R, 512) + far(R, COLS0, kind=BF),
+        [index, x0, near, inside, aux, t],
+        [((R, 512), F32), ((2 * NJ, 256), F32), ((R, COLS0), BF), ((edge, 256), F32), ((edge, 256), F32)]
+        + wide(256),
         flops=2 * R * COLS0 * 512,
     )
-    near, inside, mom1 = exchange(cross, core, mom, "tm")
-    z2, cross, core, mom, ends1, h1, z2_far, cat1 = run(
+    near, inside, mom1, (t, z1_here) = exchange(
+        cross, core, mom, "tm",
+        lambda token: run(
+            window_1, "window_1", [((COLS1, 256), BF)], [w2c], [((400, L), F32)], fetch=[Far(z1)], token=token
+        ),
+    )
+    cross, core, mom, ends1, h1, z2, cat1 = run(
         conv_two_kernel,
         "conv_two",
-        [((R, 256), F32)] + packet(256)
-        + [((4, NJ, 512), BF), ((2, NJ, 512), F32, True), ((R, 256), F32, True), ((R, COLS1), BF, True)],
-        [index, z1, near, inside, mom1, prm, aux, Far(t2a_c)],
-        [((R, COLS1), BF), ((4, NJ, 512), F32), ((2, NJ, 512), F32)] + wide(512),
+        packet(256) + far(4, NJ, 512, kind=BF) + far(2, NJ, 512) + far(R, 256) + far(R, COLS1, kind=BF),
+        [index, z1_here, near, inside, mom1, prm, aux, t],
+        [((R, 256), F32), ((R, COLS1), BF), ((4, NJ, 512), F32), ((4, NJ, 512), BF), ((2, NJ, 512), F32)]
+        + wide(512),
         flops=2 * R * COLS1 * 256,
     )
-    near, inside, mom2 = exchange(cross, core, mom, "tm")
-    rect, cross, core, mom, h2, act2, rect_far = run(
+    near, inside, mom2, (t, z2_here) = exchange(
+        cross, core, mom, "tm",
+        lambda token: run(
+            window_2, "window_2", [((512, COLS2), BF)], [w2d], [((400, L), F32)], fetch=[Far(z2)], token=token
+        ),
+    )
+    cross, core, mom, h2, act2, rect = run(
         up_two_kernel,
         "up_two",
-        [((R, 512), F32)] + packet(512)
-        + [((2, NJ, 256), F32, True), ((R, 256), BF, True), ((R, 512), F32, True)],
-        [index, z2, near, inside, mom1, mom2, prm, aux, Far(t2b_d)],
-        [((R, COLS2), BF), ((2, NJ, 256), F32)] + rim(256) + wide(256),
+        packet(512) + far(2, NJ, 256) + far(R, 256, kind=BF) + far(R, 512),
+        [index, z2_here, near, inside, mom1, mom2, prm, aux, t],
+        [((R, 512), F32), ((R, COLS2), BF), ((2, NJ, 256), F32)] + rim(256) + wide(256),
         flops=2 * R * COLS2 * 512,
     )
-    near, inside, mom3 = exchange(cross, core, mom, "tm")
+    near, inside, mom3, (t, rect_here, cat1_here, ends1_here) = exchange(
+        cross, core, mom, "tm",
+        lambda token: run(
+            window_3,
+            "window_3",
+            [((256, 2 * COLS1B), BF)],
+            [w1d],
+            fetch=[Far(rect), Far(cat1, COLS1B), Far(ends1)],
+            token=token,
+        ),
+    )
     *masks, h3, low3, sig, sigh = run(
         up_one_kernel,
         "up_one",
         [((per + 16, 256), BF)] * stems
-        + [((2, NJ, 512), F32, True), ((R, 512), BF, True), ((R, 256), F32, True), ((NJ, 256), F32, True)],
-        [index, rect, near, inside, mom1, mom3, prm, aux, ends1, Far(cat1, COLS1B), Far(t1b_d)],
+        + far(2, NJ, 512) + far(R, 512, kind=BF) + far(R, 256) + far(NJ, 256),
+        [index, rect_here, near, inside, mom1, mom3, prm, aux, ends1_here, cat1_here, t],
         [((R, COLS1B), BF), ((2, NJ, 512), F32)] + rim(512)
         + [((2, NJ, 512), F32), ((16, 256), F32), ((R, 256), F32), ((NJ, 256), F32)] + wide(512),
         flops=2 * R * 2 * COLS1B * 256,
+    )
+    _, c0_here, x0_here, hx_here = run(
+        window_swap, "window_swap", [((8, L), F32)], [mom3], fetch=[Far(c0), Far(x0_far), Far(hx)]
     )
     masks = swap(masks, "stem")
     *grads, direct = run(
         mask_kernel,
         "mask",
-        [((per + 16, 256), BF)] * stems + [((per, 256), F32, True)],
-        [index, *masks, Far(c0), Far(x0), Far(hx)],
+        [((per + 16, 256), BF)] * stems + far(per, 256),
+        [index, *masks, c0_here, x0_here, hx_here],
         [((per, 256), F32), ((16, 256), F32)],
     )
     grads = swap(grads, "stem")
-    (estimates,) = run(
+    estimates, t, sig_here, sigh_here, rect_here = run(
         estimate_kernel,
         "estimate",
-        [((stems, 2, frames, blocks * 32), BF)],
-        [index, *masks, Far(x0)],
+        [((stems, 2, frames, blocks * 32), BF), ((COLS0, 1024), BF)],
+        [index, *masks, Far(x0_far), w1d],
         [((2, frames, L), F32), ((stems, per, 256), F32)],
+        fetch=[Far(sig), Far(sigh), Far(rect)],
     )
     g3, cat0g, cross, core, mom, bias_one, gact = run(
         down_one_back_kernel,
         "down_one_back",
-        [((R, 512), F32), ((R, COLS0), BF)] + packet(512) + [((8, L), F32), ((R, 512), F32, True)],
-        [index, *grads, Far(sigh), Far(sig), aux, mom1, mom3, Far(rect_far), Far(t1a_d)],
+        [((R, 512), F32), ((R, COLS0), BF)] + packet(512) + [((8, L), F32)] + far(R, 512),
+        [index, *grads, sigh_here, sig_here, aux, mom1, mom3, rect_here, t],
         [((R, 512), F32), ((NJ, 256), F32), ((8, L), F32), ((8 * NJ, 256), F32)],
         flops=2 * R * COLS0 * 1024,
     )
-    near, inside, mom4 = exchange(cross, core, mom, "tm")
-    (w1d_grad,) = run(
-        weight_1_joined,
-        "weight_up_one",
-        [((32, L), F32)],
-        [Far(low3), Far(cat1, 512), cat0g],
-        [((512, COLS0), F32)],
-        flops=2 * R * COLS0 * 1024,
+    near, inside, mom4, (t, w1d_grad, rect_here, h3_here, z2_here) = exchange(
+        cross, core, mom, "tm",
+        lambda token: run(
+            window_4,
+            "window_4",
+            [((COLS1, 256), BF)] + far(32, L),
+            [Far(low3), Far(cat1, 512), cat0g, w2d],
+            [((512, COLS0), F32), ((400, L), F32), ((32, L), F32)],
+            flops=2 * R * COLS0 * 1024,
+            fetch=[Far(rect), Far(h3), Far(z2)],
+            token=token,
+        ),
     )
     g2, cat1g, cross, core, mom = run(
         up_two_back_kernel,
         "up_two_back",
         [((R, 256), F32), ((R, COLS1), BF)] + packet(256),
-        [index, g3, near, inside, mom4, mom1, mom3, mom2, prm, aux, kept]
-        + [Far(rect_far), Far(h3), Far(t2a_d), Far(z2_far)],
+        [index, g3, near, inside, mom4, mom1, mom3, mom2, prm, aux, kept, rect_here, h3_here, t, z2_here],
         rim(512) + wide(512),
         flops=2 * R * COLS1 * 256,
     )
-    near, inside, mom5 = exchange(cross, core, mom, "tm")
-    (w2d_grad,) = run(
-        weight_2_kernel,
-        "weight_up_two",
-        [((128, L), F32)],
-        [Far(act2), cat1g],
-        [((256, COLS1), F32)],
-        flops=2 * R * COLS1 * 256,
+    near, inside, mom5, (t, w2d_grad, z2_here, h2_here, gact_here, z1_here) = exchange(
+        cross, core, mom, "tm",
+        lambda token: run(
+            window_5,
+            "window_5",
+            [((512, COLS2), BF)] + far(128, L),
+            [Far(act2), cat1g, w2c],
+            [((256, COLS1), F32), ((400, L), F32), ((128, L), F32)],
+            flops=2 * R * COLS1 * 256,
+            fetch=[Far(z2), Far(h2), Far(gact), Far(z1)],
+            token=token,
+        ),
     )
     g1, low2, cross, core, mom = run(
         down_two_back_kernel,
         "down_two_back",
         [((R, 512), F32), ((R, 256), BF)] + packet(512),
-        [index, g2, near, inside, mom5, mom1, mom2, prm, aux, kept]
-        + [Far(z2_far), Far(h2), Far(t2b_c), Far(gact), Far(z1_far)],
+        [index, g2, near, inside, mom5, mom1, mom2, prm, aux, kept, z2_here, h2_here, t, gact_here, z1_here],
         [((R, COLS2), BF)] + rim(256) + wide(256),
         flops=2 * R * COLS2 * 512,
     )
-    near, inside, mom6 = exchange(cross, core, mom, "tm")
-    (w2c_grad,) = run(
-        weight_2_kernel,
-        "weight_down_two",
-        [((128, L), F32)],
-        [low2, Far(cat1)],
-        [((256, COLS1), F32)],
-        flops=2 * R * COLS1 * 256,
+    near, inside, mom6, (t, w2c_grad, z1_here, h1_here, cat0_here) = exchange(
+        cross, core, mom, "tm",
+        lambda token: run(
+            window_6,
+            "window_6",
+            [((256, COLS1B), BF)] + far(128, L),
+            [low2, Far(cat1), w1c],
+            [((256, COLS1), F32), ((128, L), F32)],
+            flops=2 * R * COLS1 * 256,
+            fetch=[Far(z1), Far(h1), Far(cat0)],
+            token=token,
+        ),
     )
     *nets, low1 = run(
         up_one_back_kernel,
         "up_one_back",
         [((per, 256), BF)] * stems + [((R, 512), BF)],
-        [index, g1, near, inside, mom6, mom1, prm, aux, kept, Far(z1_far), Far(h1), Far(t1b_c)],
+        [index, g1, near, inside, mom6, mom1, prm, aux, kept, z1_here, h1_here, t],
         [((R, COLS1B), BF)] + rim(512) + wide(512),
         flops=2 * R * COLS1B * 256,
     )
     nets = swap(nets, "stem")
-    (w1c_grad,) = run(
-        weight_1_first,
-        "weight_down_one",
-        [((16, L), F32)],
-        [low1, Far(cat0)],
-        [((512, COLS0), F32)],
+    keep, give, direct_here = run(
+        window_7,
+        "window_7",
+        [((HALF, L), F32), ((HALF, L), F32)],
+        [index, low1, cat0_here, bias_one, Far(w1d_grad), Far(w2d_grad), Far(w2c_grad)],
+        [((512, COLS0), F32), ((16, L), F32)],
         flops=2 * R * COLS0 * 512,
+        fetch=[Far(direct)],
     )
     (mixture_grad,) = run(
         mixture_kernel,
         "mixture",
         [((2, frames, blocks * 32), F32)],
-        [*nets, Far(direct)],
+        [*nets, direct_here],
         [((2, frames, L), F32)],
     )
-    spare = jnp.zeros((8, L), F32)
-    early = sum_halves(jnp.concatenate([w1d_grad, bias_one, spare, w2d_grad]), "tm", odd)
-    w2c_grad = sum_halves(w2c_grad, "tm", odd)
-    w1c_grad = sum_over(w1c_grad, "tm")
-
-    def outer(packed):
-        taps = packed.reshape(16, 2, 2, 4, 8)[:, :, :, :3, :TAPS].transpose(0, 2, 3, 1, 4)
-        return taps.reshape(16, 2, 6, TAPS)[:, :, 1:]
-
-    def inner(packed):
-        last = jnp.concatenate([packed[0:32, 80:], packed[32:64, 80:112]], axis=1)
-        taps = jnp.concatenate([packed[:, :80].reshape(4, 32, 80), last[None]])
-        return taps.reshape(TAPS, 32, TAPS, 16).transpose(1, 3, 0, 2)
-
-    w1d_grad = jnp.concatenate([outer(early[0:16]), outer(early[16:32])]).transpose(1, 0, 2, 3)
+    mine, other = sum_halves(keep, give, "tm")
+    w1c_grad, w2c_grad, w2d_grad, w1d_grad, bias_one = run(
+        unpack_kernel,
+        "unpack",
+        [((25, 2, 16), F32), ((25, 16, 32), F32), ((25, 16, 32), F32), ((25, 2, 32), F32), ((8, L), F32)],
+        [index, mine, other],
+    )
+
+    def turned(grad, order):
+        return grad.reshape((TAPS, TAPS) + grad.shape[1:]).transpose(order)[None]
+
     return (
         estimates,
         mixture_grad,
-        outer(w1c_grad)[None],
+        turned(w1c_grad, (3, 2, 0, 1)),
         mom6[1, :16][None],
         mom6[0, :16][None],
-        inner(w2c_grad)[None],
+        turned(w2c_grad, (3, 2, 0, 1)),
         mom5[1, :32][None],
         mom5[0, :32][None],
-        inner(early[48:176]).transpose(1, 0, 2, 3)[None],
+        turned(w2d_grad, (2, 3, 0, 1)),
         mom5[2, :16][None],
         mom4[1, :16][None],
         mom4[0, :16][None],
-        w1d_grad[None],
-        early[32:40].reshape(8, 2, 2, 32).sum((0, 1, 3))[None],
+        turned(w1d_grad, (2, 3, 0, 1)),
+        bias_one[0:1, 0:2],
     )
 
 

time: 200 us -> 161 us (0.81)
  starting transfers between devices: 58 us -> 47.2 us
  local copies, waits for them, and re-layouts: 14.4 us -> 5.22 us
  Pallas kernels: 92.8 us -> 84.5 us
  waiting for transfers between devices: 26.8 us -> 19.7 us
  other arithmetic: 6 us -> 2.52 us
    ppermute x42 -> x33, starting transfers between devices: 32.9 us -> 24.2 us  [flip(): lax.ppermute(values, axis, [(i, i ^ bit) for i in range(lax.axis_size(axi...]
    pallas_call x19 -> x22, Pallas kernels: 92.8 us -> 84.5 us  [run(): pl.pallas_call(body, out_shape=[pltpu.HBM(o[0], o[1]) if len(o) == 3 else...]
    unnamed x38 -> x24, local copies, waits for them, and re-layouts: 5.67 us -> 0.72 us
    ppermute x42 -> x33, waiting for transfers between devices: 23.3 us -> 18.9 us  [flip(): lax.ppermute(values, axis, [(i, i ^ bit) for i in range(lax.axis_size(axi...]
    ppermute x6, waiting for transfers between devices: 3.54 us -> 0.72 us  [exchange(): near = lax.ppermute(cross, axis, pairs(count, -1))]
    ppermute x6, starting transfers between devices: 13.7 us -> 11 us  [exchange(): near = lax.ppermute(cross, axis, pairs(count, -1))]
  transfers between devices with their start and end apart: 55 -> 46, of which waited for: 17 -> 15; matrix products, arithmetic and copies ran while one was open for 8% -> 4% of each run, Pallas kernels for 20% -> 18%
where the time goes in v3:
time: 161 us; the launch traced here: 160 us
  Pallas kernels  84.5 us (52%)
  starting transfers between devices  47.2 us (29%)
  waiting for transfers between devices  19.7 us (12%)
  local copies, waits for them, and re-layouts  5.22 us (3%)
  other arithmetic  2.52 us (2%)
    pallas_call x22, Pallas kernels, run(): pl.pallas_call(body, out_shape=[pltpu.HBM(o[0], o[1]) if len(o) == 3 else...  84.5 us
    ppermute x33, starting transfers between devices, flip(): lax.ppermute(values, axis, [(i, i ^ bit) for i in range(lax.axis_size(axi...  24.2 us
    ppermute x33, waiting for transfers between devices, flip(): lax.ppermute(values, axis, [(i, i ^ bit) for i in range(lax.axis_size(axi...  18.9 us
    ppermute x6, starting transfers between devices, exchange(): near = lax.ppermute(cross, axis, pairs(count, -1))  11 us
    ppermute x6, starting transfers between devices, exchange(): far = lax.ppermute(mom, axis, pairs(count, 3))  7.38 us
    ppermute x1, starting transfers between devices, per_device(): near = lax.ppermute(cross, 'tm', pairs(lax.axis_size('tm'), -1))  4.55 us
  transfers between devices with their start and end apart: 46, of which 15 were waited for; matrix products, arithmetic and copies ran while one was open for 4% of the time, Pallas kernels for 18%

profile of v3, /device:TPU:0, one launch (start us, length us, event | category | flops | bytes accessed | tf_op | source)
XLA Modules:
  0.0 160.4 jit_solution(14965446186167225815)
XLA Ops:
  1.4 3.7 %layout.1 = (bf16[80,256]{1,0:T(8,128)(2,1)S(1)}, bf16[80,256]{1,0:T(8,128)(2,1)S(1)}, bf16[1024,256]{1,0:T(8,128)(2,1)S(1)}, bf16[1024,256]{1,0:T(8,128)(2,1)}, bf16[1024,256]{1,0:T(8,128)(2,1)}) custom-call(s32[2]{0:T(128)S(1)} %pad_add_fusion.refs_0_, s32[128]{0:T(128)S(1)} %copy-done.2, bf16[2,128,1024]{2,1,0:T(8,128)(2,1)} %refs_2_.1, ...), custom_call_target="tpu_custom_call" | custom-call | bytes 2703880 | tf_op jit(solution)/shard_map/layout/pallas_call | solution.py:122
  5.1 4.6 %collective-permute-start = (bf16[80,256]{1,0:T(8,128)(2,1)S(1)}, bf16[80,256]{1,0:T(8,128)(2,1)S(1)}, u32[]{:S(2)}, u32[]{:S(2)}) collective-permute-start(bf16[80,256]{1,0:T(8,128)(2,1)S(1)} %get-tuple-element.121), channel_id=1, source_target_pairs={{0,7},{2,1},{4,3},{6,5},{7,0},{1,2},{3,4},{5,6},{8,15},{10,9},{12,... | collective-permute-start | bytes 122888 | tf_op jit(solution)/shard_map/ppermute | solution.py:1388
  13.3 5.3 %conv_one.1 = (f32[40,512]{1,0:T(8,128)S(1)}, f32[32,512]{1,0:T(8,128)}, f32[8,128]{1,0:T(8,128)S(1)}, f32[8,128]{1,0:T(8,128)S(1)}, f32[64,256]{1,0:T(8,128)}, ...) custom-call(s32[2]{0:T(128)S(1)} %pad_add_fusion.refs_0_, bf16[1024,256]{1,0:T(8,128)(2,1)S(1)} %get-tuple-element.120.refs_1_, ...), custom_call_target="tpu_custom_call" | custom-call | flops 1073741824 | bytes 6152200 | tf_op jit(solution)/shard_map/conv_one/pallas_call | solution.py:122
  20.5 2.2 %collective-permute-start.4 = (f32[8,128]{1,0:T(8,128)S(1)}, f32[8,128]{1,0:T(8,128)S(1)}, u32[]{:S(2)}, u32[]{:S(2)}) collective-permute-start(f32[8,128]{1,0:T(8,128)S(1)} %get-tuple-element.124.refs_2_), channel_id=1, source_target_pairs={{0,3},{2,5},{4,7},{6,1},{3,0},{5,2},{7,4},{1,6},{8,11},{10,13},{12... | collective-permute-start | bytes 12296 | tf_op jit(solution)/shard_map/ppermute | solution.py:1297
  26.4 5.7 %conv_two.1 = (f32[40,256]{1,0:T(8,128)S(1)}, f32[32,256]{1,0:T(8,128)S(1)}, f32[8,128]{1,0:T(8,128)S(1)}, bf16[4,32,512]{2,1,0:T(8,128)(2,1)}, f32[2,32,512]{2,...) custom-call(s32[2]{0:T(128)S(1)} %pad_add_fusion.refs_0_, f32[1024,512]{1,0:T(8,128)S(1)} %get-tuple-element.125.refs_1_, ...), custom_call_target="tpu_custom_call" | custom-call | flops 1006632960 | bytes 8384520 | tf_op jit(solution)/shard_map/conv_two/pallas_call | solution.py:122
  32.1 3.0 %collective-permute-start.7 = (f32[40,256]{1,0:T(8,128)S(1)}, f32[40,256]{1,0:T(8,128)S(1)}, u32[]{:S(2)}, u32[]{:S(2)}) collective-permute-start(f32[40,256]{1,0:T(8,128)S(1)} %get-tuple-element.133), channel_id=1, source_target_pairs={{0,7},{2,1},{4,3},{6,5},{7,0},{1,2},{3,4},{5,6},{8,15},{10,9},{12,... | collective-permute-start | bytes 122888 | tf_op jit(solution)/shard_map/ppermute | solution.py:1295
  41.3 7.4 %up_two.1 = (f32[40,512]{1,0:T(8,128)S(1)}, f32[32,512]{1,0:T(8,128)S(1)}, f32[8,128]{1,0:T(8,128)S(1)}, f32[2,32,256]{2,1,0:T(8,128)}, bf16[1024,256]{1,0:T(8,128)(2,1)}, /*index=5*/f32[1024,512]{1,0:T(8,128)}) custom-call(s32[2]{0:T(128)S(1)} %pad_add_fusion.refs_0_, f32[1024,256]{1,0:T(8,128)S(1)} %get-tuple-element.132.refs_1_, ...), custom_call_target="tpu_custom_call" | custom-call | flops 1207959552 | bytes 5171208 | tf_op jit(solution)/shard_map/up_two/pallas_call | solution.py:122
  50.0 2.8 %collective-permute-start.12 = (f32[40,512]{1,0:T(8,128)S(1)}, f32[40,512]{1,0:T(8,128)S(1)}, u32[]{:S(2)}, u32[]{:S(2)}) collective-permute-start(f32[40,512]{1,0:T(8,128)S(1)} %get-tuple-element.142), channel_id=1, source_target_pairs={{0,7},{2,1},{4,3},{6,5},{7,0},{1,2},{3,4},{5,6},{8,15},{10,9},{12,... | collective-permute-start | bytes 245768 | tf_op jit(solution)/shard_map/ppermute | solution.py:1295
  53.2 2.6 %window_3.1 = (bf16[256,3072]{1,0:T(8,128)(2,1)S(1)}, f32[1024,512]{1,0:T(8,128)S(1)}, bf16[1024,1536]{1,0:T(8,128)(2,1)S(1)}, bf16[4,32,512]{2,1,0:T(8,128)(2,1)S(1)}, f32[8,128]{1,0:T(8,128)S(1)}) custom-call(f32[2,50,128]{2,1,0:T(8,128)S(1)} %copy.52.refs_0_.refs_6_, f32[1024,512]{1,0:T(8,128)} %get-tuple-element.137.refs_1_.refs_9_.refs_4_, ...), custom_call_target="tpu_custom_call" | custom-call | bytes 13039616 | tf_op jit(solution)/shard_map/window_3/pallas_call | solution.py:122
  57.7 6.4 %up_one.1 = (bf16[272,256]{1,0:T(8,128)(2,1)S(1)}, bf16[272,256]{1,0:T(8,128)(2,1)S(1)}, bf16[272,256]{1,0:T(8,128)(2,1)S(1)}, bf16[272,256]{1,0:T(8,128)(2,1)S(...) custom-call(s32[2]{0:T(128)S(1)} %pad_add_fusion.refs_0_, ...), custom_call_target="tpu_custom_call" | custom-call | flops 1610612736 | bytes 9879560 | tf_op jit(solution)/shard_map/up_one/pallas_call | solution.py:122
  70.4 3.7 %collective-permute-done.18.refs_3_ = bf16[272,256]{1,0:T(8,128)(2,1)S(1)} collective-permute-done((bf16[272,256]{1,0:T(8,128)(2,1)S(1)}, bf16[272,256]{1,0:T(8,128)(2,1)S(1)}, u32[]{:S(2)}, u32[]{:S(2)}) %collective-permute-start.18) | collective-permute-done | bytes 139296 | tf_op jit(solution)/shard_map/ppermute | solution.py:1261
  79.7 3.6 %estimate.1 = (bf16[4,2,128,256]{3,2,1,0:T(8,128)(2,1)}, bf16[1024,1024]{1,0:T(8,128)(2,1)S(1)}, f32[1024,256]{1,0:T(8,128)S(1)}, f32[32,256]{1,0:T(8,128)S(1)}, f32[1024,512]{1,0:T(8,128)S(1)}) custom-call(s32[2]{0:T(128)S(1)} %pad_add_fusion.refs_0_, bf16[272,256]{1,0:T(8,128)(2,1)S(1)} %get-tuple-element.148.refs_1_, ...), custom_call_target="tpu_custom_call" | custom-call | bytes 9588744 | tf_op jit(solution)/shard_map/estimate/pallas_call | solution.py:122
  85.0 5.4 %down_one_back.1 = (f32[1024,512]{1,0:T(8,128)S(1)}, bf16[1024,1024]{1,0:T(8,128)(2,1)S(1)}, f32[40,512]{1,0:T(8,128)S(1)}, f32[32,512]{1,0:T(8,128)S(1)}, f32[8...) custom-call(s32[2]{0:T(128)S(1)} %pad_add_fusion.refs_0_, ...), custom_call_target="tpu_custom_call" | custom-call | flops 2147483648 | bytes 12369928 | tf_op jit(solution)/shard_map/down_one_back/pallas_call | solution.py:122
  90.8 2.3 %collective-permute-start.24 = (f32[32,512]{1,0:T(8,128)S(1)}, f32[32,512]{1,0:T(8,128)S(1)}, u32[]{:S(2)}, u32[]{:S(2)}) collective-permute-start(f32[32,512]{1,0:T(8,128)S(1)} %get-tuple-element.171), channel_id=1, source_target_pairs={{0,1},{1,0},{2,3},{3,2},{4,5},{5,4},{6,7},{7,6},{8,9},{9,8},{10,11... | collective-permute-start | bytes 196616 | tf_op jit(solution)/shard_map/ppermute | solution.py:1261
  94.6 6.4 %window_4.1 = (bf16[1920,256]{1,0:T(8,128)(2,1)S(1)}, f32[32,128]{1,0:T(8,128)}, f32[1024,512]{1,0:T(8,128)S(1)}, f32[2,32,512]{2,1,0:T(8,128)S(1)}, f32[1024,256]{1,0:T(8,128)S(1)}, /*index=5*/f32[8,128]{1,0:T(8,128)S(1)}) custom-call(bf16[1024,512]{1,0:T(8,128)(2,1)} %get-tuple-element.172.refs_0_, bf16[1024,1920]{1,0:T(8,128)(2,1)} %get-tuple-element.138.refs_2_.refs_1_, ...), custom_call_target="tpu_custom_call" | custom-call | flops 2147483648 | bytes 14537728 | tf_op jit(solution)/shard_map/window_4/pallas_call | solution.py:122
  102.3 6.4 %up_two_back.1 = (f32[1024,256]{1,0:T(8,128)S(1)}, bf16[1024,1920]{1,0:T(8,128)(2,1)S(1)}, f32[40,256]{1,0:T(8,128)S(1)}, f32[32,256]{1,0:T(8,128)S(1)}, f32[8,128]{1,0:T(8,128)S(1)}) custom-call(s32[2]{0:T(128)S(1)} %pad_add_fusion.refs_0_, f32[1024,512]{1,0:T(8,128)S(1)} %get-tuple-element.169.refs_1_, f32[40,512]{1,0:T(8,128)S(1)} %collective-permute-done.23.refs_2_, ...), custom_call_target="tpu_custom_call" | custom-call | flops 1006632960 | bytes 11669512 | tf_op jit(solution)/shard_map/up_two_back/pallas_call | solution.py:122
  113.1 4.0 %window_5.1 = (bf16[512,1152]{1,0:T(8,128)(2,1)S(1)}, f32[128,128]{1,0:T(8,128)}, f32[1024,256]{1,0:T(8,128)S(1)}, f32[2,32,256]{2,1,0:T(8,128)S(1)}, f32[1024,5...) custom-call(bf16[1024,256]{1,0:T(8,128)(2,1)} %get-tuple-element.185.refs_0_, ...), custom_call_target="tpu_custom_call" | custom-call | flops 1006632960 | bytes 16288768 | tf_op jit(solution)/shard_map/window_5/pallas_call | solution.py:122
  118.5 5.6 %down_two_back.1 = (f32[1024,512]{1,0:T(8,128)S(1)}, bf16[1024,256]{1,0:T(8,128)(2,1)S(1)}, f32[40,512]{1,0:T(8,128)S(1)}, f32[32,512]{1,0:T(8,128)S(1)}, f32[8,128]{1,0:T(8,128)S(1)}) custom-call(s32[2]{0:T(128)S(1)} %pad_add_fusion.refs_0_, f32[1024,256]{1,0:T(8,128)S(1)} %get-tuple-element.182.refs_1_, f32[40,256]{1,0:T(8,128)S(1)} %collective-permute-done.28.refs_2_, ...), custom_call_target="tpu_custom_call" | custom-call | flops 1207959552 | bytes 10485768 | tf_op jit(solution)/shard_map/down_two_back/pallas_call | solution.py:122
  124.6 2.3 %collective-permute-start.35 = (f32[8,128]{1,0:T(8,128)S(1)}, f32[8,128]{1,0:T(8,128)S(1)}, u32[]{:S(2)}, u32[]{:S(2)}) collective-permute-start(f32[8,128]{1,0:T(8,128)S(1)} %get-tuple-element.202.refs_6_), channel_id=1, source_target_pairs={{0,3},{2,5},{4,7},{6,1},{3,0},{5,2},{7,4},{1,6},{8,11},{10,13},{12... | collective-permute-start | bytes 12296 | tf_op jit(solution)/shard_map/ppermute | solution.py:1297
  128.3 5.0 %window_6.1 = (bf16[256,1536]{1,0:T(8,128)(2,1)S(1)}, f32[128,128]{1,0:T(8,128)}, f32[1024,512]{1,0:T(8,128)S(1)}, f32[2,32,512]{2,1,0:T(8,128)S(1)}, bf16[1024,...) custom-call(bf16[1024,256]{1,0:T(8,128)(2,1)S(1)} %get-tuple-element.199.refs_0_, ...), custom_call_target="tpu_custom_call" | custom-call | flops 1006632960 | bytes 13865984 | tf_op jit(solution)/shard_map/window_6/pallas_call | solution.py:122
  134.6 3.8 %up_one_back.1 = (bf16[256,256]{1,0:T(8,128)(2,1)S(1)}, bf16[256,256]{1,0:T(8,128)(2,1)S(1)}, bf16[256,256]{1,0:T(8,128)(2,1)S(1)}, bf16[256,256]{1,0:T(8,128)(2,1)S(1)}, bf16[1024,512]{1,0:T(8,128)(2,1)S(1)}) custom-call(s32[2]{0:T(128)S(1)} %pad_add_fusion.refs_0_, f32[1024,512]{1,0:T(8,128)S(1)} %get-tuple-element.196.refs_1_, ...), custom_call_target="tpu_custom_call" | custom-call | flops 805306368 | bytes 6930440 | tf_op jit(solution)/shard_map/up_one_back/pallas_call | solution.py:122
  138.4 2.8 %window_7.1 = (f32[160,128]{1,0:T(8,128)S(1)}, f32[160,128]{1,0:T(8,128)S(1)}, f32[256,256]{1,0:T(8,128)S(1)}) custom-call(s32[2]{0:T(128)S(1)} %pad_add_fusion.refs_0_, bf16[1024,512]{1,0:T(8,128)(2,1)S(1)} %get-tuple-element.211.refs_1_, bf16[1024,1024]{1,0:T(8,128)(2,1)S(1)} %get-tuple-element.212.refs_2_, f32[8,128]{1,0:T(8,128)S(1)} %get-tuple-element.213.refs_3_, ...), custom_call_target="tpu_custom_call" | custom-call | flops 1073741824 | bytes 3985416 | tf_op jit(solution)/shard_map/window_7/pallas_call | solution.py:122
  142.6 2.6 %collective-permute-start.44 = (bf16[160,128]{1,0:T(8,128)(2,1)S(1)}, bf16[160,128]{1,0:T(8,128)(2,1)S(1)}, u32[]{:S(2)}, u32[]{:S(2)}) collective-permute-start(bf16[160,128]{1,0:T(8,128)(2,1)S(1)} %add_convert_fusion), channel_id=1, source_target_pairs={{0,6},{1,7},{2,4},{3,5},{4,2},{5,3},{6,0},{7,1},{8,14},{9,15},{10,... | collective-permute-start | bytes 122888 | tf_op jit(solution)/shard_map/ppermute | solution.py:1261
  154.1 2.7 %collective-permute-done.39.refs_2_ = bf16[256,256]{1,0:T(8,128)(2,1)S(1)} collective-permute-done((bf16[256,256]{1,0:T(8,128)(2,1)S(1)}, bf16[256,256]{1,0:T(8,128)(2,1)S(1)}, u32[]{:S(2)}, u32[]{:S(2)}) %collective-permute-start.39) | collective-permute-done | bytes 131104 | tf_op jit(solution)/shard_map/ppermute | solution.py:1261
  (178 shorter events, 58.6 us)
Async XLA Ops:
  5.1 8.1 %collective-permute-start = (bf16[80,256]{1,0:T(8,128)(2,1)S(1)}, bf16[80,256]{1,0:T(8,128)(2,1)S(1)}, u32[]{:S(2)}, u32[]{:S(2)}) collective-permute-start(bf16[80,256]{1,0:T(8,128)(2,1)S(1)} %get-tuple-element.121), channel_id=1, source_target_pairs={{0,7},{2,1},{4,3},{6,5},{7,0},{1,2},{3,4},{5,6},{8,15},{10,9},{12,... | collective-permute-start | bytes 122888 | tf_op jit(solution)/shard_map/ppermute | solution.py:1388
  32.1 7.5 %collective-permute-start.7 = (f32[40,256]{1,0:T(8,128)S(1)}, f32[40,256]{1,0:T(8,128)S(1)}, u32[]{:S(2)}, u32[]{:S(2)}) collective-permute-start(f32[40,256]{1,0:T(8,128)S(1)} %get-tuple-element.133), channel_id=1, source_target_pairs={{0,7},{2,1},{4,3},{6,5},{7,0},{1,2},{3,4},{5,6},{8,15},{10,9},{12,... | collective-permute-start | bytes 122888 | tf_op jit(solution)/shard_map/ppermute | solution.py:1295
  48.7 7.2 %collective-permute-start.15 = (f32[8,128]{1,0:T(8,128)S(1)}, f32[8,128]{1,0:T(8,128)S(1)}, u32[]{:S(2)}, u32[]{:S(2)}) collective-permute-start(f32[8,128]{1,0:T(8,128)S(1)} %get-tuple-element.140.refs_4_), channel_id=1, source_target_pairs={{0,4},{1,5},{2,6},{3,7},{4,0},{5,1},{6,2},{7,3},{8,12},{9,13},{10,... | collective-permute-start | bytes 12296 | tf_op jit(solution)/shard_map/ppermute | solution.py:1261
  50.0 6.5 %collective-permute-start.12 = (f32[40,512]{1,0:T(8,128)S(1)}, f32[40,512]{1,0:T(8,128)S(1)}, u32[]{:S(2)}, u32[]{:S(2)}) collective-permute-start(f32[40,512]{1,0:T(8,128)S(1)} %get-tuple-element.142), channel_id=1, source_target_pairs={{0,7},{2,1},{4,3},{6,5},{7,0},{1,2},{3,4},{5,6},{8,15},{10,9},{12,... | collective-permute-start | bytes 245768 | tf_op jit(solution)/shard_map/ppermute | solution.py:1295
  65.7 8.4 %collective-permute-start.18 = (bf16[272,256]{1,0:T(8,128)(2,1)S(1)}, bf16[272,256]{1,0:T(8,128)(2,1)S(1)}, u32[]{:S(2)}, u32[]{:S(2)}) collective-permute-start(bf16[272,256]{1,0:T(8,128)(2,1)S(1)} %get-tuple-element.150), channel_id=1, source_target_pairs={{0,16},{8,24},{16,0},{24,8},{1,17},{9,25},{17,1},{25,9},{2,18},{10... | collective-permute-start | bytes 417800 | tf_op jit(solution)/shard_map/ppermute | solution.py:1261
  67.2 6.9 %collective-permute-start.19 = (bf16[272,256]{1,0:T(8,128)(2,1)S(1)}, bf16[272,256]{1,0:T(8,128)(2,1)S(1)}, u32[]{:S(2)}, u32[]{:S(2)}) collective-permute-start(bf16[272,256]{1,0:T(8,128)(2,1)S(1)} %get-tuple-element.151), channel_id=1, source_target_pairs={{0,24},{8,16},{16,8},{24,0},{1,25},{9,17},{17,9},{25,1},{2,26},{10... | collective-permute-start | bytes 417800 | tf_op jit(solution)/shard_map/ppermute | solution.py:1261
  76.1 7.2 %collective-permute-start.20 = (bf16[272,256]{1,0:T(8,128)(2,1)S(1)}, bf16[272,256]{1,0:T(8,128)(2,1)S(1)}, u32[]{:S(2)}, u32[]{:S(2)}) collective-permute-start(bf16[272,256]{1,0:T(8,128)(2,1)S(1)} %get-tuple-element.162), channel_id=1, source_target_pairs={{0,8},{8,0},{16,24},{24,16},{1,9},{9,1},{17,25},{25,17},{2,10},{10... | collective-permute-start | bytes 417800 | tf_op jit(solution)/shard_map/ppermute | solution.py:1261
  77.4 7.6 %collective-permute-start.21 = (bf16[272,256]{1,0:T(8,128)(2,1)S(1)}, bf16[272,256]{1,0:T(8,128)(2,1)S(1)}, u32[]{:S(2)}, u32[]{:S(2)}) collective-permute-start(bf16[272,256]{1,0:T(8,128)(2,1)S(1)} %get-tuple-element.163), channel_id=1, source_target_pairs={{0,16},{8,24},{16,0},{24,8},{1,17},{9,25},{17,1},{25,9},{2,18},{10... | collective-permute-start | bytes 417800 | tf_op jit(solution)/shard_map/ppermute | solution.py:1261
  78.2 6.8 %collective-permute-start.22 = (bf16[272,256]{1,0:T(8,128)(2,1)S(1)}, bf16[272,256]{1,0:T(8,128)(2,1)S(1)}, u32[]{:S(2)}, u32[]{:S(2)}) collective-permute-start(bf16[272,256]{1,0:T(8,128)(2,1)S(1)} %get-tuple-element.164), channel_id=1, source_target_pairs={{0,24},{8,16},{16,8},{24,0},{1,25},{9,17},{17,9},{25,1},{2,26},{10... | collective-permute-start | bytes 417800 | tf_op jit(solution)/shard_map/ppermute | solution.py:1261
  90.4 10.6 %collective-permute-start.26 = (f32[8,128]{1,0:T(8,128)S(1)}, f32[8,128]{1,0:T(8,128)S(1)}, u32[]{:S(2)}, u32[]{:S(2)}) collective-permute-start(f32[8,128]{1,0:T(8,128)S(1)} %get-tuple-element.175.refs_7_), channel_id=1, source_target_pairs={{0,4},{1,5},{2,6},{3,7},{4,0},{5,1},{6,2},{7,3},{8,12},{9,13},{10,... | collective-permute-start | bytes 12296 | tf_op jit(solution)/shard_map/ppermute | solution.py:1261
  90.8 10.2 %collective-permute-start.25 = (f32[8,128]{1,0:T(8,128)S(1)}, f32[8,128]{1,0:T(8,128)S(1)}, u32[]{:S(2)}, u32[]{:S(2)}) collective-permute-start(f32[8,128]{1,0:T(8,128)S(1)} %get-tuple-element.175.refs_7_), channel_id=1, source_target_pairs={{0,3},{2,5},{4,7},{6,1},{3,0},{5,2},{7,4},{1,6},{8,11},{10,13},{12... | collective-permute-start | bytes 12296 | tf_op jit(solution)/shard_map/ppermute | solution.py:1297
  90.8 11.5 %collective-permute-start.24 = (f32[32,512]{1,0:T(8,128)S(1)}, f32[32,512]{1,0:T(8,128)S(1)}, u32[]{:S(2)}, u32[]{:S(2)}) collective-permute-start(f32[32,512]{1,0:T(8,128)S(1)} %get-tuple-element.171), channel_id=1, source_target_pairs={{0,1},{1,0},{2,3},{3,2},{4,5},{5,4},{6,7},{7,6},{8,9},{9,8},{10,11... | collective-permute-start | bytes 196616 | tf_op jit(solution)/shard_map/ppermute | solution.py:1261
  93.1 7.9 %collective-permute-start.23 = (f32[40,512]{1,0:T(8,128)S(1)}, f32[40,512]{1,0:T(8,128)S(1)}, u32[]{:S(2)}, u32[]{:S(2)}) collective-permute-start(f32[40,512]{1,0:T(8,128)S(1)} %get-tuple-element.170), channel_id=1, source_target_pairs={{0,7},{2,1},{4,3},{6,5},{7,0},{1,2},{3,4},{5,6},{8,15},{10,9},{12,... | collective-permute-start | bytes 245768 | tf_op jit(solution)/shard_map/ppermute | solution.py:1295
  108.7 8.5 %collective-permute-start.31 = (f32[8,128]{1,0:T(8,128)S(1)}, f32[8,128]{1,0:T(8,128)S(1)}, u32[]{:S(2)}, u32[]{:S(2)}) collective-permute-start(f32[8,128]{1,0:T(8,128)S(1)} %get-tuple-element.189.refs_7_), channel_id=1, source_target_pairs={{0,4},{1,5},{2,6},{3,7},{4,0},{5,1},{6,2},{7,3},{8,12},{9,13},{10,... | collective-permute-start | bytes 12296 | tf_op jit(solution)/shard_map/ppermute | solution.py:1261
  109.5 7.7 %collective-permute-start.30 = (f32[8,128]{1,0:T(8,128)S(1)}, f32[8,128]{1,0:T(8,128)S(1)}, u32[]{:S(2)}, u32[]{:S(2)}) collective-permute-start(f32[8,128]{1,0:T(8,128)S(1)} %get-tuple-element.189.refs_7_), channel_id=1, source_target_pairs={{0,3},{2,5},{4,7},{6,1},{3,0},{5,2},{7,4},{1,6},{8,11},{10,13},{12... | collective-permute-start | bytes 12296 | tf_op jit(solution)/shard_map/ppermute | solution.py:1297
  111.1 7.3 %collective-permute-start.29 = (f32[32,256]{1,0:T(8,128)S(1)}, f32[32,256]{1,0:T(8,128)S(1)}, u32[]{:S(2)}, u32[]{:S(2)}) collective-permute-start(f32[32,256]{1,0:T(8,128)S(1)} %get-tuple-element.184), channel_id=1, source_target_pairs={{0,1},{1,0},{2,3},{3,2},{4,5},{5,4},{6,7},{7,6},{8,9},{9,8},{10,11... | collective-permute-start | bytes 98312 | tf_op jit(solution)/shard_map/ppermute | solution.py:1261
  124.1 9.2 %collective-permute-start.36 = (f32[8,128]{1,0:T(8,128)S(1)}, f32[8,128]{1,0:T(8,128)S(1)}, u32[]{:S(2)}, u32[]{:S(2)}) collective-permute-start(f32[8,128]{1,0:T(8,128)S(1)} %get-tuple-element.202.refs_6_), channel_id=1, source_target_pairs={{0,4},{1,5},{2,6},{3,7},{4,0},{5,1},{6,2},{7,3},{8,12},{9,13},{10,... | collective-permute-start | bytes 12296 | tf_op jit(solution)/shard_map/ppermute | solution.py:1261
  124.6 8.7 %collective-permute-start.35 = (f32[8,128]{1,0:T(8,128)S(1)}, f32[8,128]{1,0:T(8,128)S(1)}, u32[]{:S(2)}, u32[]{:S(2)}) collective-permute-start(f32[8,128]{1,0:T(8,128)S(1)} %get-tuple-element.202.refs_6_), channel_id=1, source_target_pairs={{0,3},{2,5},{4,7},{6,1},{3,0},{5,2},{7,4},{1,6},{8,11},{10,13},{12... | collective-permute-start | bytes 12296 | tf_op jit(solution)/shard_map/ppermute | solution.py:1297
  127.0 7.7 %collective-permute-start.34 = (f32[32,512]{1,0:T(8,128)S(1)}, f32[32,512]{1,0:T(8,128)S(1)}, u32[]{:S(2)}, u32[]{:S(2)}) collective-permute-start(f32[32,512]{1,0:T(8,128)S(1)} %get-tuple-element.198), channel_id=1, source_target_pairs={{0,1},{1,0},{2,3},{3,2},{4,5},{5,4},{6,7},{7,6},{8,9},{9,8},{10,11... | collective-permute-start | bytes 196616 | tf_op jit(solution)/shard_map/ppermute | solution.py:1261
  142.6 7.6 %collective-permute-start.44 = (bf16[160,128]{1,0:T(8,128)(2,1)S(1)}, bf16[160,128]{1,0:T(8,128)(2,1)S(1)}, u32[]{:S(2)}, u32[]{:S(2)}) collective-permute-start(bf16[160,128]{1,0:T(8,128)(2,1)S(1)} %add_convert_fusion), channel_id=1, source_target_pairs={{0,6},{1,7},{2,4},{3,5},{4,2},{5,3},{6,0},{7,1},{8,14},{9,15},{10,... | collective-permute-start | bytes 122888 | tf_op jit(solution)/shard_map/ppermute | solution.py:1261
  145.2 6.4 %collective-permute-start.43 = (bf16[160,128]{1,0:T(8,128)(2,1)S(1)}, bf16[160,128]{1,0:T(8,128)(2,1)S(1)}, u32[]{:S(2)}, u32[]{:S(2)}) collective-permute-start(bf16[160,128]{1,0:T(8,128)(2,1)S(1)} %add_convert_fusion), channel_id=1, source_target_pairs={{0,4},{1,5},{2,6},{3,7},{4,0},{5,1},{6,2},{7,3},{8,12},{9,13},{10,... | collective-permute-start | bytes 122888 | tf_op jit(solution)/shard_map/ppermute | solution.py:1261
  145.2 6.4 %collective-permute-start.42 = (bf16[160,128]{1,0:T(8,128)(2,1)S(1)}, bf16[160,128]{1,0:T(8,128)(2,1)S(1)}, u32[]{:S(2)}, u32[]{:S(2)}) collective-permute-start(bf16[160,128]{1,0:T(8,128)(2,1)S(1)} %add_convert_fusion), channel_id=1, source_target_pairs={{0,2},{1,3},{2,0},{3,1},{4,6},{5,7},{6,4},{7,5},{8,10},{9,11},{10,... | collective-permute-start | bytes 122888 | tf_op jit(solution)/shard_map/ppermute | solution.py:1261
  149.2 7.7 %collective-permute-start.39 = (bf16[256,256]{1,0:T(8,128)(2,1)S(1)}, bf16[256,256]{1,0:T(8,128)(2,1)S(1)}, u32[]{:S(2)}, u32[]{:S(2)}) collective-permute-start(bf16[256,256]{1,0:T(8,128)(2,1)S(1)} %get-tuple-element.209), channel_id=1, source_target_pairs={{0,16},{8,24},{16,0},{24,8},{1,17},{9,25},{17,1},{25,9},{2,18},{10... | collective-permute-start | bytes 393224 | tf_op jit(solution)/shard_map/ppermute | solution.py:1261
  150.3 6.6 %collective-permute-start.40 = (bf16[256,256]{1,0:T(8,128)(2,1)S(1)}, bf16[256,256]{1,0:T(8,128)(2,1)S(1)}, u32[]{:S(2)}, u32[]{:S(2)}) collective-permute-start(bf16[256,256]{1,0:T(8,128)(2,1)S(1)} %get-tuple-element.210), channel_id=1, source_target_pairs={{0,24},{8,16},{16,8},{24,0},{1,25},{9,17},{17,9},{25,1},{2,26},{10... | collective-permute-start | bytes 393224 | tf_op jit(solution)/shard_map/ppermute | solution.py:1261
  (34 other events, 177.1 us)

commit v4 on v3

--- a/solution.py
+++ b/solution.py
@@ -14,7 +14,7 @@
 M = 32
 NJ = 32
 R = M * NJ
-CHUNK = 256
+CHUNK = 512
 UNROLL = 4
 COLS0 = 1024
 COLS1 = 1920
@@ -27,19 +27,25 @@
 
 
 class Far:
-    def __init__(self, array, columns=None):
-        self.array, self.columns = array, columns
+    def __init__(self, array, columns=None, parts=1):
+        self.array, self.columns, self.parts = array, columns, parts
 
 
 class Arriving:
-    def __init__(self, source, target, sem):
-        self.copy, self.target, self.waited = pltpu.make_async_copy(source, target, sem), target, False
-        self.copy.start()
-
-    def get(self):
-        if not self.waited:
-            self.copy.wait()
-            self.waited = True
+    def __init__(self, source, target, sems, parts=1):
+        self.target, self.waited, self.copies = target, 0, []
+        size = target.shape[0] // parts
+        for k in range(parts):
+            span = pl.ds(k * size, size)
+            here = (source, target) if parts == 1 else (source.at[span], target.at[span])
+            self.copies.append(pltpu.make_async_copy(*here, sems.at[k]))
+            self.copies[-1].start()
+
+    def get(self, part=None):
+        last = len(self.copies) if part is None else part + 1
+        for copy in self.copies[self.waited : last]:
+            copy.wait()
+        self.waited = max(self.waited, last)
         return self.target
 
 
@@ -62,14 +68,16 @@
 PARTS = 6
 
 
-def run(kernel, name, outs, args, scratch=(), flops=0, fetch=(), token=None):
+def run(kernel, name, outs, args, scratch=(), flops=0, fetch=(), store=(), token=None):
     n_args = len(args)
-    args = list(args) + list(fetch) + ([] if token is None else [token])
+    args = list(args) + list(fetch) + list(store) + ([] if token is None else [token])
     n_made = len(outs)
     outs = list(outs)
     for f in fetch:
         outs.append(((f.array.shape[0], f.columns or f.array.shape[1]) + f.array.shape[2:], f.array.dtype))
     arrays = [a.array if isinstance(a, Far) else a for a in args]
+    n_stored = len(outs)
+    outs += [(a.shape, a.dtype, True) for a in store]
     if token is not None:
         outs.append((token.shape, token.dtype))
     far_in = [k for k, a in enumerate(args[:n_args]) if isinstance(a, Far)]
@@ -95,12 +103,14 @@
             return ins[k] if args[k].columns is None else ins[k].at[:, 0 : args[k].columns]
 
         for i, k in enumerate(far_in):
-            ins[k] = Arriving(cut(k), targets[i], in_sems.at[i])
+            ins[k] = Arriving(cut(k), targets[i], in_sems.at[i], args[k].parts)
         fetched = [
             Arriving(cut(n_args + i), results[n_made + i], in_sems.at[len(far_in) + i]) for i in range(len(fetch))
         ]
         for i, k in enumerate(far_out):
             results[k] = Leaving(results[k], out_sems.at[i])
+        for i in range(len(store)):
+            results[n_stored + i].put(ins[n_args + len(fetch) + i])
         if token is not None:
             results[-1][...] = ins[-1][...]
         kernel(*ins[:n_args], *results[:n_made], *own)
@@ -129,7 +139,7 @@
         scratch_shapes=[pltpu.VMEM(s, d) for s, d in scratch]
         + landing
         + [
-            pltpu.SemaphoreType.DMA((max(1, len(far_in) + len(fetch)),)),
+            pltpu.SemaphoreType.DMA((max(1, len(far_in) + len(fetch)), PARTS)),
             pltpu.SemaphoreType.DMA((max(1, len(far_out)), PARTS)),
         ],
         compiler_params=pltpu.CompilerParams(vmem_limit_bytes=24 << 20),
@@ -165,14 +175,27 @@
     lax.fori_loop(0, count // step, body, 0)
 
 
+def put_all(stores):
+    for ref, span, at, value in stores:
+        ref[span, at] = value
+
+
 def for_blocks_rims(fn):
-    def body(j, carry):
-        fn(j, True, True)
+    group = 5
+
+    def several(first, count, has_prev, has_next):
+        stores = []
+        for i in range(count):
+            stores += fn(first + i, has_prev, has_next)
+        put_all(stores)
+
+    def body(g, carry):
+        several(group * g + 1, group, True, True)
         return carry
 
-    fn(0, False, True)
-    lax.fori_loop(1, NJ - 1, body, 0)
-    fn(NJ - 1, True, False)
+    several(0, 1, False, True)
+    lax.fori_loop(0, (NJ - 2) // group, body, 0)
+    several(NJ - 1, 1, True, False)
 
 
 def from_prev(value, rim, flag):
@@ -199,35 +222,31 @@
     return jnp.where(cond, 1.0, 0.0).astype(BF)
 
 
-def fill_rims(cat, parts, low, high):
+def fill_rims(cat, parts, low):
+    zero = jnp.zeros((M, L), BF)
+    cond = mask_bf(low) > 0.5
+
     def one(j, has_prev, has_next):
+        stores = []
         for target, after, before in parts:
-            value = None
-            if has_next:
-                value = cat[rows(j + 1), after : after + L] * low
-            if has_prev:
-                other = cat[rows(j - 1), before : before + L] * high
-                value = other if value is None else value + other
-            cat[rows(j), target : target + L] = value
+            value = cat[rows(j + 1), after : after + L] if has_next else zero
+            other = cat[rows(j - 1), before : before + L] if has_prev else zero
+            stores.append((cat, rows(j), slice(target, target + L), jnp.where(cond, value, other)))
+        return stores
 
     for_blocks_rims(one)
 
 
 def rims_1(cat, groups):
-    at = lane((M, L))
-    parts = [(rim, base, base + L) for base, rim, _ in groups]
-    fill_rims(cat, parts, mask_bf(at < 32), mask_bf(at >= 112))
+    fill_rims(cat, [(rim, base, base + L) for base, rim, _ in groups], lane((M, L)) < 32)
 
 
 def rims_2(cat):
-    at = lane((M, L))
-    parts = [(768 + L * k, 256 * k, 256 * k + L) for k in range(3)]
-    fill_rims(cat, parts, mask_bf(at < 32), mask_bf(at >= 96))
+    fill_rims(cat, [(768 + L * k, 256 * k, 256 * k + L) for k in range(3)], lane((M, L)) < 32)
 
 
 def rims_0(cat):
-    at = lane((M, L)) % 32
-    fill_rims(cat, [(512 + L * k, L * k, L * k) for k in range(4)], mask_bf(at < 2), mask_bf(at == 31))
+    fill_rims(cat, [(512 + L * k, L * k, L * k) for k in range(4)], lane((M, L)) % 32 < 2)
 
 
 def matmul(left, right, transposed=False):
@@ -247,6 +266,31 @@
         return carry
 
     lax.fori_loop(0, R // size, body, 0)
+
+
+def product_sums(cat, weights, transposed, use, done=None, size=256):
+    sums = (jnp.zeros((8, L), F32), jnp.zeros((8, L), F32))
+
+    def part(r, sums):
+        rs = rows(r, size)
+        value = matmul(cat[rs, :], weights[...], transposed)
+        for i in range(size // M):
+            for k, at in enumerate(tiles(value.shape[1])):
+                if k % 4 == 0:
+                    stores = []
+                sums = use(r * (size // M) + i, k, at, value[M * i : M * i + M, at], *sums, stores)
+                if k % 4 == 3 or k == value.shape[1] // L - 1:
+                    put_all(stores)
+        if done is not None:
+            done(rs)
+        return sums
+
+    if done is None:
+        sums = lax.fori_loop(0, R // size, part, sums)
+    else:
+        for r in range(R // size):
+            sums = part(r, sums)
+    return [total_rows(v) for v in sums]
 
 
 def sum8(value):
@@ -458,24 +502,19 @@
     matrix_1_up(w1d.at[1], t, COLS1B)
 
 
-def window_swap(spare, out):
-    out[...] = spare[...]
+def window_swap(w2d, out, t, w):
+    matrix_2_down(w2d, t, w)
+    out.put(t)
 
 
 def correlate(coarse, fine, d):
-    def part(rs, first):
+    for k in range(R // CHUNK):
+        span = slice(CHUNK * k, CHUNK * k + CHUNK)
+        left, right = ready(coarse, k), ready(fine, k)
         value = lax.dot_general(
-            coarse[rs, :], fine[rs, :], (((0,), (0,)), ((), ())), preferred_element_type=F32
+            left[span, :], right[span, :], (((0,), (0,)), ((), ())), preferred_element_type=F32
         )
-        d[...] = value if first else d[...] + value
-
-    part(pl.ds(0, CHUNK), True)
-
-    def body(r, carry):
-        part(pl.ds(pl.multiple_of(r * CHUNK, CHUNK), CHUNK), False)
-        return carry
-
-    lax.fori_loop(1, R // CHUNK, body, 0)
+        d[...] = value if k == 0 else d[...] + value
 
 
 def weight_2(d, out):
@@ -523,52 +562,52 @@
     out[start : start + 16, :] = result
 
 
-def window_4(low, act, fine, w2d, t, out, d, w, kept):
-    matrix_2_down(w2d, t, w)
-    correlate(ready(low), ready(fine), d)
+def window_4(low, act, fine, out, d, kept):
+    correlate(low, fine, d)
     weight_1(d, kept, 0)
-    correlate(ready(act), ready(fine), d)
+    correlate(act, fine, d)
     weight_1(d, kept, 16)
     out.put(kept)
 
 
 def window_5(coarse, fine, w2c, t, out, d, w, kept):
     matrix_2_up(w2c, t, w)
-    correlate(ready(coarse), ready(fine), d)
+    correlate(coarse, fine, d)
     weight_2(d, kept)
     out.put(kept)
 
 
-def window_6(coarse, fine, w1c, t, out, d, kept):
+HALF = 144
+
+
+def window_6(index, coarse, fine, w1c, w1d, w2d, t, keep, give, d, kept):
     matrix_1_up(w1c, t, 0)
-    correlate(ready(coarse), ready(fine), d)
+    correlate(coarse, fine, d)
     weight_2(d, kept)
-    out.put(kept)
-
-
-HALF = 160
-
-
-def window_7(index, coarse, fine, bias, w1d, w2d, w2c, keep, give, d, first):
-    correlate(ready(coarse), ready(fine), d)
-    weight_1(d, first, 0)
     even = index[1] == 0
-    up_two, up_one, down_two = ready(w2d), ready(w1d), ready(w2c)
-    spare = jnp.zeros((8, L), F32)
+    up_two, up_one = ready(w2d), ready(w1d)
 
     def place(span, a, b):
         keep[span, :] = jnp.where(even, a, b)
         give[span, :] = jnp.where(even, b, a)
 
-    place(slice(0, 128), up_two[...], down_two[...])
-    place(slice(128, 144), up_one[0:16, :], first[...])
-    place(slice(144, 160), up_one[16:32, :], jnp.concatenate([bias[...], spare]))
+    place(slice(0, 128), up_two[...], kept[...])
+    place(slice(128, 144), up_one[0:16, :], up_one[16:32, :])
+
+
+def window_7(coarse, fine, keep, got, bias, low, d, first):
+    correlate(coarse, fine, d)
+    weight_1(d, first, 0)
+    low[0:HALF, :] = (keep[...] + got[...]).astype(BF)
+    low[HALF : HALF + 16, :] = first[...].astype(BF)
+    low[HALF + 16 : HALF + 32, :] = jnp.concatenate([bias[...], jnp.zeros((8, L), F32)]).astype(BF)
 
 
 def unpack_kernel(index, mine, other, w1c, w2c, w2d, w1d, bias):
     even = index[1] == 0
     a, b = mine[...], other[...]
     up, down = jnp.where(even, a, b), jnp.where(even, b, a)
+    own = a[HALF:] + b[HALF:]
     for half, out in ((up, w2d), (down, w2c)):
         turned = half[0:128].T
         moved = [turned] + [pltpu.roll(turned, L - 32 * tap, 1) for tap in range(1, 4)]
@@ -579,7 +618,7 @@
                 else:
                     value = moved[b // 3][80 + 16 * (b % 3) : 96 + 16 * (b % 3)]
                 out[tap * TAPS + b] = value[:, 0:32]
-    tall = jnp.concatenate([up[128:160], down[128:144], jnp.zeros((80, L), F32)]).T
+    tall = jnp.concatenate([up[128:144], down[128:144], own[0:16], jnp.zeros((80, L), F32)]).T
     other_tall = pltpu.roll(tall, L - 32, 1)
     for tap in range(TAPS):
         for b in range(TAPS):
@@ -587,7 +626,7 @@
                 row = (tap + 1) % 2 * 64 + c * 32 + (tap + 1) // 2 * 8 + b
                 w1d[tap * TAPS + b, c : c + 1, :] = tall[row : row + 1, 0:32]
                 w1c[tap * TAPS + b, c : c + 1, :] = other_tall[row : row + 1, 0:16]
-    total = total_rows(down[144:152])
+    total = total_rows(own[16:24])
     total = jnp.broadcast_to(total, (8, L))
     total = total + pltpu.roll(total, 64, 1)
     for step in (16, 8, 4, 2, 1):
@@ -595,8 +634,8 @@
     bias[...] = jnp.where(lane((8, L)) == 0, total, pltpu.roll(total, L - 31, 1))
 
 
-def ready(ref):
-    return ref.get() if isinstance(ref, Arriving) else ref
+def ready(ref, part=None):
+    return ref.get(part) if isinstance(ref, Arriving) else ref
 
 
 def spread(scr, store):
@@ -625,7 +664,7 @@
             scr[k % 2, pl.ds(2 * half + k // 2, M, stride=4), :] = value
 
 
-def layout_kernel(index, frame_mask, mix, cot, cross, core, xf, x0, c0, scr, wide, cf, ends):
+def layout_kernel(index, frame_mask, mix, cot, cross, core, x0, c0, scr, wide, ends):
     def place(out, block, row):
         def store(k, half, value):
             at = slice(L * half, L * half + L)
@@ -639,10 +678,9 @@
     def mix_tile(t):
         for c in range(2):
             scr[c] = m[c, :, pl.ds(pl.multiple_of(t * L, L), L)].astype(F32)
-        spread(scr, place(xf, 4 * t, 4 * t))
+        spread(scr, place(x0, 4 * t, 4 * t))
 
     for_blocks(mix_tile, NJ // 4)
-    x0.put(xf)
     g = cot.get()
     per_stem = g.shape[3] // L
 
@@ -650,10 +688,9 @@
         for c in range(2):
             lanes = pl.ds(pl.multiple_of((t % per_stem) * L, L), L)
             scr[c] = g[t // per_stem, c, :, lanes].astype(F32)
-        spread(scr, place(cf, 4 * t, NJ + 4 * t))
+        spread(scr, place(c0, 4 * t, NJ + 4 * t))
 
     for_blocks(cot_tile, NJ // 4)
-    c0.put(cf)
     ends[...] = jnp.zeros(ends.shape, F32)
     pack_ends(wide, index, ends.at[0], ends.at[1], 2 * NJ)
     even = index[1] == 0
@@ -679,15 +716,17 @@
 
         def one(i, which=which, first=first):
             j = first + i
+            span, stores = rows(j), []
             for half in range(2):
                 value = read(which, j, half)
-                cat[rows(j), L * half : L * half + L] = value.astype(BF)
+                stores.append((cat, span, slice(L * half, L * half + L), value.astype(BF)))
                 if half == 1:
                     moved = from_prev(value, left[rows(j, 8), L : 2 * L], a)
-                    cat[rows(j), 256:384] = moved.astype(BF)
+                    stores.append((cat, span, slice(256, 384), moved.astype(BF)))
                 else:
                     moved = from_next(value, right[rows(j, 8), 0:L], a_next)
-                    cat[rows(j), 384:512] = moved.astype(BF)
+                    stores.append((cat, span, slice(384, 512), moved.astype(BF)))
+            put_all(stores)
 
         for_blocks(one, count)
     rims_0(cat)
@@ -695,7 +734,7 @@
 
 def conv_one_kernel(
     index, x0, cross_in, core_in, aux, t,
-    cross, core, mom, kept, hxfar, zfar, catfar, z, hx, cat, lf, rf, lw, rw,
+    cross, core, mom, kept, hx, cat, zfar, z, lf, rf, lw, rw,
 ):
     even = index[1] == 0
     a, b = cross_in[...].astype(F32), core_in[...].astype(F32)
@@ -703,7 +742,6 @@
     rf[...] = jnp.where(even, b, a)
     hx[:, 0:L] = rf[0 : 2 * NJ, 0:L]
     hx[:, L : 2 * L] = lf[0 : 2 * NJ, L : 2 * L]
-    hxfar.put(hx)
     kept[...] = jnp.zeros(kept.shape, F32)
     kept[0:3, :] = lf[2 * NJ : 2 * NJ + 3, 0:L]
     kept[3:6, :] = rf[2 * NJ : 2 * NJ + 3, 0:L]
@@ -712,25 +750,16 @@
     x = ready(x0)
     read = lambda which, j, h: x[rows(j), L * h : L * h + L].astype(F32)
     columns_0(cat, [(0, NJ)], read, lw, rw, aux)
-    catfar.put(cat)
     weights = ready(t)
 
-    def chunk(rs):
-        z[rs, :] = matmul(cat[rs, :], weights[...])
-        zfar.put(z, (rs, slice(None)))
-
-    quarters(chunk)
+    def use(j, k, at, value, s1, s2, stores):
+        stores.append((z, rows(j), at, value))
+        part = value * aux[2 + k // 2]
+        return s1 + sum8(part), s2 + sum8(part * value)
+
+    stats = product_sums(cat, weights, False, use, lambda rs: zfar.put(z, (rs, slice(None))))
     pack_ends(z, index, cross, core)
-
-    def sums(j, s1, s2):
-        for k, at in enumerate(tiles(512)):
-            value = z[rows(j), at]
-            part = value * aux[2 + k // 2]
-            s1 = s1 + sum8(part)
-            s2 = s2 + sum8(part * value)
-        return s1, s2
-
-    stats = fold(stack_rows(sum_blocks(sums)), 16)
+    stats = fold(stack_rows(stats), 16)
     at = sub((8, L))
     stats = jnp.where(at == 2, total_rows(aux[2] + aux[3]) * (NJ * 16.0), stats)
     stats = jnp.where(at == 3, total_rows(aux[4]) * (NJ * 8.0), stats)
@@ -739,7 +768,7 @@
 
 def conv_two_kernel(
     index, z1, cross_in, core_in, mom1, prm, aux, t,
-    cross, core, mom, ends, h1, zfar, catfar, z2, cat, ef, eb, hf, lw, rw,
+    cross, core, mom, eb, hf, zfar, catfar, z2, cat, ef, lw, rw,
 ):
     mean, scale = norm_terms(mom1, mom1[2:3])
     gain, shift = prm[0:1], prm[1:2]
@@ -754,20 +783,21 @@
         hf[1, :, at] = right
         ef[0, :, at] = act(left)
         ef[1, :, at] = act(right)
-    h1.put(hf)
     widen(ef.at[0], lw)
     widen(ef.at[1], rw)
 
     def one(j):
+        span, stores = rows(j), []
         for k, at in enumerate(tiles(512)):
-            value = act(z1[rows(j), at])
-            cat[rows(j), at] = value.astype(BF)
+            value = act(z1[span, at])
+            stores.append((cat, span, at, value.astype(BF)))
             if k >= 2:
                 moved = from_prev(value, lw[rows(j, 8), at], a)
-                cat[rows(j), 256 + L * k : 384 + L * k] = moved.astype(BF)
+                stores.append((cat, span, slice(256 + L * k, 384 + L * k), moved.astype(BF)))
             start = 768 + L * k if k < 2 else 1280 + L * k
             moved = from_next(value, rw[rows(j, 8), at], a_next)
-            cat[rows(j), start : start + L] = moved.astype(BF)
+            stores.append((cat, span, slice(start, start + L), moved.astype(BF)))
+        put_all(stores)
 
     for_blocks(one)
     catfar.put(cat, (slice(None), slice(0, 1024)))
@@ -781,38 +811,31 @@
 
     end_rows(z1, group_out)
     eb[...] = ef[...].astype(BF)
-    ends.put(eb)
     weights = ready(t)
 
-    def chunk(rs):
-        z2[rs, :] = matmul(cat[rs, :], weights[...])
-        zfar.put(z2, (rs, slice(None)))
-
-    quarters(chunk)
+    def use(j, k, at, value, s1, s2, stores):
+        stores.append((z2, rows(j), at, value))
+        part = value * aux[4]
+        return s1 + sum8(part), s2 + sum8(part * value)
+
+    stats = product_sums(cat, weights, False, use, lambda rs: zfar.put(z2, (rs, slice(None))))
     pack_ends(z2, index, cross, core)
-
-    def sums(j, s1, s2):
-        for at in tiles(256):
-            value = z2[rows(j), at]
-            part = value * aux[4]
-            s1 = s1 + sum8(part)
-            s2 = s2 + sum8(part * value)
-        return s1, s2
-
-    pack_moments(mom, cross, fold(stack_rows(sum_blocks(sums)), 32))
+    pack_moments(mom, cross, fold(stack_rows(stats), 32))
 
 
 def columns_2(cat, read, left, right, aux):
     a, a_next = aux[0], aux[1]
 
     def one(j):
+        span, stores = rows(j), []
         for k, at in enumerate(tiles(256)):
             value = read(j, at)
-            cat[rows(j), at] = value.astype(BF)
+            stores.append((cat, span, at, value.astype(BF)))
             moved = from_prev(value, left[rows(j, 8), at], a)
-            cat[rows(j), 256 + L * k : 384 + L * k] = moved.astype(BF)
+            stores.append((cat, span, slice(256 + L * k, 384 + L * k), moved.astype(BF)))
             moved = from_next(value, right[rows(j, 8), at], a_next)
-            cat[rows(j), 512 + L * k : 640 + L * k] = moved.astype(BF)
+            stores.append((cat, span, slice(512 + L * k, 640 + L * k), moved.astype(BF)))
+        put_all(stores)
 
     for_blocks(one)
     rims_2(cat)
@@ -820,7 +843,7 @@
 
 def up_two_kernel(
     index, z2, cross_in, core_in, mom1, mom2, prm, aux, t,
-    cross, core, mom, h2, act2, rectfar, rect, cat, hf, lf, rf, lw, rw,
+    cross, core, mom, hf, act2, rectfar, rect, cat, lf, rf, lw, rw,
 ):
     mean, scale = norm_terms(mom2, mom1[3:4])
     gain, shift, bias = prm[2:3], prm[3:4], prm[6:7]
@@ -834,29 +857,19 @@
         hf[1, :, at] = right
         lf[:, at] = act(left)
         rf[:, at] = act(right)
-    h2.put(hf)
     widen(lf, lw)
     widen(rf, rw)
     columns_2(cat, lambda j, at: act(z2[rows(j), at]), lw, rw, aux)
-    act2.put(cat.at[:, 0:256])
+    act2[...] = cat[:, 0:256]
     weights = ready(t)
 
-    def chunk(rs):
-        rect[rs, :] = matmul(cat[rs, :], weights[...], True)
-
-    for_chunks(chunk)
-
-    def sums(j, s1, s2):
-        for k, at in enumerate(tiles(512)):
-            value = softplus(rect[rows(j), at] + bias)
-            rect[rows(j), at] = value
-            part = value * aux[2 + k // 2]
-            s1 = s1 + sum8(part)
-            s2 = s2 + sum8(part * value)
-        return s1, s2
-
-    stats = sum_blocks(sums)
-    rectfar.put(rect)
+    def use(j, k, at, value, s1, s2, stores):
+        value = softplus(value + bias)
+        stores.append((rect, rows(j), at, value))
+        part = value * aux[2 + k // 2]
+        return s1 + sum8(part), s2 + sum8(part * value)
+
+    stats = product_sums(cat, weights, True, use, lambda rs: rectfar.put(rect, (rs, slice(None))))
     pack_moments(mom, cross, fold(stack_rows(stats), 16))
     pack_ends(rect, index, cross, core)
 
@@ -865,15 +878,17 @@
     a, a_next = aux[0], aux[1]
 
     def one(j):
+        span, stores = rows(j), []
         for k, at in enumerate(tiles(512)):
             value = read(j, k, at)
-            cat[rows(j), at] = value.astype(BF)
+            stores.append((cat, span, at, value.astype(BF)))
             if k >= 2:
                 moved = from_prev(value, left[rows(j, 8), at], a)
-                cat[rows(j), 256 + L * k : 384 + L * k] = moved.astype(BF)
+                stores.append((cat, span, slice(256 + L * k, 384 + L * k), moved.astype(BF)))
             else:
                 moved = from_next(value, right[rows(j, 8), at], a_next)
-                cat[rows(j), 768 + L * k : 896 + L * k] = moved.astype(BF)
+                stores.append((cat, span, slice(768 + L * k, 896 + L * k), moved.astype(BF)))
+        put_all(stores)
 
     for_blocks(one)
     rims_1(cat, GROUPS1[:4])
@@ -898,7 +913,7 @@
 
 def up_one_kernel(
     index, rect, cross_in, core_in, mom1, mom3, prm, aux, ends1, cat1, t,
-    m0, m1, m2, m3, h3, low3, sig, sigh, cat, hf, lf, rf, ef, ff, sf, shf, lw, rw,
+    m0, m1, m2, m3, hf, low3, sf, shf, cat, lf, rf, ef, ff, lw, rw,
 ):
     mean, scale = norm_terms(mom3, mom1[2:3])
     gain, shift, bias = prm[4:5], prm[5:6], prm[7:8]
@@ -912,11 +927,10 @@
         hf[1, :, at] = right
         lf[:, at] = norm(left)
         rf[:, at] = norm(right)
-    h3.put(hf)
     widen(lf, lw)
     widen(rf, rw)
     columns_1b(cat, lambda j, k, at: norm(rect[rows(j), at]), lw, rw, aux)
-    low3.put(cat.at[:, 0:512])
+    low3[...] = cat[:, 0:512]
 
     def group_out(rs, at, top, low):
         ef[0, rs, at] = norm(top)
@@ -938,11 +952,11 @@
         ),
     ]
     weights, other = ready(t), ready(cat1)
+    value = matmul(jnp.concatenate([e[0] for e in edges]), weights[:, 0:COLS1B], True)
+    value = value + matmul(jnp.concatenate([e[1] for e in edges]), weights[:, COLS1B : 2 * COLS1B], True)
     for k, half in ((0, 1), (1, 0)):
-        value = matmul(edges[k][0], weights[:, 0:COLS1B], True)
-        value = value + matmul(edges[k][1], weights[:, COLS1B : 2 * COLS1B], True)
-        shf[:, L * half : L * half + L] = sigmoid(value[:, L * half : L * half + L] + bias)
-    sigh.put(shf)
+        at = slice(L * half, L * half + L)
+        shf[:, at] = sigmoid(value[NJ * k : NJ * k + NJ, at] + bias)
     masks = (m0, m1, m2, m3)
     per = R // len(masks)
     for mask, (first, count) in zip(masks, quarter_blocks(index, len(masks))):
@@ -955,7 +969,6 @@
         ff[...] = jnp.zeros(ff.shape, F32)
         ff[0:count, :] = shf[rows(lax.div(first, count), count), :]
         mask[per : per + 16, :] = ff[...].astype(BF)
-    sig.put(sf)
 
 
 def ratio_terms(masks):
@@ -976,7 +989,7 @@
     return [m * common * (c - direct) for m, c in zip(masks, cots)], direct
 
 
-def mask_kernel(index, m0, m1, m2, m3, c0, x0, hx, g0, g1, g2, g3, direct, df, ff):
+def mask_kernel(index, m0, m1, m2, m3, c0, x0, hx, g0, g1, g2, g3, df, ff):
     masks, grads = (m0, m1, m2, m3), (g0, g1, g2, g3)
     stems = len(masks)
     per, blocks = R // stems, NJ // stems
@@ -994,7 +1007,6 @@
                 grads[s][rows(j), at] = values[s].astype(BF)
 
     for_blocks(one, blocks)
-    direct.put(df)
     m = [masks[s][per : per + 16, :].astype(F32)[0:blocks] for s in range(stems)]
     c = [rim[rows(stems + (mine ^ s), blocks), :] for s in range(stems)]
     values, _ = mask_back(m, c, rim[rows(mine, blocks), :])
@@ -1033,7 +1045,7 @@
 
 def down_one_back_kernel(
     index, q0, q1, q2, q3, sigh, sig, aux, mom1, mom3, rect, t,
-    g3, cat, cross, core, mom, bias, gact, gf, hf, zf, hw,
+    g3, cat, cross, core, mom, bias, gf, hf, zf, hw,
 ):
     grads = (q0, q1, q2, q3)
     blocks = quarter_blocks(index, len(grads))
@@ -1059,25 +1071,18 @@
     bias[...] = zf[...]
     weights = ready(t)
 
-    def chunk(rs):
-        value = matmul(cat[rs, :], weights[...])
-        g3[rs, :] = value[:, 0:512]
-        gf[rs, :] = value[:, 512:1024]
-        gact.put(gf, (rs, slice(None)))
-
-    quarters(chunk)
     mean, scale = norm_terms(mom3, mom1[2:3])
+    r = ready(rect)
+
+    def use(j, k, at, value, s1, s2, stores):
+        if k >= 4:
+            stores.append((gf, rows(j), slice(L * k - 512, L * k - 384), value))
+            return s1, s2
+        stores.append((g3, rows(j), at, value))
+        return s1 + sum8(value), s2 + sum8(value * (r[rows(j), at] - mean))
+
+    s1, s2 = product_sums(cat, weights, False, use)
     pack_ends(g3, index, cross, core)
-    r = ready(rect)
-
-    def sums(j, s1, s2):
-        for at in tiles(512):
-            value = g3[rows(j), at]
-            s1 = s1 + sum8(value)
-            s2 = s2 + sum8(value * (r[rows(j), at] - mean))
-        return s1, s2
-
-    s1, s2 = sum_blocks(sums)
     pack_moments(mom, cross, fold(stack_rows([s1, s2 * scale]), 16))
 
 
@@ -1110,16 +1115,18 @@
     a, a_next = aux[0], aux[1]
 
     def one(j, total):
+        span, stores = rows(j), []
         for k, at in enumerate(tiles(512)):
-            value = back(g3[rows(j), at], r[rows(j), at], aux[2 + k // 2])
+            value = back(g3[span, at], r[span, at], aux[2 + k // 2])
             total = total + sum8(value)
-            cat[rows(j), at] = value.astype(BF)
+            stores.append((cat, span, at, value.astype(BF)))
             if k >= 2:
                 moved = from_prev(value, lw[rows(j, 8), at], a)
-                cat[rows(j), 256 + L * k : 384 + L * k] = moved.astype(BF)
+                stores.append((cat, span, slice(256 + L * k, 384 + L * k), moved.astype(BF)))
             start = 768 + L * k if k < 2 else 1280 + L * k
             moved = from_next(value, rw[rows(j, 8), at], a_next)
-            cat[rows(j), start : start + L] = moved.astype(BF)
+            stores.append((cat, span, slice(start, start + L), moved.astype(BF)))
+        put_all(stores)
         return total
 
     def four(j, total):
@@ -1131,24 +1138,17 @@
     rims_1(cat, GROUPS1)
     weights = ready(t)
 
-    def chunk(rs):
-        g2[rs, :] = matmul(cat[rs, :], weights[...])
-
-    for_chunks(chunk)
     mean2, scale2 = norm_terms(mom2, mom1[3:4])
     gain, shift = prm[2:3], prm[3:4]
     z = ready(z2)
 
-    def sums(j, s1, s2):
-        for at in tiles(256):
-            xhat = (z[rows(j), at] - mean2) * scale2
-            value = g2[rows(j), at] * silu_slope(xhat * gain + shift)
-            g2[rows(j), at] = value
-            s1 = s1 + sum8(value)
-            s2 = s2 + sum8(value * xhat)
-        return s1, s2
-
-    stats = fold(stack_rows(sum_blocks(sums)), 32)
+    def use(j, k, at, value, s1, s2, stores):
+        xhat = (z[rows(j), at] - mean2) * scale2
+        value = value * silu_slope(xhat * gain + shift)
+        stores.append((g2, rows(j), at, value))
+        return s1 + sum8(value), s2 + sum8(value * xhat)
+
+    stats = fold(stack_rows(product_sums(cat, weights, False, use)), 32)
     pack_ends(g2, index, cross, core)
     bias = fold(stack_rows([total_rows(bias)] * 3), 16)
     pack_moments(mom, cross, jnp.where(sub((8, L)) == 2, bias, stats))
@@ -1178,24 +1178,17 @@
     low2[...] = cat[:, 0:256]
     weights, added = ready(t), ready(gact)
 
-    def chunk(rs):
-        g1[rs, :] = matmul(cat[rs, :], weights[...], True) + added[rs, :]
-
-    for_chunks(chunk)
     mean1, scale1 = norm_terms(mom1, mom1[2:3])
     gain, shift = prm[0:1], prm[1:2]
     z = ready(z1)
 
-    def sums(j, s1, s2):
-        for at in tiles(512):
-            xhat = (z[rows(j), at] - mean1) * scale1
-            value = g1[rows(j), at] * silu_slope(xhat * gain + shift)
-            g1[rows(j), at] = value
-            s1 = s1 + sum8(value)
-            s2 = s2 + sum8(value * xhat)
-        return s1, s2
-
-    stats = fold(stack_rows(sum_blocks(sums)), 16)
+    def use(j, k, at, value, s1, s2, stores):
+        xhat = (z[rows(j), at] - mean1) * scale1
+        value = (value + added[rows(j), at]) * silu_slope(xhat * gain + shift)
+        stores.append((g1, rows(j), at, value))
+        return s1 + sum8(value), s2 + sum8(value * xhat)
+
+    stats = fold(stack_rows(product_sums(cat, weights, True, use)), 16)
     pack_ends(g1, index, cross, core)
     pack_moments(mom, cross, stats)
 
@@ -1275,19 +1268,19 @@
     return values
 
 
-def sum_halves(keep, give, axis):
+def sum_chips(low, axis, beside):
     count = lax.axis_size(axis)
-    mine = keep + flip(give, axis, 1)
     if count == 8:
-        low = mine.astype(BF)
         moved = [flip(low, axis, bit) for bit in (2, 4, 6)]
+        made, low = beside(low)
         mine = low.astype(F32) + moved[0].astype(F32) + moved[1].astype(F32) + moved[2].astype(F32)
     else:
-        step = 2
+        made, low = beside(low)
+        mine, step = low.astype(F32), 2
         while step < count:
             mine = mine + flip(mine, axis, step)
             step *= 2
-    return mine, flip(mine, axis, 1)
+    return mine, flip(mine, axis, 1), made
 
 
 def exchange(cross, core, mom, axis, beside):
@@ -1378,55 +1371,67 @@
     def far(*shape, kind=F32):
         return [(shape, kind, True)]
 
-    cross, core, x0, x0_far, c0 = run(
+    cross, core, x0, c0 = run(
         layout_kernel,
         "layout",
-        [((edge, 256), BF), ((edge, 256), BF), ((R, 256), BF)] + far(R, 256, kind=BF) + far(R, 256, kind=BF),
+        [((edge, 256), BF), ((edge, 256), BF), ((R, 256), BF), ((R, 256), BF)],
         [index, frame_mask, Far(mixture), Far(cotangent)],
-        [((2, frames, L), F32), ((2 * R, 256), F32), ((R, 256), BF), ((2, edge, 256), F32)],
+        [((2, frames, L), F32), ((2 * R, 256), F32), ((2, edge, 256), F32)],
     )
     near = lax.ppermute(cross, "tm", pairs(lax.axis_size("tm"), -1))
     inside = flip(core, "tm", 1)
-    (t,) = run(window_0, "window_0", [((COLS0, 512), BF)], [w1c])
-    cross, core, mom, kept, hx, z1, cat0 = run(
+    t, x0_far, c0 = run(window_0, "window_0", [((COLS0, 512), BF)], [w1c], store=[x0, c0])
+    cross, core, mom, kept, hx, cat0, z1 = run(
         conv_one_kernel,
         "conv_one",
-        packet(512) + [((8, L), F32)] + far(2 * NJ, 256) + far(R, 512) + far(R, COLS0, kind=BF),
+        packet(512) + [((8, L), F32), ((2 * NJ, 256), F32), ((R, COLS0), BF)] + far(R, 512),
         [index, x0, near, inside, aux, t],
-        [((R, 512), F32), ((2 * NJ, 256), F32), ((R, COLS0), BF), ((edge, 256), F32), ((edge, 256), F32)]
-        + wide(256),
+        [((R, 512), F32), ((edge, 256), F32), ((edge, 256), F32)] + wide(256),
         flops=2 * R * COLS0 * 512,
     )
-    near, inside, mom1, (t, z1_here) = exchange(
+    near, inside, mom1, (t, z1_here, hx, cat0) = exchange(
         cross, core, mom, "tm",
         lambda token: run(
-            window_1, "window_1", [((COLS1, 256), BF)], [w2c], [((400, L), F32)], fetch=[Far(z1)], token=token
+            window_1,
+            "window_1",
+            [((COLS1, 256), BF)],
+            [w2c],
+            [((400, L), F32)],
+            fetch=[Far(z1)],
+            store=[hx, cat0],
+            token=token,
         ),
     )
     cross, core, mom, ends1, h1, z2, cat1 = run(
         conv_two_kernel,
         "conv_two",
-        packet(256) + far(4, NJ, 512, kind=BF) + far(2, NJ, 512) + far(R, 256) + far(R, COLS1, kind=BF),
+        packet(256) + [((4, NJ, 512), BF), ((2, NJ, 512), F32)] + far(R, 256) + far(R, COLS1, kind=BF),
         [index, z1_here, near, inside, mom1, prm, aux, t],
-        [((R, 256), F32), ((R, COLS1), BF), ((4, NJ, 512), F32), ((4, NJ, 512), BF), ((2, NJ, 512), F32)]
-        + wide(512),
+        [((R, 256), F32), ((R, COLS1), BF), ((4, NJ, 512), F32)] + wide(512),
         flops=2 * R * COLS1 * 256,
     )
-    near, inside, mom2, (t, z2_here) = exchange(
+    near, inside, mom2, (t, z2_here, ends1, h1) = exchange(
         cross, core, mom, "tm",
         lambda token: run(
-            window_2, "window_2", [((512, COLS2), BF)], [w2d], [((400, L), F32)], fetch=[Far(z2)], token=token
+            window_2,
+            "window_2",
+            [((512, COLS2), BF)],
+            [w2d],
+            [((400, L), F32)],
+            fetch=[Far(z2)],
+            store=[ends1, h1],
+            token=token,
         ),
     )
     cross, core, mom, h2, act2, rect = run(
         up_two_kernel,
         "up_two",
-        packet(512) + far(2, NJ, 256) + far(R, 256, kind=BF) + far(R, 512),
+        packet(512) + [((2, NJ, 256), F32), ((R, 256), BF)] + far(R, 512),
         [index, z2_here, near, inside, mom1, mom2, prm, aux, t],
-        [((R, 512), F32), ((R, COLS2), BF), ((2, NJ, 256), F32)] + rim(256) + wide(256),
+        [((R, 512), F32), ((R, COLS2), BF)] + rim(256) + wide(256),
         flops=2 * R * COLS2 * 512,
     )
-    near, inside, mom3, (t, rect_here, cat1_here, ends1_here) = exchange(
+    near, inside, mom3, (t, rect_here, cat1_here, ends1_here, h2, act2) = exchange(
         cross, core, mom, "tm",
         lambda token: run(
             window_3,
@@ -1434,6 +1439,7 @@
             [((256, 2 * COLS1B), BF)],
             [w1d],
             fetch=[Far(rect), Far(cat1, COLS1B), Far(ends1)],
+            store=[h2, act2],
             token=token,
         ),
     )
@@ -1441,50 +1447,57 @@
         up_one_kernel,
         "up_one",
         [((per + 16, 256), BF)] * stems
-        + far(2, NJ, 512) + far(R, 512, kind=BF) + far(R, 256) + far(NJ, 256),
+        + [((2, NJ, 512), F32), ((R, 512), BF), ((R, 256), F32), ((NJ, 256), F32)],
         [index, rect_here, near, inside, mom1, mom3, prm, aux, ends1_here, cat1_here, t],
-        [((R, COLS1B), BF), ((2, NJ, 512), F32)] + rim(512)
-        + [((2, NJ, 512), F32), ((16, 256), F32), ((R, 256), F32), ((NJ, 256), F32)] + wide(512),
+        [((R, COLS1B), BF)] + rim(512) + [((2, NJ, 512), F32), ((16, 256), F32)] + wide(512),
         flops=2 * R * 2 * COLS1B * 256,
     )
-    _, c0_here, x0_here, hx_here = run(
-        window_swap, "window_swap", [((8, L), F32)], [mom3], fetch=[Far(c0), Far(x0_far), Far(hx)]
+    t2a_d, c0_here, x0_here, hx_here, h3, low3, sig, sigh = run(
+        window_swap,
+        "window_swap",
+        far(COLS1, 256, kind=BF),
+        [w2d],
+        [((COLS1, 256), BF), ((400, L), F32)],
+        fetch=[Far(c0), Far(x0_far), Far(hx)],
+        store=[h3, low3, sig, sigh],
     )
     masks = swap(masks, "stem")
     *grads, direct = run(
         mask_kernel,
         "mask",
-        [((per + 16, 256), BF)] * stems + far(per, 256),
+        [((per + 16, 256), BF)] * stems + [((per, 256), F32)],
         [index, *masks, c0_here, x0_here, hx_here],
-        [((per, 256), F32), ((16, 256), F32)],
+        [((16, 256), F32)],
     )
     grads = swap(grads, "stem")
-    estimates, t, sig_here, sigh_here, rect_here = run(
+    estimates, t, sig_here, sigh_here, rect_here, direct = run(
         estimate_kernel,
         "estimate",
         [((stems, 2, frames, blocks * 32), BF), ((COLS0, 1024), BF)],
         [index, *masks, Far(x0_far), w1d],
         [((2, frames, L), F32), ((stems, per, 256), F32)],
         fetch=[Far(sig), Far(sigh), Far(rect)],
+        store=[direct],
     )
     g3, cat0g, cross, core, mom, bias_one, gact = run(
         down_one_back_kernel,
         "down_one_back",
-        [((R, 512), F32), ((R, COLS0), BF)] + packet(512) + [((8, L), F32)] + far(R, 512),
+        [((R, 512), F32), ((R, COLS0), BF)] + packet(512) + [((8, L), F32), ((R, 512), F32)],
         [index, *grads, sigh_here, sig_here, aux, mom1, mom3, rect_here, t],
-        [((R, 512), F32), ((NJ, 256), F32), ((8, L), F32), ((8 * NJ, 256), F32)],
+        [((NJ, 256), F32), ((8, L), F32), ((8 * NJ, 256), F32)],
         flops=2 * R * COLS0 * 1024,
     )
-    near, inside, mom4, (t, w1d_grad, rect_here, h3_here, z2_here) = exchange(
+    near, inside, mom4, (w1d_grad, rect_here, t, h3_here, z2_here, gact) = exchange(
         cross, core, mom, "tm",
         lambda token: run(
             window_4,
             "window_4",
-            [((COLS1, 256), BF)] + far(32, L),
-            [Far(low3), Far(cat1, 512), cat0g, w2d],
-            [((512, COLS0), F32), ((400, L), F32), ((32, L), F32)],
+            far(32, L),
+            [Far(low3, parts=2), Far(cat1, 512, parts=2), cat0g],
+            [((512, COLS0), F32), ((32, L), F32)],
             flops=2 * R * COLS0 * 1024,
-            fetch=[Far(rect), Far(h3), Far(z2)],
+            fetch=[Far(rect), Far(t2a_d), Far(h3), Far(z2)],
+            store=[gact],
             token=token,
         ),
     )
@@ -1517,19 +1530,20 @@
         [((R, COLS2), BF)] + rim(256) + wide(256),
         flops=2 * R * COLS2 * 512,
     )
-    near, inside, mom6, (t, w2c_grad, z1_here, h1_here, cat0_here) = exchange(
+    near, inside, mom6, (t, keep, give, z1_here, h1_here, cat0_here) = exchange(
         cross, core, mom, "tm",
         lambda token: run(
             window_6,
             "window_6",
-            [((256, COLS1B), BF)] + far(128, L),
-            [low2, Far(cat1), w1c],
+            [((256, COLS1B), BF), ((HALF, L), F32), ((HALF, L), F32)],
+            [index, low2, Far(cat1, parts=2), w1c, Far(w1d_grad), Far(w2d_grad)],
             [((256, COLS1), F32), ((128, L), F32)],
             flops=2 * R * COLS1 * 256,
             fetch=[Far(z1), Far(h1), Far(cat0)],
             token=token,
         ),
     )
+    got = flip(give, "tm", 1)
     *nets, low1 = run(
         up_one_back_kernel,
         "up_one_back",
@@ -1539,23 +1553,27 @@
         flops=2 * R * COLS1B * 256,
     )
     nets = swap(nets, "stem")
-    keep, give, direct_here = run(
+    low, direct_here = run(
         window_7,
         "window_7",
-        [((HALF, L), F32), ((HALF, L), F32)],
-        [index, low1, cat0_here, bias_one, Far(w1d_grad), Far(w2d_grad), Far(w2c_grad)],
+        [((HALF + 32, L), BF)],
+        [low1, cat0_here, keep, got, bias_one],
         [((512, COLS0), F32), ((16, L), F32)],
         flops=2 * R * COLS0 * 512,
         fetch=[Far(direct)],
     )
-    (mixture_grad,) = run(
-        mixture_kernel,
-        "mixture",
-        [((2, frames, blocks * 32), F32)],
-        [*nets, direct_here],
-        [((2, frames, L), F32)],
-    )
-    mine, other = sum_halves(keep, give, "tm")
+    mine, other, mixture_grad = sum_chips(
+        low,
+        "tm",
+        lambda token: run(
+            mixture_kernel,
+            "mixture",
+            [((2, frames, blocks * 32), F32)],
+            [*nets, direct_here],
+            [((2, frames, L), F32)],
+            token=token,
+        ),
+    )
     w1c_grad, w2c_grad, w2d_grad, w1d_grad, bias_one = run(
         unpack_kernel,
         "unpack",

time: 161 us -> 150 us (0.932)
  Pallas kernels: 84.5 us -> 75.5 us
  waiting for transfers between devices: 19.7 us -> 16.5 us
    pallas_call x22, Pallas kernels: 84.5 us -> 75.5 us  [run(): pl.pallas_call(body, out_shape=[pltpu.HBM(o[0], o[1]) if len(o) == 3 else...]
    ppermute x33, starting transfers between devices: 24.2 us -> 30.1 us  [flip(): lax.ppermute(values, axis, [(i, i ^ bit) for i in range(lax.axis_size(axi...]
    ppermute x33, waiting for transfers between devices: 18.9 us -> 14.9 us  [flip(): lax.ppermute(values, axis, [(i, i ^ bit) for i in range(lax.axis_size(axi...]
    ppermute x6, starting transfers between devices: 7.38 us -> 3.53 us  [exchange(): far = lax.ppermute(mom, axis, pairs(count, 3))]
  transfers between devices with their start and end apart: 46 -> 46, of which waited for: 15 -> 11; matrix products, arithmetic and copies ran while one was open for 4% -> 4% of each run, Pallas kernels for 18% -> 23%
where the time goes in v4:
time: 150 us; the launch traced here: 149 us
  Pallas kernels  75.5 us (50%)
  starting transfers between devices  48.2 us (32%)
  waiting for transfers between devices  16.5 us (11%)
  local copies, waits for them, and re-layouts  5.22 us (3%)
  other arithmetic  2.52 us (2%)
    pallas_call x22, Pallas kernels, run(): pl.pallas_call(body, out_shape=[pltpu.HBM(o[0], o[1]) if len(o) == 3 else...  75.5 us
    ppermute x33, starting transfers between devices, flip(): lax.ppermute(values, axis, [(i, i ^ bit) for i in range(lax.axis_size(axi...  30.1 us
    ppermute x33, waiting for transfers between devices, flip(): lax.ppermute(values, axis, [(i, i ^ bit) for i in range(lax.axis_size(axi...  14.9 us
    ppermute x6, starting transfers between devices, exchange(): near = lax.ppermute(cross, axis, pairs(count, -1))  10.1 us
    ppermute x1, starting transfers between devices, per_device(): near = lax.ppermute(cross, 'tm', pairs(lax.axis_size('tm'), -1))  4.55 us
    ppermute x6, starting transfers between devices, exchange(): far = lax.ppermute(mom, axis, pairs(count, 3))  3.53 us
  transfers between devices with their start and end apart: 46, of which 11 were waited for; matrix products, arithmetic and copies ran while one was open for 4% of the time, Pallas kernels for 23%

profile of v4, /device:TPU:0, one launch (start us, length us, event | category | flops | bytes accessed | tf_op | source)
XLA Modules:
  0.0 149.3 jit_solution(11459500849110998838)
XLA Ops:
  1.4 3.1 %layout.1 = (bf16[80,256]{1,0:T(8,128)(2,1)S(1)}, bf16[80,256]{1,0:T(8,128)(2,1)S(1)}, bf16[1024,256]{1,0:T(8,128)(2,1)S(1)}, bf16[1024,256]{1,0:T(8,128)(2,1)S(1)}) custom-call(s32[2]{0:T(128)S(1)} %pad_add_fusion.refs_0_, s32[128]{0:T(128)S(1)} %copy-done.2, bf16[2,128,1024]{2,1,0:T(8,128)(2,1)} %refs_2_.1, bf16[4,2,128,256]{3,2,1,0:T(8,128)(2,1)} %refs_3_.1), custom_call_target="tpu_custom_call" | custom-call | bytes 2179592 | tf_op jit(solution)/shard_map/layout/pallas_call | solution.py:132
  4.5 4.6 %collective-permute-start = (bf16[80,256]{1,0:T(8,128)(2,1)S(1)}, bf16[80,256]{1,0:T(8,128)(2,1)S(1)}, u32[]{:S(2)}, u32[]{:S(2)}) collective-permute-start(bf16[80,256]{1,0:T(8,128)(2,1)S(1)} %get-tuple-element.138), channel_id=1, source_target_pairs={{0,7},{2,1},{4,3},{6,5},{7,0},{1,2},{3,4},{5,6},{8,15},{10,9},{12,... | collective-permute-start | bytes 122888 | tf_op jit(solution)/shard_map/ppermute | solution.py:1381
  13.5 4.2 %conv_one.1 = (f32[40,512]{1,0:T(8,128)S(1)}, f32[32,512]{1,0:T(8,128)}, f32[8,128]{1,0:T(8,128)S(1)}, f32[8,128]{1,0:T(8,128)S(1)}, f32[64,256]{1,0:T(8,128)S(1...) custom-call(s32[2]{0:T(128)S(1)} %pad_add_fusion.refs_0_, bf16[1024,256]{1,0:T(8,128)(2,1)S(1)} %get-tuple-element.137.refs_1_, ...), custom_call_target="tpu_custom_call" | custom-call | flops 1073741824 | bytes 6152200 | tf_op jit(solution)/shard_map/conv_one/pallas_call | solution.py:132
  19.2 2.6 %collective-permute-start.5 = (f32[8,128]{1,0:T(8,128)S(1)}, f32[8,128]{1,0:T(8,128)S(1)}, u32[]{:S(2)}, u32[]{:S(2)}) collective-permute-start(f32[8,128]{1,0:T(8,128)S(1)} %get-tuple-element.145.refs_4_), channel_id=1, source_target_pairs={{0,4},{1,5},{2,6},{3,7},{4,0},{5,1},{6,2},{7,3},{8,12},{9,13},{10,... | collective-permute-start | bytes 12296 | tf_op jit(solution)/shard_map/ppermute | solution.py:1254
  21.9 2.6 %window_1.1 = (bf16[1920,256]{1,0:T(8,128)(2,1)S(1)}, f32[1024,512]{1,0:T(8,128)S(1)}, f32[64,256]{1,0:T(8,128)}, bf16[1024,1024]{1,0:T(8,128)(2,1)}, f32[8,128]{1,0:T(8,128)S(1)}) custom-call(bf16[400,32]{1,0:T(8,128)(2,1)S(1)} %bitcast.63, f32[1024,512]{1,0:T(8,128)} %get-tuple-element.142.refs_1_.refs_6_, f32[64,256]{1,0:T(8,128)S(1)} %get-tuple-element.143.refs_2_, ...), custom_call_target="tpu_custom_call" | custom-call | bytes 9536512 | tf_op jit(solution)/shard_map/window_1/pallas_call | solution.py:132
  26.1 5.4 %conv_two.1 = (f32[40,256]{1,0:T(8,128)S(1)}, f32[32,256]{1,0:T(8,128)S(1)}, f32[8,128]{1,0:T(8,128)S(1)}, bf16[4,32,512]{2,1,0:T(8,128)(2,1)S(1)}, f32[2,32,512...) custom-call(s32[2]{0:T(128)S(1)} %pad_add_fusion.refs_0_, ...), custom_call_target="tpu_custom_call" | custom-call | flops 1006632960 | bytes 8384520 | tf_op jit(solution)/shard_map/conv_two/pallas_call | solution.py:132
  39.1 5.4 %up_two.1 = (f32[40,512]{1,0:T(8,128)S(1)}, f32[32,512]{1,0:T(8,128)S(1)}, f32[8,128]{1,0:T(8,128)S(1)}, f32[2,32,256]{2,1,0:T(8,128)S(1)}, bf16[1024,256]{1,0:T(8,128)(2,1)S(1)}, /*index=5*/f32[1024,512]{1,0:T(8,128)}) custom-call(s32[2]{0:T(128)S(1)} %pad_add_fusion.refs_0_, f32[1024,256]{1,0:T(8,128)S(1)} %get-tuple-element.155.refs_1_, ...), custom_call_target="tpu_custom_call" | custom-call | flops 1207959552 | bytes 5171208 | tf_op jit(solution)/shard_map/up_two/pallas_call | solution.py:132
  45.1 2.5 %collective-permute-start.15 = (f32[8,128]{1,0:T(8,128)S(1)}, f32[8,128]{1,0:T(8,128)S(1)}, u32[]{:S(2)}, u32[]{:S(2)}) collective-permute-start(f32[8,128]{1,0:T(8,128)S(1)} %get-tuple-element.165.refs_6_), channel_id=1, source_target_pairs={{0,4},{1,5},{2,6},{3,7},{4,0},{5,1},{6,2},{7,3},{8,12},{9,13},{10,... | collective-permute-start | bytes 12296 | tf_op jit(solution)/shard_map/ppermute | solution.py:1254
  49.4 3.0 %window_3.1 = (bf16[256,3072]{1,0:T(8,128)(2,1)S(1)}, f32[1024,512]{1,0:T(8,128)S(1)}, bf16[1024,1536]{1,0:T(8,128)(2,1)S(1)}, bf16[4,32,512]{2,1,0:T(8,128)(2,1...) custom-call(f32[2,50,128]{2,1,0:T(8,128)S(1)} %copy.52.refs_0_.refs_6_, ...), custom_call_target="tpu_custom_call" | custom-call | bytes 14155776 | tf_op jit(solution)/shard_map/window_3/pallas_call | solution.py:132
  55.1 4.6 %up_one.1 = (bf16[272,256]{1,0:T(8,128)(2,1)S(1)}, bf16[272,256]{1,0:T(8,128)(2,1)S(1)}, bf16[272,256]{1,0:T(8,128)(2,1)S(1)}, bf16[272,256]{1,0:T(8,128)(2,1)S(...) custom-call(s32[2]{0:T(128)S(1)} %pad_add_fusion.refs_0_, ...), custom_call_target="tpu_custom_call" | custom-call | flops 1610612736 | bytes 9879560 | tf_op jit(solution)/shard_map/up_one/pallas_call | solution.py:132
  63.3 2.2 %window_swap.1 = (bf16[1920,256]{1,0:T(8,128)(2,1)}, bf16[1024,256]{1,0:T(8,128)(2,1)S(1)}, bf16[1024,256]{1,0:T(8,128)(2,1)S(1)}, f32[64,256]{1,0:T(8,128)S(1)}...) custom-call(bf16[400,32]{1,0:T(8,128)(2,1)S(1)} %bitcast.62, ...), custom_call_target="tpu_custom_call" | custom-call | bytes 7631872 | tf_op jit(solution)/shard_map/window_swap/pallas_call | solution.py:132
  66.1 3.6 %collective-permute-done.18.refs_3_ = bf16[272,256]{1,0:T(8,128)(2,1)S(1)} collective-permute-done((bf16[272,256]{1,0:T(8,128)(2,1)S(1)}, bf16[272,256]{1,0:T(8,128)(2,1)S(1)}, u32[]{:S(2)}, u32[]{:S(2)}) %collective-permute-start.18) | collective-permute-done | bytes 139296 | tf_op jit(solution)/shard_map/ppermute | solution.py:1254
  74.5 3.9 %estimate.1 = (bf16[4,2,128,256]{3,2,1,0:T(8,128)(2,1)}, bf16[1024,1024]{1,0:T(8,128)(2,1)S(1)}, f32[1024,256]{1,0:T(8,128)S(1)}, f32[32,256]{1,0:T(8,128)S(1)},...) custom-call(s32[2]{0:T(128)S(1)} %pad_add_fusion.refs_0_, bf16[272,256]{1,0:T(8,128)(2,1)S(1)} %get-tuple-element.173.refs_1_, ...), custom_call_target="tpu_custom_call" | custom-call | bytes 10113032 | tf_op jit(solution)/shard_map/estimate/pallas_call | solution.py:132
  79.8 4.6 %down_one_back.1 = (f32[1024,512]{1,0:T(8,128)S(1)}, bf16[1024,1024]{1,0:T(8,128)(2,1)S(1)}, f32[40,512]{1,0:T(8,128)S(1)}, f32[32,512]{1,0:T(8,128)S(1)}, f32[8...) custom-call(s32[2]{0:T(128)S(1)} %pad_add_fusion.refs_0_, ...), custom_call_target="tpu_custom_call" | custom-call | flops 2147483648 | bytes 12369928 | tf_op jit(solution)/shard_map/down_one_back/pallas_call | solution.py:132
  85.3 3.0 %collective-permute-start.23 = (f32[40,512]{1,0:T(8,128)S(1)}, f32[40,512]{1,0:T(8,128)S(1)}, u32[]{:S(2)}, u32[]{:S(2)}) collective-permute-start(f32[40,512]{1,0:T(8,128)S(1)} %get-tuple-element.200), channel_id=1, source_target_pairs={{0,7},{2,1},{4,3},{6,5},{7,0},{1,2},{3,4},{5,6},{8,15},{10,9},{12,... | collective-permute-start | bytes 245768 | tf_op jit(solution)/shard_map/ppermute | solution.py:1288
  88.3 5.6 %window_4.1 = (f32[32,128]{1,0:T(8,128)}, f32[1024,512]{1,0:T(8,128)S(1)}, bf16[1920,256]{1,0:T(8,128)(2,1)S(1)}, f32[2,32,512]{2,1,0:T(8,128)S(1)}, f32[1024,25...) custom-call(bf16[1024,512]{1,0:T(8,128)(2,1)} %get-tuple-element.202.refs_0_, ...), custom_call_target="tpu_custom_call" | custom-call | flops 2147483648 | bytes 19689472 | tf_op jit(solution)/shard_map/window_4/pallas_call | solution.py:132
  95.4 5.4 %up_two_back.1 = (f32[1024,256]{1,0:T(8,128)S(1)}, bf16[1024,1920]{1,0:T(8,128)(2,1)S(1)}, f32[40,256]{1,0:T(8,128)S(1)}, f32[32,256]{1,0:T(8,128)S(1)}, f32[8,128]{1,0:T(8,128)S(1)}) custom-call(s32[2]{0:T(128)S(1)} %pad_add_fusion.refs_0_, f32[1024,512]{1,0:T(8,128)S(1)} %get-tuple-element.199.refs_1_, f32[40,512]{1,0:T(8,128)S(1)} %collective-permute-done.23.refs_2_, ...), custom_call_target="tpu_custom_call" | custom-call | flops 1006632960 | bytes 11669512 | tf_op jit(solution)/shard_map/up_two_back/pallas_call | solution.py:132
  105.4 3.5 %window_5.1 = (bf16[512,1152]{1,0:T(8,128)(2,1)S(1)}, f32[128,128]{1,0:T(8,128)}, f32[1024,256]{1,0:T(8,128)S(1)}, f32[2,32,256]{2,1,0:T(8,128)S(1)}, f32[1024,5...) custom-call(bf16[1024,256]{1,0:T(8,128)(2,1)} %get-tuple-element.217.refs_0_, ...), custom_call_target="tpu_custom_call" | custom-call | flops 1006632960 | bytes 16288768 | tf_op jit(solution)/shard_map/window_5/pallas_call | solution.py:132
  110.1 5.0 %down_two_back.1 = (f32[1024,512]{1,0:T(8,128)S(1)}, bf16[1024,256]{1,0:T(8,128)(2,1)S(1)}, f32[40,512]{1,0:T(8,128)S(1)}, f32[32,512]{1,0:T(8,128)S(1)}, f32[8,128]{1,0:T(8,128)S(1)}) custom-call(s32[2]{0:T(128)S(1)} %pad_add_fusion.refs_0_, f32[1024,256]{1,0:T(8,128)S(1)} %get-tuple-element.214.refs_1_, f32[40,256]{1,0:T(8,128)S(1)} %collective-permute-done.28.refs_2_, ...), custom_call_target="tpu_custom_call" | custom-call | flops 1207959552 | bytes 10485768 | tf_op jit(solution)/shard_map/down_two_back/pallas_call | solution.py:132
  119.5 4.4 %window_6.1 = (bf16[256,1536]{1,0:T(8,128)(2,1)S(1)}, f32[144,128]{1,0:T(8,128)S(1)}, f32[144,128]{1,0:T(8,128)S(1)}, f32[1024,512]{1,0:T(8,128)S(1)}, f32[2,32,...) custom-call(s32[2]{0:T(128)S(1)} %pad_add_fusion.refs_0_, ...), custom_call_target="tpu_custom_call" | custom-call | flops 1006632960 | bytes 14029832 | tf_op jit(solution)/shard_map/window_6/pallas_call | solution.py:132
  125.2 3.3 %up_one_back.1 = (bf16[256,256]{1,0:T(8,128)(2,1)S(1)}, bf16[256,256]{1,0:T(8,128)(2,1)S(1)}, bf16[256,256]{1,0:T(8,128)(2,1)S(1)}, bf16[256,256]{1,0:T(8,128)(2,1)S(1)}, bf16[1024,512]{1,0:T(8,128)(2,1)S(1)}) custom-call(s32[2]{0:T(128)S(1)} %pad_add_fusion.refs_0_, f32[1024,512]{1,0:T(8,128)S(1)} %get-tuple-element.228.refs_1_, ...), custom_call_target="tpu_custom_call" | custom-call | flops 805306368 | bytes 6930440 | tf_op jit(solution)/shard_map/up_one_back/pallas_call | solution.py:132
  129.7 2.4 %window_7.1 = (bf16[176,128]{1,0:T(8,128)(2,1)S(1)}, f32[256,256]{1,0:T(8,128)S(1)}) custom-call(bf16[1024,512]{1,0:T(8,128)(2,1)S(1)} %get-tuple-element.245.refs_0_, bf16[1024,1024]{1,0:T(8,128)(2,1)S(1)} %get-tuple-element.246.refs_1_, f32[144,128]{1,0:T(8,128)S(1)} %get-tuple-element.247.refs_2_, f32[144,128]{1,0:T(8,128)S(1)} %collective-permute-done.41.refs_3_, ...), custom_call_target="tpu_custom_call" | custom-call | flops 1073741824 | bytes 3866624 | tf_op jit(solution)/shard_map/window_7/pallas_call | solution.py:132
  132.2 2.2 %collective-permute-start.43 = (bf16[176,128]{1,0:T(8,128)(2,1)S(1)}, bf16[176,128]{1,0:T(8,128)(2,1)S(1)}, u32[]{:S(2)}, u32[]{:S(2)}) collective-permute-start(bf16[176,128]{1,0:T(8,128)(2,1)S(1)} %get-tuple-element.252.refs_5_), channel_id=1, source_target_pairs={{0,4},{1,5},{2,6},{3,7},{4,0},{5,1},{6,2},{7,3},{8,12},{9,13},{10,... | collective-permute-start | bytes 135176 | tf_op jit(solution)/shard_map/ppermute | solution.py:1254
  140.4 3.9 %collective-permute-done.39.refs_2_ = bf16[256,256]{1,0:T(8,128)(2,1)S(1)} collective-permute-done((bf16[256,256]{1,0:T(8,128)(2,1)S(1)}, bf16[256,256]{1,0:T(8,128)(2,1)S(1)}, u32[]{:S(2)}, u32[]{:S(2)}) %collective-permute-start.39) | collective-permute-done | bytes 131104 | tf_op jit(solution)/shard_map/ppermute | solution.py:1254
  (177 shorter events, 56.9 us)
Async XLA Ops:
  4.5 8.8 %collective-permute-start = (bf16[80,256]{1,0:T(8,128)(2,1)S(1)}, bf16[80,256]{1,0:T(8,128)(2,1)S(1)}, u32[]{:S(2)}, u32[]{:S(2)}) collective-permute-start(bf16[80,256]{1,0:T(8,128)(2,1)S(1)} %get-tuple-element.138), channel_id=1, source_target_pairs={{0,7},{2,1},{4,3},{6,5},{7,0},{1,2},{3,4},{5,6},{8,15},{10,9},{12,... | collective-permute-start | bytes 122888 | tf_op jit(solution)/shard_map/ppermute | solution.py:1381
  17.6 6.9 %collective-permute-start.2 = (f32[40,512]{1,0:T(8,128)S(1)}, f32[40,512]{1,0:T(8,128)S(1)}, u32[]{:S(2)}, u32[]{:S(2)}) collective-permute-start(f32[40,512]{1,0:T(8,128)S(1)} %get-tuple-element.147), channel_id=1, source_target_pairs={{0,7},{2,1},{4,3},{6,5},{7,0},{1,2},{3,4},{5,6},{8,15},{10,9},{12,... | collective-permute-start | bytes 245768 | tf_op jit(solution)/shard_map/ppermute | solution.py:1288
  44.5 7.9 %collective-permute-start.14 = (f32[8,128]{1,0:T(8,128)S(1)}, f32[8,128]{1,0:T(8,128)S(1)}, u32[]{:S(2)}, u32[]{:S(2)}) collective-permute-start(f32[8,128]{1,0:T(8,128)S(1)} %get-tuple-element.165.refs_6_), channel_id=1, source_target_pairs={{0,3},{2,5},{4,7},{6,1},{3,0},{5,2},{7,4},{1,6},{8,11},{10,13},{12... | collective-permute-start | bytes 12296 | tf_op jit(solution)/shard_map/ppermute | solution.py:1290
  45.1 7.3 %collective-permute-start.15 = (f32[8,128]{1,0:T(8,128)S(1)}, f32[8,128]{1,0:T(8,128)S(1)}, u32[]{:S(2)}, u32[]{:S(2)}) collective-permute-start(f32[8,128]{1,0:T(8,128)S(1)} %get-tuple-element.165.refs_6_), channel_id=1, source_target_pairs={{0,4},{1,5},{2,6},{3,7},{4,0},{5,1},{6,2},{7,3},{8,12},{9,13},{10,... | collective-permute-start | bytes 12296 | tf_op jit(solution)/shard_map/ppermute | solution.py:1254
  48.7 6.5 %collective-permute-start.13 = (f32[32,512]{1,0:T(8,128)S(1)}, f32[32,512]{1,0:T(8,128)S(1)}, u32[]{:S(2)}, u32[]{:S(2)}) collective-permute-start(f32[32,512]{1,0:T(8,128)S(1)} %get-tuple-element.168), channel_id=1, source_target_pairs={{0,1},{1,0},{2,3},{3,2},{4,5},{5,4},{6,7},{7,6},{8,9},{9,8},{10,11... | collective-permute-start | bytes 196616 | tf_op jit(solution)/shard_map/ppermute | solution.py:1254
  61.2 8.4 %collective-permute-start.18 = (bf16[272,256]{1,0:T(8,128)(2,1)S(1)}, bf16[272,256]{1,0:T(8,128)(2,1)S(1)}, u32[]{:S(2)}, u32[]{:S(2)}) collective-permute-start(bf16[272,256]{1,0:T(8,128)(2,1)S(1)} %get-tuple-element.175), channel_id=1, source_target_pairs={{0,16},{8,24},{16,0},{24,8},{1,17},{9,25},{17,1},{25,9},{2,18},{10... | collective-permute-start | bytes 417800 | tf_op jit(solution)/shard_map/ppermute | solution.py:1254
  62.7 6.9 %collective-permute-start.19 = (bf16[272,256]{1,0:T(8,128)(2,1)S(1)}, bf16[272,256]{1,0:T(8,128)(2,1)S(1)}, u32[]{:S(2)}, u32[]{:S(2)}) collective-permute-start(bf16[272,256]{1,0:T(8,128)(2,1)S(1)} %get-tuple-element.176), channel_id=1, source_target_pairs={{0,24},{8,16},{16,8},{24,0},{1,25},{9,17},{17,9},{25,1},{2,26},{10... | collective-permute-start | bytes 417800 | tf_op jit(solution)/shard_map/ppermute | solution.py:1254
  70.9 7.5 %collective-permute-start.20 = (bf16[272,256]{1,0:T(8,128)(2,1)S(1)}, bf16[272,256]{1,0:T(8,128)(2,1)S(1)}, u32[]{:S(2)}, u32[]{:S(2)}) collective-permute-start(bf16[272,256]{1,0:T(8,128)(2,1)S(1)} %get-tuple-element.192), channel_id=1, source_target_pairs={{0,8},{8,0},{16,24},{24,16},{1,9},{9,1},{17,25},{25,17},{2,10},{10... | collective-permute-start | bytes 417800 | tf_op jit(solution)/shard_map/ppermute | solution.py:1254
  72.2 7.6 %collective-permute-start.21 = (bf16[272,256]{1,0:T(8,128)(2,1)S(1)}, bf16[272,256]{1,0:T(8,128)(2,1)S(1)}, u32[]{:S(2)}, u32[]{:S(2)}) collective-permute-start(bf16[272,256]{1,0:T(8,128)(2,1)S(1)} %get-tuple-element.193), channel_id=1, source_target_pairs={{0,16},{8,24},{16,0},{24,8},{1,17},{9,25},{17,1},{25,9},{2,18},{10... | collective-permute-start | bytes 417800 | tf_op jit(solution)/shard_map/ppermute | solution.py:1254
  73.0 6.8 %collective-permute-start.22 = (bf16[272,256]{1,0:T(8,128)(2,1)S(1)}, bf16[272,256]{1,0:T(8,128)(2,1)S(1)}, u32[]{:S(2)}, u32[]{:S(2)}) collective-permute-start(bf16[272,256]{1,0:T(8,128)(2,1)S(1)} %get-tuple-element.194), channel_id=1, source_target_pairs={{0,24},{8,16},{16,8},{24,0},{1,25},{9,17},{17,9},{25,1},{2,26},{10... | collective-permute-start | bytes 417800 | tf_op jit(solution)/shard_map/ppermute | solution.py:1254
  84.4 9.5 %collective-permute-start.25 = (f32[8,128]{1,0:T(8,128)S(1)}, f32[8,128]{1,0:T(8,128)S(1)}, u32[]{:S(2)}, u32[]{:S(2)}) collective-permute-start(f32[8,128]{1,0:T(8,128)S(1)} %get-tuple-element.207.refs_8_), channel_id=1, source_target_pairs={{0,3},{2,5},{4,7},{6,1},{3,0},{5,2},{7,4},{1,6},{8,11},{10,13},{12... | collective-permute-start | bytes 12296 | tf_op jit(solution)/shard_map/ppermute | solution.py:1290
  84.5 9.5 %collective-permute-start.26 = (f32[8,128]{1,0:T(8,128)S(1)}, f32[8,128]{1,0:T(8,128)S(1)}, u32[]{:S(2)}, u32[]{:S(2)}) collective-permute-start(f32[8,128]{1,0:T(8,128)S(1)} %get-tuple-element.207.refs_8_), channel_id=1, source_target_pairs={{0,4},{1,5},{2,6},{3,7},{4,0},{5,1},{6,2},{7,3},{8,12},{9,13},{10,... | collective-permute-start | bytes 12296 | tf_op jit(solution)/shard_map/ppermute | solution.py:1254
  85.3 8.7 %collective-permute-start.23 = (f32[40,512]{1,0:T(8,128)S(1)}, f32[40,512]{1,0:T(8,128)S(1)}, u32[]{:S(2)}, u32[]{:S(2)}) collective-permute-start(f32[40,512]{1,0:T(8,128)S(1)} %get-tuple-element.200), channel_id=1, source_target_pairs={{0,7},{2,1},{4,3},{6,5},{7,0},{1,2},{3,4},{5,6},{8,15},{10,9},{12,... | collective-permute-start | bytes 245768 | tf_op jit(solution)/shard_map/ppermute | solution.py:1288
  88.3 7.1 %collective-permute-start.24 = (f32[32,512]{1,0:T(8,128)S(1)}, f32[32,512]{1,0:T(8,128)S(1)}, u32[]{:S(2)}, u32[]{:S(2)}) collective-permute-start(f32[32,512]{1,0:T(8,128)S(1)} %get-tuple-element.201), channel_id=1, source_target_pairs={{0,1},{1,0},{2,3},{3,2},{4,5},{5,4},{6,7},{7,6},{8,9},{9,8},{10,11... | collective-permute-start | bytes 196616 | tf_op jit(solution)/shard_map/ppermute | solution.py:1254
  100.8 8.0 %collective-permute-start.30 = (f32[8,128]{1,0:T(8,128)S(1)}, f32[8,128]{1,0:T(8,128)S(1)}, u32[]{:S(2)}, u32[]{:S(2)}) collective-permute-start(f32[8,128]{1,0:T(8,128)S(1)} %get-tuple-element.221.refs_7_), channel_id=1, source_target_pairs={{0,3},{2,5},{4,7},{6,1},{3,0},{5,2},{7,4},{1,6},{8,11},{10,13},{12... | collective-permute-start | bytes 12296 | tf_op jit(solution)/shard_map/ppermute | solution.py:1290
  100.9 7.9 %collective-permute-start.31 = (f32[8,128]{1,0:T(8,128)S(1)}, f32[8,128]{1,0:T(8,128)S(1)}, u32[]{:S(2)}, u32[]{:S(2)}) collective-permute-start(f32[8,128]{1,0:T(8,128)S(1)} %get-tuple-element.221.refs_7_), channel_id=1, source_target_pairs={{0,4},{1,5},{2,6},{3,7},{4,0},{5,1},{6,2},{7,3},{8,12},{9,13},{10,... | collective-permute-start | bytes 12296 | tf_op jit(solution)/shard_map/ppermute | solution.py:1254
  115.2 8.7 %collective-permute-start.35 = (f32[8,128]{1,0:T(8,128)S(1)}, f32[8,128]{1,0:T(8,128)S(1)}, u32[]{:S(2)}, u32[]{:S(2)}) collective-permute-start(f32[8,128]{1,0:T(8,128)S(1)} %get-tuple-element.236.refs_9_), channel_id=1, source_target_pairs={{0,3},{2,5},{4,7},{6,1},{3,0},{5,2},{7,4},{1,6},{8,11},{10,13},{12... | collective-permute-start | bytes 12296 | tf_op jit(solution)/shard_map/ppermute | solution.py:1290
  115.2 8.7 %collective-permute-start.36 = (f32[8,128]{1,0:T(8,128)S(1)}, f32[8,128]{1,0:T(8,128)S(1)}, u32[]{:S(2)}, u32[]{:S(2)}) collective-permute-start(f32[8,128]{1,0:T(8,128)S(1)} %get-tuple-element.236.refs_9_), channel_id=1, source_target_pairs={{0,4},{1,5},{2,6},{3,7},{4,0},{5,1},{6,2},{7,3},{8,12},{9,13},{10,... | collective-permute-start | bytes 12296 | tf_op jit(solution)/shard_map/ppermute | solution.py:1254
  117.2 6.7 %collective-permute-start.33 = (f32[40,512]{1,0:T(8,128)S(1)}, f32[40,512]{1,0:T(8,128)S(1)}, u32[]{:S(2)}, u32[]{:S(2)}) collective-permute-start(f32[40,512]{1,0:T(8,128)S(1)} %get-tuple-element.229), channel_id=1, source_target_pairs={{0,7},{2,1},{4,3},{6,5},{7,0},{1,2},{3,4},{5,6},{8,15},{10,9},{12,... | collective-permute-start | bytes 245768 | tf_op jit(solution)/shard_map/ppermute | solution.py:1288
  128.4 9.6 %collective-permute-start.38 = (bf16[256,256]{1,0:T(8,128)(2,1)S(1)}, bf16[256,256]{1,0:T(8,128)(2,1)S(1)}, u32[]{:S(2)}, u32[]{:S(2)}) collective-permute-start(bf16[256,256]{1,0:T(8,128)(2,1)S(1)} %get-tuple-element.242), channel_id=1, source_target_pairs={{0,8},{8,0},{16,24},{24,16},{1,9},{9,1},{17,25},{25,17},{2,10},{10... | collective-permute-start | bytes 393224 | tf_op jit(solution)/shard_map/ppermute | solution.py:1254
  132.1 13.4 %collective-permute-start.42 = (bf16[176,128]{1,0:T(8,128)(2,1)S(1)}, bf16[176,128]{1,0:T(8,128)(2,1)S(1)}, u32[]{:S(2)}, u32[]{:S(2)}) collective-permute-start(bf16[176,128]{1,0:T(8,128)(2,1)S(1)} %get-tuple-element.252.refs_5_), channel_id=1, source_target_pairs={{0,2},{1,3},{2,0},{3,1},{4,6},{5,7},{6,4},{7,5},{8,10},{9,11},{10,... | collective-permute-start | bytes 135176 | tf_op jit(solution)/shard_map/ppermute | solution.py:1254
  132.2 13.3 %collective-permute-start.43 = (bf16[176,128]{1,0:T(8,128)(2,1)S(1)}, bf16[176,128]{1,0:T(8,128)(2,1)S(1)}, u32[]{:S(2)}, u32[]{:S(2)}) collective-permute-start(bf16[176,128]{1,0:T(8,128)(2,1)S(1)} %get-tuple-element.252.refs_5_), channel_id=1, source_target_pairs={{0,4},{1,5},{2,6},{3,7},{4,0},{5,1},{6,2},{7,3},{8,12},{9,13},{10,... | collective-permute-start | bytes 135176 | tf_op jit(solution)/shard_map/ppermute | solution.py:1254
  134.4 11.1 %collective-permute-start.44 = (bf16[176,128]{1,0:T(8,128)(2,1)S(1)}, bf16[176,128]{1,0:T(8,128)(2,1)S(1)}, u32[]{:S(2)}, u32[]{:S(2)}) collective-permute-start(bf16[176,128]{1,0:T(8,128)(2,1)S(1)} %get-tuple-element.252.refs_5_), channel_id=1, source_target_pairs={{0,6},{1,7},{2,4},{3,5},{4,2},{5,3},{6,0},{7,1},{8,14},{9,15},{10,... | collective-permute-start | bytes 135176 | tf_op jit(solution)/shard_map/ppermute | solution.py:1254
  136.6 7.8 %collective-permute-start.39 = (bf16[256,256]{1,0:T(8,128)(2,1)S(1)}, bf16[256,256]{1,0:T(8,128)(2,1)S(1)}, u32[]{:S(2)}, u32[]{:S(2)}) collective-permute-start(bf16[256,256]{1,0:T(8,128)(2,1)S(1)} %get-tuple-element.243), channel_id=1, source_target_pairs={{0,16},{8,24},{16,0},{24,8},{1,17},{9,25},{17,1},{25,9},{2,18},{10... | collective-permute-start | bytes 393224 | tf_op jit(solution)/shard_map/ppermute | solution.py:1254
  (34 other events, 148.6 us)

commit v5 on v4

--- a/solution.py
+++ b/solution.py
@@ -17,10 +17,14 @@
 CHUNK = 512
 UNROLL = 4
 COLS0 = 1024
+SPAN0 = (slice(0, 768), slice(256, 1024))
 COLS1 = 1920
 COLS1B = 1536
 COLS2 = 1152
+SPAN2 = (slice(0, 768), slice(0, 1152))
+GROUPS2 = ((0, 512), (256, 640), (768, 1024))
 GROUPS1 = ((0, 1024, 1), (256, 1152, 2), (512, 1280, 0), (768, 1408, 3), (1536, 1792, 4))
+TILES0 = ((0, 128), (256, 512), (384, 640), (768, 896))
 FULL = pl.BlockSpec(memory_space=pltpu.VMEM)
 SCALAR = pl.BlockSpec(memory_space=pltpu.SMEM)
 FAR = pl.BlockSpec(memory_space=pltpu.HBM)
@@ -91,7 +95,8 @@
         shape = args[k].array.shape
         if args[k].columns is not None:
             shape = (shape[0], args[k].columns)
-        landing.append(pltpu.VMEM(shape, args[k].array.dtype))
+        space = pltpu.SMEM if args[k].array.dtype == jnp.int32 else pltpu.VMEM
+        landing.append(space(shape, args[k].array.dtype))
 
     def body(*refs):
         ins, results = list(refs[:n_in]), list(refs[n_in : n_in + n_out])
@@ -126,7 +131,7 @@
         if isinstance(a, Far):
             in_specs.append(FAR)
         else:
-            in_specs.append(SCALAR if a.dtype == jnp.int32 else FULL)
+            in_specs.append(SCALAR if a.dtype == jnp.int32 and a.ndim == 1 else FULL)
     bytes_all = sum(a.size * a.dtype.itemsize for a in arrays)
     bytes_all += sum(jnp.zeros((), o[1]).dtype.itemsize * o[0][0] * o[0][-1] for o in outs)
     return pl.pallas_call(
@@ -242,11 +247,11 @@
 
 
 def rims_2(cat):
-    fill_rims(cat, [(768 + L * k, 256 * k, 256 * k + L) for k in range(3)], lane((M, L)) < 32)
+    fill_rims(cat, [(rim, base, base + L) for base, rim in GROUPS2], lane((M, L)) < 32)
 
 
 def rims_0(cat):
-    fill_rims(cat, [(512 + L * k, L * k, L * k) for k in range(4)], lane((M, L)) % 32 < 2)
+    fill_rims(cat, [(rim, base, base) for base, rim in TILES0], lane((M, L)) % 32 < 2)
 
 
 def matmul(left, right, transposed=False):
@@ -268,18 +273,19 @@
     lax.fori_loop(0, R // size, body, 0)
 
 
-def product_sums(cat, weights, transposed, use, done=None, size=256):
+def product_sums(product, use, done=None, size=256):
     sums = (jnp.zeros((8, L), F32), jnp.zeros((8, L), F32))
 
     def part(r, sums):
         rs = rows(r, size)
-        value = matmul(cat[rs, :], weights[...], transposed)
+        value = [(piece, at) for piece in product(rs) for at in tiles(piece.shape[1])]
         for i in range(size // M):
-            for k, at in enumerate(tiles(value.shape[1])):
+            for k, (piece, at) in enumerate(value):
                 if k % 4 == 0:
                     stores = []
-                sums = use(r * (size // M) + i, k, at, value[M * i : M * i + M, at], *sums, stores)
-                if k % 4 == 3 or k == value.shape[1] // L - 1:
+                tile = piece[M * i : M * i + M, at]
+                sums = use(r * (size // M) + i, k, slice(L * k, L * k + L), tile, *sums, stores)
+                if k % 4 == 3 or k == len(value) - 1:
                     put_all(stores)
         if done is not None:
             done(rs)
@@ -291,6 +297,26 @@
         for r in range(R // size):
             sums = part(r, sums)
     return [total_rows(v) for v in sums]
+
+
+def rows_from_0(cat, weights):
+    def product(rs):
+        pieces = []
+        for k in range(weights.shape[1] // 256):
+            span = SPAN0[k % 2]
+            pieces.append(matmul(cat[rs, span], weights[span, 256 * k : 256 * k + 256]))
+        return pieces
+
+    return product
+
+
+def rows_from_2(cat, weights):
+    def product(rs):
+        return [
+            matmul(cat[rs, span], weights[256 * k : 256 * k + 256, span], True) for k, span in enumerate(SPAN2)
+        ]
+
+    return product
 
 
 def sum8(value):
@@ -427,11 +453,11 @@
     zero = jnp.zeros((16, L), BF)
     at = lane((16, L))
     for row in range(2):
-        for k, tap in enumerate((row + 1, row + 3, row - 1)):
+        for (base, edge), tap in zip(GROUPS2, (row + 1, row + 3, row - 1)):
             for q in range(16):
                 span = slice(row * 256 + q * 16, row * 256 + q * 16 + 16)
                 for half in range(2):
-                    cols = slice(256 * k + L * half, 256 * k + L * half + L)
+                    cols = slice(base + L * half, base + L * half + L)
                     t[span, cols] = tile_2(w, tap, q, half) if 0 <= tap < TAPS else zero
                 rim = zero
                 if 0 <= tap < TAPS and q in (0, 1, 15):
@@ -439,7 +465,7 @@
                     start = (tap * TAPS + b) * 16
                     cond = at < 32 if q == 15 else at >= 96
                     rim = jnp.where(cond, w[start : start + 16, :], 0.0).astype(BF)
-                t[span, 768 + L * k : 768 + L * k + L] = rim
+                t[span, edge : edge + L] = rim
 
 
 def band(w, tap, channel, offset):
@@ -458,13 +484,17 @@
         rim = jnp.where(q == 31, -2 * p, jnp.where(q == 0, 33 - 2 * p, jnp.where(q == 1, 34 - 2 * p, -9)))
         for row in range(2):
             cols = slice(col + row * 256 + half * L, col + row * 256 + half * L + L)
-            for part, frame in enumerate((0, 1, 2, 3, None, -1, 4, 5)):
-                tap = -1 if frame is None else frame - 2 * row + 1
-                for c in range(2):
-                    start = part * 64 + c * 32
-                    ok = 0 <= tap < TAPS
-                    t[start : start + 32, cols] = band(w, tap, c, inner) if ok else zero
-                    t[512 + start : 544 + start, cols] = band(w, tap, c, rim) if ok else zero
+            for (base, edge), frames in zip(TILES0, ((None, -1), (0, 1), (2, 3), (4, 5))):
+                if not SPAN0[row].start <= base < SPAN0[row].stop:
+                    continue
+                for part, frame in enumerate(frames):
+                    tap = -1 if frame is None else frame - 2 * row + 1
+                    for c in range(2):
+                        start = part * 64 + c * 32
+                        ok = 0 <= tap < TAPS
+                        for offset, bins in ((base, inner), (edge, rim)):
+                            span = slice(offset + start, offset + start + 32)
+                            t[span, cols] = band(w, tap, c, bins) if ok else zero
 
 
 def matrix_1_up(w, t, col):
@@ -485,8 +515,56 @@
                 t[span, start : start + L] = band(w, tap, c, rim) if ok else zero
 
 
-def window_0(w1c, t):
+def double_lanes(value, first):
+    while first < L:
+        value = value + pltpu.roll(value, first, 1)
+        first *= 2
+    return value
+
+
+def window_0(
+    index, seg_lengths, frame_mask, raw_c, raw_d, gain1, shift1, gain2, shift2, gain3, shift3, bias2, bias1,
+    t, w1c, w1d, aux, prm,
+):
+    w1c[...] = jnp.zeros(w1c.shape, F32)
+    w1d[...] = jnp.zeros(w1d.shape, F32)
+    for k in range(TAPS * TAPS):
+        span = slice(2 * k, 2 * k + 2)
+        w1c[span, 0:16] = raw_c[k].astype(F32)
+        value = raw_d[k].astype(F32)
+        w1d[0, span, 0:16] = value[:, 0:16]
+        w1d[1, span, 0:16] = value[:, 16:32]
+    w1c[...] = double_lanes(w1c[...], 16)
+    for k in range(2):
+        w1d[k] = double_lanes(w1d[k], 16)
     matrix_1_down(w1c, t, 0)
+    prm[...] = jnp.zeros(prm.shape, F32)
+    for k, value in enumerate((gain1, shift1, gain2, shift2, gain3, shift3, bias2)):
+        prm[k : k + 1, 0 : value.shape[1]] = value[...]
+    rows8, at = sub((8, L)), lane((8, L))
+    value = prm[...]
+    wide = (rows8 == 2) | (rows8 == 3)
+    value = double_lanes(value + jnp.where(wide, 0.0, pltpu.roll(value, 16, 1)), 32)
+    last = jnp.where(at // 32 % 2 == 0, bias1[0:1, 0:1], bias1[0:1, 1:2])
+    prm[...] = jnp.where(rows8 == 7, last, value)
+    row, at = sub((M, L)), lane((M, L))
+    kept = jnp.broadcast_to(frame_mask[...].astype(F32), (8, L))
+    kept = jnp.minimum(kept, pltpu.roll(kept, L - 1, 1))[0:1]
+    keep = []
+    for i in range(2):
+        value = jnp.sum(jnp.where(at == 4 * row + 2 * i, kept, 0.0), axis=1, keepdims=True)
+        keep.append(jnp.broadcast_to(value, (M, L)))
+        aux[2 + i] = keep[i]
+    aux[4] = keep[0] * keep[1]
+    lengths = seg_lengths.get()
+    start = jnp.int32(0)
+    here = (index[2] * M + row) * 4
+    shut = [here == index[3], here + 4 == index[3]]
+    for k in range(lengths.shape[0]):
+        shut = [shut[0] | (here == start), shut[1] | (here + 4 == start)]
+        start = start + 4 * lengths[k]
+    aux[0] = jnp.where(shut[0], 0.0, 1.0)
+    aux[1] = jnp.where(shut[1], 0.0, 1.0)
 
 
 def window_1(w2c, t, w):
@@ -502,19 +580,26 @@
     matrix_1_up(w1d.at[1], t, COLS1B)
 
 
-def window_swap(w2d, out, t, w):
-    matrix_2_down(w2d, t, w)
-    out.put(t)
-
-
-def correlate(coarse, fine, d):
+def window_swap(w2c, w2d, w1c, t2a, t2b, t1b, a, b, c, w):
+    matrix_2_down(w2d, a, w)
+    t2a.put(a)
+    matrix_2_up(w2c, b, w)
+    t2b.put(b)
+    matrix_1_up(w1c, c, 0)
+    t1b.put(c)
+
+
+def correlate(coarse, fine, d, spans=(slice(None),)):
     for k in range(R // CHUNK):
         span = slice(CHUNK * k, CHUNK * k + CHUNK)
         left, right = ready(coarse, k), ready(fine, k)
-        value = lax.dot_general(
-            left[span, :], right[span, :], (((0,), (0,)), ((), ())), preferred_element_type=F32
-        )
-        d[...] = value if k == 0 else d[...] + value
+        width = d.shape[0] // len(spans)
+        for i, columns in enumerate(spans):
+            out = slice(width * i, width * i + width)
+            value = lax.dot_general(
+                left[span, out], right[span, columns], (((0,), (0,)), ((), ())), preferred_element_type=F32
+            )
+            d[out, :] = value if k == 0 else d[out, :] + value
 
 
 def weight_2(d, out):
@@ -546,14 +631,14 @@
     for k in range(3):
         total = jnp.zeros((16, L), F32)
         for row in range(2):
-            tile = (2, 0, 1)[k] if row == 0 else (0, 1, 3)[k]
+            base, edge = TILES0[k + row]
+            base, edge = base - SPAN0[row].start, edge - SPAN0[row].start
             for p in range(16):
                 first = row * 256 + p * 16
                 span = slice(first, first + 16)
-                value = pltpu.roll(d[span, L * tile : L * tile + L], (1 - 2 * p) % L, 1)
+                value = pltpu.roll(d[span, base : base + L], (1 - 2 * p) % L, 1)
                 if p in (0, 15):
-                    rim = d[span, 512 + L * tile : 512 + L * tile + L]
-                    rim = pltpu.roll(rim, L - 31 if p == 0 else 3, 1)
+                    rim = pltpu.roll(d[span, edge : edge + L], L - 31 if p == 0 else 3, 1)
                     value = jnp.where(at == 0 if p == 0 else at >= 3, rim, value)
                 total = total + value
         if k > 0:
@@ -563,15 +648,14 @@
 
 
 def window_4(low, act, fine, out, d, kept):
-    correlate(low, fine, d)
+    correlate(low, fine, d, SPAN0)
     weight_1(d, kept, 0)
-    correlate(act, fine, d)
+    correlate(act, fine, d, SPAN0)
     weight_1(d, kept, 16)
     out.put(kept)
 
 
-def window_5(coarse, fine, w2c, t, out, d, w, kept):
-    matrix_2_up(w2c, t, w)
+def window_5(coarse, fine, out, d, kept):
     correlate(coarse, fine, d)
     weight_2(d, kept)
     out.put(kept)
@@ -580,8 +664,7 @@
 HALF = 144
 
 
-def window_6(index, coarse, fine, w1c, w1d, w2d, t, keep, give, d, kept):
-    matrix_1_up(w1c, t, 0)
+def window_6(index, coarse, fine, w1d, w2d, keep, give, d, kept):
     correlate(coarse, fine, d)
     weight_2(d, kept)
     even = index[1] == 0
@@ -596,7 +679,7 @@
 
 
 def window_7(coarse, fine, keep, got, bias, low, d, first):
-    correlate(coarse, fine, d)
+    correlate(coarse, fine, d, SPAN0)
     weight_1(d, first, 0)
     low[0:HALF, :] = (keep[...] + got[...]).astype(BF)
     low[HALF : HALF + 16, :] = first[...].astype(BF)
@@ -695,10 +778,12 @@
     pack_ends(wide, index, ends.at[0], ends.at[1], 2 * NJ)
     even = index[1] == 0
 
+    kept = frame_mask.get()
+
     def least(first, count):
-        value = frame_mask[first]
+        value = kept[first]
         for k in range(1, count):
-            value = jnp.minimum(value, frame_mask[first + k])
+            value = jnp.minimum(value, kept[first + k])
         return value.astype(F32)
 
     for i, (first, count) in enumerate(((0, 2), (2, 2), (0, 4))):
@@ -719,13 +804,13 @@
             span, stores = rows(j), []
             for half in range(2):
                 value = read(which, j, half)
-                stores.append((cat, span, slice(L * half, L * half + L), value.astype(BF)))
+                stores.append((cat, span, slice(256 + L * half, 384 + L * half), value.astype(BF)))
                 if half == 1:
                     moved = from_prev(value, left[rows(j, 8), L : 2 * L], a)
-                    stores.append((cat, span, slice(256, 384), moved.astype(BF)))
+                    stores.append((cat, span, slice(0, 128), moved.astype(BF)))
                 else:
                     moved = from_next(value, right[rows(j, 8), 0:L], a_next)
-                    stores.append((cat, span, slice(384, 512), moved.astype(BF)))
+                    stores.append((cat, span, slice(768, 896), moved.astype(BF)))
             put_all(stores)
 
         for_blocks(one, count)
@@ -757,7 +842,7 @@
         part = value * aux[2 + k // 2]
         return s1 + sum8(part), s2 + sum8(part * value)
 
-    stats = product_sums(cat, weights, False, use, lambda rs: zfar.put(z, (rs, slice(None))))
+    stats = product_sums(rows_from_0(cat, weights), use, lambda rs: zfar.put(z, (rs, slice(None))))
     pack_ends(z, index, cross, core)
     stats = fold(stack_rows(stats), 16)
     at = sub((8, L))
@@ -768,7 +853,7 @@
 
 def conv_two_kernel(
     index, z1, cross_in, core_in, mom1, prm, aux, t,
-    cross, core, mom, eb, hf, zfar, catfar, z2, cat, ef, lw, rw,
+    z2, cross, core, mom, eb, hf, zfar, catfar, cat, ef, lw, rw,
 ):
     mean, scale = norm_terms(mom1, mom1[2:3])
     gain, shift = prm[0:1], prm[1:2]
@@ -818,7 +903,9 @@
         part = value * aux[4]
         return s1 + sum8(part), s2 + sum8(part * value)
 
-    stats = product_sums(cat, weights, False, use, lambda rs: zfar.put(z2, (rs, slice(None))))
+    stats = product_sums(
+        lambda rs: [matmul(cat[rs, :], weights[...])], use, lambda rs: zfar.put(z2, (rs, slice(None)))
+    )
     pack_ends(z2, index, cross, core)
     pack_moments(mom, cross, fold(stack_rows(stats), 32))
 
@@ -834,7 +921,7 @@
             moved = from_prev(value, left[rows(j, 8), at], a)
             stores.append((cat, span, slice(256 + L * k, 384 + L * k), moved.astype(BF)))
             moved = from_next(value, right[rows(j, 8), at], a_next)
-            stores.append((cat, span, slice(512 + L * k, 640 + L * k), moved.astype(BF)))
+            stores.append((cat, span, slice(768 + L * k, 896 + L * k), moved.astype(BF)))
         put_all(stores)
 
     for_blocks(one)
@@ -843,7 +930,7 @@
 
 def up_two_kernel(
     index, z2, cross_in, core_in, mom1, mom2, prm, aux, t,
-    cross, core, mom, hf, act2, rectfar, rect, cat, lf, rf, lw, rw,
+    rect, cross, core, mom, hf, act2, rectfar, cat, lf, rf, lw, rw,
 ):
     mean, scale = norm_terms(mom2, mom1[3:4])
     gain, shift, bias = prm[2:3], prm[3:4], prm[6:7]
@@ -869,7 +956,7 @@
         part = value * aux[2 + k // 2]
         return s1 + sum8(part), s2 + sum8(part * value)
 
-    stats = product_sums(cat, weights, True, use, lambda rs: rectfar.put(rect, (rs, slice(None))))
+    stats = product_sums(rows_from_2(cat, weights), use, lambda rs: rectfar.put(rect, (rs, slice(None))))
     pack_moments(mom, cross, fold(stack_rows(stats), 16))
     pack_ends(rect, index, cross, core)
 
@@ -1081,7 +1168,7 @@
         stores.append((g3, rows(j), at, value))
         return s1 + sum8(value), s2 + sum8(value * (r[rows(j), at] - mean))
 
-    s1, s2 = product_sums(cat, weights, False, use)
+    s1, s2 = product_sums(rows_from_0(cat, weights), use)
     pack_ends(g3, index, cross, core)
     pack_moments(mom, cross, fold(stack_rows([s1, s2 * scale]), 16))
 
@@ -1148,7 +1235,7 @@
         stores.append((g2, rows(j), at, value))
         return s1 + sum8(value), s2 + sum8(value * xhat)
 
-    stats = fold(stack_rows(product_sums(cat, weights, False, use)), 32)
+    stats = fold(stack_rows(product_sums(lambda rs: [matmul(cat[rs, :], weights[...])], use)), 32)
     pack_ends(g2, index, cross, core)
     bias = fold(stack_rows([total_rows(bias)] * 3), 16)
     pack_moments(mom, cross, jnp.where(sub((8, L)) == 2, bias, stats))
@@ -1188,7 +1275,7 @@
         stores.append((g1, rows(j), at, value))
         return s1 + sum8(value), s2 + sum8(value * xhat)
 
-    stats = fold(stack_rows(product_sums(cat, weights, True, use)), 16)
+    stats = fold(stack_rows(product_sums(rows_from_2(cat, weights), use)), 16)
     pack_ends(g1, index, cross, core)
     pack_moments(mom, cross, stats)
 
@@ -1300,19 +1387,6 @@
 
 def swap(blocks, axis):
     return [blocks[0]] + [flip(blocks[k], axis, k) for k in range(1, len(blocks))]
-
-
-def flags(seg_lengths, frame_mask, position, total):
-    order = jnp.arange(seg_lengths.shape[0])
-    earlier = order[None, :] < order[:, None]
-    starts = 4 * jnp.sum(jnp.where(earlier, seg_lengths[None, :], 0), axis=1)
-    frames = (position * M + jnp.arange(M + 1, dtype=jnp.int32)) * 4
-    shut = jnp.any(frames[:, None] == starts[None, :], axis=1) | (frames == total)
-    a = 1.0 - shut.astype(F32)
-    keep_one = jnp.min(frame_mask.reshape(M, 2, 2), axis=2).astype(F32)
-    keep_two = jnp.min(frame_mask.reshape(M, 4), axis=1).astype(F32)
-    columns = jnp.stack([a[:M], a[1:], keep_one[:, 0], keep_one[:, 1], keep_two])
-    return jnp.broadcast_to(columns[:, :, None], (5, M, L))
 
 
 def per_device(
@@ -1336,25 +1410,10 @@
     position = lax.axis_index("tm")
     stems = lax.axis_size("stem")
     odd = position % 2
-    index = jnp.stack([lax.axis_index("stem"), odd]).astype(jnp.int32)
+    total = mixture.shape[1] * lax.axis_size("tm")
+    index = jnp.stack([lax.axis_index("stem"), odd, position, total]).astype(jnp.int32)
     frames = mixture.shape[1]
     per, blocks = R // stems, NJ // stems
-    aux = flags(seg_lengths, frame_mask, position, frames * lax.axis_size("tm"))
-    prm = jnp.stack(
-        [
-            jnp.tile(encoder_gain_vector[0], 8),
-            jnp.tile(shift_first[0], 8),
-            jnp.tile(gain_second[0], 4),
-            jnp.tile(shift_second[0], 4),
-            jnp.tile(decoder_gain_vector[0], 8),
-            jnp.tile(shift_third[0], 8),
-            jnp.tile(bias_second[0], 8),
-            jnp.tile(jnp.repeat(bias_first[0], 32), 2),
-        ]
-    )
-    w1c = jnp.tile(conv_first[0].transpose(2, 3, 1, 0).reshape(50, 16).astype(F32), (1, 8))
-    w1d = deconv_first[0].transpose(2, 3, 0, 1).reshape(50, 2, 16).astype(F32)
-    w1d = jnp.tile(w1d.transpose(1, 0, 2), (1, 1, 8))
     w2c = conv_second[0].transpose(2, 3, 1, 0).reshape(400, 32)
     w2d = deconv_second[0].transpose(2, 3, 0, 1).reshape(400, 32)
     edge = 2 * NJ + 16
@@ -1371,16 +1430,27 @@
     def far(*shape, kind=F32):
         return [(shape, kind, True)]
 
-    cross, core, x0, c0 = run(
+    raw = [conv_first[0].transpose(2, 3, 1, 0).reshape(25, 2, 16)]
+    raw += [deconv_first[0].transpose(2, 3, 0, 1).reshape(25, 2, 32)]
+    raw += [encoder_gain_vector, shift_first, gain_second, shift_second]
+    raw += [decoder_gain_vector, shift_third, bias_second, bias_first]
+    cross, core, x0, c0, *raw = run(
         layout_kernel,
         "layout",
         [((edge, 256), BF), ((edge, 256), BF), ((R, 256), BF), ((R, 256), BF)],
-        [index, frame_mask, Far(mixture), Far(cotangent)],
+        [index, Far(frame_mask), Far(mixture), Far(cotangent)],
         [((2, frames, L), F32), ((2 * R, 256), F32), ((2, edge, 256), F32)],
+        fetch=[Far(frame_mask.reshape(1, 4 * M))] + [Far(v) for v in raw],
     )
     near = lax.ppermute(cross, "tm", pairs(lax.axis_size("tm"), -1))
     inside = flip(core, "tm", 1)
-    t, x0_far, c0 = run(window_0, "window_0", [((COLS0, 512), BF)], [w1c], store=[x0, c0])
+    t, w1c, w1d, aux, prm, x0_far, c0 = run(
+        window_0,
+        "window_0",
+        [((COLS0, 512), BF), ((56, L), F32), ((2, 56, L), F32), ((5, M, L), F32), ((8, L), F32)],
+        [index, Far(seg_lengths), *raw],
+        store=[x0, c0],
+    )
     cross, core, mom, kept, hx, cat0, z1 = run(
         conv_one_kernel,
         "conv_one",
@@ -1402,15 +1472,15 @@
             token=token,
         ),
     )
-    cross, core, mom, ends1, h1, z2, cat1 = run(
+    z2_here, cross, core, mom, ends1, h1, z2, cat1 = run(
         conv_two_kernel,
         "conv_two",
-        packet(256) + [((4, NJ, 512), BF), ((2, NJ, 512), F32)] + far(R, 256) + far(R, COLS1, kind=BF),
+        [((R, 256), F32)] + packet(256) + [((4, NJ, 512), BF), ((2, NJ, 512), F32)] + far(R, 256) + far(R, COLS1, kind=BF),
         [index, z1_here, near, inside, mom1, prm, aux, t],
-        [((R, 256), F32), ((R, COLS1), BF), ((4, NJ, 512), F32)] + wide(512),
+        [((R, COLS1), BF), ((4, NJ, 512), F32)] + wide(512),
         flops=2 * R * COLS1 * 256,
     )
-    near, inside, mom2, (t, z2_here, ends1, h1) = exchange(
+    near, inside, mom2, (t, ends1, h1) = exchange(
         cross, core, mom, "tm",
         lambda token: run(
             window_2,
@@ -1418,27 +1488,26 @@
             [((512, COLS2), BF)],
             [w2d],
             [((400, L), F32)],
-            fetch=[Far(z2)],
             store=[ends1, h1],
             token=token,
         ),
     )
-    cross, core, mom, h2, act2, rect = run(
+    rect_here, cross, core, mom, h2, act2, rect = run(
         up_two_kernel,
         "up_two",
-        packet(512) + [((2, NJ, 256), F32), ((R, 256), BF)] + far(R, 512),
+        [((R, 512), F32)] + packet(512) + [((2, NJ, 256), F32), ((R, 256), BF)] + far(R, 512),
         [index, z2_here, near, inside, mom1, mom2, prm, aux, t],
-        [((R, 512), F32), ((R, COLS2), BF)] + rim(256) + wide(256),
+        [((R, COLS2), BF)] + rim(256) + wide(256),
         flops=2 * R * COLS2 * 512,
     )
-    near, inside, mom3, (t, rect_here, cat1_here, ends1_here, h2, act2) = exchange(
+    near, inside, mom3, (t, cat1_here, ends1_here, h2, act2) = exchange(
         cross, core, mom, "tm",
         lambda token: run(
             window_3,
             "window_3",
             [((256, 2 * COLS1B), BF)],
             [w1d],
-            fetch=[Far(rect), Far(cat1, COLS1B), Far(ends1)],
+            fetch=[Far(cat1, COLS1B), Far(ends1)],
             store=[h2, act2],
             token=token,
         ),
@@ -1452,12 +1521,12 @@
         [((R, COLS1B), BF)] + rim(512) + [((2, NJ, 512), F32), ((16, 256), F32)] + wide(512),
         flops=2 * R * 2 * COLS1B * 256,
     )
-    t2a_d, c0_here, x0_here, hx_here, h3, low3, sig, sigh = run(
+    t2a_d, t2b_c, t1b_c, c0_here, x0_here, hx_here, h3, low3, sig, sigh = run(
         window_swap,
         "window_swap",
-        far(COLS1, 256, kind=BF),
-        [w2d],
-        [((COLS1, 256), BF), ((400, L), F32)],
+        far(COLS1, 256, kind=BF) + far(512, COLS2, kind=BF) + far(256, COLS1B, kind=BF),
+        [w2c, w2d, w1c],
+        [((COLS1, 256), BF), ((512, COLS2), BF), ((256, COLS1B), BF), ((400, L), F32)],
         fetch=[Far(c0), Far(x0_far), Far(hx)],
         store=[h3, low3, sig, sigh],
     )
@@ -1494,7 +1563,7 @@
             "window_4",
             far(32, L),
             [Far(low3, parts=2), Far(cat1, 512, parts=2), cat0g],
-            [((512, COLS0), F32), ((32, L), F32)],
+            [((512, 768), F32), ((32, L), F32)],
             flops=2 * R * COLS0 * 1024,
             fetch=[Far(rect), Far(t2a_d), Far(h3), Far(z2)],
             store=[gact],
@@ -1509,16 +1578,16 @@
         rim(512) + wide(512),
         flops=2 * R * COLS1 * 256,
     )
-    near, inside, mom5, (t, w2d_grad, z2_here, h2_here, gact_here, z1_here) = exchange(
+    near, inside, mom5, (w2d_grad, z2_here, t, h2_here, gact_here, z1_here) = exchange(
         cross, core, mom, "tm",
         lambda token: run(
             window_5,
             "window_5",
-            [((512, COLS2), BF)] + far(128, L),
-            [Far(act2), cat1g, w2c],
-            [((256, COLS1), F32), ((400, L), F32), ((128, L), F32)],
+            far(128, L),
+            [Far(act2, parts=2), cat1g],
+            [((256, COLS1), F32), ((128, L), F32)],
             flops=2 * R * COLS1 * 256,
-            fetch=[Far(z2), Far(h2), Far(gact), Far(z1)],
+            fetch=[Far(z2), Far(t2b_c), Far(h2), Far(gact), Far(z1)],
             token=token,
         ),
     )
@@ -1530,16 +1599,16 @@
         [((R, COLS2), BF)] + rim(256) + wide(256),
         flops=2 * R * COLS2 * 512,
     )
-    near, inside, mom6, (t, keep, give, z1_here, h1_here, cat0_here) = exchange(
+    near, inside, mom6, (keep, give, t, z1_here, h1_here, cat0_here) = exchange(
         cross, core, mom, "tm",
         lambda token: run(
             window_6,
             "window_6",
-            [((256, COLS1B), BF), ((HALF, L), F32), ((HALF, L), F32)],
-            [index, low2, Far(cat1, parts=2), w1c, Far(w1d_grad), Far(w2d_grad)],
+            [((HALF, L), F32), ((HALF, L), F32)],
+            [index, low2, Far(cat1, parts=2), Far(w1d_grad), Far(w2d_grad)],
             [((256, COLS1), F32), ((128, L), F32)],
             flops=2 * R * COLS1 * 256,
-            fetch=[Far(z1), Far(h1), Far(cat0)],
+            fetch=[Far(t1b_c), Far(z1), Far(h1), Far(cat0)],
             token=token,
         ),
     )
@@ -1558,7 +1627,7 @@
         "window_7",
         [((HALF + 32, L), BF)],
         [low1, cat0_here, keep, got, bias_one],
-        [((512, COLS0), F32), ((16, L), F32)],
+        [((512, 768), F32), ((16, L), F32)],
         flops=2 * R * COLS0 * 512,
         fetch=[Far(direct)],
     )

time: 150 us -> 144 us (0.960)
  local copies, waits for them, and re-layouts: 5.22 us -> 2.59 us
  other arithmetic: 2.52 us -> 0.16 us
  Pallas kernels: 75.5 us -> 73.7 us
  waiting for transfers between devices: 16.5 us -> 18 us
    ppermute x6, starting transfers between devices: 10.1 us -> 13.3 us  [exchange(): near = lax.ppermute(cross, axis, pairs(count, -1))]
    ppermute x33, waiting for transfers between devices: 14.9 us -> 17.9 us  [flip(): lax.ppermute(values, axis, [(i, i ^ bit) for i in range(lax.axis_size(axi...]
    ppermute x33, starting transfers between devices: 30.1 us -> 28.2 us  [flip(): lax.ppermute(values, axis, [(i, i ^ bit) for i in range(lax.axis_size(axi...]
    pallas_call x22, Pallas kernels: 75.5 us -> 73.7 us  [run(): pl.pallas_call(body, out_shape=[pltpu.HBM(o[0], o[1]) if len(o) == 3 else...]
    ppermute x6, starting transfers between devices: 3.53 us -> 1.96 us  [exchange(): far = lax.ppermute(mom, axis, pairs(count, 3))]
    ppermute x6, waiting for transfers between devices: 1.56 us -> 0.02 us  [exchange(): near = lax.ppermute(cross, axis, pairs(count, -1))]
  transfers between devices with their start and end apart: 46 -> 46, of which waited for: 11 -> 13; matrix products, arithmetic and copies ran while one was open for 4% -> 1% of each run, Pallas kernels for 23% -> 24%
where the time goes in v5:
time: 144 us
  Pallas kernels  73.7 us (51%)
  starting transfers between devices  48 us (33%)
  waiting for transfers between devices  18 us (12%)
  local copies, waits for them, and re-layouts  2.59 us (2%)
    pallas_call x22, Pallas kernels, run(): pl.pallas_call(body, out_shape=[pltpu.HBM(o[0], o[1]) if len(o) == 3 else...  73.7 us
    ppermute x33, starting transfers between devices, flip(): lax.ppermute(values, axis, [(i, i ^ bit) for i in range(lax.axis_size(axi...  28.2 us
    ppermute x33, waiting for transfers between devices, flip(): lax.ppermute(values, axis, [(i, i ^ bit) for i in range(lax.axis_size(axi...  17.9 us
    ppermute x6, starting transfers between devices, exchange(): near = lax.ppermute(cross, axis, pairs(count, -1))  13.3 us
    ppermute x1, starting transfers between devices, per_device(): near = lax.ppermute(cross, 'tm', pairs(lax.axis_size('tm'), -1))  4.55 us
  transfers between devices with their start and end apart: 46, of which 13 were waited for; matrix products, arithmetic and copies ran while one was open for 1% of the time, Pallas kernels for 24%

profile of v5, /device:TPU:0, one launch (start us, length us, event | category | flops | bytes accessed | tf_op | source)
XLA Modules:
  0.0 143.6 jit_solution(12387214743062208156)
XLA Ops:
  0.7 3.8 %layout.1 = (bf16[80,256]{1,0:T(8,128)(2,1)S(1)}, bf16[80,256]{1,0:T(8,128)(2,1)S(1)}, bf16[1024,256]{1,0:T(8,128)(2,1)S(1)}, bf16[1024,256]{1,0:T(8,128)(2,1)S(...) custom-call(s32[4]{0:T(128)S(1)} %pad_add_fusion.refs_0_, ...), custom_call_target="tpu_custom_call" | custom-call | bytes 2188992 | tf_op jit(solution)/shard_map/layout/pallas_call | solution.py:137
  4.6 4.6 %collective-permute-start = (bf16[80,256]{1,0:T(8,128)(2,1)S(1)}, bf16[80,256]{1,0:T(8,128)(2,1)S(1)}, u32[]{:S(2)}, u32[]{:S(2)}) collective-permute-start(bf16[80,256]{1,0:T(8,128)(2,1)S(1)} %get-tuple-element.155), channel_id=1, source_target_pairs={{0,7},{2,1},{4,3},{6,5},{7,0},{1,2},{3,4},{5,6},{8,15},{10,9},{12,... | collective-permute-start | bytes 122888 | tf_op jit(solution)/shard_map/ppermute | solution.py:1445
  10.9 3.3 %conv_one.1 = (f32[40,512]{1,0:T(8,128)S(1)}, f32[32,512]{1,0:T(8,128)S(1)}, f32[8,128]{1,0:T(8,128)S(1)}, f32[8,128]{1,0:T(8,128)S(1)}, f32[64,256]{1,0:T(8,128...) custom-call(s32[4]{0:T(128)S(1)} %pad_add_fusion.refs_0_, ...), custom_call_target="tpu_custom_call" | custom-call | flops 1073741824 | bytes 6152208 | tf_op jit(solution)/shard_map/conv_one/pallas_call | solution.py:137
  14.2 3.5 %collective-permute-start.2 = (f32[40,512]{1,0:T(8,128)S(1)}, f32[40,512]{1,0:T(8,128)S(1)}, u32[]{:S(2)}, u32[]{:S(2)}) collective-permute-start(f32[40,512]{1,0:T(8,128)S(1)} %get-tuple-element.176), channel_id=1, source_target_pairs={{0,7},{2,1},{4,3},{6,5},{7,0},{1,2},{3,4},{5,6},{8,15},{10,9},{12,... | collective-permute-start | bytes 245768 | tf_op jit(solution)/shard_map/ppermute | solution.py:1375
  18.4 2.5 %window_1.1 = (bf16[1920,256]{1,0:T(8,128)(2,1)S(1)}, f32[1024,512]{1,0:T(8,128)S(1)}, f32[64,256]{1,0:T(8,128)}, bf16[1024,1024]{1,0:T(8,128)(2,1)}, f32[8,128]{1,0:T(8,128)S(1)}) custom-call(bf16[400,32]{1,0:T(8,128)(2,1)S(1)} %bitcast.46, f32[1024,512]{1,0:T(8,128)} %get-tuple-element.171.refs_1_.refs_6_, f32[64,256]{1,0:T(8,128)S(1)} %get-tuple-element.172.refs_2_, ...), custom_call_target="tpu_custom_call" | custom-call | bytes 9536512 | tf_op jit(solution)/shard_map/window_1/pallas_call | solution.py:137
  23.5 5.1 %conv_two.1 = (f32[1024,256]{1,0:T(8,128)S(1)}, f32[40,256]{1,0:T(8,128)S(1)}, f32[32,256]{1,0:T(8,128)S(1)}, f32[8,128]{1,0:T(8,128)S(1)}, bf16[4,32,512]{2,1,0...) custom-call(s32[4]{0:T(128)S(1)} %pad_add_fusion.refs_0_, ...), custom_call_target="tpu_custom_call" | custom-call | flops 1006632960 | bytes 9433104 | tf_op jit(solution)/shard_map/conv_two/pallas_call | solution.py:137
  28.6 2.1 %collective-permute-start.7 = (f32[40,256]{1,0:T(8,128)S(1)}, f32[40,256]{1,0:T(8,128)S(1)}, u32[]{:S(2)}, u32[]{:S(2)}) collective-permute-start(f32[40,256]{1,0:T(8,128)S(1)} %get-tuple-element.182), channel_id=1, source_target_pairs={{0,7},{2,1},{4,3},{6,5},{7,0},{1,2},{3,4},{5,6},{8,15},{10,9},{12,... | collective-permute-start | bytes 122888 | tf_op jit(solution)/shard_map/ppermute | solution.py:1375
  37.1 5.1 %up_two.1 = (f32[1024,512]{1,0:T(8,128)S(1)}, f32[40,512]{1,0:T(8,128)S(1)}, f32[32,512]{1,0:T(8,128)S(1)}, f32[8,128]{1,0:T(8,128)S(1)}, f32[2,32,256]{2,1,0:T(...) custom-call(s32[4]{0:T(128)S(1)} %pad_add_fusion.refs_0_, f32[1024,256]{1,0:T(8,128)S(1)} %get-tuple-element.181.refs_1_, ...), custom_call_target="tpu_custom_call" | custom-call | flops 1207959552 | bytes 7268368 | tf_op jit(solution)/shard_map/up_two/pallas_call | solution.py:137
  43.8 2.5 %collective-permute-start.15 = (f32[8,128]{1,0:T(8,128)S(1)}, f32[8,128]{1,0:T(8,128)S(1)}, u32[]{:S(2)}, u32[]{:S(2)}) collective-permute-start(f32[8,128]{1,0:T(8,128)S(1)} %get-tuple-element.197.refs_5_), channel_id=1, source_target_pairs={{0,4},{1,5},{2,6},{3,7},{4,0},{5,1},{6,2},{7,3},{8,12},{9,13},{10,... | collective-permute-start | bytes 12296 | tf_op jit(solution)/shard_map/ppermute | solution.py:1341
  46.4 2.3 %window_3.1 = (bf16[256,3072]{1,0:T(8,128)(2,1)S(1)}, bf16[1024,1536]{1,0:T(8,128)(2,1)S(1)}, bf16[4,32,512]{2,1,0:T(8,128)(2,1)S(1)}, f32[2,32,256]{2,1,0:T(8,1...) custom-call(f32[2,56,128]{2,1,0:T(8,128)S(1)} %get-tuple-element.192.refs_0_.refs_6_, ...), custom_call_target="tpu_custom_call" | custom-call | bytes 9967616 | tf_op jit(solution)/shard_map/window_3/pallas_call | solution.py:137
  50.2 4.6 %up_one.1 = (bf16[272,256]{1,0:T(8,128)(2,1)S(1)}, bf16[272,256]{1,0:T(8,128)(2,1)S(1)}, bf16[272,256]{1,0:T(8,128)(2,1)S(1)}, bf16[272,256]{1,0:T(8,128)(2,1)S(...) custom-call(s32[4]{0:T(128)S(1)} %pad_add_fusion.refs_0_, ...), custom_call_target="tpu_custom_call" | custom-call | flops 1610612736 | bytes 9879568 | tf_op jit(solution)/shard_map/up_one/pallas_call | solution.py:137
  58.4 3.4 %window_swap.1 = (bf16[1920,256]{1,0:T(8,128)(2,1)}, bf16[512,1152]{1,0:T(8,128)(2,1)}, bf16[256,1536]{1,0:T(8,128)(2,1)}, bf16[1024,256]{1,0:T(8,128)(2,1)S(1)}...) custom-call(bf16[400,32]{1,0:T(8,128)(2,1)S(1)} %bitcast.47, ...), custom_call_target="tpu_custom_call" | custom-call | bytes 9652224 | tf_op jit(solution)/shard_map/window_swap/pallas_call | solution.py:137
  61.8 3.2 %collective-permute-done.18.refs_3_ = bf16[272,256]{1,0:T(8,128)(2,1)S(1)} collective-permute-done((bf16[272,256]{1,0:T(8,128)(2,1)S(1)}, bf16[272,256]{1,0:T(8,128)(2,1)S(1)}, u32[]{:S(2)}, u32[]{:S(2)}) %collective-permute-start.18) | collective-permute-done | bytes 139296 | tf_op jit(solution)/shard_map/ppermute | solution.py:1341
  69.8 3.9 %estimate.1 = (bf16[4,2,128,256]{3,2,1,0:T(8,128)(2,1)}, bf16[1024,1024]{1,0:T(8,128)(2,1)S(1)}, f32[1024,256]{1,0:T(8,128)S(1)}, f32[32,256]{1,0:T(8,128)S(1)},...) custom-call(s32[4]{0:T(128)S(1)} %pad_add_fusion.refs_0_, bf16[272,256]{1,0:T(8,128)(2,1)S(1)} %get-tuple-element.202.refs_1_, ...), custom_call_target="tpu_custom_call" | custom-call | bytes 10119184 | tf_op jit(solution)/shard_map/estimate/pallas_call | solution.py:137
  75.3 4.1 %down_one_back.1 = (f32[1024,512]{1,0:T(8,128)S(1)}, bf16[1024,1024]{1,0:T(8,128)(2,1)S(1)}, f32[40,512]{1,0:T(8,128)S(1)}, f32[32,512]{1,0:T(8,128)S(1)}, f32[8...) custom-call(s32[4]{0:T(128)S(1)} %pad_add_fusion.refs_0_, ...), custom_call_target="tpu_custom_call" | custom-call | flops 2147483648 | bytes 12369936 | tf_op jit(solution)/shard_map/down_one_back/pallas_call | solution.py:137
  81.1 2.2 %collective-permute-start.23 = (f32[40,512]{1,0:T(8,128)S(1)}, f32[40,512]{1,0:T(8,128)S(1)}, u32[]{:S(2)}, u32[]{:S(2)}) collective-permute-start(f32[40,512]{1,0:T(8,128)S(1)} %get-tuple-element.231), channel_id=1, source_target_pairs={{0,7},{2,1},{4,3},{6,5},{7,0},{1,2},{3,4},{5,6},{8,15},{10,9},{12,... | collective-permute-start | bytes 245768 | tf_op jit(solution)/shard_map/ppermute | solution.py:1375
  83.3 5.1 %window_4.1 = (f32[32,128]{1,0:T(8,128)}, f32[1024,512]{1,0:T(8,128)S(1)}, bf16[1920,256]{1,0:T(8,128)(2,1)S(1)}, f32[2,32,512]{2,1,0:T(8,128)S(1)}, f32[1024,25...) custom-call(bf16[1024,512]{1,0:T(8,128)(2,1)} %get-tuple-element.233.refs_0_, ...), custom_call_target="tpu_custom_call" | custom-call | flops 2147483648 | bytes 19689472 | tf_op jit(solution)/shard_map/window_4/pallas_call | solution.py:137
  89.9 5.3 %up_two_back.1 = (f32[1024,256]{1,0:T(8,128)S(1)}, bf16[1024,1920]{1,0:T(8,128)(2,1)S(1)}, f32[40,256]{1,0:T(8,128)S(1)}, f32[32,256]{1,0:T(8,128)S(1)}, f32[8,128]{1,0:T(8,128)S(1)}) custom-call(s32[4]{0:T(128)S(1)} %pad_add_fusion.refs_0_, f32[1024,512]{1,0:T(8,128)S(1)} %get-tuple-element.230.refs_1_, f32[40,512]{1,0:T(8,128)S(1)} %collective-permute-done.23.refs_2_, ...), custom_call_target="tpu_custom_call" | custom-call | flops 1006632960 | bytes 11669520 | tf_op jit(solution)/shard_map/up_two_back/pallas_call | solution.py:137
  99.8 3.6 %window_5.1 = (f32[128,128]{1,0:T(8,128)}, f32[1024,256]{1,0:T(8,128)S(1)}, bf16[512,1152]{1,0:T(8,128)(2,1)S(1)}, f32[2,32,256]{2,1,0:T(8,128)S(1)}, f32[1024,5...) custom-call(bf16[1024,256]{1,0:T(8,128)(2,1)} %get-tuple-element.249.refs_0_, ...), custom_call_target="tpu_custom_call" | custom-call | flops 1006632960 | bytes 17442816 | tf_op jit(solution)/shard_map/window_5/pallas_call | solution.py:137
  104.7 4.6 %down_two_back.1 = (f32[1024,512]{1,0:T(8,128)S(1)}, bf16[1024,256]{1,0:T(8,128)(2,1)S(1)}, f32[40,512]{1,0:T(8,128)S(1)}, f32[32,512]{1,0:T(8,128)S(1)}, f32[8,128]{1,0:T(8,128)S(1)}) custom-call(s32[4]{0:T(128)S(1)} %pad_add_fusion.refs_0_, f32[1024,256]{1,0:T(8,128)S(1)} %get-tuple-element.246.refs_1_, f32[40,256]{1,0:T(8,128)S(1)} %collective-permute-done.28.refs_2_, ...), custom_call_target="tpu_custom_call" | custom-call | flops 1207959552 | bytes 10485776 | tf_op jit(solution)/shard_map/down_two_back/pallas_call | solution.py:137
  113.6 4.7 %window_6.1 = (f32[144,128]{1,0:T(8,128)S(1)}, f32[144,128]{1,0:T(8,128)S(1)}, bf16[256,1536]{1,0:T(8,128)(2,1)S(1)}, f32[1024,512]{1,0:T(8,128)S(1)}, f32[2,32,...) custom-call(s32[4]{0:T(128)S(1)} %pad_add_fusion.refs_0_, ...), custom_call_target="tpu_custom_call" | custom-call | flops 1006632960 | bytes 14790672 | tf_op jit(solution)/shard_map/window_6/pallas_call | solution.py:137
  119.6 3.3 %up_one_back.1 = (bf16[256,256]{1,0:T(8,128)(2,1)S(1)}, bf16[256,256]{1,0:T(8,128)(2,1)S(1)}, bf16[256,256]{1,0:T(8,128)(2,1)S(1)}, bf16[256,256]{1,0:T(8,128)(2,1)S(1)}, bf16[1024,512]{1,0:T(8,128)(2,1)S(1)}) custom-call(s32[4]{0:T(128)S(1)} %pad_add_fusion.refs_0_, f32[1024,512]{1,0:T(8,128)S(1)} %get-tuple-element.261.refs_1_, ...), custom_call_target="tpu_custom_call" | custom-call | flops 805306368 | bytes 6930448 | tf_op jit(solution)/shard_map/up_one_back/pallas_call | solution.py:137
  128.7 2.3 %collective-permute-start.44 = (bf16[176,128]{1,0:T(8,128)(2,1)S(1)}, bf16[176,128]{1,0:T(8,128)(2,1)S(1)}, u32[]{:S(2)}, u32[]{:S(2)}) collective-permute-start(bf16[176,128]{1,0:T(8,128)(2,1)S(1)} %get-tuple-element.286.refs_5_), channel_id=1, source_target_pairs={{0,6},{1,7},{2,4},{3,5},{4,2},{5,3},{6,0},{7,1},{8,14},{9,15},{10,... | collective-permute-start | bytes 135176 | tf_op jit(solution)/shard_map/ppermute | solution.py:1341
  134.5 4.1 %collective-permute-done.39.refs_2_ = bf16[256,256]{1,0:T(8,128)(2,1)S(1)} collective-permute-done((bf16[256,256]{1,0:T(8,128)(2,1)S(1)}, bf16[256,256]{1,0:T(8,128)(2,1)S(1)}, u32[]{:S(2)}, u32[]{:S(2)}) %collective-permute-start.39) | collective-permute-done | bytes 131104 | tf_op jit(solution)/shard_map/ppermute | solution.py:1341
  (113 shorter events, 53.2 us)
Async XLA Ops:
  14.2 8.0 %collective-permute-start.2 = (f32[40,512]{1,0:T(8,128)S(1)}, f32[40,512]{1,0:T(8,128)S(1)}, u32[]{:S(2)}, u32[]{:S(2)}) collective-permute-start(f32[40,512]{1,0:T(8,128)S(1)} %get-tuple-element.176), channel_id=1, source_target_pairs={{0,7},{2,1},{4,3},{6,5},{7,0},{1,2},{3,4},{5,6},{8,15},{10,9},{12,... | collective-permute-start | bytes 245768 | tf_op jit(solution)/shard_map/ppermute | solution.py:1375
  28.6 6.7 %collective-permute-start.7 = (f32[40,256]{1,0:T(8,128)S(1)}, f32[40,256]{1,0:T(8,128)S(1)}, u32[]{:S(2)}, u32[]{:S(2)}) collective-permute-start(f32[40,256]{1,0:T(8,128)S(1)} %get-tuple-element.182), channel_id=1, source_target_pairs={{0,7},{2,1},{4,3},{6,5},{7,0},{1,2},{3,4},{5,6},{8,15},{10,9},{12,... | collective-permute-start | bytes 122888 | tf_op jit(solution)/shard_map/ppermute | solution.py:1375
  42.2 6.5 %collective-permute-start.12 = (f32[40,512]{1,0:T(8,128)S(1)}, f32[40,512]{1,0:T(8,128)S(1)}, u32[]{:S(2)}, u32[]{:S(2)}) collective-permute-start(f32[40,512]{1,0:T(8,128)S(1)} %get-tuple-element.190), channel_id=1, source_target_pairs={{0,7},{2,1},{4,3},{6,5},{7,0},{1,2},{3,4},{5,6},{8,15},{10,9},{12,... | collective-permute-start | bytes 245768 | tf_op jit(solution)/shard_map/ppermute | solution.py:1375
  54.8 7.0 %collective-permute-start.17 = (bf16[272,256]{1,0:T(8,128)(2,1)S(1)}, bf16[272,256]{1,0:T(8,128)(2,1)S(1)}, u32[]{:S(2)}, u32[]{:S(2)}) collective-permute-start(bf16[272,256]{1,0:T(8,128)(2,1)S(1)} %get-tuple-element.203), channel_id=1, source_target_pairs={{0,8},{8,0},{16,24},{24,16},{1,9},{9,1},{17,25},{25,17},{2,10},{10... | collective-permute-start | bytes 417800 | tf_op jit(solution)/shard_map/ppermute | solution.py:1341
  56.4 8.6 %collective-permute-start.18 = (bf16[272,256]{1,0:T(8,128)(2,1)S(1)}, bf16[272,256]{1,0:T(8,128)(2,1)S(1)}, u32[]{:S(2)}, u32[]{:S(2)}) collective-permute-start(bf16[272,256]{1,0:T(8,128)(2,1)S(1)} %get-tuple-element.204), channel_id=1, source_target_pairs={{0,16},{8,24},{16,0},{24,8},{1,17},{9,25},{17,1},{25,9},{2,18},{10... | collective-permute-start | bytes 417800 | tf_op jit(solution)/shard_map/ppermute | solution.py:1341
  57.9 7.1 %collective-permute-start.19 = (bf16[272,256]{1,0:T(8,128)(2,1)S(1)}, bf16[272,256]{1,0:T(8,128)(2,1)S(1)}, u32[]{:S(2)}, u32[]{:S(2)}) collective-permute-start(bf16[272,256]{1,0:T(8,128)(2,1)S(1)} %get-tuple-element.205), channel_id=1, source_target_pairs={{0,24},{8,16},{16,8},{24,0},{1,25},{9,17},{17,9},{25,1},{2,26},{10... | collective-permute-start | bytes 417800 | tf_op jit(solution)/shard_map/ppermute | solution.py:1341
  66.2 7.5 %collective-permute-start.20 = (bf16[272,256]{1,0:T(8,128)(2,1)S(1)}, bf16[272,256]{1,0:T(8,128)(2,1)S(1)}, u32[]{:S(2)}, u32[]{:S(2)}) collective-permute-start(bf16[272,256]{1,0:T(8,128)(2,1)S(1)} %get-tuple-element.223), channel_id=1, source_target_pairs={{0,8},{8,0},{16,24},{24,16},{1,9},{9,1},{17,25},{25,17},{2,10},{10... | collective-permute-start | bytes 417800 | tf_op jit(solution)/shard_map/ppermute | solution.py:1341
  67.5 7.8 %collective-permute-start.21 = (bf16[272,256]{1,0:T(8,128)(2,1)S(1)}, bf16[272,256]{1,0:T(8,128)(2,1)S(1)}, u32[]{:S(2)}, u32[]{:S(2)}) collective-permute-start(bf16[272,256]{1,0:T(8,128)(2,1)S(1)} %get-tuple-element.224), channel_id=1, source_target_pairs={{0,16},{8,24},{16,0},{24,8},{1,17},{9,25},{17,1},{25,9},{2,18},{10... | collective-permute-start | bytes 417800 | tf_op jit(solution)/shard_map/ppermute | solution.py:1341
  68.3 7.0 %collective-permute-start.22 = (bf16[272,256]{1,0:T(8,128)(2,1)S(1)}, bf16[272,256]{1,0:T(8,128)(2,1)S(1)}, u32[]{:S(2)}, u32[]{:S(2)}) collective-permute-start(bf16[272,256]{1,0:T(8,128)(2,1)S(1)} %get-tuple-element.225), channel_id=1, source_target_pairs={{0,24},{8,16},{16,8},{24,0},{1,25},{9,17},{17,9},{25,1},{2,26},{10... | collective-permute-start | bytes 417800 | tf_op jit(solution)/shard_map/ppermute | solution.py:1341
  79.4 9.1 %collective-permute-start.25 = (f32[8,128]{1,0:T(8,128)S(1)}, f32[8,128]{1,0:T(8,128)S(1)}, u32[]{:S(2)}, u32[]{:S(2)}) collective-permute-start(f32[8,128]{1,0:T(8,128)S(1)} %get-tuple-element.239.refs_8_), channel_id=1, source_target_pairs={{0,3},{2,5},{4,7},{6,1},{3,0},{5,2},{7,4},{1,6},{8,11},{10,13},{12... | collective-permute-start | bytes 12296 | tf_op jit(solution)/shard_map/ppermute | solution.py:1377
  79.5 9.0 %collective-permute-start.26 = (f32[8,128]{1,0:T(8,128)S(1)}, f32[8,128]{1,0:T(8,128)S(1)}, u32[]{:S(2)}, u32[]{:S(2)}) collective-permute-start(f32[8,128]{1,0:T(8,128)S(1)} %get-tuple-element.239.refs_8_), channel_id=1, source_target_pairs={{0,4},{1,5},{2,6},{3,7},{4,0},{5,1},{6,2},{7,3},{8,12},{9,13},{10,... | collective-permute-start | bytes 12296 | tf_op jit(solution)/shard_map/ppermute | solution.py:1341
  81.1 7.4 %collective-permute-start.23 = (f32[40,512]{1,0:T(8,128)S(1)}, f32[40,512]{1,0:T(8,128)S(1)}, u32[]{:S(2)}, u32[]{:S(2)}) collective-permute-start(f32[40,512]{1,0:T(8,128)S(1)} %get-tuple-element.231), channel_id=1, source_target_pairs={{0,7},{2,1},{4,3},{6,5},{7,0},{1,2},{3,4},{5,6},{8,15},{10,9},{12,... | collective-permute-start | bytes 245768 | tf_op jit(solution)/shard_map/ppermute | solution.py:1375
  83.3 6.6 %collective-permute-start.24 = (f32[32,512]{1,0:T(8,128)S(1)}, f32[32,512]{1,0:T(8,128)S(1)}, u32[]{:S(2)}, u32[]{:S(2)}) collective-permute-start(f32[32,512]{1,0:T(8,128)S(1)} %get-tuple-element.232), channel_id=1, source_target_pairs={{0,1},{1,0},{2,3},{3,2},{4,5},{5,4},{6,7},{7,6},{8,9},{9,8},{10,11... | collective-permute-start | bytes 196616 | tf_op jit(solution)/shard_map/ppermute | solution.py:1341
  95.3 8.1 %collective-permute-start.30 = (f32[8,128]{1,0:T(8,128)S(1)}, f32[8,128]{1,0:T(8,128)S(1)}, u32[]{:S(2)}, u32[]{:S(2)}) collective-permute-start(f32[8,128]{1,0:T(8,128)S(1)} %get-tuple-element.254.refs_7_), channel_id=1, source_target_pairs={{0,3},{2,5},{4,7},{6,1},{3,0},{5,2},{7,4},{1,6},{8,11},{10,13},{12... | collective-permute-start | bytes 12296 | tf_op jit(solution)/shard_map/ppermute | solution.py:1377
  95.4 8.0 %collective-permute-start.31 = (f32[8,128]{1,0:T(8,128)S(1)}, f32[8,128]{1,0:T(8,128)S(1)}, u32[]{:S(2)}, u32[]{:S(2)}) collective-permute-start(f32[8,128]{1,0:T(8,128)S(1)} %get-tuple-element.254.refs_7_), channel_id=1, source_target_pairs={{0,4},{1,5},{2,6},{3,7},{4,0},{5,1},{6,2},{7,3},{8,12},{9,13},{10,... | collective-permute-start | bytes 12296 | tf_op jit(solution)/shard_map/ppermute | solution.py:1341
  109.3 9.0 %collective-permute-start.35 = (f32[8,128]{1,0:T(8,128)S(1)}, f32[8,128]{1,0:T(8,128)S(1)}, u32[]{:S(2)}, u32[]{:S(2)}) collective-permute-start(f32[8,128]{1,0:T(8,128)S(1)} %get-tuple-element.270.refs_9_), channel_id=1, source_target_pairs={{0,3},{2,5},{4,7},{6,1},{3,0},{5,2},{7,4},{1,6},{8,11},{10,13},{12... | collective-permute-start | bytes 12296 | tf_op jit(solution)/shard_map/ppermute | solution.py:1377
  109.4 8.9 %collective-permute-start.36 = (f32[8,128]{1,0:T(8,128)S(1)}, f32[8,128]{1,0:T(8,128)S(1)}, u32[]{:S(2)}, u32[]{:S(2)}) collective-permute-start(f32[8,128]{1,0:T(8,128)S(1)} %get-tuple-element.270.refs_9_), channel_id=1, source_target_pairs={{0,4},{1,5},{2,6},{3,7},{4,0},{5,1},{6,2},{7,3},{8,12},{9,13},{10,... | collective-permute-start | bytes 12296 | tf_op jit(solution)/shard_map/ppermute | solution.py:1341
  111.2 7.1 %collective-permute-start.33 = (f32[40,512]{1,0:T(8,128)S(1)}, f32[40,512]{1,0:T(8,128)S(1)}, u32[]{:S(2)}, u32[]{:S(2)}) collective-permute-start(f32[40,512]{1,0:T(8,128)S(1)} %get-tuple-element.262), channel_id=1, source_target_pairs={{0,7},{2,1},{4,3},{6,5},{7,0},{1,2},{3,4},{5,6},{8,15},{10,9},{12,... | collective-permute-start | bytes 245768 | tf_op jit(solution)/shard_map/ppermute | solution.py:1375
  122.9 9.3 %collective-permute-start.38 = (bf16[256,256]{1,0:T(8,128)(2,1)S(1)}, bf16[256,256]{1,0:T(8,128)(2,1)S(1)}, u32[]{:S(2)}, u32[]{:S(2)}) collective-permute-start(bf16[256,256]{1,0:T(8,128)(2,1)S(1)} %get-tuple-element.276), channel_id=1, source_target_pairs={{0,8},{8,0},{16,24},{24,16},{1,9},{9,1},{17,25},{25,17},{2,10},{10... | collective-permute-start | bytes 393224 | tf_op jit(solution)/shard_map/ppermute | solution.py:1341
  126.5 13.3 %collective-permute-start.42 = (bf16[176,128]{1,0:T(8,128)(2,1)S(1)}, bf16[176,128]{1,0:T(8,128)(2,1)S(1)}, u32[]{:S(2)}, u32[]{:S(2)}) collective-permute-start(bf16[176,128]{1,0:T(8,128)(2,1)S(1)} %get-tuple-element.286.refs_5_), channel_id=1, source_target_pairs={{0,2},{1,3},{2,0},{3,1},{4,6},{5,7},{6,4},{7,5},{8,10},{9,11},{10,... | collective-permute-start | bytes 135176 | tf_op jit(solution)/shard_map/ppermute | solution.py:1341
  126.6 13.2 %collective-permute-start.43 = (bf16[176,128]{1,0:T(8,128)(2,1)S(1)}, bf16[176,128]{1,0:T(8,128)(2,1)S(1)}, u32[]{:S(2)}, u32[]{:S(2)}) collective-permute-start(bf16[176,128]{1,0:T(8,128)(2,1)S(1)} %get-tuple-element.286.refs_5_), channel_id=1, source_target_pairs={{0,4},{1,5},{2,6},{3,7},{4,0},{5,1},{6,2},{7,3},{8,12},{9,13},{10,... | collective-permute-start | bytes 135176 | tf_op jit(solution)/shard_map/ppermute | solution.py:1341
  128.7 11.2 %collective-permute-start.44 = (bf16[176,128]{1,0:T(8,128)(2,1)S(1)}, bf16[176,128]{1,0:T(8,128)(2,1)S(1)}, u32[]{:S(2)}, u32[]{:S(2)}) collective-permute-start(bf16[176,128]{1,0:T(8,128)(2,1)S(1)} %get-tuple-element.286.refs_5_), channel_id=1, source_target_pairs={{0,6},{1,7},{2,4},{3,5},{4,2},{5,3},{6,0},{7,1},{8,14},{9,15},{10,... | collective-permute-start | bytes 135176 | tf_op jit(solution)/shard_map/ppermute | solution.py:1341
  131.0 7.6 %collective-permute-start.39 = (bf16[256,256]{1,0:T(8,128)(2,1)S(1)}, bf16[256,256]{1,0:T(8,128)(2,1)S(1)}, u32[]{:S(2)}, u32[]{:S(2)}) collective-permute-start(bf16[256,256]{1,0:T(8,128)(2,1)S(1)} %get-tuple-element.277), channel_id=1, source_target_pairs={{0,16},{8,24},{16,0},{24,8},{1,17},{9,25},{17,1},{25,9},{2,18},{10... | collective-permute-start | bytes 393224 | tf_op jit(solution)/shard_map/ppermute | solution.py:1341
  132.1 6.5 %collective-permute-start.40 = (bf16[256,256]{1,0:T(8,128)(2,1)S(1)}, bf16[256,256]{1,0:T(8,128)(2,1)S(1)}, u32[]{:S(2)}, u32[]{:S(2)}) collective-permute-start(bf16[256,256]{1,0:T(8,128)(2,1)S(1)} %get-tuple-element.278), channel_id=1, source_target_pairs={{0,24},{8,16},{16,8},{24,0},{1,25},{9,17},{17,9},{25,1},{2,26},{10... | collective-permute-start | bytes 393224 | tf_op jit(solution)/shard_map/ppermute | solution.py:1341
  (24 other events, 101.4 us)

commit v6 on v5

--- a/solution.py
+++ b/solution.py
@@ -72,7 +72,7 @@
 PARTS = 6
 
 
-def run(kernel, name, outs, args, scratch=(), flops=0, fetch=(), store=(), token=None):
+def run(kernel, name, outs, args, scratch=(), flops=0, fetch=(), store=(), token=None, carry=()):
     n_args = len(args)
     args = list(args) + list(fetch) + list(store) + ([] if token is None else [token])
     n_made = len(outs)
@@ -84,6 +84,15 @@
     outs += [(a.shape, a.dtype, True) for a in store]
     if token is not None:
         outs.append((token.shape, token.dtype))
+    aliases = {}
+    for value in carry:
+        at = [k for k, a in enumerate(args) if a is value]
+        if not at:
+            at = [len(args)]
+            args.append(value)
+        aliases[at[0]] = len(outs)
+        outs.append((value.shape, value.dtype))
+    n_token = n_args + len(fetch) + len(store)
     far_in = [k for k, a in enumerate(args[:n_args]) if isinstance(a, Far)]
     far_out = [k for k, o in enumerate(outs) if len(o) == 3]
     n_in, n_out, n_own = len(args), len(outs), len(scratch)
@@ -117,7 +126,7 @@
         for i in range(len(store)):
             results[n_stored + i].put(ins[n_args + len(fetch) + i])
         if token is not None:
-            results[-1][...] = ins[-1][...]
+            results[n_stored + len(store)][...] = ins[n_token][...]
         kernel(*ins[:n_args], *results[:n_made], *own)
         for k in far_in:
             ins[k].get()
@@ -141,6 +150,7 @@
         ],
         in_specs=in_specs,
         out_specs=[FAR if len(o) == 3 else FULL for o in outs],
+        input_output_aliases=aliases,
         scratch_shapes=[pltpu.VMEM(s, d) for s, d in scratch]
         + landing
         + [
@@ -647,18 +657,16 @@
     out[start : start + 16, :] = result
 
 
-def window_4(low, act, fine, out, d, kept):
+def window_4(low, act, fine, out, d):
     correlate(low, fine, d, SPAN0)
-    weight_1(d, kept, 0)
+    weight_1(d, out, 0)
     correlate(act, fine, d, SPAN0)
-    weight_1(d, kept, 16)
-    out.put(kept)
-
-
-def window_5(coarse, fine, out, d, kept):
+    weight_1(d, out, 16)
+
+
+def window_5(coarse, fine, out, d):
     correlate(coarse, fine, d)
-    weight_2(d, kept)
-    out.put(kept)
+    weight_2(d, out)
 
 
 HALF = 144
@@ -686,7 +694,10 @@
     low[HALF + 16 : HALF + 32, :] = jnp.concatenate([bias[...], jnp.zeros((8, L), F32)]).astype(BF)
 
 
-def unpack_kernel(index, mine, other, w1c, w2c, w2d, w1d, bias):
+def unpack_kernel(
+    index, mine, other, mom4, mom5, mom6,
+    w1c, w2c, w2d, w1d, bias1, gain1, shift1, gain2, shift2, bias2, gain3, shift3,
+):
     even = index[1] == 0
     a, b = mine[...], other[...]
     up, down = jnp.where(even, a, b), jnp.where(even, b, a)
@@ -714,7 +725,13 @@
     total = total + pltpu.roll(total, 64, 1)
     for step in (16, 8, 4, 2, 1):
         total = total + pltpu.roll(total, L - step, 1)
-    bias[...] = jnp.where(lane((8, L)) == 0, total, pltpu.roll(total, L - 31, 1))
+    total = jnp.where(lane((8, L)) == 0, total, pltpu.roll(total, L - 31, 1))
+    bias1[...] = total[0:1, 0:2]
+    for out, mom, row in (
+        (gain1, mom6, 1), (shift1, mom6, 0), (gain2, mom5, 1), (shift2, mom5, 0),
+        (bias2, mom5, 2), (gain3, mom4, 1), (shift3, mom4, 0),
+    ):
+        out[...] = mom[row : row + 1, 0 : out.shape[1]]
 
 
 def ready(ref, part=None):
@@ -1539,76 +1556,78 @@
         [((16, 256), F32)],
     )
     grads = swap(grads, "stem")
-    estimates, t, sig_here, sigh_here, rect_here, direct = run(
+    estimates, t, sig_here, sigh_here, rect_here, low3_here, act_here, direct = run(
         estimate_kernel,
         "estimate",
         [((stems, 2, frames, blocks * 32), BF), ((COLS0, 1024), BF)],
         [index, *masks, Far(x0_far), w1d],
         [((2, frames, L), F32), ((stems, per, 256), F32)],
-        fetch=[Far(sig), Far(sigh), Far(rect)],
+        fetch=[Far(sig), Far(sigh), Far(rect), Far(low3), Far(cat1, 512)],
         store=[direct],
     )
-    g3, cat0g, cross, core, mom, bias_one, gact = run(
+    g3, cat0g, cross, core, mom, bias_one, gact, rect_here, low3_here, act_here = run(
         down_one_back_kernel,
         "down_one_back",
         [((R, 512), F32), ((R, COLS0), BF)] + packet(512) + [((8, L), F32), ((R, 512), F32)],
         [index, *grads, sigh_here, sig_here, aux, mom1, mom3, rect_here, t],
         [((NJ, 256), F32), ((8, L), F32), ((8 * NJ, 256), F32)],
         flops=2 * R * COLS0 * 1024,
-    )
-    near, inside, mom4, (w1d_grad, rect_here, t, h3_here, z2_here, gact) = exchange(
+        carry=[rect_here, low3_here, act_here],
+    )
+    near, inside, mom4, (w1d_grad, t, h3_here, z2_here, act2_here) = exchange(
         cross, core, mom, "tm",
         lambda token: run(
             window_4,
             "window_4",
-            far(32, L),
-            [Far(low3, parts=2), Far(cat1, 512, parts=2), cat0g],
-            [((512, 768), F32), ((32, L), F32)],
+            [((32, L), F32)],
+            [low3_here, act_here, cat0g],
+            [((512, 768), F32)],
             flops=2 * R * COLS0 * 1024,
-            fetch=[Far(rect), Far(t2a_d), Far(h3), Far(z2)],
-            store=[gact],
+            fetch=[Far(t2a_d), Far(h3), Far(z2), Far(act2)],
             token=token,
         ),
     )
-    g2, cat1g, cross, core, mom = run(
+    g2, cat1g, cross, core, mom, gact, z2_here, act2_here, w1d_grad = run(
         up_two_back_kernel,
         "up_two_back",
         [((R, 256), F32), ((R, COLS1), BF)] + packet(256),
         [index, g3, near, inside, mom4, mom1, mom3, mom2, prm, aux, kept, rect_here, h3_here, t, z2_here],
         rim(512) + wide(512),
         flops=2 * R * COLS1 * 256,
-    )
-    near, inside, mom5, (w2d_grad, z2_here, t, h2_here, gact_here, z1_here) = exchange(
+        carry=[gact, z2_here, act2_here, w1d_grad],
+    )
+    near, inside, mom5, (w2d_grad, t, h2_here, z1_here) = exchange(
         cross, core, mom, "tm",
         lambda token: run(
             window_5,
             "window_5",
-            far(128, L),
-            [Far(act2, parts=2), cat1g],
-            [((256, COLS1), F32), ((128, L), F32)],
+            [((128, L), F32)],
+            [act2_here, cat1g],
+            [((256, COLS1), F32)],
             flops=2 * R * COLS1 * 256,
-            fetch=[Far(z2), Far(t2b_c), Far(h2), Far(gact), Far(z1)],
+            fetch=[Far(t2b_c), Far(h2), Far(z1)],
             token=token,
         ),
     )
-    g1, low2, cross, core, mom = run(
+    g1, low2, cross, core, mom, z1_here, w1d_grad, w2d_grad = run(
         down_two_back_kernel,
         "down_two_back",
         [((R, 512), F32), ((R, 256), BF)] + packet(512),
-        [index, g2, near, inside, mom5, mom1, mom2, prm, aux, kept, z2_here, h2_here, t, gact_here, z1_here],
+        [index, g2, near, inside, mom5, mom1, mom2, prm, aux, kept, z2_here, h2_here, t, gact, z1_here],
         [((R, COLS2), BF)] + rim(256) + wide(256),
         flops=2 * R * COLS2 * 512,
-    )
-    near, inside, mom6, (keep, give, t, z1_here, h1_here, cat0_here) = exchange(
+        carry=[z1_here, w1d_grad, w2d_grad],
+    )
+    near, inside, mom6, (keep, give, t, h1_here, cat0_here) = exchange(
         cross, core, mom, "tm",
         lambda token: run(
             window_6,
             "window_6",
             [((HALF, L), F32), ((HALF, L), F32)],
-            [index, low2, Far(cat1, parts=2), Far(w1d_grad), Far(w2d_grad)],
+            [index, low2, Far(cat1, parts=2), w1d_grad, w2d_grad],
             [((256, COLS1), F32), ((128, L), F32)],
             flops=2 * R * COLS1 * 256,
-            fetch=[Far(t1b_c), Far(z1), Far(h1), Far(cat0)],
+            fetch=[Far(t1b_c), Far(h1), Far(cat0)],
             token=token,
         ),
     )
@@ -1643,11 +1662,12 @@
             token=token,
         ),
     )
-    w1c_grad, w2c_grad, w2d_grad, w1d_grad, bias_one = run(
+    w1c_grad, w2c_grad, w2d_grad, w1d_grad, bias1, gain1, shift1, gain2, shift2, bias2, gain3, shift3 = run(
         unpack_kernel,
         "unpack",
-        [((25, 2, 16), F32), ((25, 16, 32), F32), ((25, 16, 32), F32), ((25, 2, 32), F32), ((8, L), F32)],
-        [index, mine, other],
+        [((25, 2, 16), F32), ((25, 16, 32), F32), ((25, 16, 32), F32), ((25, 2, 32), F32), ((1, 2), F32)]
+        + [((1, n), F32) for n in (16, 16, 32, 32, 16, 16, 16)],
+        [index, mine, other, mom4, mom5, mom6],
     )
 
     def turned(grad, order):
@@ -1657,17 +1677,17 @@
         estimates,
         mixture_grad,
         turned(w1c_grad, (3, 2, 0, 1)),
-        mom6[1, :16][None],
-        mom6[0, :16][None],
+        gain1,
+        shift1,
         turned(w2c_grad, (3, 2, 0, 1)),
-        mom5[1, :32][None],
-        mom5[0, :32][None],
+        gain2,
+        shift2,
         turned(w2d_grad, (2, 3, 0, 1)),
-        mom5[2, :16][None],
-        mom4[1, :16][None],
-        mom4[0, :16][None],
+        bias2,
+        gain3,
+        shift3,
         turned(w1d_grad, (2, 3, 0, 1)),
-        bias_one[0:1, 0:2],
+        bias1,
     )
 
 

time: 144 us -> 138 us (0.958)
  Pallas kernels: 73.7 us -> 70.9 us
  local copies, waits for them, and re-layouts: 2.59 us -> 0.01 us
    ppermute x6, starting transfers between devices: 1.96 us -> 8.21 us  [exchange(): far = lax.ppermute(mom, axis, pairs(count, 3))]
    ppermute x33, starting transfers between devices: 28.2 us -> 22.3 us  [flip(): lax.ppermute(values, axis, [(i, i ^ bit) for i in range(lax.axis_size(axi...]
    pallas_call x22, Pallas kernels: 73.7 us -> 70.9 us  [run(): pl.pallas_call(body, out_shape=[pltpu.HBM(o[0], o[1]) if len(o) == 3 else...]
    slice x5 -> x0, local copies, waits for them, and re-layouts: 2.58 us -> none  [the longest x1 0.52 us: per_device(): mom6[0, :16][None]]
    ppermute x33, waiting for transfers between devices: 17.9 us -> 15.4 us  [flip(): lax.ppermute(values, axis, [(i, i ^ bit) for i in range(lax.axis_size(axi...]
    ppermute x6, waiting for transfers between devices: 0.02 us -> 2.31 us  [exchange(): near = lax.ppermute(cross, axis, pairs(count, -1))]
  transfers between devices with their start and end apart: 46 -> 46, of which waited for: 13 -> 17; matrix products, arithmetic and copies ran while one was open for 1% -> 0% of each run, Pallas kernels for 24% -> 23%
where the time goes in v6:
time: 138 us; the launch traced here: 137 us
  Pallas kernels  70.9 us (51%)
  starting transfers between devices  47.4 us (34%)
  waiting for transfers between devices  17.7 us (13%)
    pallas_call x22, Pallas kernels, run(): pl.pallas_call(body, out_shape=[pltpu.HBM(o[0], o[1]) if len(o) == 3 else...  70.9 us
    ppermute x33, starting transfers between devices, flip(): lax.ppermute(values, axis, [(i, i ^ bit) for i in range(lax.axis_size(axi...  22.3 us
    ppermute x33, waiting for transfers between devices, flip(): lax.ppermute(values, axis, [(i, i ^ bit) for i in range(lax.axis_size(axi...  15.4 us
    ppermute x6, starting transfers between devices, exchange(): near = lax.ppermute(cross, axis, pairs(count, -1))  12.3 us
    ppermute x6, starting transfers between devices, exchange(): far = lax.ppermute(mom, axis, pairs(count, 3))  8.21 us
    ppermute x1, starting transfers between devices, per_device(): near = lax.ppermute(cross, 'tm', pairs(lax.axis_size('tm'), -1))  4.55 us
  transfers between devices with their start and end apart: 46, of which 17 were waited for; matrix products, arithmetic and copies ran while one was open for 0% of the time, Pallas kernels for 23%

profile of v6, /device:TPU:0, one launch (start us, length us, event | category | flops | bytes accessed | tf_op | source)
XLA Modules:
  0.0 137.4 jit_solution(945079420031866869)
XLA Ops:
  0.7 3.8 %layout.1 = (bf16[80,256]{1,0:T(8,128)(2,1)S(1)}, bf16[80,256]{1,0:T(8,128)(2,1)S(1)}, bf16[1024,256]{1,0:T(8,128)(2,1)S(1)}, bf16[1024,256]{1,0:T(8,128)(2,1)S(...) custom-call(s32[4]{0:T(128)S(1)} %pad_add_fusion.refs_0_, ...), custom_call_target="tpu_custom_call" | custom-call | bytes 2188992 | tf_op jit(solution)/shard_map/layout/pallas_call | solution.py:146
  4.6 4.6 %collective-permute-start = (bf16[80,256]{1,0:T(8,128)(2,1)S(1)}, bf16[80,256]{1,0:T(8,128)(2,1)S(1)}, u32[]{:S(2)}, u32[]{:S(2)}) collective-permute-start(bf16[80,256]{1,0:T(8,128)(2,1)S(1)} %get-tuple-element.170), channel_id=1, source_target_pairs={{0,7},{2,1},{4,3},{6,5},{7,0},{1,2},{3,4},{5,6},{8,15},{10,9},{12,... | collective-permute-start | bytes 122888 | tf_op jit(solution)/shard_map/ppermute | solution.py:1462
  10.9 3.3 %conv_one.1 = (f32[40,512]{1,0:T(8,128)S(1)}, f32[32,512]{1,0:T(8,128)S(1)}, f32[8,128]{1,0:T(8,128)S(1)}, f32[8,128]{1,0:T(8,128)S(1)}, f32[64,256]{1,0:T(8,128...) custom-call(s32[4]{0:T(128)S(1)} %pad_add_fusion.refs_0_, ...), custom_call_target="tpu_custom_call" | custom-call | flops 1073741824 | bytes 6152208 | tf_op jit(solution)/shard_map/conv_one/pallas_call | solution.py:146
  14.3 3.5 %collective-permute-start.2 = (f32[40,512]{1,0:T(8,128)S(1)}, f32[40,512]{1,0:T(8,128)S(1)}, u32[]{:S(2)}, u32[]{:S(2)}) collective-permute-start(f32[40,512]{1,0:T(8,128)S(1)} %get-tuple-element.191), channel_id=1, source_target_pairs={{0,7},{2,1},{4,3},{6,5},{7,0},{1,2},{3,4},{5,6},{8,15},{10,9},{12,... | collective-permute-start | bytes 245768 | tf_op jit(solution)/shard_map/ppermute | solution.py:1392
  18.9 2.5 %window_1.1 = (bf16[1920,256]{1,0:T(8,128)(2,1)S(1)}, f32[1024,512]{1,0:T(8,128)S(1)}, f32[64,256]{1,0:T(8,128)}, bf16[1024,1024]{1,0:T(8,128)(2,1)}, f32[8,128]{1,0:T(8,128)S(1)}) custom-call(bf16[400,32]{1,0:T(8,128)(2,1)S(1)} %bitcast.46, f32[1024,512]{1,0:T(8,128)} %get-tuple-element.186.refs_1_.refs_4_, f32[64,256]{1,0:T(8,128)S(1)} %get-tuple-element.187.refs_2_, ...), custom_call_target="tpu_custom_call" | custom-call | bytes 9536512 | tf_op jit(solution)/shard_map/window_1/pallas_call | solution.py:146
  23.5 5.1 %conv_two.1 = (f32[1024,256]{1,0:T(8,128)S(1)}, f32[40,256]{1,0:T(8,128)S(1)}, f32[32,256]{1,0:T(8,128)S(1)}, f32[8,128]{1,0:T(8,128)S(1)}, bf16[4,32,512]{2,1,0...) custom-call(s32[4]{0:T(128)S(1)} %pad_add_fusion.refs_0_, ...), custom_call_target="tpu_custom_call" | custom-call | flops 1006632960 | bytes 9433104 | tf_op jit(solution)/shard_map/conv_two/pallas_call | solution.py:146
  28.6 2.4 %collective-permute-start.7 = (f32[40,256]{1,0:T(8,128)S(1)}, f32[40,256]{1,0:T(8,128)S(1)}, u32[]{:S(2)}, u32[]{:S(2)}) collective-permute-start(f32[40,256]{1,0:T(8,128)S(1)} %get-tuple-element.197), channel_id=1, source_target_pairs={{0,7},{2,1},{4,3},{6,5},{7,0},{1,2},{3,4},{5,6},{8,15},{10,9},{12,... | collective-permute-start | bytes 122888 | tf_op jit(solution)/shard_map/ppermute | solution.py:1392
  37.4 5.1 %up_two.1 = (f32[1024,512]{1,0:T(8,128)S(1)}, f32[40,512]{1,0:T(8,128)S(1)}, f32[32,512]{1,0:T(8,128)S(1)}, f32[8,128]{1,0:T(8,128)S(1)}, f32[2,32,256]{2,1,0:T(...) custom-call(s32[4]{0:T(128)S(1)} %pad_add_fusion.refs_0_, f32[1024,256]{1,0:T(8,128)S(1)} %get-tuple-element.196.refs_1_, ...), custom_call_target="tpu_custom_call" | custom-call | flops 1207959552 | bytes 7268368 | tf_op jit(solution)/shard_map/up_two/pallas_call | solution.py:146
  43.8 2.5 %collective-permute-start.14 = (f32[8,128]{1,0:T(8,128)S(1)}, f32[8,128]{1,0:T(8,128)S(1)}, u32[]{:S(2)}, u32[]{:S(2)}) collective-permute-start(f32[8,128]{1,0:T(8,128)S(1)} %get-tuple-element.212.refs_5_), channel_id=1, source_target_pairs={{0,3},{2,5},{4,7},{6,1},{3,0},{5,2},{7,4},{1,6},{8,11},{10,13},{12... | collective-permute-start | bytes 12296 | tf_op jit(solution)/shard_map/ppermute | solution.py:1394
  47.0 2.3 %window_3.1 = (bf16[256,3072]{1,0:T(8,128)(2,1)S(1)}, bf16[1024,1536]{1,0:T(8,128)(2,1)S(1)}, bf16[4,32,512]{2,1,0:T(8,128)(2,1)S(1)}, f32[2,32,256]{2,1,0:T(8,1...) custom-call(f32[2,56,128]{2,1,0:T(8,128)S(1)} %get-tuple-element.207.refs_0_.refs_6_, ...), custom_call_target="tpu_custom_call" | custom-call | bytes 9967616 | tf_op jit(solution)/shard_map/window_3/pallas_call | solution.py:146
  50.6 4.6 %up_one.1 = (bf16[272,256]{1,0:T(8,128)(2,1)S(1)}, bf16[272,256]{1,0:T(8,128)(2,1)S(1)}, bf16[272,256]{1,0:T(8,128)(2,1)S(1)}, bf16[272,256]{1,0:T(8,128)(2,1)S(...) custom-call(s32[4]{0:T(128)S(1)} %pad_add_fusion.refs_0_, ...), custom_call_target="tpu_custom_call" | custom-call | flops 1610612736 | bytes 9879568 | tf_op jit(solution)/shard_map/up_one/pallas_call | solution.py:146
  58.8 3.4 %window_swap.1 = (bf16[1920,256]{1,0:T(8,128)(2,1)}, bf16[512,1152]{1,0:T(8,128)(2,1)}, bf16[256,1536]{1,0:T(8,128)(2,1)}, bf16[1024,256]{1,0:T(8,128)(2,1)S(1)}...) custom-call(bf16[400,32]{1,0:T(8,128)(2,1)S(1)} %bitcast.47, ...), custom_call_target="tpu_custom_call" | custom-call | bytes 9652224 | tf_op jit(solution)/shard_map/window_swap/pallas_call | solution.py:146
  62.2 3.0 %collective-permute-done.18.refs_3_ = bf16[272,256]{1,0:T(8,128)(2,1)S(1)} collective-permute-done((bf16[272,256]{1,0:T(8,128)(2,1)S(1)}, bf16[272,256]{1,0:T(8,128)(2,1)S(1)}, u32[]{:S(2)}, u32[]{:S(2)}) %collective-permute-start.18) | collective-permute-done | bytes 139296 | tf_op jit(solution)/shard_map/ppermute | solution.py:1358
  70.0 4.5 %estimate.1 = (bf16[4,2,128,256]{3,2,1,0:T(8,128)(2,1)}, bf16[1024,1024]{1,0:T(8,128)(2,1)S(1)}, f32[1024,256]{1,0:T(8,128)S(1)}, f32[32,256]{1,0:T(8,128)S(1)},...) custom-call(s32[4]{0:T(128)S(1)} %pad_add_fusion.refs_0_, ...), custom_call_target="tpu_custom_call" | custom-call | bytes 17197072 | tf_op jit(solution)/shard_map/estimate/pallas_call | solution.py:146
  75.4 4.1 %down_one_back.1 = (f32[1024,512]{1,0:T(8,128)S(1)}, bf16[1024,1024]{1,0:T(8,128)(2,1)S(1)}, f32[40,512]{1,0:T(8,128)S(1)}, f32[32,512]{1,0:T(8,128)S(1)}, f32[8...) custom-call(s32[4]{0:T(128)S(1)} %pad_add_fusion.refs_0_, ...), custom_call_target="tpu_custom_call", output_to_operand_aliasing={{7}: (10, {}), {8}: (12, {}), {9}: (13, {})} | custom-call | flops 2147483648 | bytes 16564240 | tf_op jit(solution)/shard_map/down_one_back/pallas_call | solution.py:146
  80.0 2.5 %collective-permute-start.24 = (f32[32,512]{1,0:T(8,128)S(1)}, f32[32,512]{1,0:T(8,128)S(1)}, u32[]{:S(2)}, u32[]{:S(2)}) collective-permute-start(f32[32,512]{1,0:T(8,128)S(1)} %get-tuple-element.250), channel_id=1, source_target_pairs={{0,1},{1,0},{2,3},{3,2},{4,5},{5,4},{6,7},{7,6},{8,9},{9,8},{10,11... | collective-permute-start | bytes 196616 | tf_op jit(solution)/shard_map/ppermute | solution.py:1358
  83.7 3.8 %window_4.1 = (f32[32,128]{1,0:T(8,128)S(1)}, bf16[1920,256]{1,0:T(8,128)(2,1)S(1)}, f32[2,32,512]{2,1,0:T(8,128)S(1)}, f32[1024,256]{1,0:T(8,128)S(1)}, bf16[10...) custom-call(bf16[1024,512]{1,0:T(8,128)(2,1)S(1)} %get-tuple-element.251.refs_0_, ...), custom_call_target="tpu_custom_call" | custom-call | flops 2147483648 | bytes 9465856 | tf_op jit(solution)/shard_map/window_4/pallas_call | solution.py:146
  89.6 5.4 %up_two_back.1 = (f32[1024,256]{1,0:T(8,128)S(1)}, bf16[1024,1920]{1,0:T(8,128)(2,1)S(1)}, f32[40,256]{1,0:T(8,128)S(1)}, f32[32,256]{1,0:T(8,128)S(1)}, f32[8,1...) custom-call(s32[4]{0:T(128)S(1)} %pad_add_fusion.refs_0_, ...), custom_call_target="tpu_custom_call", output_to_operand_aliasing={{5}: (15, {}), {6}: (14, {}), {7}: (16, {}), {8}: (17, {})} | custom-call | flops 1006632960 | bytes 15355920 | tf_op jit(solution)/shard_map/up_two_back/pallas_call | solution.py:146
  99.1 2.2 %window_5.1 = (f32[128,128]{1,0:T(8,128)S(1)}, bf16[512,1152]{1,0:T(8,128)(2,1)S(1)}, f32[2,32,256]{2,1,0:T(8,128)S(1)}, f32[1024,512]{1,0:T(8,128)S(1)}, f32[8,128]{1,0:T(8,128)S(1)}) custom-call(bf16[1024,256]{1,0:T(8,128)(2,1)S(1)} %get-tuple-element.271.refs_0_, bf16[1024,1920]{1,0:T(8,128)(2,1)S(1)} %get-tuple-element.272.refs_1_, ...), custom_call_target="tpu_custom_call" | custom-call | flops 1006632960 | bytes 11151360 | tf_op jit(solution)/shard_map/window_5/pallas_call | solution.py:146
  103.8 4.6 %down_two_back.1 = (f32[1024,512]{1,0:T(8,128)S(1)}, bf16[1024,256]{1,0:T(8,128)(2,1)S(1)}, f32[40,512]{1,0:T(8,128)S(1)}, f32[32,512]{1,0:T(8,128)S(1)}, f32[8,...) custom-call(s32[4]{0:T(128)S(1)} %pad_add_fusion.refs_0_, ...), custom_call_target="tpu_custom_call", output_to_operand_aliasing={{5}: (14, {}), {6}: (15, {}), {7}: (16, {})} | custom-call | flops 1207959552 | bytes 12664848 | tf_op jit(solution)/shard_map/down_two_back/pallas_call | solution.py:146
  110.5 2.1 %collective-permute-start.33 = (f32[40,512]{1,0:T(8,128)S(1)}, f32[40,512]{1,0:T(8,128)S(1)}, u32[]{:S(2)}, u32[]{:S(2)}) collective-permute-start(f32[40,512]{1,0:T(8,128)S(1)} %get-tuple-element.285), channel_id=1, source_target_pairs={{0,7},{2,1},{4,3},{6,5},{7,0},{1,2},{3,4},{5,6},{8,15},{10,9},{12,... | collective-permute-start | bytes 245768 | tf_op jit(solution)/shard_map/ppermute | solution.py:1392
  112.6 4.0 %window_6.1 = (f32[144,128]{1,0:T(8,128)S(1)}, f32[144,128]{1,0:T(8,128)S(1)}, bf16[256,1536]{1,0:T(8,128)(2,1)S(1)}, f32[2,32,512]{2,1,0:T(8,128)S(1)}, bf16[10...) custom-call(s32[4]{0:T(128)S(1)} %pad_add_fusion.refs_0_, bf16[1024,256]{1,0:T(8,128)(2,1)S(1)} %get-tuple-element.287.refs_1_, ...), custom_call_target="tpu_custom_call" | custom-call | flops 1006632960 | bytes 10596368 | tf_op jit(solution)/shard_map/window_6/pallas_call | solution.py:146
  117.9 3.3 %up_one_back.1 = (bf16[256,256]{1,0:T(8,128)(2,1)S(1)}, bf16[256,256]{1,0:T(8,128)(2,1)S(1)}, bf16[256,256]{1,0:T(8,128)(2,1)S(1)}, bf16[256,256]{1,0:T(8,128)(2,1)S(1)}, bf16[1024,512]{1,0:T(8,128)(2,1)S(1)}) custom-call(s32[4]{0:T(128)S(1)} %pad_add_fusion.refs_0_, f32[1024,512]{1,0:T(8,128)S(1)} %get-tuple-element.284.refs_1_, ...), custom_call_target="tpu_custom_call" | custom-call | flops 805306368 | bytes 6930448 | tf_op jit(solution)/shard_map/up_one_back/pallas_call | solution.py:146
  128.5 2.8 %collective-permute-start.42 = (bf16[176,128]{1,0:T(8,128)(2,1)S(1)}, bf16[176,128]{1,0:T(8,128)(2,1)S(1)}, u32[]{:S(2)}, u32[]{:S(2)}) collective-permute-start(bf16[176,128]{1,0:T(8,128)(2,1)S(1)} %get-tuple-element.309.refs_5_), channel_id=1, source_target_pairs={{0,2},{1,3},{2,0},{3,1},{4,6},{5,7},{6,4},{7,5},{8,10},{9,11},{10,... | collective-permute-start | bytes 135176 | tf_op jit(solution)/shard_map/ppermute | solution.py:1358
  (108 shorter events, 50.7 us)
Async XLA Ops:
  4.6 6.3 %collective-permute-start = (bf16[80,256]{1,0:T(8,128)(2,1)S(1)}, bf16[80,256]{1,0:T(8,128)(2,1)S(1)}, u32[]{:S(2)}, u32[]{:S(2)}) collective-permute-start(bf16[80,256]{1,0:T(8,128)(2,1)S(1)} %get-tuple-element.170), channel_id=1, source_target_pairs={{0,7},{2,1},{4,3},{6,5},{7,0},{1,2},{3,4},{5,6},{8,15},{10,9},{12,... | collective-permute-start | bytes 122888 | tf_op jit(solution)/shard_map/ppermute | solution.py:1462
  14.3 8.0 %collective-permute-start.2 = (f32[40,512]{1,0:T(8,128)S(1)}, f32[40,512]{1,0:T(8,128)S(1)}, u32[]{:S(2)}, u32[]{:S(2)}) collective-permute-start(f32[40,512]{1,0:T(8,128)S(1)} %get-tuple-element.191), channel_id=1, source_target_pairs={{0,7},{2,1},{4,3},{6,5},{7,0},{1,2},{3,4},{5,6},{8,15},{10,9},{12,... | collective-permute-start | bytes 245768 | tf_op jit(solution)/shard_map/ppermute | solution.py:1392
  28.6 6.9 %collective-permute-start.7 = (f32[40,256]{1,0:T(8,128)S(1)}, f32[40,256]{1,0:T(8,128)S(1)}, u32[]{:S(2)}, u32[]{:S(2)}) collective-permute-start(f32[40,256]{1,0:T(8,128)S(1)} %get-tuple-element.197), channel_id=1, source_target_pairs={{0,7},{2,1},{4,3},{6,5},{7,0},{1,2},{3,4},{5,6},{8,15},{10,9},{12,... | collective-permute-start | bytes 122888 | tf_op jit(solution)/shard_map/ppermute | solution.py:1392
  42.5 6.9 %collective-permute-start.12 = (f32[40,512]{1,0:T(8,128)S(1)}, f32[40,512]{1,0:T(8,128)S(1)}, u32[]{:S(2)}, u32[]{:S(2)}) collective-permute-start(f32[40,512]{1,0:T(8,128)S(1)} %get-tuple-element.205), channel_id=1, source_target_pairs={{0,7},{2,1},{4,3},{6,5},{7,0},{1,2},{3,4},{5,6},{8,15},{10,9},{12,... | collective-permute-start | bytes 245768 | tf_op jit(solution)/shard_map/ppermute | solution.py:1392
  55.2 7.0 %collective-permute-start.17 = (bf16[272,256]{1,0:T(8,128)(2,1)S(1)}, bf16[272,256]{1,0:T(8,128)(2,1)S(1)}, u32[]{:S(2)}, u32[]{:S(2)}) collective-permute-start(bf16[272,256]{1,0:T(8,128)(2,1)S(1)} %get-tuple-element.218), channel_id=1, source_target_pairs={{0,8},{8,0},{16,24},{24,16},{1,9},{9,1},{17,25},{25,17},{2,10},{10... | collective-permute-start | bytes 417800 | tf_op jit(solution)/shard_map/ppermute | solution.py:1358
  56.8 8.4 %collective-permute-start.18 = (bf16[272,256]{1,0:T(8,128)(2,1)S(1)}, bf16[272,256]{1,0:T(8,128)(2,1)S(1)}, u32[]{:S(2)}, u32[]{:S(2)}) collective-permute-start(bf16[272,256]{1,0:T(8,128)(2,1)S(1)} %get-tuple-element.219), channel_id=1, source_target_pairs={{0,16},{8,24},{16,0},{24,8},{1,17},{9,25},{17,1},{25,9},{2,18},{10... | collective-permute-start | bytes 417800 | tf_op jit(solution)/shard_map/ppermute | solution.py:1358
  58.3 6.9 %collective-permute-start.19 = (bf16[272,256]{1,0:T(8,128)(2,1)S(1)}, bf16[272,256]{1,0:T(8,128)(2,1)S(1)}, u32[]{:S(2)}, u32[]{:S(2)}) collective-permute-start(bf16[272,256]{1,0:T(8,128)(2,1)S(1)} %get-tuple-element.220), channel_id=1, source_target_pairs={{0,24},{8,16},{16,8},{24,0},{1,25},{9,17},{17,9},{25,1},{2,26},{10... | collective-permute-start | bytes 417800 | tf_op jit(solution)/shard_map/ppermute | solution.py:1358
  66.4 8.0 %collective-permute-start.20 = (bf16[272,256]{1,0:T(8,128)(2,1)S(1)}, bf16[272,256]{1,0:T(8,128)(2,1)S(1)}, u32[]{:S(2)}, u32[]{:S(2)}) collective-permute-start(bf16[272,256]{1,0:T(8,128)(2,1)S(1)} %get-tuple-element.239), channel_id=1, source_target_pairs={{0,8},{8,0},{16,24},{24,16},{1,9},{9,1},{17,25},{25,17},{2,10},{10... | collective-permute-start | bytes 417800 | tf_op jit(solution)/shard_map/ppermute | solution.py:1358
  67.8 7.6 %collective-permute-start.21 = (bf16[272,256]{1,0:T(8,128)(2,1)S(1)}, bf16[272,256]{1,0:T(8,128)(2,1)S(1)}, u32[]{:S(2)}, u32[]{:S(2)}) collective-permute-start(bf16[272,256]{1,0:T(8,128)(2,1)S(1)} %get-tuple-element.240), channel_id=1, source_target_pairs={{0,16},{8,24},{16,0},{24,8},{1,17},{9,25},{17,1},{25,9},{2,18},{10... | collective-permute-start | bytes 417800 | tf_op jit(solution)/shard_map/ppermute | solution.py:1358
  68.6 6.8 %collective-permute-start.22 = (bf16[272,256]{1,0:T(8,128)(2,1)S(1)}, bf16[272,256]{1,0:T(8,128)(2,1)S(1)}, u32[]{:S(2)}, u32[]{:S(2)}) collective-permute-start(bf16[272,256]{1,0:T(8,128)(2,1)S(1)} %get-tuple-element.241), channel_id=1, source_target_pairs={{0,24},{8,16},{16,8},{24,0},{1,25},{9,17},{17,9},{25,1},{2,26},{10... | collective-permute-start | bytes 417800 | tf_op jit(solution)/shard_map/ppermute | solution.py:1358
  79.5 8.0 %collective-permute-start.26 = (f32[8,128]{1,0:T(8,128)S(1)}, f32[8,128]{1,0:T(8,128)S(1)}, u32[]{:S(2)}, u32[]{:S(2)}) collective-permute-start(f32[8,128]{1,0:T(8,128)S(1)} %get-tuple-element.258.refs_7_), channel_id=1, source_target_pairs={{0,4},{1,5},{2,6},{3,7},{4,0},{5,1},{6,2},{7,3},{8,12},{9,13},{10,... | collective-permute-start | bytes 12296 | tf_op jit(solution)/shard_map/ppermute | solution.py:1358
  80.0 7.6 %collective-permute-start.25 = (f32[8,128]{1,0:T(8,128)S(1)}, f32[8,128]{1,0:T(8,128)S(1)}, u32[]{:S(2)}, u32[]{:S(2)}) collective-permute-start(f32[8,128]{1,0:T(8,128)S(1)} %get-tuple-element.258.refs_7_), channel_id=1, source_target_pairs={{0,3},{2,5},{4,7},{6,1},{3,0},{5,2},{7,4},{1,6},{8,11},{10,13},{12... | collective-permute-start | bytes 12296 | tf_op jit(solution)/shard_map/ppermute | solution.py:1394
  80.0 9.6 %collective-permute-start.24 = (f32[32,512]{1,0:T(8,128)S(1)}, f32[32,512]{1,0:T(8,128)S(1)}, u32[]{:S(2)}, u32[]{:S(2)}) collective-permute-start(f32[32,512]{1,0:T(8,128)S(1)} %get-tuple-element.250), channel_id=1, source_target_pairs={{0,1},{1,0},{2,3},{3,2},{4,5},{5,4},{6,7},{7,6},{8,9},{9,8},{10,11... | collective-permute-start | bytes 196616 | tf_op jit(solution)/shard_map/ppermute | solution.py:1358
  94.9 6.4 %collective-permute-start.31 = (f32[8,128]{1,0:T(8,128)S(1)}, f32[8,128]{1,0:T(8,128)S(1)}, u32[]{:S(2)}, u32[]{:S(2)}) collective-permute-start(f32[8,128]{1,0:T(8,128)S(1)} %get-tuple-element.275.refs_5_), channel_id=1, source_target_pairs={{0,4},{1,5},{2,6},{3,7},{4,0},{5,1},{6,2},{7,3},{8,12},{9,13},{10,... | collective-permute-start | bytes 12296 | tf_op jit(solution)/shard_map/ppermute | solution.py:1358
  95.0 6.3 %collective-permute-start.30 = (f32[8,128]{1,0:T(8,128)S(1)}, f32[8,128]{1,0:T(8,128)S(1)}, u32[]{:S(2)}, u32[]{:S(2)}) collective-permute-start(f32[8,128]{1,0:T(8,128)S(1)} %get-tuple-element.275.refs_5_), channel_id=1, source_target_pairs={{0,3},{2,5},{4,7},{6,1},{3,0},{5,2},{7,4},{1,6},{8,11},{10,13},{12... | collective-permute-start | bytes 12296 | tf_op jit(solution)/shard_map/ppermute | solution.py:1394
  96.8 6.9 %collective-permute-start.29 = (f32[32,256]{1,0:T(8,128)S(1)}, f32[32,256]{1,0:T(8,128)S(1)}, u32[]{:S(2)}, u32[]{:S(2)}) collective-permute-start(f32[32,256]{1,0:T(8,128)S(1)} %get-tuple-element.270), channel_id=1, source_target_pairs={{0,1},{1,0},{2,3},{3,2},{4,5},{5,4},{6,7},{7,6},{8,9},{9,8},{10,11... | collective-permute-start | bytes 98312 | tf_op jit(solution)/shard_map/ppermute | solution.py:1358
  108.4 8.2 %collective-permute-start.36 = (f32[8,128]{1,0:T(8,128)S(1)}, f32[8,128]{1,0:T(8,128)S(1)}, u32[]{:S(2)}, u32[]{:S(2)}) collective-permute-start(f32[8,128]{1,0:T(8,128)S(1)} %get-tuple-element.293.refs_8_), channel_id=1, source_target_pairs={{0,4},{1,5},{2,6},{3,7},{4,0},{5,1},{6,2},{7,3},{8,12},{9,13},{10,... | collective-permute-start | bytes 12296 | tf_op jit(solution)/shard_map/ppermute | solution.py:1358
  108.5 8.1 %collective-permute-start.35 = (f32[8,128]{1,0:T(8,128)S(1)}, f32[8,128]{1,0:T(8,128)S(1)}, u32[]{:S(2)}, u32[]{:S(2)}) collective-permute-start(f32[8,128]{1,0:T(8,128)S(1)} %get-tuple-element.293.refs_8_), channel_id=1, source_target_pairs={{0,3},{2,5},{4,7},{6,1},{3,0},{5,2},{7,4},{1,6},{8,11},{10,13},{12... | collective-permute-start | bytes 12296 | tf_op jit(solution)/shard_map/ppermute | solution.py:1394
  110.5 7.5 %collective-permute-start.34 = (f32[32,512]{1,0:T(8,128)S(1)}, f32[32,512]{1,0:T(8,128)S(1)}, u32[]{:S(2)}, u32[]{:S(2)}) collective-permute-start(f32[32,512]{1,0:T(8,128)S(1)} %get-tuple-element.286), channel_id=1, source_target_pairs={{0,1},{1,0},{2,3},{3,2},{4,5},{5,4},{6,7},{7,6},{8,9},{9,8},{10,11... | collective-permute-start | bytes 196616 | tf_op jit(solution)/shard_map/ppermute | solution.py:1358
  116.8 8.0 %collective-permute-start.41 = (f32[144,128]{1,0:T(8,128)S(1)}, f32[144,128]{1,0:T(8,128)S(1)}, u32[]{:S(2)}, u32[]{:S(2)}) collective-permute-start(f32[144,128]{1,0:T(8,128)S(1)} %get-tuple-element.305), channel_id=1, source_target_pairs={{0,1},{1,0},{2,3},{3,2},{4,5},{5,4},{6,7},{7,6},{8,9},{9,8},{10,11... | collective-permute-start | bytes 221192 | tf_op jit(solution)/shard_map/ppermute | solution.py:1358
  121.2 7.3 %collective-permute-start.38 = (bf16[256,256]{1,0:T(8,128)(2,1)S(1)}, bf16[256,256]{1,0:T(8,128)(2,1)S(1)}, u32[]{:S(2)}, u32[]{:S(2)}) collective-permute-start(bf16[256,256]{1,0:T(8,128)(2,1)S(1)} %get-tuple-element.299), channel_id=1, source_target_pairs={{0,8},{8,0},{16,24},{24,16},{1,9},{9,1},{17,25},{25,17},{2,10},{10... | collective-permute-start | bytes 393224 | tf_op jit(solution)/shard_map/ppermute | solution.py:1358
  122.4 8.9 %collective-permute-start.39 = (bf16[256,256]{1,0:T(8,128)(2,1)S(1)}, bf16[256,256]{1,0:T(8,128)(2,1)S(1)}, u32[]{:S(2)}, u32[]{:S(2)}) collective-permute-start(bf16[256,256]{1,0:T(8,128)(2,1)S(1)} %get-tuple-element.300), channel_id=1, source_target_pairs={{0,16},{8,24},{16,0},{24,8},{1,17},{9,25},{17,1},{25,9},{2,18},{10... | collective-permute-start | bytes 393224 | tf_op jit(solution)/shard_map/ppermute | solution.py:1358
  123.4 7.9 %collective-permute-start.40 = (bf16[256,256]{1,0:T(8,128)(2,1)S(1)}, bf16[256,256]{1,0:T(8,128)(2,1)S(1)}, u32[]{:S(2)}, u32[]{:S(2)}) collective-permute-start(bf16[256,256]{1,0:T(8,128)(2,1)S(1)} %get-tuple-element.301), channel_id=1, source_target_pairs={{0,24},{8,16},{16,8},{24,0},{1,25},{9,17},{17,9},{25,1},{2,26},{10... | collective-permute-start | bytes 393224 | tf_op jit(solution)/shard_map/ppermute | solution.py:1358
  126.8 6.3 %collective-permute-start.44 = (bf16[176,128]{1,0:T(8,128)(2,1)S(1)}, bf16[176,128]{1,0:T(8,128)(2,1)S(1)}, u32[]{:S(2)}, u32[]{:S(2)}) collective-permute-start(bf16[176,128]{1,0:T(8,128)(2,1)S(1)} %get-tuple-element.309.refs_5_), channel_id=1, source_target_pairs={{0,6},{1,7},{2,4},{3,5},{4,2},{5,3},{6,0},{7,1},{8,14},{9,15},{10,... | collective-permute-start | bytes 135176 | tf_op jit(solution)/shard_map/ppermute | solution.py:1358
  (24 other events, 102.6 us)

commit v7 on v6

--- a/solution.py
+++ b/solution.py
@@ -69,12 +69,12 @@
             copy.wait()
 
 
-PARTS = 6
+PARTS = 8
 
 
 def run(kernel, name, outs, args, scratch=(), flops=0, fetch=(), store=(), token=None, carry=()):
     n_args = len(args)
-    args = list(args) + list(fetch) + list(store) + ([] if token is None else [token])
+    args = list(args) + list(fetch) + list(store)
     n_made = len(outs)
     outs = list(outs)
     for f in fetch:
@@ -82,8 +82,6 @@
     arrays = [a.array if isinstance(a, Far) else a for a in args]
     n_stored = len(outs)
     outs += [(a.shape, a.dtype, True) for a in store]
-    if token is not None:
-        outs.append((token.shape, token.dtype))
     aliases = {}
     for value in carry:
         at = [k for k, a in enumerate(args) if a is value]
@@ -92,7 +90,9 @@
             args.append(value)
         aliases[at[0]] = len(outs)
         outs.append((value.shape, value.dtype))
-    n_token = n_args + len(fetch) + len(store)
+    if token is not None:
+        args.append(token)
+        outs.append((token.shape, token.dtype))
     far_in = [k for k, a in enumerate(args[:n_args]) if isinstance(a, Far)]
     far_out = [k for k, o in enumerate(outs) if len(o) == 3]
     n_in, n_out, n_own = len(args), len(outs), len(scratch)
@@ -126,7 +126,7 @@
         for i in range(len(store)):
             results[n_stored + i].put(ins[n_args + len(fetch) + i])
         if token is not None:
-            results[n_stored + len(store)][...] = ins[n_token][...]
+            results[-1][...] = ins[-1][...]
         kernel(*ins[:n_args], *results[:n_made], *own)
         for k in far_in:
             ins[k].get()
@@ -283,7 +283,7 @@
     lax.fori_loop(0, R // size, body, 0)
 
 
-def product_sums(product, use, done=None, size=256):
+def product_sums(product, use, done=None, size=R):
     sums = (jnp.zeros((8, L), F32), jnp.zeros((8, L), F32))
 
     def part(r, sums):
@@ -836,7 +836,7 @@
 
 def conv_one_kernel(
     index, x0, cross_in, core_in, aux, t,
-    cross, core, mom, kept, hx, cat, zfar, z, lf, rf, lw, rw,
+    z, cross, core, mom, kept, hx, cat, lf, rf, lw, rw,
 ):
     even = index[1] == 0
     a, b = cross_in[...].astype(F32), core_in[...].astype(F32)
@@ -859,7 +859,7 @@
         part = value * aux[2 + k // 2]
         return s1 + sum8(part), s2 + sum8(part * value)
 
-    stats = product_sums(rows_from_0(cat, weights), use, lambda rs: zfar.put(z, (rs, slice(None))))
+    stats = product_sums(rows_from_0(cat, weights), use)
     pack_ends(z, index, cross, core)
     stats = fold(stack_rows(stats), 16)
     at = sub((8, L))
@@ -870,7 +870,7 @@
 
 def conv_two_kernel(
     index, z1, cross_in, core_in, mom1, prm, aux, t,
-    z2, cross, core, mom, eb, hf, zfar, catfar, cat, ef, lw, rw,
+    z2, cross, core, mom, eb, hf, cat, ef, lw, rw,
 ):
     mean, scale = norm_terms(mom1, mom1[2:3])
     gain, shift = prm[0:1], prm[1:2]
@@ -902,11 +902,7 @@
         put_all(stores)
 
     for_blocks(one)
-    catfar.put(cat, (slice(None), slice(0, 1024)))
-    catfar.put(cat, (slice(None), slice(1536, 1792)))
     rims_1(cat, GROUPS1)
-    catfar.put(cat, (slice(None), slice(1024, 1536)))
-    catfar.put(cat, (slice(None), slice(1792, 1920)))
     def group_out(rs, at, top, low):
         ef[2, rs, at] = act(top)
         ef[3, rs, at] = act(low)
@@ -920,9 +916,7 @@
         part = value * aux[4]
         return s1 + sum8(part), s2 + sum8(part * value)
 
-    stats = product_sums(
-        lambda rs: [matmul(cat[rs, :], weights[...])], use, lambda rs: zfar.put(z2, (rs, slice(None)))
-    )
+    stats = product_sums(lambda rs: [matmul(cat[rs, :], weights[...])], use)
     pack_ends(z2, index, cross, core)
     pack_moments(mom, cross, fold(stack_rows(stats), 32))
 
@@ -947,7 +941,7 @@
 
 def up_two_kernel(
     index, z2, cross_in, core_in, mom1, mom2, prm, aux, t,
-    rect, cross, core, mom, hf, act2, rectfar, cat, lf, rf, lw, rw,
+    rect, cross, core, mom, hf, act2, cat, lf, rf, lw, rw,
 ):
     mean, scale = norm_terms(mom2, mom1[3:4])
     gain, shift, bias = prm[2:3], prm[3:4], prm[6:7]
@@ -973,7 +967,7 @@
         part = value * aux[2 + k // 2]
         return s1 + sum8(part), s2 + sum8(part * value)
 
-    stats = product_sums(rows_from_2(cat, weights), use, lambda rs: rectfar.put(rect, (rs, slice(None))))
+    stats = product_sums(rows_from_2(cat, weights), use)
     pack_moments(mom, cross, fold(stack_rows(stats), 16))
     pack_ends(rect, index, cross, core)
 
@@ -1468,15 +1462,15 @@
         [index, Far(seg_lengths), *raw],
         store=[x0, c0],
     )
-    cross, core, mom, kept, hx, cat0, z1 = run(
+    z1_here, cross, core, mom, kept, hx, cat0 = run(
         conv_one_kernel,
         "conv_one",
-        packet(512) + [((8, L), F32), ((2 * NJ, 256), F32), ((R, COLS0), BF)] + far(R, 512),
+        [((R, 512), F32)] + packet(512) + [((8, L), F32), ((2 * NJ, 256), F32), ((R, COLS0), BF)],
         [index, x0, near, inside, aux, t],
-        [((R, 512), F32), ((edge, 256), F32), ((edge, 256), F32)] + wide(256),
+        [((edge, 256), F32), ((edge, 256), F32)] + wide(256),
         flops=2 * R * COLS0 * 512,
     )
-    near, inside, mom1, (t, z1_here, hx, cat0) = exchange(
+    near, inside, mom1, (t, z1, hx, cat0, z1_here) = exchange(
         cross, core, mom, "tm",
         lambda token: run(
             window_1,
@@ -1484,20 +1478,20 @@
             [((COLS1, 256), BF)],
             [w2c],
             [((400, L), F32)],
-            fetch=[Far(z1)],
-            store=[hx, cat0],
+            store=[z1_here, hx, cat0],
+            carry=[z1_here],
             token=token,
         ),
     )
-    z2_here, cross, core, mom, ends1, h1, z2, cat1 = run(
+    z2_here, cross, core, mom, ends1, h1, cat1 = run(
         conv_two_kernel,
         "conv_two",
-        [((R, 256), F32)] + packet(256) + [((4, NJ, 512), BF), ((2, NJ, 512), F32)] + far(R, 256) + far(R, COLS1, kind=BF),
+        [((R, 256), F32)] + packet(256) + [((4, NJ, 512), BF), ((2, NJ, 512), F32), ((R, COLS1), BF)],
         [index, z1_here, near, inside, mom1, prm, aux, t],
-        [((R, COLS1), BF), ((4, NJ, 512), F32)] + wide(512),
+        [((4, NJ, 512), F32)] + wide(512),
         flops=2 * R * COLS1 * 256,
     )
-    near, inside, mom2, (t, ends1, h1) = exchange(
+    near, inside, mom2, (t, cat1, z2, ends1, h1, z2_here) = exchange(
         cross, core, mom, "tm",
         lambda token: run(
             window_2,
@@ -1505,19 +1499,20 @@
             [((512, COLS2), BF)],
             [w2d],
             [((400, L), F32)],
-            store=[ends1, h1],
+            store=[cat1, z2_here, ends1, h1],
+            carry=[z2_here],
             token=token,
         ),
     )
-    rect_here, cross, core, mom, h2, act2, rect = run(
+    rect_here, cross, core, mom, h2, act2 = run(
         up_two_kernel,
         "up_two",
-        [((R, 512), F32)] + packet(512) + [((2, NJ, 256), F32), ((R, 256), BF)] + far(R, 512),
+        [((R, 512), F32)] + packet(512) + [((2, NJ, 256), F32), ((R, 256), BF)],
         [index, z2_here, near, inside, mom1, mom2, prm, aux, t],
         [((R, COLS2), BF)] + rim(256) + wide(256),
         flops=2 * R * COLS2 * 512,
     )
-    near, inside, mom3, (t, cat1_here, ends1_here, h2, act2) = exchange(
+    near, inside, mom3, (t, cat1_here, ends1_here, rect, h2, act2, rect_here) = exchange(
         cross, core, mom, "tm",
         lambda token: run(
             window_3,
@@ -1525,7 +1520,8 @@
             [((256, 2 * COLS1B), BF)],
             [w1d],
             fetch=[Far(cat1, COLS1B), Far(ends1)],
-            store=[h2, act2],
+            store=[rect_here, h2, act2],
+            carry=[rect_here],
             token=token,
         ),
     )

time: 138 us -> 135 us (0.978)
  waiting for transfers between devices: 17.7 us -> 15.1 us
    ppermute x33, waiting for transfers between devices: 15.4 us -> 13.4 us  [flip(): lax.ppermute(values, axis, [(i, i ^ bit) for i in range(lax.axis_size(axi...]
  transfers between devices with their start and end apart: 46 -> 46, of which waited for: 17 -> 14; matrix products, arithmetic and copies ran while one was open for 0% -> 0% of each run, Pallas kernels for 23% -> 26%
where the time goes in v7:
time: 135 us
  Pallas kernels  71.1 us (53%)
  starting transfers between devices  47.2 us (35%)
  waiting for transfers between devices  15.1 us (11%)
    pallas_call x22, Pallas kernels, run(): pl.pallas_call(body, out_shape=[pltpu.HBM(o[0], o[1]) if len(o) == 3 else...  71.1 us
    ppermute x33, starting transfers between devices, flip(): lax.ppermute(values, axis, [(i, i ^ bit) for i in range(lax.axis_size(axi...  22.2 us
    ppermute x33, waiting for transfers between devices, flip(): lax.ppermute(values, axis, [(i, i ^ bit) for i in range(lax.axis_size(axi...  13.4 us
    ppermute x6, starting transfers between devices, exchange(): near = lax.ppermute(cross, axis, pairs(count, -1))  13.4 us
    ppermute x6, starting transfers between devices, exchange(): far = lax.ppermute(mom, axis, pairs(count, 3))  7.13 us
    ppermute x1, starting transfers between devices, per_device(): near = lax.ppermute(cross, 'tm', pairs(lax.axis_size('tm'), -1))  4.55 us
  transfers between devices with their start and end apart: 46, of which 14 were waited for; matrix products, arithmetic and copies ran while one was open for 0% of the time, Pallas kernels for 26%

profile of v7, /device:TPU:0, one launch (start us, length us, event | category | flops | bytes accessed | tf_op | source)
XLA Modules:
  0.0 134.9 jit_solution(3505542441641915137)
XLA Ops:
  0.7 4.1 %layout.1 = (bf16[80,256]{1,0:T(8,128)(2,1)S(1)}, bf16[80,256]{1,0:T(8,128)(2,1)S(1)}, bf16[1024,256]{1,0:T(8,128)(2,1)S(1)}, bf16[1024,256]{1,0:T(8,128)(2,1)S(...) custom-call(s32[4]{0:T(128)S(1)} %pad_add_fusion.refs_0_, ...), custom_call_target="tpu_custom_call" | custom-call | bytes 2188992 | tf_op jit(solution)/shard_map/layout/pallas_call | solution.py:146
  4.8 4.6 %collective-permute-start = (bf16[80,256]{1,0:T(8,128)(2,1)S(1)}, bf16[80,256]{1,0:T(8,128)(2,1)S(1)}, u32[]{:S(2)}, u32[]{:S(2)}) collective-permute-start(bf16[80,256]{1,0:T(8,128)(2,1)S(1)} %get-tuple-element.187), channel_id=1, source_target_pairs={{0,7},{2,1},{4,3},{6,5},{7,0},{1,2},{3,4},{5,6},{8,15},{10,9},{12,... | collective-permute-start | bytes 122888 | tf_op jit(solution)/shard_map/ppermute | solution.py:1456
  11.2 2.7 %conv_one.1 = (f32[1024,512]{1,0:T(8,128)S(1)}, f32[40,512]{1,0:T(8,128)S(1)}, f32[32,512]{1,0:T(8,128)S(1)}, f32[8,128]{1,0:T(8,128)S(1)}, f32[8,128]{1,0:T(8,1...) custom-call(s32[4]{0:T(128)S(1)} %pad_add_fusion.refs_0_, ...), custom_call_target="tpu_custom_call" | custom-call | flops 1073741824 | bytes 6152208 | tf_op jit(solution)/shard_map/conv_one/pallas_call | solution.py:146
  13.9 3.5 %collective-permute-start.2 = (f32[40,512]{1,0:T(8,128)S(1)}, f32[40,512]{1,0:T(8,128)S(1)}, u32[]{:S(2)}, u32[]{:S(2)}) collective-permute-start(f32[40,512]{1,0:T(8,128)S(1)} %get-tuple-element.196), channel_id=1, source_target_pairs={{0,7},{2,1},{4,3},{6,5},{7,0},{1,2},{3,4},{5,6},{8,15},{10,9},{12,... | collective-permute-start | bytes 245768 | tf_op jit(solution)/shard_map/ppermute | solution.py:1386
  18.5 2.4 %window_1.1 = (bf16[1920,256]{1,0:T(8,128)(2,1)S(1)}, f32[1024,512]{1,0:T(8,128)}, f32[64,256]{1,0:T(8,128)}, bf16[1024,1024]{1,0:T(8,128)(2,1)}, f32[1024,512]{1,0:T(8,128)S(1)}, /*index=5*/f32[8,128]{1,0:T(8,128)S(1)}) custom-call(bf16[400,32]{1,0:T(8,128)(2,1)S(1)} %bitcast.46, ...), custom_call_target="tpu_custom_call", output_to_operand_aliasing={{4}: (1, {})} | custom-call | bytes 11629568 | tf_op jit(solution)/shard_map/window_1/pallas_call | solution.py:146
  23.1 4.3 %conv_two.1 = (f32[1024,256]{1,0:T(8,128)S(1)}, f32[40,256]{1,0:T(8,128)S(1)}, f32[32,256]{1,0:T(8,128)S(1)}, f32[8,128]{1,0:T(8,128)S(1)}, bf16[4,32,512]{2,1,0...) custom-call(s32[4]{0:T(128)S(1)} %pad_add_fusion.refs_0_, ...), custom_call_target="tpu_custom_call" | custom-call | flops 1006632960 | bytes 8384528 | tf_op jit(solution)/shard_map/conv_two/pallas_call | solution.py:146
  27.4 2.2 %collective-permute-start.7 = (f32[40,256]{1,0:T(8,128)S(1)}, f32[40,256]{1,0:T(8,128)S(1)}, u32[]{:S(2)}, u32[]{:S(2)}) collective-permute-start(f32[40,256]{1,0:T(8,128)S(1)} %get-tuple-element.209), channel_id=1, source_target_pairs={{0,7},{2,1},{4,3},{6,5},{7,0},{1,2},{3,4},{5,6},{8,15},{10,9},{12,... | collective-permute-start | bytes 122888 | tf_op jit(solution)/shard_map/ppermute | solution.py:1386
  31.7 2.7 %window_2.1 = (bf16[512,1152]{1,0:T(8,128)(2,1)S(1)}, bf16[1024,1920]{1,0:T(8,128)(2,1)}, f32[1024,256]{1,0:T(8,128)}, bf16[4,32,512]{2,1,0:T(8,128)(2,1)}, f32[...) custom-call(bf16[400,32]{1,0:T(8,128)(2,1)S(1)} %bitcast.44, ...), custom_call_target="tpu_custom_call", output_to_operand_aliasing={{5}: (2, {})} | custom-call | bytes 12489728 | tf_op jit(solution)/shard_map/window_2/pallas_call | solution.py:146
  36.0 4.4 %up_two.1 = (f32[1024,512]{1,0:T(8,128)S(1)}, f32[40,512]{1,0:T(8,128)S(1)}, f32[32,512]{1,0:T(8,128)S(1)}, f32[8,128]{1,0:T(8,128)S(1)}, f32[2,32,256]{2,1,0:T(8,128)S(1)}, /*index=5*/bf16[1024,256]{1,0:T(8,128)(2,1)S(1)}) custom-call(s32[4]{0:T(128)S(1)} %pad_add_fusion.refs_0_, f32[1024,256]{1,0:T(8,128)S(1)} %get-tuple-element.208.refs_1_, ...), custom_call_target="tpu_custom_call" | custom-call | flops 1207959552 | bytes 5171216 | tf_op jit(solution)/shard_map/up_two/pallas_call | solution.py:146
  44.9 3.2 %window_3.1 = (bf16[256,3072]{1,0:T(8,128)(2,1)S(1)}, bf16[1024,1536]{1,0:T(8,128)(2,1)S(1)}, bf16[4,32,512]{2,1,0:T(8,128)(2,1)S(1)}, f32[1024,512]{1,0:T(8,128...) custom-call(f32[2,56,128]{2,1,0:T(8,128)S(1)} %get-tuple-element.186, ...), custom_call_target="tpu_custom_call", output_to_operand_aliasing={{6}: (3, {})} | custom-call | bytes 16254976 | tf_op jit(solution)/shard_map/window_3/pallas_call | solution.py:146
  49.4 4.7 %up_one.1 = (bf16[272,256]{1,0:T(8,128)(2,1)S(1)}, bf16[272,256]{1,0:T(8,128)(2,1)S(1)}, bf16[272,256]{1,0:T(8,128)(2,1)S(1)}, bf16[272,256]{1,0:T(8,128)(2,1)S(...) custom-call(s32[4]{0:T(128)S(1)} %pad_add_fusion.refs_0_, ...), custom_call_target="tpu_custom_call" | custom-call | flops 1610612736 | bytes 9879568 | tf_op jit(solution)/shard_map/up_one/pallas_call | solution.py:146
  57.7 3.6 %window_swap.1 = (bf16[1920,256]{1,0:T(8,128)(2,1)}, bf16[512,1152]{1,0:T(8,128)(2,1)}, bf16[256,1536]{1,0:T(8,128)(2,1)}, bf16[1024,256]{1,0:T(8,128)(2,1)S(1)}...) custom-call(bf16[400,32]{1,0:T(8,128)(2,1)S(1)} %bitcast.47, ...), custom_call_target="tpu_custom_call" | custom-call | bytes 9652224 | tf_op jit(solution)/shard_map/window_swap/pallas_call | solution.py:146
  61.3 2.9 %collective-permute-done.18.refs_3_ = bf16[272,256]{1,0:T(8,128)(2,1)S(1)} collective-permute-done((bf16[272,256]{1,0:T(8,128)(2,1)S(1)}, bf16[272,256]{1,0:T(8,128)(2,1)S(1)}, u32[]{:S(2)}, u32[]{:S(2)}) %collective-permute-start.18) | collective-permute-done | bytes 139296 | tf_op jit(solution)/shard_map/ppermute | solution.py:1352
  68.9 4.6 %estimate.1 = (bf16[4,2,128,256]{3,2,1,0:T(8,128)(2,1)}, bf16[1024,1024]{1,0:T(8,128)(2,1)S(1)}, f32[1024,256]{1,0:T(8,128)S(1)}, f32[32,256]{1,0:T(8,128)S(1)},...) custom-call(s32[4]{0:T(128)S(1)} %pad_add_fusion.refs_0_, ...), custom_call_target="tpu_custom_call" | custom-call | bytes 17197072 | tf_op jit(solution)/shard_map/estimate/pallas_call | solution.py:146
  74.3 3.4 %down_one_back.1 = (f32[1024,512]{1,0:T(8,128)S(1)}, bf16[1024,1024]{1,0:T(8,128)(2,1)S(1)}, f32[40,512]{1,0:T(8,128)S(1)}, f32[32,512]{1,0:T(8,128)S(1)}, f32[8...) custom-call(s32[4]{0:T(128)S(1)} %pad_add_fusion.refs_0_, ...), custom_call_target="tpu_custom_call", output_to_operand_aliasing={{7}: (10, {}), {8}: (12, {}), {9}: (13, {})} | custom-call | flops 2147483648 | bytes 16564240 | tf_op jit(solution)/shard_map/down_one_back/pallas_call | solution.py:146
  81.8 3.9 %window_4.1 = (f32[32,128]{1,0:T(8,128)S(1)}, bf16[1920,256]{1,0:T(8,128)(2,1)S(1)}, f32[2,32,512]{2,1,0:T(8,128)S(1)}, f32[1024,256]{1,0:T(8,128)S(1)}, bf16[10...) custom-call(bf16[1024,512]{1,0:T(8,128)(2,1)S(1)} %get-tuple-element.258.refs_0_, ...), custom_call_target="tpu_custom_call" | custom-call | flops 2147483648 | bytes 9461760 | tf_op jit(solution)/shard_map/window_4/pallas_call | solution.py:146
  87.4 5.3 %up_two_back.1 = (f32[1024,256]{1,0:T(8,128)S(1)}, bf16[1024,1920]{1,0:T(8,128)(2,1)S(1)}, f32[40,256]{1,0:T(8,128)S(1)}, f32[32,256]{1,0:T(8,128)S(1)}, f32[8,1...) custom-call(s32[4]{0:T(128)S(1)} %pad_add_fusion.refs_0_, ...), custom_call_target="tpu_custom_call", output_to_operand_aliasing={{5}: (15, {}), {6}: (14, {}), {7}: (16, {}), {8}: (17, {})} | custom-call | flops 1006632960 | bytes 15355920 | tf_op jit(solution)/shard_map/up_two_back/pallas_call | solution.py:146
  96.9 2.3 %window_5.1 = (f32[128,128]{1,0:T(8,128)S(1)}, bf16[512,1152]{1,0:T(8,128)(2,1)S(1)}, f32[2,32,256]{2,1,0:T(8,128)S(1)}, f32[1024,512]{1,0:T(8,128)S(1)}, f32[8,128]{1,0:T(8,128)S(1)}) custom-call(bf16[1024,256]{1,0:T(8,128)(2,1)S(1)} %get-tuple-element.278.refs_0_, bf16[1024,1920]{1,0:T(8,128)(2,1)S(1)} %get-tuple-element.279.refs_1_, ...), custom_call_target="tpu_custom_call" | custom-call | flops 1006632960 | bytes 11147264 | tf_op jit(solution)/shard_map/window_5/pallas_call | solution.py:146
  101.6 4.1 %down_two_back.1 = (f32[1024,512]{1,0:T(8,128)S(1)}, bf16[1024,256]{1,0:T(8,128)(2,1)S(1)}, f32[40,512]{1,0:T(8,128)S(1)}, f32[32,512]{1,0:T(8,128)S(1)}, f32[8,...) custom-call(s32[4]{0:T(128)S(1)} %pad_add_fusion.refs_0_, ...), custom_call_target="tpu_custom_call", output_to_operand_aliasing={{5}: (14, {}), {6}: (15, {}), {7}: (16, {})} | custom-call | flops 1207959552 | bytes 12664848 | tf_op jit(solution)/shard_map/down_two_back/pallas_call | solution.py:146
  107.7 2.2 %collective-permute-start.33 = (f32[40,512]{1,0:T(8,128)S(1)}, f32[40,512]{1,0:T(8,128)S(1)}, u32[]{:S(2)}, u32[]{:S(2)}) collective-permute-start(f32[40,512]{1,0:T(8,128)S(1)} %get-tuple-element.293), channel_id=1, source_target_pairs={{0,7},{2,1},{4,3},{6,5},{7,0},{1,2},{3,4},{5,6},{8,15},{10,9},{12,... | collective-permute-start | bytes 245768 | tf_op jit(solution)/shard_map/ppermute | solution.py:1386
  109.9 4.1 %window_6.1 = (f32[144,128]{1,0:T(8,128)S(1)}, f32[144,128]{1,0:T(8,128)S(1)}, bf16[256,1536]{1,0:T(8,128)(2,1)S(1)}, f32[2,32,512]{2,1,0:T(8,128)S(1)}, bf16[10...) custom-call(s32[4]{0:T(128)S(1)} %pad_add_fusion.refs_0_, bf16[1024,256]{1,0:T(8,128)(2,1)S(1)} %get-tuple-element.295.refs_1_, ...), custom_call_target="tpu_custom_call" | custom-call | flops 1006632960 | bytes 10592272 | tf_op jit(solution)/shard_map/window_6/pallas_call | solution.py:146
  115.3 3.3 %up_one_back.1 = (bf16[256,256]{1,0:T(8,128)(2,1)S(1)}, bf16[256,256]{1,0:T(8,128)(2,1)S(1)}, bf16[256,256]{1,0:T(8,128)(2,1)S(1)}, bf16[256,256]{1,0:T(8,128)(2,1)S(1)}, bf16[1024,512]{1,0:T(8,128)(2,1)S(1)}) custom-call(s32[4]{0:T(128)S(1)} %pad_add_fusion.refs_0_, f32[1024,512]{1,0:T(8,128)S(1)} %get-tuple-element.292.refs_1_, ...), custom_call_target="tpu_custom_call" | custom-call | flops 805306368 | bytes 6930448 | tf_op jit(solution)/shard_map/up_one_back/pallas_call | solution.py:146
  122.2 2.1 %window_7.1 = (bf16[176,128]{1,0:T(8,128)(2,1)S(1)}, f32[256,256]{1,0:T(8,128)S(1)}) custom-call(bf16[1024,512]{1,0:T(8,128)(2,1)S(1)} %get-tuple-element.310.refs_0_, bf16[1024,1024]{1,0:T(8,128)(2,1)S(1)} %get-tuple-element.311.refs_1_, f32[144,128]{1,0:T(8,128)S(1)} %get-tuple-element.312.refs_2_, f32[144,128]{1,0:T(8,128)S(1)} %collective-permute-done.41.refs_3_, ...), custom_call_target="tpu_custom_call" | custom-call | flops 1073741824 | bytes 3866624 | tf_op jit(solution)/shard_map/window_7/pallas_call | solution.py:146
  125.9 2.8 %collective-permute-start.42 = (bf16[176,128]{1,0:T(8,128)(2,1)S(1)}, bf16[176,128]{1,0:T(8,128)(2,1)S(1)}, u32[]{:S(2)}, u32[]{:S(2)}) collective-permute-start(bf16[176,128]{1,0:T(8,128)(2,1)S(1)} %get-tuple-element.317.refs_5_), channel_id=1, source_target_pairs={{0,2},{1,3},{2,0},{3,1},{4,6},{5,7},{6,4},{7,5},{8,10},{9,11},{10,... | collective-permute-start | bytes 135176 | tf_op jit(solution)/shard_map/ppermute | solution.py:1352
  (108 shorter events, 50.5 us)
Async XLA Ops:
  4.8 6.3 %collective-permute-start = (bf16[80,256]{1,0:T(8,128)(2,1)S(1)}, bf16[80,256]{1,0:T(8,128)(2,1)S(1)}, u32[]{:S(2)}, u32[]{:S(2)}) collective-permute-start(bf16[80,256]{1,0:T(8,128)(2,1)S(1)} %get-tuple-element.187), channel_id=1, source_target_pairs={{0,7},{2,1},{4,3},{6,5},{7,0},{1,2},{3,4},{5,6},{8,15},{10,9},{12,... | collective-permute-start | bytes 122888 | tf_op jit(solution)/shard_map/ppermute | solution.py:1456
  13.9 8.0 %collective-permute-start.2 = (f32[40,512]{1,0:T(8,128)S(1)}, f32[40,512]{1,0:T(8,128)S(1)}, u32[]{:S(2)}, u32[]{:S(2)}) collective-permute-start(f32[40,512]{1,0:T(8,128)S(1)} %get-tuple-element.196), channel_id=1, source_target_pairs={{0,7},{2,1},{4,3},{6,5},{7,0},{1,2},{3,4},{5,6},{8,15},{10,9},{12,... | collective-permute-start | bytes 245768 | tf_op jit(solution)/shard_map/ppermute | solution.py:1386
  27.4 7.1 %collective-permute-start.7 = (f32[40,256]{1,0:T(8,128)S(1)}, f32[40,256]{1,0:T(8,128)S(1)}, u32[]{:S(2)}, u32[]{:S(2)}) collective-permute-start(f32[40,256]{1,0:T(8,128)S(1)} %get-tuple-element.209), channel_id=1, source_target_pairs={{0,7},{2,1},{4,3},{6,5},{7,0},{1,2},{3,4},{5,6},{8,15},{10,9},{12,... | collective-permute-start | bytes 122888 | tf_op jit(solution)/shard_map/ppermute | solution.py:1386
  40.4 7.8 %collective-permute-start.12 = (f32[40,512]{1,0:T(8,128)S(1)}, f32[40,512]{1,0:T(8,128)S(1)}, u32[]{:S(2)}, u32[]{:S(2)}) collective-permute-start(f32[40,512]{1,0:T(8,128)S(1)} %get-tuple-element.218), channel_id=1, source_target_pairs={{0,7},{2,1},{4,3},{6,5},{7,0},{1,2},{3,4},{5,6},{8,15},{10,9},{12,... | collective-permute-start | bytes 245768 | tf_op jit(solution)/shard_map/ppermute | solution.py:1386
  54.1 7.1 %collective-permute-start.17 = (bf16[272,256]{1,0:T(8,128)(2,1)S(1)}, bf16[272,256]{1,0:T(8,128)(2,1)S(1)}, u32[]{:S(2)}, u32[]{:S(2)}) collective-permute-start(bf16[272,256]{1,0:T(8,128)(2,1)S(1)} %get-tuple-element.225), channel_id=1, source_target_pairs={{0,8},{8,0},{16,24},{24,16},{1,9},{9,1},{17,25},{25,17},{2,10},{10... | collective-permute-start | bytes 417800 | tf_op jit(solution)/shard_map/ppermute | solution.py:1352
  55.7 8.5 %collective-permute-start.18 = (bf16[272,256]{1,0:T(8,128)(2,1)S(1)}, bf16[272,256]{1,0:T(8,128)(2,1)S(1)}, u32[]{:S(2)}, u32[]{:S(2)}) collective-permute-start(bf16[272,256]{1,0:T(8,128)(2,1)S(1)} %get-tuple-element.226), channel_id=1, source_target_pairs={{0,16},{8,24},{16,0},{24,8},{1,17},{9,25},{17,1},{25,9},{2,18},{10... | collective-permute-start | bytes 417800 | tf_op jit(solution)/shard_map/ppermute | solution.py:1352
  57.2 6.9 %collective-permute-start.19 = (bf16[272,256]{1,0:T(8,128)(2,1)S(1)}, bf16[272,256]{1,0:T(8,128)(2,1)S(1)}, u32[]{:S(2)}, u32[]{:S(2)}) collective-permute-start(bf16[272,256]{1,0:T(8,128)(2,1)S(1)} %get-tuple-element.227), channel_id=1, source_target_pairs={{0,24},{8,16},{16,8},{24,0},{1,25},{9,17},{17,9},{25,1},{2,26},{10... | collective-permute-start | bytes 417800 | tf_op jit(solution)/shard_map/ppermute | solution.py:1352
  65.4 8.2 %collective-permute-start.20 = (bf16[272,256]{1,0:T(8,128)(2,1)S(1)}, bf16[272,256]{1,0:T(8,128)(2,1)S(1)}, u32[]{:S(2)}, u32[]{:S(2)}) collective-permute-start(bf16[272,256]{1,0:T(8,128)(2,1)S(1)} %get-tuple-element.246), channel_id=1, source_target_pairs={{0,8},{8,0},{16,24},{24,16},{1,9},{9,1},{17,25},{25,17},{2,10},{10... | collective-permute-start | bytes 417800 | tf_op jit(solution)/shard_map/ppermute | solution.py:1352
  66.7 7.6 %collective-permute-start.21 = (bf16[272,256]{1,0:T(8,128)(2,1)S(1)}, bf16[272,256]{1,0:T(8,128)(2,1)S(1)}, u32[]{:S(2)}, u32[]{:S(2)}) collective-permute-start(bf16[272,256]{1,0:T(8,128)(2,1)S(1)} %get-tuple-element.247), channel_id=1, source_target_pairs={{0,16},{8,24},{16,0},{24,8},{1,17},{9,25},{17,1},{25,9},{2,18},{10... | collective-permute-start | bytes 417800 | tf_op jit(solution)/shard_map/ppermute | solution.py:1352
  67.5 6.8 %collective-permute-start.22 = (bf16[272,256]{1,0:T(8,128)(2,1)S(1)}, bf16[272,256]{1,0:T(8,128)(2,1)S(1)}, u32[]{:S(2)}, u32[]{:S(2)}) collective-permute-start(bf16[272,256]{1,0:T(8,128)(2,1)S(1)} %get-tuple-element.248), channel_id=1, source_target_pairs={{0,24},{8,16},{16,8},{24,0},{1,25},{9,17},{17,9},{25,1},{2,26},{10... | collective-permute-start | bytes 417800 | tf_op jit(solution)/shard_map/ppermute | solution.py:1352
  77.7 8.1 %collective-permute-start.26 = (f32[8,128]{1,0:T(8,128)S(1)}, f32[8,128]{1,0:T(8,128)S(1)}, u32[]{:S(2)}, u32[]{:S(2)}) collective-permute-start(f32[8,128]{1,0:T(8,128)S(1)} %get-tuple-element.265.refs_7_), channel_id=1, source_target_pairs={{0,4},{1,5},{2,6},{3,7},{4,0},{5,1},{6,2},{7,3},{8,12},{9,13},{10,... | collective-permute-start | bytes 12296 | tf_op jit(solution)/shard_map/ppermute | solution.py:1352
  78.7 7.1 %collective-permute-start.25 = (f32[8,128]{1,0:T(8,128)S(1)}, f32[8,128]{1,0:T(8,128)S(1)}, u32[]{:S(2)}, u32[]{:S(2)}) collective-permute-start(f32[8,128]{1,0:T(8,128)S(1)} %get-tuple-element.265.refs_7_), channel_id=1, source_target_pairs={{0,3},{2,5},{4,7},{6,1},{3,0},{5,2},{7,4},{1,6},{8,11},{10,13},{12... | collective-permute-start | bytes 12296 | tf_op jit(solution)/shard_map/ppermute | solution.py:1388
  78.7 8.7 %collective-permute-start.24 = (f32[32,512]{1,0:T(8,128)S(1)}, f32[32,512]{1,0:T(8,128)S(1)}, u32[]{:S(2)}, u32[]{:S(2)}) collective-permute-start(f32[32,512]{1,0:T(8,128)S(1)} %get-tuple-element.257), channel_id=1, source_target_pairs={{0,1},{1,0},{2,3},{3,2},{4,5},{5,4},{6,7},{7,6},{8,9},{9,8},{10,11... | collective-permute-start | bytes 196616 | tf_op jit(solution)/shard_map/ppermute | solution.py:1352
  92.7 6.5 %collective-permute-start.31 = (f32[8,128]{1,0:T(8,128)S(1)}, f32[8,128]{1,0:T(8,128)S(1)}, u32[]{:S(2)}, u32[]{:S(2)}) collective-permute-start(f32[8,128]{1,0:T(8,128)S(1)} %get-tuple-element.283.refs_5_), channel_id=1, source_target_pairs={{0,4},{1,5},{2,6},{3,7},{4,0},{5,1},{6,2},{7,3},{8,12},{9,13},{10,... | collective-permute-start | bytes 12296 | tf_op jit(solution)/shard_map/ppermute | solution.py:1352
  94.4 7.2 %collective-permute-start.29 = (f32[32,256]{1,0:T(8,128)S(1)}, f32[32,256]{1,0:T(8,128)S(1)}, u32[]{:S(2)}, u32[]{:S(2)}) collective-permute-start(f32[32,256]{1,0:T(8,128)S(1)} %get-tuple-element.277), channel_id=1, source_target_pairs={{0,1},{1,0},{2,3},{3,2},{4,5},{5,4},{6,7},{7,6},{8,9},{9,8},{10,11... | collective-permute-start | bytes 98312 | tf_op jit(solution)/shard_map/ppermute | solution.py:1352
  105.7 8.2 %collective-permute-start.36 = (f32[8,128]{1,0:T(8,128)S(1)}, f32[8,128]{1,0:T(8,128)S(1)}, u32[]{:S(2)}, u32[]{:S(2)}) collective-permute-start(f32[8,128]{1,0:T(8,128)S(1)} %get-tuple-element.301.refs_8_), channel_id=1, source_target_pairs={{0,4},{1,5},{2,6},{3,7},{4,0},{5,1},{6,2},{7,3},{8,12},{9,13},{10,... | collective-permute-start | bytes 12296 | tf_op jit(solution)/shard_map/ppermute | solution.py:1352
  105.8 8.2 %collective-permute-start.35 = (f32[8,128]{1,0:T(8,128)S(1)}, f32[8,128]{1,0:T(8,128)S(1)}, u32[]{:S(2)}, u32[]{:S(2)}) collective-permute-start(f32[8,128]{1,0:T(8,128)S(1)} %get-tuple-element.301.refs_8_), channel_id=1, source_target_pairs={{0,3},{2,5},{4,7},{6,1},{3,0},{5,2},{7,4},{1,6},{8,11},{10,13},{12... | collective-permute-start | bytes 12296 | tf_op jit(solution)/shard_map/ppermute | solution.py:1388
  107.7 7.5 %collective-permute-start.34 = (f32[32,512]{1,0:T(8,128)S(1)}, f32[32,512]{1,0:T(8,128)S(1)}, u32[]{:S(2)}, u32[]{:S(2)}) collective-permute-start(f32[32,512]{1,0:T(8,128)S(1)} %get-tuple-element.294), channel_id=1, source_target_pairs={{0,1},{1,0},{2,3},{3,2},{4,5},{5,4},{6,7},{7,6},{8,9},{9,8},{10,11... | collective-permute-start | bytes 196616 | tf_op jit(solution)/shard_map/ppermute | solution.py:1352
  107.7 6.3 %collective-permute-start.33 = (f32[40,512]{1,0:T(8,128)S(1)}, f32[40,512]{1,0:T(8,128)S(1)}, u32[]{:S(2)}, u32[]{:S(2)}) collective-permute-start(f32[40,512]{1,0:T(8,128)S(1)} %get-tuple-element.293), channel_id=1, source_target_pairs={{0,7},{2,1},{4,3},{6,5},{7,0},{1,2},{3,4},{5,6},{8,15},{10,9},{12,... | collective-permute-start | bytes 245768 | tf_op jit(solution)/shard_map/ppermute | solution.py:1386
  114.1 8.0 %collective-permute-start.41 = (f32[144,128]{1,0:T(8,128)S(1)}, f32[144,128]{1,0:T(8,128)S(1)}, u32[]{:S(2)}, u32[]{:S(2)}) collective-permute-start(f32[144,128]{1,0:T(8,128)S(1)} %get-tuple-element.313), channel_id=1, source_target_pairs={{0,1},{1,0},{2,3},{3,2},{4,5},{5,4},{6,7},{7,6},{8,9},{9,8},{10,11... | collective-permute-start | bytes 221192 | tf_op jit(solution)/shard_map/ppermute | solution.py:1352
  118.6 7.3 %collective-permute-start.38 = (bf16[256,256]{1,0:T(8,128)(2,1)S(1)}, bf16[256,256]{1,0:T(8,128)(2,1)S(1)}, u32[]{:S(2)}, u32[]{:S(2)}) collective-permute-start(bf16[256,256]{1,0:T(8,128)(2,1)S(1)} %get-tuple-element.307), channel_id=1, source_target_pairs={{0,8},{8,0},{16,24},{24,16},{1,9},{9,1},{17,25},{25,17},{2,10},{10... | collective-permute-start | bytes 393224 | tf_op jit(solution)/shard_map/ppermute | solution.py:1352
  119.8 8.9 %collective-permute-start.39 = (bf16[256,256]{1,0:T(8,128)(2,1)S(1)}, bf16[256,256]{1,0:T(8,128)(2,1)S(1)}, u32[]{:S(2)}, u32[]{:S(2)}) collective-permute-start(bf16[256,256]{1,0:T(8,128)(2,1)S(1)} %get-tuple-element.308), channel_id=1, source_target_pairs={{0,16},{8,24},{16,0},{24,8},{1,17},{9,25},{17,1},{25,9},{2,18},{10... | collective-permute-start | bytes 393224 | tf_op jit(solution)/shard_map/ppermute | solution.py:1352
  120.8 7.9 %collective-permute-start.40 = (bf16[256,256]{1,0:T(8,128)(2,1)S(1)}, bf16[256,256]{1,0:T(8,128)(2,1)S(1)}, u32[]{:S(2)}, u32[]{:S(2)}) collective-permute-start(bf16[256,256]{1,0:T(8,128)(2,1)S(1)} %get-tuple-element.309), channel_id=1, source_target_pairs={{0,24},{8,16},{16,8},{24,0},{1,25},{9,17},{17,9},{25,1},{2,26},{10... | collective-permute-start | bytes 393224 | tf_op jit(solution)/shard_map/ppermute | solution.py:1352
  124.3 6.3 %collective-permute-start.44 = (bf16[176,128]{1,0:T(8,128)(2,1)S(1)}, bf16[176,128]{1,0:T(8,128)(2,1)S(1)}, u32[]{:S(2)}, u32[]{:S(2)}) collective-permute-start(bf16[176,128]{1,0:T(8,128)(2,1)S(1)} %get-tuple-element.317.refs_5_), channel_id=1, source_target_pairs={{0,6},{1,7},{2,4},{3,5},{4,2},{5,3},{6,0},{7,1},{8,14},{9,15},{10,... | collective-permute-start | bytes 135176 | tf_op jit(solution)/shard_map/ppermute | solution.py:1352
  (24 other events, 102.9 us)

commit v8 on v7

--- a/solution.py
+++ b/solution.py
@@ -196,7 +196,7 @@
 
 
 def for_blocks_rims(fn):
-    group = 5
+    group = 10
 
     def several(first, count, has_prev, has_next):
         stores = []

time: 135 us -> 135 us (level)
  no operation moved by 1% of the time
where the time goes in v8:
time: 135 us
  Pallas kernels  71 us (53%)
  starting transfers between devices  47.2 us (35%)
  waiting for transfers between devices  15.2 us (11%)
    pallas_call x22, Pallas kernels, run(): pl.pallas_call(body, out_shape=[pltpu.HBM(o[0], o[1]) if len(o) == 3 else...  71 us
    ppermute x33, starting transfers between devices, flip(): lax.ppermute(values, axis, [(i, i ^ bit) for i in range(lax.axis_size(axi...  22.2 us
    ppermute x33, waiting for transfers between devices, flip(): lax.ppermute(values, axis, [(i, i ^ bit) for i in range(lax.axis_size(axi...  13.4 us
    ppermute x6, starting transfers between devices, exchange(): near = lax.ppermute(cross, axis, pairs(count, -1))  13.4 us
    ppermute x6, starting transfers between devices, exchange(): far = lax.ppermute(mom, axis, pairs(count, 3))  7.12 us
    ppermute x1, starting transfers between devices, per_device(): near = lax.ppermute(cross, 'tm', pairs(lax.axis_size('tm'), -1))  4.55 us
  transfers between devices with their start and end apart: 46, of which 14 were waited for; matrix products, arithmetic and copies ran while one was open for 0% of the time, Pallas kernels for 26%

profile of v8, /device:TPU:0, one launch (start us, length us, event | category | flops | bytes accessed | tf_op | source)
XLA Modules:
  0.0 134.8 jit_solution(11139075942617913604)
XLA Ops:
  0.7 4.1 %layout.1 = (bf16[80,256]{1,0:T(8,128)(2,1)S(1)}, bf16[80,256]{1,0:T(8,128)(2,1)S(1)}, bf16[1024,256]{1,0:T(8,128)(2,1)S(1)}, bf16[1024,256]{1,0:T(8,128)(2,1)S(...) custom-call(s32[4]{0:T(128)S(1)} %pad_add_fusion.refs_0_, ...), custom_call_target="tpu_custom_call" | custom-call | bytes 2188992 | tf_op jit(solution)/shard_map/layout/pallas_call | solution.py:146
  4.8 4.6 %collective-permute-start = (bf16[80,256]{1,0:T(8,128)(2,1)S(1)}, bf16[80,256]{1,0:T(8,128)(2,1)S(1)}, u32[]{:S(2)}, u32[]{:S(2)}) collective-permute-start(bf16[80,256]{1,0:T(8,128)(2,1)S(1)} %get-tuple-element.187), channel_id=1, source_target_pairs={{0,7},{2,1},{4,3},{6,5},{7,0},{1,2},{3,4},{5,6},{8,15},{10,9},{12,... | collective-permute-start | bytes 122888 | tf_op jit(solution)/shard_map/ppermute | solution.py:1456
  11.2 2.6 %conv_one.1 = (f32[1024,512]{1,0:T(8,128)S(1)}, f32[40,512]{1,0:T(8,128)S(1)}, f32[32,512]{1,0:T(8,128)S(1)}, f32[8,128]{1,0:T(8,128)S(1)}, f32[8,128]{1,0:T(8,1...) custom-call(s32[4]{0:T(128)S(1)} %pad_add_fusion.refs_0_, ...), custom_call_target="tpu_custom_call" | custom-call | flops 1073741824 | bytes 6152208 | tf_op jit(solution)/shard_map/conv_one/pallas_call | solution.py:146
  13.8 3.5 %collective-permute-start.2 = (f32[40,512]{1,0:T(8,128)S(1)}, f32[40,512]{1,0:T(8,128)S(1)}, u32[]{:S(2)}, u32[]{:S(2)}) collective-permute-start(f32[40,512]{1,0:T(8,128)S(1)} %get-tuple-element.196), channel_id=1, source_target_pairs={{0,7},{2,1},{4,3},{6,5},{7,0},{1,2},{3,4},{5,6},{8,15},{10,9},{12,... | collective-permute-start | bytes 245768 | tf_op jit(solution)/shard_map/ppermute | solution.py:1386
  18.5 2.4 %window_1.1 = (bf16[1920,256]{1,0:T(8,128)(2,1)S(1)}, f32[1024,512]{1,0:T(8,128)}, f32[64,256]{1,0:T(8,128)}, bf16[1024,1024]{1,0:T(8,128)(2,1)}, f32[1024,512]{1,0:T(8,128)S(1)}, /*index=5*/f32[8,128]{1,0:T(8,128)S(1)}) custom-call(bf16[400,32]{1,0:T(8,128)(2,1)S(1)} %bitcast.46, ...), custom_call_target="tpu_custom_call", output_to_operand_aliasing={{4}: (1, {})} | custom-call | bytes 11629568 | tf_op jit(solution)/shard_map/window_1/pallas_call | solution.py:146
  23.1 4.3 %conv_two.1 = (f32[1024,256]{1,0:T(8,128)S(1)}, f32[40,256]{1,0:T(8,128)S(1)}, f32[32,256]{1,0:T(8,128)S(1)}, f32[8,128]{1,0:T(8,128)S(1)}, bf16[4,32,512]{2,1,0...) custom-call(s32[4]{0:T(128)S(1)} %pad_add_fusion.refs_0_, ...), custom_call_target="tpu_custom_call" | custom-call | flops 1006632960 | bytes 8384528 | tf_op jit(solution)/shard_map/conv_two/pallas_call | solution.py:146
  27.3 2.2 %collective-permute-start.7 = (f32[40,256]{1,0:T(8,128)S(1)}, f32[40,256]{1,0:T(8,128)S(1)}, u32[]{:S(2)}, u32[]{:S(2)}) collective-permute-start(f32[40,256]{1,0:T(8,128)S(1)} %get-tuple-element.209), channel_id=1, source_target_pairs={{0,7},{2,1},{4,3},{6,5},{7,0},{1,2},{3,4},{5,6},{8,15},{10,9},{12,... | collective-permute-start | bytes 122888 | tf_op jit(solution)/shard_map/ppermute | solution.py:1386
  31.7 2.7 %window_2.1 = (bf16[512,1152]{1,0:T(8,128)(2,1)S(1)}, bf16[1024,1920]{1,0:T(8,128)(2,1)}, f32[1024,256]{1,0:T(8,128)}, bf16[4,32,512]{2,1,0:T(8,128)(2,1)}, f32[...) custom-call(bf16[400,32]{1,0:T(8,128)(2,1)S(1)} %bitcast.44, ...), custom_call_target="tpu_custom_call", output_to_operand_aliasing={{5}: (2, {})} | custom-call | bytes 12489728 | tf_op jit(solution)/shard_map/window_2/pallas_call | solution.py:146
  36.0 4.4 %up_two.1 = (f32[1024,512]{1,0:T(8,128)S(1)}, f32[40,512]{1,0:T(8,128)S(1)}, f32[32,512]{1,0:T(8,128)S(1)}, f32[8,128]{1,0:T(8,128)S(1)}, f32[2,32,256]{2,1,0:T(8,128)S(1)}, /*index=5*/bf16[1024,256]{1,0:T(8,128)(2,1)S(1)}) custom-call(s32[4]{0:T(128)S(1)} %pad_add_fusion.refs_0_, f32[1024,256]{1,0:T(8,128)S(1)} %get-tuple-element.208.refs_1_, ...), custom_call_target="tpu_custom_call" | custom-call | flops 1207959552 | bytes 5171216 | tf_op jit(solution)/shard_map/up_two/pallas_call | solution.py:146
  44.9 3.2 %window_3.1 = (bf16[256,3072]{1,0:T(8,128)(2,1)S(1)}, bf16[1024,1536]{1,0:T(8,128)(2,1)S(1)}, bf16[4,32,512]{2,1,0:T(8,128)(2,1)S(1)}, f32[1024,512]{1,0:T(8,128...) custom-call(f32[2,56,128]{2,1,0:T(8,128)S(1)} %get-tuple-element.186, ...), custom_call_target="tpu_custom_call", output_to_operand_aliasing={{6}: (3, {})} | custom-call | bytes 16254976 | tf_op jit(solution)/shard_map/window_3/pallas_call | solution.py:146
  49.4 4.7 %up_one.1 = (bf16[272,256]{1,0:T(8,128)(2,1)S(1)}, bf16[272,256]{1,0:T(8,128)(2,1)S(1)}, bf16[272,256]{1,0:T(8,128)(2,1)S(1)}, bf16[272,256]{1,0:T(8,128)(2,1)S(...) custom-call(s32[4]{0:T(128)S(1)} %pad_add_fusion.refs_0_, ...), custom_call_target="tpu_custom_call" | custom-call | flops 1610612736 | bytes 9879568 | tf_op jit(solution)/shard_map/up_one/pallas_call | solution.py:146
  57.6 3.6 %window_swap.1 = (bf16[1920,256]{1,0:T(8,128)(2,1)}, bf16[512,1152]{1,0:T(8,128)(2,1)}, bf16[256,1536]{1,0:T(8,128)(2,1)}, bf16[1024,256]{1,0:T(8,128)(2,1)S(1)}...) custom-call(bf16[400,32]{1,0:T(8,128)(2,1)S(1)} %bitcast.47, ...), custom_call_target="tpu_custom_call" | custom-call | bytes 9652224 | tf_op jit(solution)/shard_map/window_swap/pallas_call | solution.py:146
  61.2 2.9 %collective-permute-done.18.refs_3_ = bf16[272,256]{1,0:T(8,128)(2,1)S(1)} collective-permute-done((bf16[272,256]{1,0:T(8,128)(2,1)S(1)}, bf16[272,256]{1,0:T(8,128)(2,1)S(1)}, u32[]{:S(2)}, u32[]{:S(2)}) %collective-permute-start.18) | collective-permute-done | bytes 139296 | tf_op jit(solution)/shard_map/ppermute | solution.py:1352
  68.9 4.6 %estimate.1 = (bf16[4,2,128,256]{3,2,1,0:T(8,128)(2,1)}, bf16[1024,1024]{1,0:T(8,128)(2,1)S(1)}, f32[1024,256]{1,0:T(8,128)S(1)}, f32[32,256]{1,0:T(8,128)S(1)},...) custom-call(s32[4]{0:T(128)S(1)} %pad_add_fusion.refs_0_, ...), custom_call_target="tpu_custom_call" | custom-call | bytes 17197072 | tf_op jit(solution)/shard_map/estimate/pallas_call | solution.py:146
  74.3 3.3 %down_one_back.1 = (f32[1024,512]{1,0:T(8,128)S(1)}, bf16[1024,1024]{1,0:T(8,128)(2,1)S(1)}, f32[40,512]{1,0:T(8,128)S(1)}, f32[32,512]{1,0:T(8,128)S(1)}, f32[8...) custom-call(s32[4]{0:T(128)S(1)} %pad_add_fusion.refs_0_, ...), custom_call_target="tpu_custom_call", output_to_operand_aliasing={{7}: (10, {}), {8}: (12, {}), {9}: (13, {})} | custom-call | flops 2147483648 | bytes 16564240 | tf_op jit(solution)/shard_map/down_one_back/pallas_call | solution.py:146
  81.8 3.9 %window_4.1 = (f32[32,128]{1,0:T(8,128)S(1)}, bf16[1920,256]{1,0:T(8,128)(2,1)S(1)}, f32[2,32,512]{2,1,0:T(8,128)S(1)}, f32[1024,256]{1,0:T(8,128)S(1)}, bf16[10...) custom-call(bf16[1024,512]{1,0:T(8,128)(2,1)S(1)} %get-tuple-element.258.refs_0_, ...), custom_call_target="tpu_custom_call" | custom-call | flops 2147483648 | bytes 9461760 | tf_op jit(solution)/shard_map/window_4/pallas_call | solution.py:146
  87.3 5.3 %up_two_back.1 = (f32[1024,256]{1,0:T(8,128)S(1)}, bf16[1024,1920]{1,0:T(8,128)(2,1)S(1)}, f32[40,256]{1,0:T(8,128)S(1)}, f32[32,256]{1,0:T(8,128)S(1)}, f32[8,1...) custom-call(s32[4]{0:T(128)S(1)} %pad_add_fusion.refs_0_, ...), custom_call_target="tpu_custom_call", output_to_operand_aliasing={{5}: (15, {}), {6}: (14, {}), {7}: (16, {}), {8}: (17, {})} | custom-call | flops 1006632960 | bytes 15355920 | tf_op jit(solution)/shard_map/up_two_back/pallas_call | solution.py:146
  96.8 2.3 %window_5.1 = (f32[128,128]{1,0:T(8,128)S(1)}, bf16[512,1152]{1,0:T(8,128)(2,1)S(1)}, f32[2,32,256]{2,1,0:T(8,128)S(1)}, f32[1024,512]{1,0:T(8,128)S(1)}, f32[8,128]{1,0:T(8,128)S(1)}) custom-call(bf16[1024,256]{1,0:T(8,128)(2,1)S(1)} %get-tuple-element.278.refs_0_, bf16[1024,1920]{1,0:T(8,128)(2,1)S(1)} %get-tuple-element.279.refs_1_, ...), custom_call_target="tpu_custom_call" | custom-call | flops 1006632960 | bytes 11147264 | tf_op jit(solution)/shard_map/window_5/pallas_call | solution.py:146
  101.6 4.1 %down_two_back.1 = (f32[1024,512]{1,0:T(8,128)S(1)}, bf16[1024,256]{1,0:T(8,128)(2,1)S(1)}, f32[40,512]{1,0:T(8,128)S(1)}, f32[32,512]{1,0:T(8,128)S(1)}, f32[8,...) custom-call(s32[4]{0:T(128)S(1)} %pad_add_fusion.refs_0_, ...), custom_call_target="tpu_custom_call", output_to_operand_aliasing={{5}: (14, {}), {6}: (15, {}), {7}: (16, {})} | custom-call | flops 1207959552 | bytes 12664848 | tf_op jit(solution)/shard_map/down_two_back/pallas_call | solution.py:146
  107.7 2.2 %collective-permute-start.33 = (f32[40,512]{1,0:T(8,128)S(1)}, f32[40,512]{1,0:T(8,128)S(1)}, u32[]{:S(2)}, u32[]{:S(2)}) collective-permute-start(f32[40,512]{1,0:T(8,128)S(1)} %get-tuple-element.293), channel_id=1, source_target_pairs={{0,7},{2,1},{4,3},{6,5},{7,0},{1,2},{3,4},{5,6},{8,15},{10,9},{12,... | collective-permute-start | bytes 245768 | tf_op jit(solution)/shard_map/ppermute | solution.py:1386
  109.9 4.1 %window_6.1 = (f32[144,128]{1,0:T(8,128)S(1)}, f32[144,128]{1,0:T(8,128)S(1)}, bf16[256,1536]{1,0:T(8,128)(2,1)S(1)}, f32[2,32,512]{2,1,0:T(8,128)S(1)}, bf16[10...) custom-call(s32[4]{0:T(128)S(1)} %pad_add_fusion.refs_0_, bf16[1024,256]{1,0:T(8,128)(2,1)S(1)} %get-tuple-element.295.refs_1_, ...), custom_call_target="tpu_custom_call" | custom-call | flops 1006632960 | bytes 10592272 | tf_op jit(solution)/shard_map/window_6/pallas_call | solution.py:146
  115.2 3.3 %up_one_back.1 = (bf16[256,256]{1,0:T(8,128)(2,1)S(1)}, bf16[256,256]{1,0:T(8,128)(2,1)S(1)}, bf16[256,256]{1,0:T(8,128)(2,1)S(1)}, bf16[256,256]{1,0:T(8,128)(2,1)S(1)}, bf16[1024,512]{1,0:T(8,128)(2,1)S(1)}) custom-call(s32[4]{0:T(128)S(1)} %pad_add_fusion.refs_0_, f32[1024,512]{1,0:T(8,128)S(1)} %get-tuple-element.292.refs_1_, ...), custom_call_target="tpu_custom_call" | custom-call | flops 805306368 | bytes 6930448 | tf_op jit(solution)/shard_map/up_one_back/pallas_call | solution.py:146
  122.1 2.1 %window_7.1 = (bf16[176,128]{1,0:T(8,128)(2,1)S(1)}, f32[256,256]{1,0:T(8,128)S(1)}) custom-call(bf16[1024,512]{1,0:T(8,128)(2,1)S(1)} %get-tuple-element.310.refs_0_, bf16[1024,1024]{1,0:T(8,128)(2,1)S(1)} %get-tuple-element.311.refs_1_, f32[144,128]{1,0:T(8,128)S(1)} %get-tuple-element.312.refs_2_, f32[144,128]{1,0:T(8,128)S(1)} %collective-permute-done.41.refs_3_, ...), custom_call_target="tpu_custom_call" | custom-call | flops 1073741824 | bytes 3866624 | tf_op jit(solution)/shard_map/window_7/pallas_call | solution.py:146
  125.8 2.8 %collective-permute-start.42 = (bf16[176,128]{1,0:T(8,128)(2,1)S(1)}, bf16[176,128]{1,0:T(8,128)(2,1)S(1)}, u32[]{:S(2)}, u32[]{:S(2)}) collective-permute-start(bf16[176,128]{1,0:T(8,128)(2,1)S(1)} %get-tuple-element.317.refs_5_), channel_id=1, source_target_pairs={{0,2},{1,3},{2,0},{3,1},{4,6},{5,7},{6,4},{7,5},{8,10},{9,11},{10,... | collective-permute-start | bytes 135176 | tf_op jit(solution)/shard_map/ppermute | solution.py:1352
  (108 shorter events, 50.5 us)
Async XLA Ops:
  4.8 6.3 %collective-permute-start = (bf16[80,256]{1,0:T(8,128)(2,1)S(1)}, bf16[80,256]{1,0:T(8,128)(2,1)S(1)}, u32[]{:S(2)}, u32[]{:S(2)}) collective-permute-start(bf16[80,256]{1,0:T(8,128)(2,1)S(1)} %get-tuple-element.187), channel_id=1, source_target_pairs={{0,7},{2,1},{4,3},{6,5},{7,0},{1,2},{3,4},{5,6},{8,15},{10,9},{12,... | collective-permute-start | bytes 122888 | tf_op jit(solution)/shard_map/ppermute | solution.py:1456
  13.8 8.0 %collective-permute-start.2 = (f32[40,512]{1,0:T(8,128)S(1)}, f32[40,512]{1,0:T(8,128)S(1)}, u32[]{:S(2)}, u32[]{:S(2)}) collective-permute-start(f32[40,512]{1,0:T(8,128)S(1)} %get-tuple-element.196), channel_id=1, source_target_pairs={{0,7},{2,1},{4,3},{6,5},{7,0},{1,2},{3,4},{5,6},{8,15},{10,9},{12,... | collective-permute-start | bytes 245768 | tf_op jit(solution)/shard_map/ppermute | solution.py:1386
  27.3 7.1 %collective-permute-start.7 = (f32[40,256]{1,0:T(8,128)S(1)}, f32[40,256]{1,0:T(8,128)S(1)}, u32[]{:S(2)}, u32[]{:S(2)}) collective-permute-start(f32[40,256]{1,0:T(8,128)S(1)} %get-tuple-element.209), channel_id=1, source_target_pairs={{0,7},{2,1},{4,3},{6,5},{7,0},{1,2},{3,4},{5,6},{8,15},{10,9},{12,... | collective-permute-start | bytes 122888 | tf_op jit(solution)/shard_map/ppermute | solution.py:1386
  40.4 7.8 %collective-permute-start.12 = (f32[40,512]{1,0:T(8,128)S(1)}, f32[40,512]{1,0:T(8,128)S(1)}, u32[]{:S(2)}, u32[]{:S(2)}) collective-permute-start(f32[40,512]{1,0:T(8,128)S(1)} %get-tuple-element.218), channel_id=1, source_target_pairs={{0,7},{2,1},{4,3},{6,5},{7,0},{1,2},{3,4},{5,6},{8,15},{10,9},{12,... | collective-permute-start | bytes 245768 | tf_op jit(solution)/shard_map/ppermute | solution.py:1386
  54.1 7.1 %collective-permute-start.17 = (bf16[272,256]{1,0:T(8,128)(2,1)S(1)}, bf16[272,256]{1,0:T(8,128)(2,1)S(1)}, u32[]{:S(2)}, u32[]{:S(2)}) collective-permute-start(bf16[272,256]{1,0:T(8,128)(2,1)S(1)} %get-tuple-element.225), channel_id=1, source_target_pairs={{0,8},{8,0},{16,24},{24,16},{1,9},{9,1},{17,25},{25,17},{2,10},{10... | collective-permute-start | bytes 417800 | tf_op jit(solution)/shard_map/ppermute | solution.py:1352
  55.6 8.4 %collective-permute-start.18 = (bf16[272,256]{1,0:T(8,128)(2,1)S(1)}, bf16[272,256]{1,0:T(8,128)(2,1)S(1)}, u32[]{:S(2)}, u32[]{:S(2)}) collective-permute-start(bf16[272,256]{1,0:T(8,128)(2,1)S(1)} %get-tuple-element.226), channel_id=1, source_target_pairs={{0,16},{8,24},{16,0},{24,8},{1,17},{9,25},{17,1},{25,9},{2,18},{10... | collective-permute-start | bytes 417800 | tf_op jit(solution)/shard_map/ppermute | solution.py:1352
  57.2 6.9 %collective-permute-start.19 = (bf16[272,256]{1,0:T(8,128)(2,1)S(1)}, bf16[272,256]{1,0:T(8,128)(2,1)S(1)}, u32[]{:S(2)}, u32[]{:S(2)}) collective-permute-start(bf16[272,256]{1,0:T(8,128)(2,1)S(1)} %get-tuple-element.227), channel_id=1, source_target_pairs={{0,24},{8,16},{16,8},{24,0},{1,25},{9,17},{17,9},{25,1},{2,26},{10... | collective-permute-start | bytes 417800 | tf_op jit(solution)/shard_map/ppermute | solution.py:1352
  65.3 8.2 %collective-permute-start.20 = (bf16[272,256]{1,0:T(8,128)(2,1)S(1)}, bf16[272,256]{1,0:T(8,128)(2,1)S(1)}, u32[]{:S(2)}, u32[]{:S(2)}) collective-permute-start(bf16[272,256]{1,0:T(8,128)(2,1)S(1)} %get-tuple-element.246), channel_id=1, source_target_pairs={{0,8},{8,0},{16,24},{24,16},{1,9},{9,1},{17,25},{25,17},{2,10},{10... | collective-permute-start | bytes 417800 | tf_op jit(solution)/shard_map/ppermute | solution.py:1352
  66.6 7.6 %collective-permute-start.21 = (bf16[272,256]{1,0:T(8,128)(2,1)S(1)}, bf16[272,256]{1,0:T(8,128)(2,1)S(1)}, u32[]{:S(2)}, u32[]{:S(2)}) collective-permute-start(bf16[272,256]{1,0:T(8,128)(2,1)S(1)} %get-tuple-element.247), channel_id=1, source_target_pairs={{0,16},{8,24},{16,0},{24,8},{1,17},{9,25},{17,1},{25,9},{2,18},{10... | collective-permute-start | bytes 417800 | tf_op jit(solution)/shard_map/ppermute | solution.py:1352
  67.5 6.8 %collective-permute-start.22 = (bf16[272,256]{1,0:T(8,128)(2,1)S(1)}, bf16[272,256]{1,0:T(8,128)(2,1)S(1)}, u32[]{:S(2)}, u32[]{:S(2)}) collective-permute-start(bf16[272,256]{1,0:T(8,128)(2,1)S(1)} %get-tuple-element.248), channel_id=1, source_target_pairs={{0,24},{8,16},{16,8},{24,0},{1,25},{9,17},{17,9},{25,1},{2,26},{10... | collective-permute-start | bytes 417800 | tf_op jit(solution)/shard_map/ppermute | solution.py:1352
  77.6 8.1 %collective-permute-start.26 = (f32[8,128]{1,0:T(8,128)S(1)}, f32[8,128]{1,0:T(8,128)S(1)}, u32[]{:S(2)}, u32[]{:S(2)}) collective-permute-start(f32[8,128]{1,0:T(8,128)S(1)} %get-tuple-element.265.refs_7_), channel_id=1, source_target_pairs={{0,4},{1,5},{2,6},{3,7},{4,0},{5,1},{6,2},{7,3},{8,12},{9,13},{10,... | collective-permute-start | bytes 12296 | tf_op jit(solution)/shard_map/ppermute | solution.py:1352
  78.6 7.1 %collective-permute-start.25 = (f32[8,128]{1,0:T(8,128)S(1)}, f32[8,128]{1,0:T(8,128)S(1)}, u32[]{:S(2)}, u32[]{:S(2)}) collective-permute-start(f32[8,128]{1,0:T(8,128)S(1)} %get-tuple-element.265.refs_7_), channel_id=1, source_target_pairs={{0,3},{2,5},{4,7},{6,1},{3,0},{5,2},{7,4},{1,6},{8,11},{10,13},{12... | collective-permute-start | bytes 12296 | tf_op jit(solution)/shard_map/ppermute | solution.py:1388
  78.6 8.7 %collective-permute-start.24 = (f32[32,512]{1,0:T(8,128)S(1)}, f32[32,512]{1,0:T(8,128)S(1)}, u32[]{:S(2)}, u32[]{:S(2)}) collective-permute-start(f32[32,512]{1,0:T(8,128)S(1)} %get-tuple-element.257), channel_id=1, source_target_pairs={{0,1},{1,0},{2,3},{3,2},{4,5},{5,4},{6,7},{7,6},{8,9},{9,8},{10,11... | collective-permute-start | bytes 196616 | tf_op jit(solution)/shard_map/ppermute | solution.py:1352
  92.7 6.5 %collective-permute-start.31 = (f32[8,128]{1,0:T(8,128)S(1)}, f32[8,128]{1,0:T(8,128)S(1)}, u32[]{:S(2)}, u32[]{:S(2)}) collective-permute-start(f32[8,128]{1,0:T(8,128)S(1)} %get-tuple-element.283.refs_5_), channel_id=1, source_target_pairs={{0,4},{1,5},{2,6},{3,7},{4,0},{5,1},{6,2},{7,3},{8,12},{9,13},{10,... | collective-permute-start | bytes 12296 | tf_op jit(solution)/shard_map/ppermute | solution.py:1352
  94.4 7.2 %collective-permute-start.29 = (f32[32,256]{1,0:T(8,128)S(1)}, f32[32,256]{1,0:T(8,128)S(1)}, u32[]{:S(2)}, u32[]{:S(2)}) collective-permute-start(f32[32,256]{1,0:T(8,128)S(1)} %get-tuple-element.277), channel_id=1, source_target_pairs={{0,1},{1,0},{2,3},{3,2},{4,5},{5,4},{6,7},{7,6},{8,9},{9,8},{10,11... | collective-permute-start | bytes 98312 | tf_op jit(solution)/shard_map/ppermute | solution.py:1352
  105.7 8.2 %collective-permute-start.36 = (f32[8,128]{1,0:T(8,128)S(1)}, f32[8,128]{1,0:T(8,128)S(1)}, u32[]{:S(2)}, u32[]{:S(2)}) collective-permute-start(f32[8,128]{1,0:T(8,128)S(1)} %get-tuple-element.301.refs_8_), channel_id=1, source_target_pairs={{0,4},{1,5},{2,6},{3,7},{4,0},{5,1},{6,2},{7,3},{8,12},{9,13},{10,... | collective-permute-start | bytes 12296 | tf_op jit(solution)/shard_map/ppermute | solution.py:1352
  105.8 8.2 %collective-permute-start.35 = (f32[8,128]{1,0:T(8,128)S(1)}, f32[8,128]{1,0:T(8,128)S(1)}, u32[]{:S(2)}, u32[]{:S(2)}) collective-permute-start(f32[8,128]{1,0:T(8,128)S(1)} %get-tuple-element.301.refs_8_), channel_id=1, source_target_pairs={{0,3},{2,5},{4,7},{6,1},{3,0},{5,2},{7,4},{1,6},{8,11},{10,13},{12... | collective-permute-start | bytes 12296 | tf_op jit(solution)/shard_map/ppermute | solution.py:1388
  107.7 7.5 %collective-permute-start.34 = (f32[32,512]{1,0:T(8,128)S(1)}, f32[32,512]{1,0:T(8,128)S(1)}, u32[]{:S(2)}, u32[]{:S(2)}) collective-permute-start(f32[32,512]{1,0:T(8,128)S(1)} %get-tuple-element.294), channel_id=1, source_target_pairs={{0,1},{1,0},{2,3},{3,2},{4,5},{5,4},{6,7},{7,6},{8,9},{9,8},{10,11... | collective-permute-start | bytes 196616 | tf_op jit(solution)/shard_map/ppermute | solution.py:1352
  107.7 6.3 %collective-permute-start.33 = (f32[40,512]{1,0:T(8,128)S(1)}, f32[40,512]{1,0:T(8,128)S(1)}, u32[]{:S(2)}, u32[]{:S(2)}) collective-permute-start(f32[40,512]{1,0:T(8,128)S(1)} %get-tuple-element.293), channel_id=1, source_target_pairs={{0,7},{2,1},{4,3},{6,5},{7,0},{1,2},{3,4},{5,6},{8,15},{10,9},{12,... | collective-permute-start | bytes 245768 | tf_op jit(solution)/shard_map/ppermute | solution.py:1386
  114.1 8.0 %collective-permute-start.41 = (f32[144,128]{1,0:T(8,128)S(1)}, f32[144,128]{1,0:T(8,128)S(1)}, u32[]{:S(2)}, u32[]{:S(2)}) collective-permute-start(f32[144,128]{1,0:T(8,128)S(1)} %get-tuple-element.313), channel_id=1, source_target_pairs={{0,1},{1,0},{2,3},{3,2},{4,5},{5,4},{6,7},{7,6},{8,9},{9,8},{10,11... | collective-permute-start | bytes 221192 | tf_op jit(solution)/shard_map/ppermute | solution.py:1352
  118.5 7.3 %collective-permute-start.38 = (bf16[256,256]{1,0:T(8,128)(2,1)S(1)}, bf16[256,256]{1,0:T(8,128)(2,1)S(1)}, u32[]{:S(2)}, u32[]{:S(2)}) collective-permute-start(bf16[256,256]{1,0:T(8,128)(2,1)S(1)} %get-tuple-element.307), channel_id=1, source_target_pairs={{0,8},{8,0},{16,24},{24,16},{1,9},{9,1},{17,25},{25,17},{2,10},{10... | collective-permute-start | bytes 393224 | tf_op jit(solution)/shard_map/ppermute | solution.py:1352
  119.7 8.9 %collective-permute-start.39 = (bf16[256,256]{1,0:T(8,128)(2,1)S(1)}, bf16[256,256]{1,0:T(8,128)(2,1)S(1)}, u32[]{:S(2)}, u32[]{:S(2)}) collective-permute-start(bf16[256,256]{1,0:T(8,128)(2,1)S(1)} %get-tuple-element.308), channel_id=1, source_target_pairs={{0,16},{8,24},{16,0},{24,8},{1,17},{9,25},{17,1},{25,9},{2,18},{10... | collective-permute-start | bytes 393224 | tf_op jit(solution)/shard_map/ppermute | solution.py:1352
  120.7 7.9 %collective-permute-start.40 = (bf16[256,256]{1,0:T(8,128)(2,1)S(1)}, bf16[256,256]{1,0:T(8,128)(2,1)S(1)}, u32[]{:S(2)}, u32[]{:S(2)}) collective-permute-start(bf16[256,256]{1,0:T(8,128)(2,1)S(1)} %get-tuple-element.309), channel_id=1, source_target_pairs={{0,24},{8,16},{16,8},{24,0},{1,25},{9,17},{17,9},{25,1},{2,26},{10... | collective-permute-start | bytes 393224 | tf_op jit(solution)/shard_map/ppermute | solution.py:1352
  124.2 6.3 %collective-permute-start.44 = (bf16[176,128]{1,0:T(8,128)(2,1)S(1)}, bf16[176,128]{1,0:T(8,128)(2,1)S(1)}, u32[]{:S(2)}, u32[]{:S(2)}) collective-permute-start(bf16[176,128]{1,0:T(8,128)(2,1)S(1)} %get-tuple-element.317.refs_5_), channel_id=1, source_target_pairs={{0,6},{1,7},{2,4},{3,5},{4,2},{5,3},{6,0},{7,1},{8,14},{9,15},{10,... | collective-permute-start | bytes 135176 | tf_op jit(solution)/shard_map/ppermute | solution.py:1352
  (24 other events, 102.9 us)
